TPU v7x, 32 devices: a whole 2x2x4 slice. The times are simulated.
32 devices in a mesh: az: 8 (over z, y), ax: 4 (over x, core).
Axes of the slice: x: 2, y: 2, z: 4, core: 2. Of those that a mesh axis runs over, the one named last changes fastest.
Arguments:
- velocity: float32 [3, 256, 512, 128], P(None, 'az', 'ax'), may hold values from -60 to 60
Outputs:
- increment: float32 [3, 256, 512, 128], P(None, 'az', 'ax')
- time_step: float32 [], replicated
All inputs are finite; a program needn't handle non-finite values.
Results may differ from a plain program's by a relative error of at most 0.0003.
Values sent between devices are 32-bit elements; how exact they have to be, the bound alone decides.
No kernel may reach another device: no remote copies, remote signals or barrier semaphores. Data moves between devices by JAX's collectives and lax.ppermute only.
A program may use at most 192 MiB of HBM per device.

v0:
```python
import math

import jax
import jax.numpy as jnp
from jax import lax
from jax.sharding import PartitionSpec as P

AXIAL_STEP = 0.01
VISCOSITY = 0.001
CFL_TARGET = 1.2
GAMMA = 8.0 / 15.0


def with_halo(cells, sides, width):
    for axis, dim in sides:
        count = lax.axis_size(axis)
        head = lax.slice_in_dim(cells, 0, width, axis=dim)
        tail = lax.slice_in_dim(cells, cells.shape[dim] - width, cells.shape[dim], axis=dim)
        cells = jnp.concatenate(
            [
                lax.ppermute(tail, axis, [(i, (i + 1) % count) for i in range(count)]),
                cells,
                lax.ppermute(head, axis, [((i + 1) % count, i) for i in range(count)]),
            ],
            axis=dim,
        )
    return cells


def shifted(block, axis, distance):
    devices = range(lax.axis_size(axis))
    route = [((i - distance) % len(devices), i) for i in devices]
    return lax.ppermute(block, axis, route)


def explicit_terms(padded, partner, theta_step):
    tangent_count = padded.shape[1] - 4
    axial_count = padded.shape[2] - 4
    radial_count = padded.shape[3]
    spacing_r = 1.0 / radial_count
    radial_index = jnp.arange(radial_count).astype(jnp.float32)
    centre = (radial_index + 0.5) * spacing_r
    facing = (radial_index + 1.0) * spacing_r
    wall_mask = jnp.where(radial_index < radial_count - 1.5, 1.0, 0.0).astype(jnp.float32)

    def values_at(component, theta_off, axial_off):
        piece = padded[
            component,
            2 + theta_off : 2 + theta_off + tangent_count,
            2 + axial_off : 2 + axial_off + axial_count,
            :,
        ]
        if component == 0:
            piece = piece * wall_mask
        return piece

    def inward(field, ghost):
        return jnp.concatenate([ghost[..., None], field[..., :-1]], axis=-1)

    def outward(field, ghost):
        return jnp.concatenate([field[..., 1:], ghost[..., None]], axis=-1)

    def below_axis(field):
        return inward(field, jnp.zeros_like(field[..., 0]))

    def beyond_wall(field):
        return outward(field, -field[..., -1])

    def periodic_parts(component, theta_flag):

        def sample(offset):
            return (
                values_at(component, offset, 0) if theta_flag else values_at(component, 0, offset)
            )

        spacing = theta_step if theta_flag else AXIAL_STEP
        first_der = (8.0 * (sample(1) - sample(-1)) - (sample(2) - sample(-2))) / (12.0 * spacing)
        second_der = (
            -sample(2) + 16.0 * sample(1) - 30.0 * sample(0) + 16.0 * sample(-1) - sample(-2)
        ) / (12.0 * spacing * spacing)
        return (first_der, second_der)

    def radial_parts(field, inner_ghost, outer_ghost):
        lower_vals = inward(field, inner_ghost)
        upper_vals = outward(field, outer_ghost)
        return (
            (upper_vals - lower_vals) / (2.0 * spacing_r),
            (upper_vals - 2.0 * field + lower_vals) / (spacing_r * spacing_r),
        )

    radial_vel = values_at(0, 0, 0)
    azim_vel = values_at(1, 0, 0)
    axial_vel = values_at(2, 0, 0)
    vr_dr, vr_drr = radial_parts(radial_vel, -partner[0], jnp.zeros_like(radial_vel[..., 0]))
    vt_dr, vt_drr = radial_parts(azim_vel, -partner[1], -azim_vel[..., -1])
    vz_dr, vz_drr = radial_parts(axial_vel, partner[2], -axial_vel[..., -1])
    vr_dt, vr_dtt = periodic_parts(0, True)
    vr_dz, vr_dzz = periodic_parts(0, False)
    vt_dt, vt_dtt = periodic_parts(1, True)
    vt_dz, vt_dzz = periodic_parts(1, False)
    vz_dt, vz_dtt = periodic_parts(2, True)
    vz_dz, vz_dzz = periodic_parts(2, False)
    azim_on_axial = 0.25 * (
        values_at(1, -1, 0) + azim_vel + values_at(1, -1, 1) + values_at(1, 0, 1)
    )
    radial_next = values_at(0, 0, 1)
    rad_on_axial = 0.25 * (
        radial_vel + below_axis(radial_vel) + radial_next + below_axis(radial_next)
    )
    axial_adv = -(rad_on_axial * vz_dr + azim_on_axial / centre * vz_dt + axial_vel * vz_dz)
    axial_visc = VISCOSITY * (vz_drr + vz_dr / centre + vz_dtt / (centre * centre) + vz_dzz)
    axial_on_azim = 0.25 * (
        values_at(2, 0, -1) + axial_vel + values_at(2, 1, -1) + values_at(2, 1, 0)
    )
    radial_side = values_at(0, 1, 0)
    rad_on_azim = 0.25 * (
        radial_vel + below_axis(radial_vel) + radial_side + below_axis(radial_side)
    )
    azim_adv = -(
        rad_on_azim * vt_dr
        + azim_vel / centre * vt_dt
        + axial_on_azim * vt_dz
        + rad_on_azim * azim_vel / centre
    )
    radial_turn = (
        radial_side + below_axis(radial_side) - (radial_vel + below_axis(radial_vel))
    ) / (2.0 * theta_step)
    azim_visc = VISCOSITY * (
        vt_drr
        + vt_dr / centre
        + vt_dtt / (centre * centre)
        + vt_dzz
        - azim_vel / (centre * centre)
        + 2.0 * radial_turn / (centre * centre)
    )
    azim_back = values_at(1, -1, 0)
    azim_on_radial = 0.25 * (azim_back + azim_vel + beyond_wall(azim_back) + beyond_wall(azim_vel))
    axial_back = values_at(2, 0, -1)
    axial_on_radial = 0.25 * (
        axial_back + axial_vel + beyond_wall(axial_back) + beyond_wall(axial_vel)
    )
    radial_adv = (
        -(radial_vel * vr_dr + azim_on_radial / facing * vr_dt + axial_on_radial * vr_dz)
        + azim_on_radial * azim_on_radial / facing
    )
    azim_turn = (azim_vel + beyond_wall(azim_vel) - (azim_back + beyond_wall(azim_back))) / (
        2.0 * theta_step
    )
    radial_visc = VISCOSITY * (
        vr_drr
        + vr_dr / facing
        + vr_dtt / (facing * facing)
        + vr_dzz
        - radial_vel / (facing * facing)
        - 2.0 * azim_turn / (facing * facing)
    )
    explicit = jnp.stack(
        [(radial_adv + radial_visc) * wall_mask, azim_adv + azim_visc, axial_adv + axial_visc]
    )
    cfl_rate = (
        jnp.abs(radial_vel) / spacing_r
        + jnp.abs(azim_vel) / (centre * theta_step)
        + jnp.abs(axial_vel) / AXIAL_STEP
    )
    return (explicit, cfl_rate)


def per_device(velocity):
    cycle_size = lax.axis_size("az")
    theta_step = 2.0 * math.pi / (cycle_size * velocity.shape[1])
    padded = with_halo(velocity, (("az", 1), ("ax", 2)), 2)
    inner_row = velocity[:, :, :, 0]
    partner = shifted(inner_row, "az", cycle_size // 2)
    explicit, cfl_rate = explicit_terms(padded, partner, theta_step)
    largest = lax.pmax(jnp.max(cfl_rate), ("az", "ax"))
    time_step = CFL_TARGET / (largest + 1e-06)
    return (GAMMA * time_step * explicit, time_step)


def solution(mesh):
    placed = (P(None, "az", "ax", None),)
    return jax.shard_map(
        per_device,
        mesh=mesh,
        in_specs=placed,
        out_specs=(P(None, "az", "ax", None), P()),
        check_vma=False,
    )
```

profile of v0, /device:TPU:0, one launch (start us, length us, event | category | flops | bytes accessed | tf_op | source)
XLA Modules:
  0.0 153.4 jit_solution(15768315361880078644)
XLA Ops:
  0.6 1.9 %fusion.68 = (f32[3,2,128,128]{3,2,1,0:T(8,128)S(1)}, f32[3,2,128,128]{3,2,1,0:T(8,128)}) fusion(f32[3,32,128,128]{3,2,1,0:T(8,128)} %param.1), kind=kLoop, calls=%fused_computation.135 | loop fusion | bytes 1572864 | tf_op jit(solution)/shard_map/slice | solution.py:17
  2.5 3.0 %collective-permute-start.1 = (f32[3,2,128,128]{3,2,1,0:T(8,128)}, f32[3,2,128,128]{3,2,1,0:T(8,128)S(1)}, u32[]{:S(2)}, u32[]{:S(2)}) collective-permute-start(f32[3,2,128,128]{3,2,1,0:T(8,128)} %get-tuple-element.15), channel_id=1, source_target_pairs={{0,4},{4,8},{8,12},{12,16},{16,20},{20,24},{24,28},{28,0},{1,5},{5... | collective-permute-start | bytes 1179656 | tf_op jit(solution)/shard_map/ppermute | solution.py:21
  5.5 3.0 %collective-permute-start.2 = (f32[3,2,128,128]{3,2,1,0:T(8,128)S(1)}, f32[3,2,128,128]{3,2,1,0:T(8,128)S(1)}, u32[]{:S(2)}, u32[]{:S(2)}) collective-permute-start(f32[3,2,128,128]{3,2,1,0:T(8,128)S(1)} %get-tuple-element.14), channel_id=1, source_target_pairs={{4,0},{8,4},{12,8},{16,12},{20,16},{24,20},{28,24},{0,28},{5,1},{9... | collective-permute-start | bytes 1179656 | tf_op jit(solution)/shard_map/ppermute | solution.py:23
  8.6 4.4 %copy.10 = f32[3,32,128,1]{2,1,0,3:T(8,128)S(1)} copy(f32[3,32,128,1]{3,2,1,0:T(8,128)} %bitcast.193) | data formatting | bytes 98304
  13.0 1.0 collective-permute-start
  14.0 2.6 %slice_bitcast_fusion.13 = (f32[32,128,128]{2,1,0:T(8,128)S(1)}, f32[32,128,128]{2,1,0:T(8,128)S(1)}) fusion(f32[3,32,128,128]{3,2,1,0:T(8,128)} %param.1), kind=kLoop, calls=%fused_computation.114 | loop fusion | bytes 8388608 | tf_op jit(solution)/shard_map/squeeze | solution.py:47
  16.6 0.0 slice-start.1
  16.7 4.4 %fusion.69 = (f32[32,128,127]{2,1,0:T(8,128)}, f32[32,128,127]{2,1,0:T(8,128)}, f32[32,128,127]{2,1,0:T(8,128)}, f32[32,128,127]{2,1,0:T(8,128)}) fusion(f32[32,128,128]{2,1,0:T(8,128)S(1)} %get-tuple-element.9, f32[32,128,128]{2,1,0:T(8,128)S(1)} %get-tuple-element.10), kind=kLoop, calls=%fused_computation.136 | loop fusion | bytes 16646144 | tf_op jit(solution)/shard_map/slice | solution.py:58
  21.1 3.3 %slice_negate_fusion = (f32[32,128,1]{2,1,0:T(8,128)}, f32[32,128,1]{2,1,0:T(8,128)}) fusion(f32[32,128,128]{2,1,0:T(8,128)S(1)} %get-tuple-element.10, f32[32,128,128]{2,1,0:T(8,128)S(1)} %get-tuple-element.9), kind=kLoop, calls=%fused_computation.80 | loop fusion | flops 8192 | bytes 65536 | tf_op jit(solution)/shard_map/neg | solution.py:67
  24.3 0.0 slice-done
  24.3 0.0 slice-done.1
  24.3 1.4 add_reduce_fusion
  25.7 2.7 %fusion.71 = (f32[32,128,127]{2,1,0:T(8,128)}, f32[32,128,127]{2,1,0:T(8,128)}) fusion(f32[32,128,128]{2,1,0:T(8,128)S(1)} %get-tuple-element.3), kind=kLoop, calls=%fused_computation.138 | loop fusion | bytes 8323072 | tf_op jit(solution)/shard_map/slice | solution.py:61
  28.4 39.6 %pmax.7 = f32[]{:T(128)} all-reduce(f32[]{:T(128)} %get-tuple-element.2), channel_id=1, replica_groups=mesh['az'=8,'ax'=4] {'az','ax'}, use_global_device_ids=true, to_apply=%region_1.2 | all-reduce | flops 1 | bytes 8 | tf_op jit(solution)/shard_map/pmax | solution.py:175
  68.7 0.0 collective-permute-done
  68.8 2.0 %copy.7 = f32[32,128,1]{2,1,0:T(8,128)} copy(f32[32,128,1]{1,0,2:T(8,128)S(1)} %get-tuple-element.28) | data formatting | bytes 32768 | tf_op jit(solution)/shard_map/neg | solution.py:94
  70.8 1.9 %copy.8 = f32[32,128,1]{2,1,0:T(8,128)} copy(f32[32,128,1]{1,0,2:T(8,128)S(1)} %get-tuple-element.26) | data formatting | bytes 32768 | tf_op jit(solution)/shard_map/neg | solution.py:95
  72.7 2.0 %copy.9 = f32[32,128,1]{2,1,0:T(8,128)} copy(f32[32,128,1]{1,0,2:T(8,128)S(1)} %get-tuple-element.27) | data formatting | bytes 32768 | tf_op jit(solution)/shard_map/broadcast_in_dim;squeeze | solution.py:58
  74.7 0.0 collective-permute-done.1
  74.7 1.0 constant_dynamic-update-slice_fusion.1
  75.6 11.9 %constant_dynamic-update-slice_fusion = (f32[3,34,128,128]{3,2,1,0:T(8,128)}, f32[3,36,128,128]{3,2,1,0:T(8,128)}, f32[3,34,128,128]{3,2,1,0:T(8,128)}) fusion(f32[3,34,128,128]{3,2,1,0:T(8,128)} %get-tuple-element.22, f32[3,32,128,128]{3,2,1,0:T(8,128)} %param.1, f32[3,36,128,128]{3,2,1,0:T(8,128)} %get-tuple-element.23), kind=kLoop, calls=%fused_computation.120 | loop fusion | bytes 25165824 | tf_op jit(solution)/shard_map/concatenate | solution.py:19
  87.5 0.0 collective-permute-done.2
  87.5 1.0 constant_dynamic-update-slice_fusion.2
  88.5 1.4 fusion.67
  89.9 0.1 collective-permute-start.3
  90.0 1.8 %slice_bitcast_fusion.11 = f32[32,128,128]{2,1,0:T(8,128)S(1)} fusion(f32[3,34,128,128]{3,2,1,0:T(8,128)} %get-tuple-element.11), kind=kLoop, calls=%fused_computation.92 | loop fusion | bytes 4194304 | tf_op jit(solution)/shard_map/squeeze | solution.py:47
  91.8 0.0 slice-start.5
  91.8 1.9 %slice_negate_fusion.3 = f32[32,128,1]{2,1,0:T(8,128)} fusion(f32[32,128,128]{2,1,0:T(8,128)S(1)} %slice_bitcast_fusion.11), kind=kLoop, calls=%fused_computation.91 | loop fusion | flops 4096 | bytes 32768 | tf_op jit(solution)/shard_map/neg | solution.py:67
  93.7 1.9 %slice.284 = f32[32,128,127]{2,1,0:T(8,128)} slice(f32[32,128,128]{2,1,0:T(8,128)S(1)} %slice_bitcast_fusion.11), slice={[0:32], [0:128], [1:128]} | slice | bytes 4161536 | tf_op jit(solution)/shard_map/slice | solution.py:61
  95.6 1.6 %collective-permute-start.4 = (f32[3,36,2,128]{3,2,1,0:T(2,128)S(1)}, f32[3,36,2,128]{3,2,1,0:T(2,128)S(1)}, u32[]{:S(2)}, u32[]{:S(2)}) collective-permute-start(f32[3,36,2,128]{3,2,1,0:T(2,128)S(1)} %get-tuple-element.7), channel_id=1, source_target_pairs={{1,0},{2,1},{3,2},{0,3},{5,4},{6,5},{7,6},{4,7},{9,8},{10,9},{11,1... | collective-permute-start | bytes 331784 | tf_op jit(solution)/shard_map/ppermute | solution.py:23
  97.3 0.0 collective-permute-done.3
  97.3 0.0 slice-done.4
  97.3 0.0 slice-done.5
  97.3 0.3 fusion.24
  97.6 0.0 copy-start
  97.6 1.9 %slice_negate_fusion.1 = f32[32,128,1]{2,1,0:T(8,128)} fusion(f32[32,128,128]{2,1,0:T(8,128)S(1)} %fusion.24), kind=kLoop, calls=%fused_computation.81 | loop fusion | flops 4096 | bytes 32768 | tf_op jit(solution)/shard_map/neg | solution.py:67
  99.5 2.0 %slice.295 = f32[32,128,127]{2,1,0:T(8,128)} slice(f32[32,128,128]{2,1,0:T(8,128)S(1)} %fusion.24), slice={[0:32], [0:128], [1:128]} | slice | bytes 4161536 | tf_op jit(solution)/shard_map/slice | solution.py:61
  101.5 0.0 collective-permute-done.4
  101.5 0.0 slice-done.6
  101.5 0.0 slice-done.2
  101.5 0.0 slice-done.3
  101.5 0.0 slice-done.7
  101.5 0.2 copy-done.1
  101.8 14.0 %fusion.58 = (f32[1,32,128,128]{3,2,1,0:T(8,128)}, f32[32,128,128]{2,1,0:T(8,128)}, f32[32,128,128]{2,1,0:T(8,128)}) fusion(f32[32,128,1]{2,1,0:T(8,128)} %slice_negate_fusion.1, f32[32,128,127]{2,1,0:T(8,128)} %slice.295, f32[32,128,128]{2,1,0:T(8,128)S(1)} %get-tuple-element.3, f32[3,36,128,128]{3,2,1,0:T(8,128)S(1)} %bitcast.199, ...), kind=kLoop, calls=%fused_computation.105 | loop fusion | flops 44040192 | bytes 45032960 | tf_op jit(solution)/shard_map/stack | solution.py:157
  115.8 0.0 copy-done
  115.8 10.7 %fusion.41 = f32[1,32,128,128]{3,2,1,0:T(8,128)} fusion(f32[3,36,128,128]{3,2,1,0:T(8,128)S(1)} %bitcast.199, f32[3,36,2,128]{3,2,1,0:T(2,128)S(1)} %collective-permute-done.3, f32[32,128,128]{2,1,0:T(8,128)} %get-tuple-element.5, f32[3,36,2,128]{3,2,1,0:T(2,128)S(1)} %collective-permute-done.4, f32[3,34,128,128]{3,2,1,0:T(8,128)S(1)} %bitcast.201, ...), kind=kLoop, calls=%fused_computation.66 | loop fusion | flops 37748736 | bytes 38724608 | tf_op jit(solution)/shard_map/stack | solution.py:157
  126.5 19.1 %add_bitcast_fusion = f32[1,32,128,128]{3,2,1,0:T(8,128)} fusion(f32[32,128,128]{2,1,0:T(8,128)} %copy-done, f32[3,36,2,128]{3,2,1,0:T(2,128)S(1)} %collective-permute-done.4, f32[3,36,128,128]{3,2,1,0:T(8,128)} %get-tuple-element.25, f32[3,36,2,128]{3,2,1,0:T(2,128)S(1)} %collective-permute-done.3, f32[3,34,128,128]{3,2,1,0:T(8,128)} %get-tuple-element.24, ...), kind=kLoop, calls=%fused_computation.110 | loop fusion | flops 32505856 | bytes 38724608 | tf_op jit(solution)/shard_map/stack | solution.py:157
  145.6 6.7 %maximum_multiply_fusion = f32[3,32,128,128]{3,2,1,0:T(8,128)} fusion(f32[1,32,128,128]{3,2,1,0:T(8,128)} %add_bitcast_fusion, f32[1,32,128,128]{3,2,1,0:T(8,128)} %fusion.41, f32[1,32,128,128]{3,2,1,0:T(8,128)} %get-tuple-element.4, f32[]{:T(128)S(6)} %mul_shard_map.3), kind=kLoop, calls=%fused_computation.24 | loop fusion | flops 4718592 | bytes 12582916 | tf_op jit(solution)/shard_map/mul | solution.py:177
  (16 shorter events, 0.0 us)
Async XLA Ops:
  2.5 72.1 %collective-permute-start.1 = (f32[3,2,128,128]{3,2,1,0:T(8,128)}, f32[3,2,128,128]{3,2,1,0:T(8,128)S(1)}, u32[]{:S(2)}, u32[]{:S(2)}) collective-permute-start(f32[3,2,128,128]{3,2,1,0:T(8,128)} %get-tuple-element.15), channel_id=1, source_target_pairs={{0,4},{4,8},{8,12},{12,16},{16,20},{20,24},{24,28},{28,0},{1,5},{5... | collective-permute-start | bytes 1179656 | tf_op jit(solution)/shard_map/ppermute | solution.py:21
  5.5 82.0 %collective-permute-start.2 = (f32[3,2,128,128]{3,2,1,0:T(8,128)S(1)}, f32[3,2,128,128]{3,2,1,0:T(8,128)S(1)}, u32[]{:S(2)}, u32[]{:S(2)}) collective-permute-start(f32[3,2,128,128]{3,2,1,0:T(8,128)S(1)} %get-tuple-element.14), channel_id=1, source_target_pairs={{4,0},{8,4},{12,8},{16,12},{20,16},{24,20},{28,24},{0,28},{5,1},{9... | collective-permute-start | bytes 1179656 | tf_op jit(solution)/shard_map/ppermute | solution.py:23
  13.0 55.8 %collective-permute-start = (f32[3,32,128]{2,1,0:T(8,128)S(1)}, f32[3,32,128]{2,1,0:T(8,128)S(1)}, u32[]{:S(2)}, u32[]{:S(2)}) collective-permute-start(f32[3,32,128]{2,1,0:T(8,128)S(1)} %bitcast.204), channel_id=1, source_target_pairs={{16,0},{20,4},{24,8},{28,12},{0,16},{4,20},{8,24},{12,28},{17,1},{... | collective-permute-start | bytes 147464 | tf_op jit(solution)/shard_map/ppermute | solution.py:33
  14.0 10.3 %slice-start = ((s8[6291456]{0:T(1024)(128)(4,1)}), s8[4194304]{0:T(1024)(128)(4,1)S(1)}, s32[]{:S(2)}) async-start(s8[6291456]{0:T(1024)(128)(4,1)} %bitcast.194), calls=%async_computation | async-start | bytes 8388608
  16.6 7.7 %slice-start.1 = ((s8[6291456]{0:T(1024)(128)(4,1)}), s8[2097152]{0:T(1024)(128)(4,1)S(1)}, s32[]{:S(2)}) async-start(s8[6291456]{0:T(1024)(128)(4,1)} %bitcast.194), calls=%async_computation.1 | async-start | bytes 4194304
  88.5 8.8 %slice-start.4 = ((s8[7077888]{0:T(1024)(128)(4,1)}), s8[4194304]{0:T(1024)(128)(4,1)S(1)}, s32[]{:S(2)}) async-start(s8[7077888]{0:T(1024)(128)(4,1)} %bitcast.198), calls=%async_computation.4 | async-start | bytes 8388608
  89.9 7.4 %collective-permute-start.3 = (f32[3,36,2,128]{3,2,1,0:T(2,128)S(1)}, f32[3,36,2,128]{3,2,1,0:T(2,128)S(1)}, u32[]{:S(2)}, u32[]{:S(2)}) collective-permute-start(f32[3,36,2,128]{3,2,1,0:T(2,128)S(1)} %get-tuple-element.8), channel_id=1, source_target_pairs={{0,1},{1,2},{2,3},{3,0},{4,5},{5,6},{6,7},{7,4},{8,9},{9,10},{10,1... | collective-permute-start | bytes 331784 | tf_op jit(solution)/shard_map/ppermute | solution.py:21
  91.8 5.5 %slice-start.5 = ((s8[7077888]{0:T(1024)(128)(4,1)}), s8[2883584]{0:T(1024)(128)(4,1)S(1)}, s32[]{:S(2)}) async-start(s8[7077888]{0:T(1024)(128)(4,1)} %bitcast.198), calls=%async_computation.5 | async-start | bytes 5767168
  93.7 7.8 %slice-start.6 = ((s8[6684672]{0:T(1024)(128)(4,1)}), s8[4194304]{0:T(1024)(128)(4,1)S(1)}, s32[]{:S(2)}) async-start(s8[6684672]{0:T(1024)(128)(4,1)} %bitcast.200), calls=%async_computation.6 | async-start | bytes 8388608
  95.6 5.9 %slice-start.2 = ((s8[6291456]{0:T(1024)(128)(4,1)}), s8[4194304]{0:T(1024)(128)(4,1)S(1)}, s32[]{:S(2)}) async-start(s8[6291456]{0:T(1024)(128)(4,1)} %bitcast.196), calls=%async_computation.2 | async-start | bytes 8388608
  95.6 5.9 %slice-start.3 = ((s8[6291456]{0:T(1024)(128)(4,1)}), s8[2097152]{0:T(1024)(128)(4,1)S(1)}, s32[]{:S(2)}) async-start(s8[6291456]{0:T(1024)(128)(4,1)} %bitcast.196), calls=%async_computation.3 | async-start | bytes 4194304
  95.6 5.9 %slice-start.7 = ((s8[6684672]{0:T(1024)(128)(4,1)}), s8[2490368]{0:T(1024)(128)(4,1)S(1)}, s32[]{:S(2)}) async-start(s8[6684672]{0:T(1024)(128)(4,1)} %bitcast.200), calls=%async_computation.7 | async-start | bytes 4980736
  95.6 5.9 %collective-permute-start.4 = (f32[3,36,2,128]{3,2,1,0:T(2,128)S(1)}, f32[3,36,2,128]{3,2,1,0:T(2,128)S(1)}, u32[]{:S(2)}, u32[]{:S(2)}) collective-permute-start(f32[3,36,2,128]{3,2,1,0:T(2,128)S(1)} %get-tuple-element.7), channel_id=1, source_target_pairs={{1,0},{2,1},{3,2},{0,3},{5,4},{6,5},{7,6},{4,7},{9,8},{10,9},{11,1... | collective-permute-start | bytes 331784 | tf_op jit(solution)/shard_map/ppermute | solution.py:23
  97.6 18.2 %copy-start = (f32[32,128,128]{2,1,0:T(8,128)}, f32[32,128,128]{2,1,0:T(8,128)S(1)}, u32[]{:S(2)}) copy-start(f32[32,128,128]{2,1,0:T(8,128)S(1)} %fusion.24) | copy-start | bytes 6291460
  99.5 2.3 %copy-start.1 = (f32[32,128,127]{2,1,0:T(8,128)S(1)}, f32[32,128,127]{2,1,0:T(8,128)}, u32[]{:S(2)}) copy-start(f32[32,128,127]{2,1,0:T(8,128)} %get-tuple-element.21) | copy-start | bytes 6242308
where the time goes:
time: 156 us; the launch traced here: 153 us
  other arithmetic  59.2 us (38%)
  local copies, waits for them, and re-layouts  43.2 us (28%)
  blocking collectives  39.6 us (25%)
  starting transfers between devices  8.72 us (6%)
  between operations  2.6 us (2%)
    another operation x3, other arithmetic, explicit_terms(): jnp.stack([(radial_adv + radial_visc) * wall_mask, azim_adv + azim_visc,...  43.8 us
    pmax x1, blocking collectives, per_device(): largest = lax.pmax(jnp.max(cfl_rate), ('az', 'ax'))  39.6 us
    concatenate x2, local copies, waits for them, and re-layouts, with_halo(): jnp.concatenate([lax.ppermute(tail, axis, [(i, (i + 1) % count) for i in...  12.9 us
    neg x3, other arithmetic, beyond_wall(): return outward(field, -field[..., -1])  7.08 us
    mul x1, other arithmetic, per_device(): return (GAMMA * time_step * explicit, time_step)  6.66 us
    slice x3, local copies, waits for them, and re-layouts, outward(): return jnp.concatenate([field[..., 1:], ghost[..., None]], axis=-1)  6.59 us
    unnamed x22, local copies, waits for them, and re-layouts  5.66 us
    ppermute x2, starting transfers between devices, with_halo(): lax.ppermute(head, axis, [((i + 1) % count, i) for i in range(count)])  4.68 us
  transfers between devices with their start and end apart: 5, of which 0 were waited for; matrix products, arithmetic and copies ran while one was open for 31% of the time, Pallas kernels for 0%

commit v1 on v0

v1 whole, which is shorter than its diff:
```python
import functools
import math

import jax
import jax.numpy as jnp
import numpy as np
from jax import lax
from jax.experimental import pallas as pl
from jax.experimental.pallas import tpu as pltpu
from jax.sharding import PartitionSpec as P

AXIAL_STEP = 0.01
VISCOSITY = 0.001
CFL_TARGET = 1.2
GAMMA = 8.0 / 15.0

PAD = 8
GROUP = 4
VMEM_LIMIT = 40 * 2**20

(
    WALL,
    RATE_R,
    RATE_T,
    RADIAL_C,
    THETA_C,
    SECOND_C,
    CENTRE_Z,
    CENTRE_T,
    CURVE_T,
    TURN_T,
    RADIAL_F,
    THETA_F,
    SECOND_F,
    CENTRE_R,
    CURVE_R,
    TURN_R,
    COUNT,
) = range(17)


def coefficients(radial, theta_step):
    dr = 1.0 / radial
    index = np.arange(radial, dtype=np.float64)
    centre = (index + 0.5) * dr
    face = (index + 1.0) * dr
    wall = np.where(index < radial - 1.5, 1.0, 0.0)
    h = theta_step
    nu = VISCOSITY
    rows = np.zeros((COUNT, radial))
    rows[WALL] = wall
    rows[RATE_R] = wall / dr
    rows[RATE_T] = 1.0 / (centre * h)
    common = -2.0 * nu / dr**2 - 30.0 * nu / (12.0 * AXIAL_STEP**2)
    rows[RADIAL_C] = nu / (2.0 * dr * centre)
    rows[THETA_C] = -1.0 / (12.0 * h * centre)
    rows[SECOND_C] = nu / (12.0 * h * h * centre**2)
    rows[CENTRE_Z] = common - 30.0 * rows[SECOND_C]
    rows[CENTRE_T] = rows[CENTRE_Z] - nu / centre**2
    rows[CURVE_T] = 0.25 / centre
    rows[TURN_T] = nu / (h * centre**2)
    rows[RADIAL_F] = nu / (2.0 * dr * face)
    rows[THETA_F] = -0.25 / (12.0 * h * face)
    rows[SECOND_F] = nu / (12.0 * h * h * face**2)
    rows[CENTRE_R] = common - 30.0 * rows[SECOND_F] - nu / face**2
    rows[CURVE_R] = 1.0 / (16.0 * face)
    rows[TURN_R] = -nu / (h * face**2)
    return np.broadcast_to(rows[:, None, :], (COUNT, 8, radial)).astype(np.float32)


def terms(vel, ghost, coef, j, k, dr):
    lane = lax.broadcasted_iota(jnp.int32, (8, 128), 1)
    first_lane = lane == 0
    last_lane = lane == 127

    def at(component, dj, dk):
        return vel[component, j + dj, pl.ds(k + PAD + dk, 8), :]

    def out(x):
        return pltpu.roll(x, 127, 1)

    def inn(x):
        return pltpu.roll(x, 1, 1)

    nu = VISCOSITY
    lap = nu / dr**2
    adv_z = -1.0 / (12.0 * AXIAL_STEP)
    vis_z = nu / (12.0 * AXIAL_STEP**2)

    def pieces(component):
        p1, m1, p2, m2 = (at(component, d, 0) for d in (1, -1, 2, -2))
        first_t = 8.0 * (p1 - m1) - (p2 - m2)
        second_t = 16.0 * (p1 + m1) - (p2 + m2)
        p1, m1, p2, m2 = (at(component, 0, d) for d in (1, -1, 2, -2))
        first_z = 8.0 * (p1 - m1) - (p2 - m2)
        second_z = 16.0 * (p1 + m1) - (p2 + m2)
        return first_t, second_t, first_z, second_z

    a, b, c = (at(i, 0, 0) for i in range(3))
    a_in = inn(a)
    pair_a = a + a_in
    a_side = at(0, 1, 0)
    pair_side = a_side + inn(a_side)
    a_next = at(0, 0, 1)
    pair_next = a_next + inn(a_next)

    first_t, second_t, first_z, second_z = pieces(2)
    c_out = out(c)
    up = jnp.where(last_lane, -c, c_out)
    low = jnp.where(first_lane, ghost(2), inn(c))
    u_r = pair_a + pair_next
    u_t = (at(1, -1, 0) + b) + (at(1, -1, 1) + at(1, 0, 1))
    h_z = (up - low) * (coef(RADIAL_C) - u_r * (0.125 / dr)) + (up + low) * lap
    h_z = h_z + first_t * (u_t * (0.25 * coef(THETA_C)))
    h_z = h_z + second_t * coef(SECOND_C) + second_z * vis_z
    h_z = h_z + c * (coef(CENTRE_Z) + first_z * adv_z)

    first_t, second_t, first_z, second_z = pieces(1)
    b_out = out(b)
    up = jnp.where(last_lane, -b, b_out)
    low = jnp.where(first_lane, ghost(1), inn(b))
    u_r = pair_a + pair_side
    c_back = at(2, 0, -1)
    u_z = (c_back + c) + (at(2, 1, -1) + at(2, 1, 0))
    h_t = (up - low) * (coef(RADIAL_C) - u_r * (0.125 / dr)) + (up + low) * lap
    h_t = h_t + b * (coef(CENTRE_T) + first_t * coef(THETA_C) - u_r * coef(CURVE_T))
    h_t = h_t + second_t * coef(SECOND_C) + second_z * vis_z
    h_t = h_t + first_z * (u_z * (0.25 * adv_z))
    h_t = h_t + (pair_side - pair_a) * coef(TURN_T)

    first_t, second_t, first_z, second_z = pieces(0)
    up = out(a)
    low = jnp.where(first_lane, ghost(0), a_in)
    b_back = at(1, -1, 0)
    pair_b = b + b_out
    pair_back = b_back + out(b_back)
    u_t = pair_b + pair_back
    u_z = (c + c_out) + (c_back + out(c_back))
    h_r = (up - low) * (coef(RADIAL_F) - a * (0.5 / dr)) + (up + low) * lap
    h_r = h_r + u_t * (u_t * coef(CURVE_R) + first_t * coef(THETA_F))
    h_r = h_r + second_t * coef(SECOND_F) + second_z * vis_z
    h_r = h_r + first_z * (u_z * (0.25 * adv_z)) + a * coef(CENTRE_R)
    h_r = h_r + (pair_b - pair_back) * coef(TURN_R)
    return h_r, h_t, h_z


def theta_edges(v_ref, head_ref, tail_ref, sems):
    count = v_ref.shape[1]
    copies = [
        pltpu.make_async_copy(v_ref.at[:, 0:2], head_ref, sems.at[0]),
        pltpu.make_async_copy(v_ref.at[:, count - 2 : count], tail_ref, sems.at[1]),
    ]
    for copy in copies:
        copy.start()
    for copy in copies:
        copy.wait()


def first_pass(v_ref, coef_ref, low_ref, high_ref, inner_ref, pay_ref, vel, sems):
    _, planes, axial, radial = v_ref.shape
    groups = planes // GROUP

    def fetch(g):
        part = pl.ds(g * GROUP, GROUP)
        return pltpu.make_async_copy(v_ref.at[:, part], vel.at[:, part], sems.at[g])

    for g in range(groups):
        fetch(g).start()
    inner_ref[...] = jnp.zeros_like(inner_ref)
    lane = lax.broadcasted_iota(jnp.int32, (8, radial), 1)

    def step(g, largest):
        fetch(g).wait()
        for q in range(GROUP):
            j = g * GROUP + q
            for n in range(3):
                mask = coef_ref[WALL, 0:2] if n == 0 else 1.0
                low_ref[n, j] = vel[n, j, 0:2, :] * mask
                high_ref[n, j] = vel[n, j, axial - 2 : axial, :] * mask

        def rows(i, largest):
            k = pl.ds(pl.multiple_of(i * 8, 8), 8)
            inner = inner_ref[k, :]
            for q in range(GROUP):
                j = g * GROUP + q
                a, b, c = (vel[n, j, k, :] for n in range(3))
                rate = (
                    jnp.abs(a) * coef_ref[RATE_R]
                    + jnp.abs(b) * coef_ref[RATE_T]
                    + jnp.abs(c) * (1.0 / AXIAL_STEP)
                )
                largest = jnp.maximum(largest, rate)
                for n, x in enumerate((a, b, c)):
                    place = n * planes + j
                    inner = jnp.where(lane == place, pltpu.roll(x, place, 1), inner)
            inner_ref[k, :] = inner
            return largest

        return lax.fori_loop(0, axial // 8, rows, largest)

    largest = lax.fori_loop(0, groups, step, jnp.zeros((8, radial), jnp.float32))
    sign = jnp.where(lane < 2 * planes, -1.0, 1.0).astype(jnp.float32)

    def turn(i, carry):
        k = pl.ds(pl.multiple_of(i * 8, 8), 8)
        inner_ref[k, :] = inner_ref[k, :] * sign
        return carry

    lax.fori_loop(0, axial // 8, turn, 0)
    top = jnp.max(largest, axis=(0, 1), keepdims=True)
    pay_ref[...] = jnp.broadcast_to(top, pay_ref.shape)
    pay_ref[1:2, :] = vel[1, planes - 1, 0:1, :]
    pay_ref[2:3, :] = vel[2, 0, axial - 1 : axial, :]


def interior(
    scale_ref, v_ref, low_ref, high_ref, inner_ref, coef_ref, out_ref, vel, res, in_sems, out_sems
):
    _, planes, axial, radial = v_ref.shape
    dr = 1.0 / radial

    def fetch(j):
        return pltpu.make_async_copy(
            v_ref.at[:, j], vel.at[:, j, pl.ds(PAD, axial)], in_sems.at[j]
        )

    def store(j):
        slot = j % 2
        return pltpu.make_async_copy(res.at[slot], out_ref.at[:, j], out_sems.at[slot])

    def ready(j):
        fetch(j).wait()
        vel[:, j, PAD - 2 : PAD, :] = low_ref[:, j]
        vel[:, j, PAD + axial : PAD + axial + 2, :] = high_ref[:, j]
        for i in range(axial // 8):
            k = pl.ds(PAD + 8 * i, 8)
            vel[0, j, k, :] = vel[0, j, k, :] * coef_ref[WALL]

    def launch(j, carry):
        fetch(j).start()
        return carry

    lax.fori_loop(0, planes, launch, 0)
    for j in range(4):
        ready(j)
    scale = scale_ref[0]

    def plane(j, carry):
        ready(j + 2)

        @pl.when(j >= 4)
        def _():
            store(j - 2).wait()

        slot = j % 2

        def rows(i, carry):
            k = pl.multiple_of(i * 8, 8)
            inner = inner_ref[pl.ds(k, 8), :]

            def ghost(component):
                return pltpu.roll(inner, radial - (component * planes + j), 1)

            h_r, h_t, h_z = terms(vel, ghost, lambda n: coef_ref[n], j, k, dr)
            k = pl.ds(k, 8)
            res[slot, 0, k, :] = h_r * (scale * coef_ref[WALL])
            res[slot, 1, k, :] = h_t * scale
            res[slot, 2, k, :] = h_z * scale
            return carry

        lax.fori_loop(0, axial // 8, rows, 0)
        store(j).start()
        return carry

    lax.fori_loop(2, planes - 2, plane, 0)
    store(planes - 4).wait()
    store(planes - 3).wait()


def edges(
    scale_ref,
    v_ref,
    below_ref,
    above_ref,
    low_ref,
    high_ref,
    corner_ref,
    inner_ref,
    coef_ref,
    part_ref,
    out_ref,
    vel,
    res,
    in_sems,
    out_sems,
):
    del part_ref
    _, planes, axial, radial = v_ref.shape
    dr = 1.0 / radial
    cells = pl.ds(PAD, axial)
    fetches = [
        pltpu.make_async_copy(below_ref, vel.at[:, 0:2, cells], in_sems.at[0]),
        pltpu.make_async_copy(v_ref.at[:, 0:4], vel.at[:, 2:6, cells], in_sems.at[1]),
        pltpu.make_async_copy(
            v_ref.at[:, planes - 4 : planes], vel.at[:, 6:10, cells], in_sems.at[2]
        ),
        pltpu.make_async_copy(above_ref, vel.at[:, 10:12, cells], in_sems.at[3]),
    ]
    for fetch in fetches:
        fetch.start()
    for fetch in fetches:
        fetch.wait()
    own = {2: 0, 3: 1, 4: 2, 7: planes - 3, 8: planes - 2, 9: planes - 1}
    for q in own:
        vel[:, q, PAD - 2 : PAD, :] = low_ref[:, own[q]]
        vel[:, q, PAD + axial : PAD + axial + 2, :] = high_ref[:, own[q]]
    vel[1, 1, PAD + axial : PAD + axial + 1, :] = corner_ref[0:1, :]
    vel[2, 10, PAD - 1 : PAD, :] = corner_ref[1:2, :]
    for q in range(12):
        for i in range(axial // 8):
            k = pl.ds(PAD + 8 * i, 8)
            vel[0, q, k, :] = vel[0, q, k, :] * coef_ref[WALL]
    scale = scale_ref[0]
    copies = []
    for side, (start, first) in enumerate(((2, 0), (8, planes - 2))):
        for q in range(2):

            def rows(i, carry, side=side, start=start, first=first, q=q):
                k = pl.multiple_of(i * 8, 8)
                inner = inner_ref[pl.ds(k, 8), :]

                def ghost(component):
                    place = component * planes + first + q
                    return pltpu.roll(inner, (radial - place) % radial, 1)

                h_r, h_t, h_z = terms(vel, ghost, lambda n: coef_ref[n], start + q, k, dr)
                k = pl.ds(k, 8)
                res[side, 0, q, k, :] = h_r * (scale * coef_ref[WALL])
                res[side, 1, q, k, :] = h_t * scale
                res[side, 2, q, k, :] = h_z * scale
                return carry

            lax.fori_loop(0, axial // 8, rows, 0)
        copy = pltpu.make_async_copy(
            res.at[side], out_ref.at[:, first : first + 2], out_sems.at[side]
        )
        copy.start()
        copies.append(copy)
    for copy in copies:
        copy.wait()


def shifted(block, axis, distance):
    count = lax.axis_size(axis)
    return lax.ppermute(block, axis, [((i - distance) % count, i) for i in range(count)])


def per_device(velocity):
    _, planes, axial, radial = velocity.shape
    az, ax = lax.axis_size("az"), lax.axis_size("ax")
    theta_step = 2.0 * math.pi / (az * planes)
    coef = jnp.asarray(coefficients(radial, theta_step))
    f32 = jnp.float32
    anywhere = pl.BlockSpec(memory_space=pl.ANY)
    vmem = pl.BlockSpec(memory_space=pltpu.VMEM)
    smem = pl.BlockSpec(memory_space=pltpu.SMEM)
    params = pltpu.CompilerParams(vmem_limit_bytes=VMEM_LIMIT)
    shape = jax.ShapeDtypeStruct

    pair = shape((3, 2, axial, radial), f32)
    head, tail = pl.pallas_call(
        theta_edges,
        out_shape=(pair, pair),
        in_specs=[anywhere],
        out_specs=(anywhere, anywhere),
        scratch_shapes=[pltpu.SemaphoreType.DMA((2,))],
        name="theta_edges",
    )(velocity)
    below = shifted(tail, "az", 1)
    above = shifted(head, "az", -1)

    edge = shape((3, planes, 2, radial), f32)
    first, last, inner, pay = pl.pallas_call(
        first_pass,
        out_shape=(edge, edge, shape((axial, radial), f32), shape((8, radial), f32)),
        in_specs=[anywhere, vmem],
        out_specs=(vmem,) * 4,
        scratch_shapes=[
            pltpu.VMEM(velocity.shape, f32),
            pltpu.SemaphoreType.DMA((planes // GROUP,)),
        ],
        compiler_params=params,
        name="first_pass",
    )(velocity, coef)
    low = shifted(last, "ax", 1)
    high = shifted(first, "ax", -1)
    inner = shifted(inner, "az", az // 2)
    everyone = lax.all_gather(pay, ("az", "ax"))
    largest = jnp.max(everyone[:, 0, 0])
    time_step = CFL_TARGET / (largest + 1e-06)
    scale = (GAMMA * time_step).reshape(1)
    i, k = lax.axis_index("az"), lax.axis_index("ax")
    source_t = ((i - 1) % az) * ax + (k + 1) % ax
    source_z = ((i + 1) % az) * ax + (k - 1) % ax
    corner = jnp.stack([everyone[source_t, 1], everyone[source_z, 2]])

    rows = axial + 2 * PAD
    part = pl.pallas_call(
        interior,
        out_shape=shape(velocity.shape, f32),
        in_specs=[smem, anywhere, vmem, vmem, vmem, vmem],
        out_specs=anywhere,
        scratch_shapes=[
            pltpu.VMEM((3, planes, rows, radial), f32),
            pltpu.VMEM((2, 3, axial, radial), f32),
            pltpu.SemaphoreType.DMA((planes,)),
            pltpu.SemaphoreType.DMA((2,)),
        ],
        compiler_params=params,
        name="interior",
    )(scale, velocity, low, high, inner, coef)
    increment = pl.pallas_call(
        edges,
        out_shape=shape(velocity.shape, f32),
        in_specs=[smem, anywhere, anywhere, anywhere, vmem, vmem, vmem, vmem, vmem, anywhere],
        out_specs=anywhere,
        scratch_shapes=[
            pltpu.VMEM((3, 12, rows, radial), f32),
            pltpu.VMEM((2, 3, 2, axial, radial), f32),
            pltpu.SemaphoreType.DMA((4,)),
            pltpu.SemaphoreType.DMA((2,)),
        ],
        input_output_aliases={9: 0},
        compiler_params=params,
        name="edges",
    )(scale, velocity, below, above, low, high, corner, inner, coef, part)
    return increment, time_step


def solution(mesh):
    return jax.shard_map(
        per_device,
        mesh=mesh,
        in_specs=(P(None, "az", "ax", None),),
        out_specs=(P(None, "az", "ax", None), P()),
        check_vma=False,
    )
```

time: 156 us -> 154 us (0.987); the launches traced: 153 us -> 153 us
  Pallas kernels: 0 us -> 89.5 us
  other arithmetic: 59.2 us -> 0.64 us
  local copies, waits for them, and re-layouts: 43.2 us -> 6.42 us
  blocking collectives: 39.6 us -> 43.6 us
  starting transfers between devices: 8.72 us -> 10.6 us
    pallas_call x0 -> x4, Pallas kernels: none -> 89.5 us  [the longest x1 45.8 us: per_device(): pl.pallas_call(interior, out_shape=shape(velocity.shape, f32), in_specs=[...]
    another operation x3 -> x1, other arithmetic: 43.8 us -> 0.01 us  [per_device(): corner = jnp.stack([everyone[source_t, 1], everyone[source_z, 2]])]
    all_gather x0 -> x1, blocking collectives: none -> 43.6 us  [per_device(): everyone = lax.all_gather(pay, ('az', 'ax'))]
    pmax x1 -> x0, blocking collectives: 39.6 us -> none  [per_device(): largest = lax.pmax(jnp.max(cfl_rate), ('az', 'ax'))]
    slice x6 -> x0, local copies, waits for them, and re-layouts: 14.3 us -> none  [the longest x3 6.59 us: outward(): return jnp.concatenate([field[..., 1:], ghost[..., None]], axis=-1)]
    concatenate x2 -> x0, local copies, waits for them, and re-layouts: 12.9 us -> none  [with_halo(): jnp.concatenate([lax.ppermute(tail, axis, [(i, (i + 1) % count) for i in...]
    neg x4 -> x0, other arithmetic: 7.08 us -> none  [the longest x3 7.08 us: beyond_wall(): return outward(field, -field[..., -1])]
    mul x4 -> x0, other arithmetic: 6.67 us -> none  [the longest x1 6.66 us: per_device(): return (GAMMA * time_step * explicit, time_step)]
  transfers between devices with their start and end apart: 5 -> 5, of which waited for: 0 -> 0; matrix products, arithmetic and copies ran while one was open for 31% -> 0% of each run, Pallas kernels for 0% -> 46%
where the time goes in v1:
time: 154 us; the launch traced here: 153 us
  Pallas kernels  89.5 us (58%)
  blocking collectives  43.6 us (28%)
  starting transfers between devices  10.6 us (7%)
  local copies, waits for them, and re-layouts  6.42 us (4%)
  between operations  2.57 us (2%)
    pallas_call x1, Pallas kernels, per_device(): pl.pallas_call(interior, out_shape=shape(velocity.shape, f32), in_specs=[...  45.8 us
    all_gather x1, blocking collectives, per_device(): everyone = lax.all_gather(pay, ('az', 'ax'))  43.6 us
    pallas_call x1, Pallas kernels, per_device(): pl.pallas_call(theta_edges, out_shape=(pair, pair), in_specs=[anywhere],...  24.9 us
    pallas_call x1, Pallas kernels, per_device(): pl.pallas_call(first_pass, out_shape=(edge, edge, shape((axial, radial),...  11.9 us
    ppermute x5, starting transfers between devices, shifted(): lax.ppermute(block, axis, [((i - distance) % count, i) for i in range(cou...  10.6 us
    pallas_call x1, Pallas kernels, per_device(): pl.pallas_call(edges, out_shape=shape(velocity.shape, f32), in_specs=[sme...  6.9 us
    unnamed x8, local copies, waits for them, and re-layouts  6.4 us
  transfers between devices with their start and end apart: 5, of which 0 were waited for; matrix products, arithmetic and copies ran while one was open for 0% of the time, Pallas kernels for 46%

profile of v1, /device:TPU:0, one launch (start us, length us, event | category | flops | bytes accessed | tf_op | source)
XLA Modules:
  0.0 153.4 jit_solution(13606031743916431108)
XLA Ops:
  0.6 0.0 copy-start
  0.6 2.8 %copy-done = f32[3,32,128,128]{3,2,1,0:T(8,128)S(1)} copy-done((f32[3,32,128,128]{3,2,1,0:T(8,128)S(1)}, f32[3,32,128,128]{3,2,1,0:T(8,128)}, u32[]{:S(2)}) %copy-start) | copy-done | bytes 6291480
  3.4 0.0 copy-start.2
  3.4 0.8 copy-done.2
  4.3 0.0 copy-start.3
  4.3 11.9 %first_pass.1 = (f32[3,32,2,128]{3,2,1,0:T(2,128)S(1)}, f32[3,32,2,128]{3,2,1,0:T(2,128)S(1)}, f32[128,128]{1,0:T(8,128)S(1)}, f32[8,128]{1,0:T(8,128)S(1)}) custom-call(f32[3,32,128,128]{3,2,1,0:T(8,128)S(1)} %copy-done, f32[16,8,128]{2,1,0:T(8,128)S(1)} %copy-done.2), custom_call_target="tpu_custom_call" | custom-call | tf_op jit(solution)/shard_map/first_pass/pallas_call | solution.py:383
  16.1 4.1 %collective-permute-start.4 = (f32[128,128]{1,0:T(8,128)S(1)}, f32[128,128]{1,0:T(8,128)S(1)}, u32[]{:S(2)}, u32[]{:S(2)}) collective-permute-start(f32[128,128]{1,0:T(8,128)S(1)} %get-tuple-element.13), channel_id=1, source_target_pairs={{16,0},{20,4},{24,8},{28,12},{0,16},{4,20},{8,24},{12,28},{17,1},{... | collective-permute-start | bytes 196616 | tf_op jit(solution)/shard_map/ppermute | solution.py:355
  20.2 0.0 collective-permute-start.2
  20.2 1.7 %collective-permute-start.3 = (f32[3,32,2,128]{3,2,1,0:T(2,128)S(1)}, f32[3,32,2,128]{3,2,1,0:T(2,128)S(1)}, u32[]{:S(2)}, u32[]{:S(2)}) collective-permute-start(f32[3,32,2,128]{3,2,1,0:T(2,128)S(1)} %get-tuple-element.12), channel_id=1, source_target_pairs={{1,0},{2,1},{3,2},{0,3},{5,4},{6,5},{7,6},{4,7},{9,8},{10,9},{11,1... | collective-permute-start | bytes 294920 | tf_op jit(solution)/shard_map/ppermute | solution.py:355
  22.0 24.9 %theta_edges.1 = (f32[3,2,128,128]{3,2,1,0:T(8,128)}, f32[3,2,128,128]{3,2,1,0:T(8,128)}) custom-call(f32[3,32,128,128]{3,2,1,0:T(8,128)} %v_ref.7), custom_call_target="tpu_custom_call" | custom-call | tf_op jit(solution)/shard_map/theta_edges/pallas_call | solution.py:371
  46.9 1.6 %collective-permute-start = (f32[3,2,128,128]{3,2,1,0:T(8,128)}, f32[3,2,128,128]{3,2,1,0:T(8,128)S(1)}, u32[]{:S(2)}, u32[]{:S(2)}) collective-permute-start(f32[3,2,128,128]{3,2,1,0:T(8,128)} %get-tuple-element.9), channel_id=1, source_target_pairs={{28,0},{0,4},{4,8},{8,12},{12,16},{16,20},{20,24},{24,28},{29,1},{... | collective-permute-start | bytes 1179656 | tf_op jit(solution)/shard_map/ppermute | solution.py:355
  48.5 3.2 %collective-permute-start.1 = (f32[3,2,128,128]{3,2,1,0:T(8,128)}, f32[3,2,128,128]{3,2,1,0:T(8,128)S(1)}, u32[]{:S(2)}, u32[]{:S(2)}) collective-permute-start(f32[3,2,128,128]{3,2,1,0:T(8,128)} %get-tuple-element.10), channel_id=1, source_target_pairs={{4,0},{8,4},{12,8},{16,12},{20,16},{24,20},{28,24},{0,28},{5,1},{9... | collective-permute-start | bytes 1179656 | tf_op jit(solution)/shard_map/ppermute | solution.py:355
  51.7 43.6 %all-gather = f32[256,128]{1,0:T(8,128)S(1)} all-gather(f32[8,128]{1,0:T(8,128)S(1)} %get-tuple-element.8), channel_id=2, replica_groups=mesh['az'=8,'ax'=4] {'az','ax'}, dimensions={0}, use_global_device_ids=true | all-gather | bytes 135168 | tf_op jit(solution)/shard_map/all_gather | solution.py:398
  95.3 0.6 slice_reduce_fusion
  96.7 0.0 collective-permute-done.4.inner_ref
  96.7 0.0 collective-permute-done.2.low_ref
  96.7 0.0 collective-permute-done.3.high_ref
  96.7 0.0 copy-done.3
  96.7 0.0 copy-start.1
  96.7 2.8 %copy-done.1 = f32[3,32,128,128]{3,2,1,0:T(8,128)S(1)} copy-done((f32[3,32,128,128]{3,2,1,0:T(8,128)S(1)}, f32[3,32,128,128]{3,2,1,0:T(8,128)}, u32[]{:S(2)}) %copy-start.1) | copy-done | bytes 6291480
  99.5 45.8 %interior.1.part_ref = f32[3,32,128,128]{3,2,1,0:T(8,128)} custom-call(f32[1]{0:T(128)} %bitcast.1.scale_ref, f32[3,32,128,128]{3,2,1,0:T(8,128)S(1)} %copy-done.1, f32[3,32,2,128]{3,2,1,0:T(2,128)S(1)} %collective-permute-done.2.low_ref, f32[3,32,2,128]{3,2,1,0:T(2,128)S(1)} %collective-permute-done.3.high_ref, ...), custom_call_target="tpu_custom_call" | custom-call | tf_op jit(solution)/shard_map/interior/pallas_call | solution.py:408
  145.3 0.0 collective-permute-done.below_ref
  145.3 0.0 collective-permute-done.1.above_ref
  145.3 6.9 %edges.1 = f32[3,32,128,128]{3,2,1,0:T(8,128)} custom-call(f32[1]{0:T(128)} %bitcast.1.scale_ref, f32[3,32,128,128]{3,2,1,0:T(8,128)S(1)} %copy-done.1, f32[3,2,128,128]{3,2,1,0:T(8,128)S(1)} %collective-permute-done.below_ref, f32[3,2,128,128]{3,2,1,0:T(8,128)S(1)} %collective-permute-done.1.above_ref, ...), custom_call_target="tpu_custom_call", output_to_operand_aliasing={{}: (9, {})} | custom-call | tf_op jit(solution)/shard_map/edges/pallas_call | solution.py:422
  (2 shorter events, 0.0 us)
Async XLA Ops:
  0.6 2.8 %copy-start = (f32[3,32,128,128]{3,2,1,0:T(8,128)S(1)}, f32[3,32,128,128]{3,2,1,0:T(8,128)}, u32[]{:S(2)}) copy-start(f32[3,32,128,128]{3,2,1,0:T(8,128)} %v_ref.7) | copy-start | bytes 18874372
  3.4 0.8 copy-start.2
  4.3 92.4 %copy-start.3 = (f32[16,8,128]{2,1,0:T(8,128)S(1)}, f32[16,8,128]{2,1,0:T(8,128)}, u32[]{:S(2)}) copy-start(f32[16,8,128]{2,1,0:T(8,128)} %constant.60.clone.coef_ref) | copy-start | bytes 196612
  16.1 80.5 %collective-permute-start.4 = (f32[128,128]{1,0:T(8,128)S(1)}, f32[128,128]{1,0:T(8,128)S(1)}, u32[]{:S(2)}, u32[]{:S(2)}) collective-permute-start(f32[128,128]{1,0:T(8,128)S(1)} %get-tuple-element.13), channel_id=1, source_target_pairs={{16,0},{20,4},{24,8},{28,12},{0,16},{4,20},{8,24},{12,28},{17,1},{... | collective-permute-start | bytes 196616 | tf_op jit(solution)/shard_map/ppermute | solution.py:355
  20.2 76.4 %collective-permute-start.2 = (f32[3,32,2,128]{3,2,1,0:T(2,128)S(1)}, f32[3,32,2,128]{3,2,1,0:T(2,128)S(1)}, u32[]{:S(2)}, u32[]{:S(2)}) collective-permute-start(f32[3,32,2,128]{3,2,1,0:T(2,128)S(1)} %get-tuple-element.11), channel_id=1, source_target_pairs={{3,0},{0,1},{1,2},{2,3},{7,4},{4,5},{5,6},{6,7},{11,8},{8,9},{9,10... | collective-permute-start | bytes 294920 | tf_op jit(solution)/shard_map/ppermute | solution.py:355
  20.2 76.5 %collective-permute-start.3 = (f32[3,32,2,128]{3,2,1,0:T(2,128)S(1)}, f32[3,32,2,128]{3,2,1,0:T(2,128)S(1)}, u32[]{:S(2)}, u32[]{:S(2)}) collective-permute-start(f32[3,32,2,128]{3,2,1,0:T(2,128)S(1)} %get-tuple-element.12), channel_id=1, source_target_pairs={{1,0},{2,1},{3,2},{0,3},{5,4},{6,5},{7,6},{4,7},{9,8},{10,9},{11,1... | collective-permute-start | bytes 294920 | tf_op jit(solution)/shard_map/ppermute | solution.py:355
  46.9 98.4 %collective-permute-start = (f32[3,2,128,128]{3,2,1,0:T(8,128)}, f32[3,2,128,128]{3,2,1,0:T(8,128)S(1)}, u32[]{:S(2)}, u32[]{:S(2)}) collective-permute-start(f32[3,2,128,128]{3,2,1,0:T(8,128)} %get-tuple-element.9), channel_id=1, source_target_pairs={{28,0},{0,4},{4,8},{8,12},{12,16},{16,20},{20,24},{24,28},{29,1},{... | collective-permute-start | bytes 1179656 | tf_op jit(solution)/shard_map/ppermute | solution.py:355
  48.5 96.8 %collective-permute-start.1 = (f32[3,2,128,128]{3,2,1,0:T(8,128)}, f32[3,2,128,128]{3,2,1,0:T(8,128)S(1)}, u32[]{:S(2)}, u32[]{:S(2)}) collective-permute-start(f32[3,2,128,128]{3,2,1,0:T(8,128)} %get-tuple-element.10), channel_id=1, source_target_pairs={{4,0},{8,4},{12,8},{16,12},{20,16},{24,20},{28,24},{0,28},{5,1},{9... | collective-permute-start | bytes 1179656 | tf_op jit(solution)/shard_map/ppermute | solution.py:355
  96.7 2.8 %copy-start.1 = (f32[3,32,128,128]{3,2,1,0:T(8,128)S(1)}, f32[3,32,128,128]{3,2,1,0:T(8,128)}, u32[]{:S(2)}) copy-start(f32[3,32,128,128]{3,2,1,0:T(8,128)} %v_ref.7) | copy-start | bytes 18874372

commit v2 on v1

v2 whole, which is shorter than its diff:
```python
import functools
import math

import jax
import jax.numpy as jnp
import numpy as np
from jax import lax
from jax.experimental import pallas as pl
from jax.experimental.pallas import tpu as pltpu
from jax.sharding import PartitionSpec as P

AXIAL_STEP = 0.01
VISCOSITY = 0.001
CFL_TARGET = 1.2
GAMMA = 8.0 / 15.0

PAD = 8
HALO = 2
GROUP = 4
UNROLL = 4

(
    WALL,
    RATE_R,
    RATE_T,
    RADIAL_C,
    THETA_C,
    SECOND_C,
    CENTRE_Z,
    CENTRE_T,
    CURVE_T,
    TURN_T,
    RADIAL_F,
    THETA_F,
    SECOND_F,
    CENTRE_R,
    CURVE_R,
    TURN_R,
    COUNT,
) = range(17)


def coefficients(radial, theta_step):
    dr = 1.0 / radial
    index = np.arange(radial, dtype=np.float64)
    centre = (index + 0.5) * dr
    face = (index + 1.0) * dr
    wall = np.where(index < radial - 1.5, 1.0, 0.0)
    h = theta_step
    nu = VISCOSITY
    rows = np.zeros((COUNT, radial))
    rows[WALL] = wall
    rows[RATE_R] = wall / dr
    rows[RATE_T] = 1.0 / (centre * h)
    common = -2.0 * nu / dr**2 - 30.0 * nu / (12.0 * AXIAL_STEP**2)
    rows[RADIAL_C] = nu / (2.0 * dr * centre)
    rows[THETA_C] = -1.0 / (12.0 * h * centre)
    rows[SECOND_C] = nu / (12.0 * h * h * centre**2)
    rows[CENTRE_Z] = common - 30.0 * rows[SECOND_C]
    rows[CENTRE_T] = rows[CENTRE_Z] - nu / centre**2
    rows[CURVE_T] = 0.25 / centre
    rows[TURN_T] = nu / (h * centre**2)
    rows[RADIAL_F] = nu / (2.0 * dr * face)
    rows[THETA_F] = -0.25 / (12.0 * h * face)
    rows[SECOND_F] = nu / (12.0 * h * h * face**2)
    rows[CENTRE_R] = common - 30.0 * rows[SECOND_F] - nu / face**2
    rows[CURVE_R] = 1.0 / (16.0 * face)
    rows[TURN_R] = -nu / (h * face**2)
    return np.broadcast_to(rows[:, None, :], (COUNT, 8, radial)).astype(np.float32)


def terms(vel, ghost, coef, j, k, dr):
    lane = lax.broadcasted_iota(jnp.int32, (8, 128), 1)
    first_lane = lane == 0
    last_lane = lane == 127

    def at(component, dj, dk):
        return vel[component, j + HALO + dj, pl.ds(k + PAD + dk, 8), :]

    def out(x):
        return pltpu.roll(x, 127, 1)

    def inn(x):
        return pltpu.roll(x, 1, 1)

    nu = VISCOSITY
    lap = nu / dr**2
    adv_z = -1.0 / (12.0 * AXIAL_STEP)
    vis_z = nu / (12.0 * AXIAL_STEP**2)

    def pieces(component):
        p1, m1, p2, m2 = (at(component, d, 0) for d in (1, -1, 2, -2))
        first_t = 8.0 * (p1 - m1) - (p2 - m2)
        second_t = 16.0 * (p1 + m1) - (p2 + m2)
        p1, m1, p2, m2 = (at(component, 0, d) for d in (1, -1, 2, -2))
        first_z = 8.0 * (p1 - m1) - (p2 - m2)
        second_z = 16.0 * (p1 + m1) - (p2 + m2)
        return first_t, second_t, first_z, second_z

    a, b, c = (at(i, 0, 0) for i in range(3))
    a_in = inn(a)
    pair_a = a + a_in
    a_side = at(0, 1, 0)
    pair_side = a_side + inn(a_side)
    a_next = at(0, 0, 1)
    pair_next = a_next + inn(a_next)

    first_t, second_t, first_z, second_z = pieces(2)
    c_out = out(c)
    up = jnp.where(last_lane, -c, c_out)
    low = jnp.where(first_lane, ghost(2), inn(c))
    u_r = pair_a + pair_next
    u_t = (at(1, -1, 0) + b) + (at(1, -1, 1) + at(1, 0, 1))
    h_z = (up - low) * (coef(RADIAL_C) - u_r * (0.125 / dr)) + (up + low) * lap
    h_z = h_z + first_t * (u_t * (0.25 * coef(THETA_C)))
    h_z = h_z + second_t * coef(SECOND_C) + second_z * vis_z
    h_z = h_z + c * (coef(CENTRE_Z) + first_z * adv_z)

    first_t, second_t, first_z, second_z = pieces(1)
    b_out = out(b)
    up = jnp.where(last_lane, -b, b_out)
    low = jnp.where(first_lane, ghost(1), inn(b))
    u_r = pair_a + pair_side
    c_back = at(2, 0, -1)
    u_z = (c_back + c) + (at(2, 1, -1) + at(2, 1, 0))
    h_t = (up - low) * (coef(RADIAL_C) - u_r * (0.125 / dr)) + (up + low) * lap
    h_t = h_t + b * (coef(CENTRE_T) + first_t * coef(THETA_C) - u_r * coef(CURVE_T))
    h_t = h_t + second_t * coef(SECOND_C) + second_z * vis_z
    h_t = h_t + first_z * (u_z * (0.25 * adv_z))
    h_t = h_t + (pair_side - pair_a) * coef(TURN_T)

    first_t, second_t, first_z, second_z = pieces(0)
    up = out(a)
    low = jnp.where(first_lane, ghost(0), a_in)
    b_back = at(1, -1, 0)
    pair_b = b + b_out
    pair_back = b_back + out(b_back)
    u_t = pair_b + pair_back
    u_z = (c + c_out) + (c_back + out(c_back))
    h_r = (up - low) * (coef(RADIAL_F) - a * (0.5 / dr)) + (up + low) * lap
    h_r = h_r + u_t * (u_t * coef(CURVE_R) + first_t * coef(THETA_F))
    h_r = h_r + second_t * coef(SECOND_F) + second_z * vis_z
    h_r = h_r + first_z * (u_z * (0.25 * adv_z)) + a * coef(CENTRE_R)
    h_r = h_r + (pair_b - pair_back) * coef(TURN_R)
    return h_r, h_t, h_z


def theta_edges(v_ref, head_ref, tail_ref):
    count = v_ref.shape[1]
    for n in range(3):
        for q in range(HALO):
            head_ref[n, q] = v_ref[n, q]
            tail_ref[n, q] = v_ref[n, count - HALO + q]


def first_pass(v_ref, coef_ref, vel_ref, low_ref, high_ref, inner_ref, pay_ref):
    _, planes, axial, radial = v_ref.shape
    lane = lax.broadcasted_iota(jnp.int32, (8, radial), 1)
    sign = jnp.where(lane < 2 * planes, -1.0, 1.0).astype(jnp.float32)

    def rows(i, largest):
        k = pl.ds(pl.multiple_of(i * 8, 8), 8)
        padded = pl.ds(pl.multiple_of(i * 8 + PAD, 8), 8)

        def group(g, carry):
            largest, inner = carry
            for q in range(GROUP):
                j = g * GROUP + q
                a, b, c = (v_ref[n, j, k, :] for n in range(3))
                a = a * coef_ref[WALL]
                rate = (
                    jnp.abs(a) * float(radial)
                    + jnp.abs(b) * coef_ref[RATE_T]
                    + jnp.abs(c) * (1.0 / AXIAL_STEP)
                )
                largest = jnp.maximum(largest, rate)
                for n, x in enumerate((a, b, c)):
                    vel_ref[n, j + HALO, padded, :] = x
                    place = n * planes + j
                    inner = jnp.where(lane == place, pltpu.roll(x, place, 1), inner)
            return largest, inner

        zero = jnp.zeros((8, radial), jnp.float32)
        largest, inner = lax.fori_loop(0, planes // GROUP, group, (largest, zero))
        inner_ref[k, :] = inner * sign
        return largest

    largest = lax.fori_loop(0, axial // 8, rows, jnp.zeros((8, radial), jnp.float32))
    top = jnp.max(largest, axis=(0, 1), keepdims=True)
    pay_ref[...] = jnp.broadcast_to(top, pay_ref.shape)
    inner_ref[0:8, :] = jnp.where(lane == radial - 1, top, inner_ref[0:8, :])

    def ends(j, carry):
        for n in range(3):
            low_ref[n, j] = v_ref[n, j, 0:2, :]
            high_ref[n, j] = v_ref[n, j, axial - 2 : axial, :]
        return carry

    lax.fori_loop(0, planes, ends, 0)
    last = lax.broadcasted_iota(jnp.int32, (2, radial), 1) == radial - 1
    for ref in (low_ref, high_ref):
        ref[0, 0] = jnp.where(last, top, ref[0, 0])


def fold(low_ref, high_ref, inner_ref, pay_ref, coef_ref, vel_in, out_ref, vel_ref):
    del vel_in
    planes, radial = low_ref.shape[1], low_ref.shape[3]
    axial = inner_ref.shape[0]
    top = jnp.maximum(
        jnp.maximum(low_ref[0, 0, 0:1, :], high_ref[0, 0, 0:1, :]), inner_ref[0:1, :]
    )
    lane = lax.broadcasted_iota(jnp.int32, (1, radial), 1)
    top = jnp.max(jnp.where(lane == radial - 1, top, 0.0), axis=(0, 1), keepdims=True)
    out_ref[...] = jnp.maximum(pay_ref[...], top)
    out_ref[1:2, :] = high_ref[1, planes - 1, 0:1, :]
    out_ref[2:3, :] = low_ref[2, 0, 1:2, :]
    wall = coef_ref[WALL, 0:2, :]

    def plane(j, carry):
        for n in range(3):
            mask = wall if n == 0 else 1.0
            vel_ref[n, j + HALO, PAD - 2 : PAD, :] = low_ref[n, j] * mask
            vel_ref[n, j + HALO, PAD + axial : PAD + axial + 2, :] = high_ref[n, j] * mask
        return carry

    lax.fori_loop(0, planes, plane, 0)


def sweep(vel_ref, inner_ref, coef_ref, first, last, write):
    axial, radial = inner_ref.shape
    planes = vel_ref.shape[1] - 2 * HALO

    def plane(j, carry):
        def rows(i, carry):
            k = pl.multiple_of(i * 8, 8)
            inner = inner_ref[pl.ds(k, 8), :]

            def ghost(component):
                turn = lax.rem(2 * radial - component * planes - j, radial)
                return pltpu.roll(inner, turn, 1)

            found = terms(vel_ref, ghost, lambda n: coef_ref[n], j, k, 1.0 / radial)
            for n, value in enumerate(found):
                write(n, j, pl.ds(k, 8), value)
            return carry

        return lax.fori_loop(0, axial // 8, rows, carry, unroll=UNROLL)

    lax.fori_loop(first, last, plane, 0)


def interior(first, last, vel_ref, inner_ref, coef_ref, _, out_ref):
    def write(n, j, k, value):
        out_ref[n, j - first, k, :] = value

    sweep(vel_ref, inner_ref, coef_ref, first, last, write)


def finish(
    spans,
    below_ref,
    above_ref,
    up_ref,
    down_ref,
    pay_ref,
    far_ref,
    inner_ref,
    coef_ref,
    *refs,
):
    parts, (vel_in, out_ref, step_ref, vel_ref, res, sems) = refs[: len(spans)], refs[len(spans) :]
    del vel_in
    axial, radial = inner_ref.shape
    planes = res.shape[1]
    largest = jnp.max(jnp.maximum(pay_ref[0:1, :], far_ref[0:1, :]))
    time_step = CFL_TARGET / (largest + 1e-06)
    step_ref[0] = time_step
    scale = GAMMA * time_step

    def store(first, last, n):
        part = pl.ds(first, last - first)
        return pltpu.make_async_copy(res.at[:, part], out_ref.at[:, part], sems.at[n])

    def write(n, j, k, value):
        factor = scale * coef_ref[WALL] if n == 0 else scale
        res[n, j, k, :] = value * factor

    pending = []
    for part, (first, last) in zip(parts, spans):

        def plane(j, carry, part=part, first=first):
            def rows(i, carry):
                k = pl.ds(pl.multiple_of(i * 8, 8), 8)
                for n in range(3):
                    write(n, j, k, part[n, j - first, k, :])
                return carry

            return lax.fori_loop(0, axial // 8, rows, carry, unroll=UNROLL)

        lax.fori_loop(first, last, plane, 0)
        pending.append(store(first, last, len(pending)))
        pending[-1].start()

    cells = pl.ds(PAD, axial)
    for q in range(HALO):
        for ref, place in ((below_ref, q), (above_ref, HALO + planes + q)):
            vel_ref[0, place, cells, :] = ref[0, q] * coef_ref[WALL, 0:1, :]
            vel_ref[1, place, cells, :] = ref[1, q]
            vel_ref[2, place, cells, :] = ref[2, q]
    vel_ref[1, HALO - 1, PAD + axial : PAD + axial + 1, :] = up_ref[1:2, :]
    vel_ref[2, HALO + planes, PAD - 1 : PAD, :] = down_ref[2:3, :]
    for first in (0, planes - HALO):
        sweep(vel_ref, inner_ref, coef_ref, first, first + HALO, write)
        pending.append(store(first, first + HALO, len(pending)))
        pending[-1].start()
    for copy in pending:
        copy.wait()


def shifted(block, distance):
    sizes = lax.axis_size("az"), lax.axis_size("ax")
    route = []
    for i in range(sizes[0]):
        for k in range(sizes[1]):
            source = (i - distance[0]) % sizes[0], (k - distance[1]) % sizes[1]
            route.append((source[0] * sizes[1] + source[1], i * sizes[1] + k))
    return lax.ppermute(block, ("az", "ax"), route)


def rounds(sizes, covered):
    plan = []
    shifts = [(i, k) for i in range(sizes[0]) for k in range(sizes[1])]

    def moved(cells, by):
        return {((i + by[0]) % sizes[0], (k + by[1]) % sizes[1]) for i, k in cells}

    def hops(by):
        return min(by[0], sizes[0] - by[0]) + min(by[1], sizes[1] - by[1])

    while len(covered) < sizes[0] * sizes[1]:
        best = max(shifts, key=lambda by: (len(covered | moved(covered, by)), -hops(by)))
        covered = covered | moved(covered, best)
        plan.append(best)
    return plan


def per_device(velocity):
    _, planes, axial, radial = velocity.shape
    sizes = lax.axis_size("az"), lax.axis_size("ax")
    theta_step = 2.0 * math.pi / (sizes[0] * planes)
    coef = jnp.asarray(coefficients(radial, theta_step))
    f32 = jnp.float32
    anywhere = pl.BlockSpec(memory_space=pl.ANY)
    vmem = pl.BlockSpec(memory_space=pltpu.VMEM)
    smem = pl.BlockSpec(memory_space=pltpu.SMEM)

    def shape(*sizes):
        return jax.ShapeDtypeStruct(sizes, f32)

    def call(kernel, name, work, scratch=0, **kwargs):
        return pl.pallas_call(
            kernel,
            name=name,
            compiler_params=pltpu.CompilerParams(vmem_limit_bytes=(4 + scratch) * 2**20),
            cost_estimate=pl.CostEstimate(
                flops=work, bytes_accessed=velocity.size * 4, transcendentals=0
            ),
            **kwargs,
        )

    pair = shape(3, HALO, axial, radial)
    head, tail = call(
        theta_edges,
        "theta_edges",
        0,
        out_shape=(pair, pair),
        in_specs=[vmem],
        out_specs=(vmem, vmem),
    )(velocity)
    below = shifted(tail, (1, 0))
    above = shifted(head, (-1, 0))

    edge = shape(3, planes, 2, radial)
    padded = shape(3, planes + 2 * HALO, axial + 2 * PAD, radial)
    vel, first, last, inner, pay = call(
        first_pass,
        "first_pass",
        10 * velocity.size,
        out_shape=(padded, edge, edge, shape(axial, radial), shape(8, radial)),
        in_specs=[vmem, vmem],
        out_specs=(vmem,) * 5,
    )(velocity, coef)
    low = shifted(last, (0, 1))
    high = shifted(first, (0, -1))
    inner = shifted(inner, (sizes[0] // 2, 0))
    pay, vel = call(
        fold,
        "fold",
        velocity.size // planes,
        out_shape=(shape(8, radial), padded),
        in_specs=[vmem] * 6,
        out_specs=(vmem, vmem),
        input_output_aliases={5: 1},
    )(low, high, inner, pay, coef, vel)
    up = shifted(pay, (1, 0))
    down = shifted(pay, (-1, 0))

    known = {(0, 0), (0, 1), (0, sizes[1] - 1), (sizes[0] // 2, 0)}
    known = {((i + d) % sizes[0], k) for i, k in known for d in (-1, 0, 1)}
    plan = rounds(sizes, known)
    count = len(plan) + 1
    bounds = [
        HALO + (planes - 2 * HALO) * n // count for n in range(count + 1)
    ]
    spans = list(zip(bounds[:-1], bounds[1:]))
    parts = []
    token = pay
    for n, (first, last) in enumerate(spans):
        parts.append(
            call(
                functools.partial(interior, first, last),
                f"interior_{n}",
                400 * (last - first) * axial * radial,
                out_shape=shape(3, last - first, axial, radial),
                in_specs=[vmem] * 4,
                out_specs=vmem,
            )(vel, inner, coef, token)
        )
        if n == 0:
            pay = jnp.maximum(pay, jnp.maximum(up, down))
            token = up
        else:
            pay = jnp.maximum(pay, far)
            token = far
        if n < len(plan):
            far = shifted(pay, plan[n])
    increment, time_step, _ = call(
        functools.partial(finish, spans),
        "finish",
        160 * velocity.size,
        scratch=8,
        out_shape=(shape(*velocity.shape), shape(1), padded),
        in_specs=[vmem] * (9 + len(parts)),
        out_specs=(anywhere, smem, vmem),
        scratch_shapes=[
            pltpu.VMEM(velocity.shape, f32),
            pltpu.SemaphoreType.DMA((len(parts) + 2,)),
        ],
        input_output_aliases={8 + len(parts): 2},
    )(below, above, up, down, pay, far, inner, coef, *parts, vel)
    return increment, time_step.reshape(())


def solution(mesh):
    return jax.shard_map(
        per_device,
        mesh=mesh,
        in_specs=(P(None, "az", "ax", None),),
        out_specs=(P(None, "az", "ax", None), P()),
        check_vma=False,
    )
```

time: 154 us -> 54.9 us (0.36)
  Pallas kernels: 89.5 us -> 31.6 us
  blocking collectives: 43.6 us -> 0 us
  waiting for transfers between devices: 0.01 us -> 7.3 us
  local copies, waits for them, and re-layouts: 6.42 us -> 2.78 us
  between operations: 2.57 us -> 0.74 us
    pallas_call x4 -> x7, Pallas kernels: 89.5 us -> 31.6 us  [the longest x3 15.5 us: per_device(): call(functools.partial(interior, first, last), f'interior_{n}', 400 * (la...]
    all_gather x1 -> x0, blocking collectives: 43.6 us -> none  [per_device(): everyone = lax.all_gather(pay, ('az', 'ax'))]
    ppermute x5 -> x9, waiting for transfers between devices: 0.01 us -> 7.3 us  [shifted(): return lax.ppermute(block, ('az', 'ax'), route)]
    unnamed x8 -> x4, local copies, waits for them, and re-layouts: 6.4 us -> 2.78 us
    ppermute x5 -> x9, starting transfers between devices: 10.6 us -> 11.5 us  [shifted(): return lax.ppermute(block, ('az', 'ax'), route)]
  transfers between devices with their start and end apart: 5 -> 9, of which waited for: 0 -> 3; matrix products, arithmetic and copies ran while one was open for 0% -> 0% of each run, Pallas kernels for 46% -> 50%
where the time goes in v2:
time: 54.9 us; the launch traced here: 53.9 us
  Pallas kernels  31.6 us (58%)
  starting transfers between devices  11.5 us (21%)
  waiting for transfers between devices  7.3 us (13%)
  local copies, waits for them, and re-layouts  2.78 us (5%)
  between operations  0.74 us (1%)
    pallas_call x3, Pallas kernels, per_device(): call(functools.partial(interior, first, last), f'interior_{n}', 400 * (la...  15.5 us
    ppermute x9, starting transfers between devices, shifted(): return lax.ppermute(block, ('az', 'ax'), route)  11.5 us
    pallas_call x1, Pallas kernels, per_device(): call(first_pass, 'first_pass', 10 * velocity.size, out_shape=(padded, edg...  11 us
    ppermute x9, waiting for transfers between devices, shifted(): return lax.ppermute(block, ('az', 'ax'), route)  7.3 us
    pallas_call x1, Pallas kernels, per_device(): call(functools.partial(finish, spans), 'finish', 160 * velocity.size, scr...  4.75 us
    unnamed x4, local copies, waits for them, and re-layouts  2.78 us
  transfers between devices with their start and end apart: 9, of which 3 were waited for; matrix products, arithmetic and copies ran while one was open for 0% of the time, Pallas kernels for 50%

profile of v2, /device:TPU:0, one launch (start us, length us, event | category | flops | bytes accessed | tf_op | source)
XLA Modules:
  0.0 53.9 jit_solution(10660442170430365721)
XLA Ops:
  0.6 0.0 copy-start
  0.6 2.8 %copy-done = f32[3,32,128,128]{3,2,1,0:T(8,128)S(1)} copy-done((f32[3,32,128,128]{3,2,1,0:T(8,128)S(1)}, f32[3,32,128,128]{3,2,1,0:T(8,128)}, u32[]{:S(2)}) %copy-start) | copy-done | bytes 6291480
  3.4 0.0 copy-start.1
  3.4 0.1 theta_edges.1
  3.5 3.0 %collective-permute-start = (f32[3,2,128,128]{3,2,1,0:T(8,128)S(1)}, f32[3,2,128,128]{3,2,1,0:T(8,128)S(1)}, u32[]{:S(2)}, u32[]{:S(2)}) collective-permute-start(f32[3,2,128,128]{3,2,1,0:T(8,128)S(1)} %get-tuple-element.13), channel_id=1, source_target_pairs={{28,0},{29,1},{30,2},{31,3},{0,4},{1,5},{2,6},{3,7},{4,8},{5,9},{6... | collective-permute-start | bytes 1179656 | tf_op jit(solution)/shard_map/ppermute | solution.py:327
  6.5 3.1 %collective-permute-start.1 = (f32[3,2,128,128]{3,2,1,0:T(8,128)S(1)}, f32[3,2,128,128]{3,2,1,0:T(8,128)S(1)}, u32[]{:S(2)}, u32[]{:S(2)}) collective-permute-start(f32[3,2,128,128]{3,2,1,0:T(8,128)S(1)} %get-tuple-element.14), channel_id=1, source_target_pairs={{4,0},{5,1},{6,2},{7,3},{8,4},{9,5},{10,6},{11,7},{12,8},{13,9},{1... | collective-permute-start | bytes 1179656 | tf_op jit(solution)/shard_map/ppermute | solution.py:327
  9.6 0.0 copy-done.1
  9.6 11.0 %first_pass.1 = (f32[3,36,144,128]{3,2,1,0:T(8,128)S(1)}, f32[3,32,2,128]{3,2,1,0:T(2,128)S(1)}, f32[3,32,2,128]{3,2,1,0:T(2,128)S(1)}, f32[128,128]{1,0:T(8,128)S(1)}, f32[8,128]{1,0:T(8,128)S(1)}) custom-call(f32[3,32,128,128]{3,2,1,0:T(8,128)S(1)} %copy-done, f32[16,8,128]{2,1,0:T(8,128)S(1)} %copy-done.1), custom_call_target="tpu_custom_call" | custom-call | flops 15728640 | bytes 6291456 | tf_op jit(solution)/shard_map/first_pass/pallas_call | solution.py:385
  20.6 0.1 collective-permute-start.2
  20.6 1.7 %collective-permute-start.3 = (f32[3,32,2,128]{3,2,1,0:T(2,128)S(1)}, f32[3,32,2,128]{3,2,1,0:T(2,128)S(1)}, u32[]{:S(2)}, u32[]{:S(2)}) collective-permute-start(f32[3,32,2,128]{3,2,1,0:T(2,128)S(1)} %get-tuple-element.16), channel_id=1, source_target_pairs={{1,0},{2,1},{3,2},{0,3},{5,4},{6,5},{7,6},{4,7},{9,8},{10,9},{11,1... | collective-permute-start | bytes 294920 | tf_op jit(solution)/shard_map/ppermute | solution.py:327
  22.4 0.9 %collective-permute-start.4 = (f32[128,128]{1,0:T(8,128)S(1)}, f32[128,128]{1,0:T(8,128)S(1)}, u32[]{:S(2)}, u32[]{:S(2)}) collective-permute-start(f32[128,128]{1,0:T(8,128)S(1)} %get-tuple-element.17), channel_id=1, source_target_pairs={{16,0},{17,1},{18,2},{19,3},{20,4},{21,5},{22,6},{23,7},{24,8},{25... | collective-permute-start | bytes 196616 | tf_op jit(solution)/shard_map/ppermute | solution.py:327
  23.3 4.7 %collective-permute-done.4.inner_ref = f32[128,128]{1,0:T(8,128)S(1)} collective-permute-done((f32[128,128]{1,0:T(8,128)S(1)}, f32[128,128]{1,0:T(8,128)S(1)}, u32[]{:S(2)}, u32[]{:S(2)}) %collective-permute-start.4) | collective-permute-done | bytes 65568 | tf_op jit(solution)/shard_map/ppermute | solution.py:327
  27.9 0.0 collective-permute-done.2.low_ref
  27.9 0.0 collective-permute-done.3.high_ref
  27.9 0.4 fold.1
  28.3 2.5 %collective-permute-start.6 = (f32[8,128]{1,0:T(8,128)S(1)}, f32[8,128]{1,0:T(8,128)S(1)}, u32[]{:S(2)}, u32[]{:S(2)}) collective-permute-start(f32[8,128]{1,0:T(8,128)S(1)} %get-tuple-element.20._), channel_id=1, source_target_pairs={{4,0},{5,1},{6,2},{7,3},{8,4},{9,5},{10,6},{11,7},{12,8},{13,9},{1... | collective-permute-start | bytes 12296 | tf_op jit(solution)/shard_map/ppermute | solution.py:327
  30.8 0.0 collective-permute-start.5
  30.8 5.0 %interior_0.1.refs_0_ = f32[3,9,128,128]{3,2,1,0:T(8,128)S(1)} custom-call(f32[3,36,144,128]{3,2,1,0:T(8,128)S(1)} %get-tuple-element.21.vel_ref.refs_3_, f32[128,128]{1,0:T(8,128)S(1)} %collective-permute-done.4.inner_ref, f32[16,8,128]{2,1,0:T(8,128)S(1)} %copy-done.1, f32[8,128]{1,0:T(8,128)S(1)} %get-tuple-element.20._), custom_call_target="tpu_custom_call" | custom-call | flops 58982400 | bytes 6291456 | tf_op jit(solution)/shard_map/interior_0/pallas_call | solution.py:420
  35.8 0.0 collective-permute-done.6.down_ref
  35.8 1.3 %collective-permute-done.5._.up_ref = f32[8,128]{1,0:T(8,128)S(1)} collective-permute-done((f32[8,128]{1,0:T(8,128)S(1)}, f32[8,128]{1,0:T(8,128)S(1)}, u32[]{:S(2)}, u32[]{:S(2)}) %collective-permute-start.5) | collective-permute-done | bytes 4128 | tf_op jit(solution)/shard_map/ppermute | solution.py:327
  37.1 0.0 collective-permute-start.7
  37.1 5.0 %interior_1.1.refs_1_ = f32[3,9,128,128]{3,2,1,0:T(8,128)S(1)} custom-call(f32[3,36,144,128]{3,2,1,0:T(8,128)S(1)} %get-tuple-element.21.vel_ref.refs_3_, f32[128,128]{1,0:T(8,128)S(1)} %collective-permute-done.4.inner_ref, f32[16,8,128]{2,1,0:T(8,128)S(1)} %copy-done.1, f32[8,128]{1,0:T(8,128)S(1)} %collective-permute-done.5._.up_ref), custom_call_target="tpu_custom_call" | custom-call | flops 58982400 | bytes 6291456 | tf_op jit(solution)/shard_map/interior_1/pallas_call | solution.py:420
  42.1 1.3 %collective-permute-done.7._ = f32[8,128]{1,0:T(8,128)S(1)} collective-permute-done((f32[8,128]{1,0:T(8,128)S(1)}, f32[8,128]{1,0:T(8,128)S(1)}, u32[]{:S(2)}, u32[]{:S(2)}) %collective-permute-start.7) | collective-permute-done | bytes 4128 | tf_op jit(solution)/shard_map/ppermute | solution.py:327
  43.4 0.2 collective-permute-start.8
  43.6 5.5 %interior_2.1.refs_2_ = f32[3,10,128,128]{3,2,1,0:T(8,128)S(1)} custom-call(f32[3,36,144,128]{3,2,1,0:T(8,128)S(1)} %get-tuple-element.21.vel_ref.refs_3_, f32[128,128]{1,0:T(8,128)S(1)} %collective-permute-done.4.inner_ref, f32[16,8,128]{2,1,0:T(8,128)S(1)} %copy-done.1, f32[8,128]{1,0:T(8,128)S(1)} %collective-permute-done.7._), custom_call_target="tpu_custom_call" | custom-call | flops 65536000 | bytes 6291456 | tf_op jit(solution)/shard_map/interior_2/pallas_call | solution.py:420
  49.1 0.0 collective-permute-done.8.far_ref
  49.2 0.0 collective-permute-done.below_ref
  49.2 0.0 collective-permute-done.1.above_ref
  49.2 4.7 %finish.1 = (f32[3,32,128,128]{3,2,1,0:T(8,128)}, f32[1]{0:T(128)}, f32[3,36,144,128]{3,2,1,0:T(8,128)S(1)}) custom-call(f32[3,2,128,128]{3,2,1,0:T(8,128)S(1)} %collective-permute-done.below_ref, f32[3,2,128,128]{3,2,1,0:T(8,128)S(1)} %collective-permute-done.1.above_ref, ...), custom_call_target="tpu_custom_call", output_to_operand_aliasing={{2}: (11, {})} | custom-call | flops 251658240 | bytes 6291456 | tf_op jit(solution)/shard_map/finish/pallas_call | solution.py:437
  (3 shorter events, 0.0 us)
Async XLA Ops:
  0.6 2.8 %copy-start = (f32[3,32,128,128]{3,2,1,0:T(8,128)S(1)}, f32[3,32,128,128]{3,2,1,0:T(8,128)}, u32[]{:S(2)}) copy-start(f32[3,32,128,128]{3,2,1,0:T(8,128)} %v_ref.3) | copy-start | bytes 18874372
  3.4 6.2 %copy-start.1 = (f32[16,8,128]{2,1,0:T(8,128)S(1)}, f32[16,8,128]{2,1,0:T(8,128)}, u32[]{:S(2)}) copy-start(f32[16,8,128]{2,1,0:T(8,128)} %constant.2.clone.coef_ref) | copy-start | bytes 196612
  3.5 45.7 %collective-permute-start = (f32[3,2,128,128]{3,2,1,0:T(8,128)S(1)}, f32[3,2,128,128]{3,2,1,0:T(8,128)S(1)}, u32[]{:S(2)}, u32[]{:S(2)}) collective-permute-start(f32[3,2,128,128]{3,2,1,0:T(8,128)S(1)} %get-tuple-element.13), channel_id=1, source_target_pairs={{28,0},{29,1},{30,2},{31,3},{0,4},{1,5},{2,6},{3,7},{4,8},{5,9},{6... | collective-permute-start | bytes 1179656 | tf_op jit(solution)/shard_map/ppermute | solution.py:327
  6.5 42.7 %collective-permute-start.1 = (f32[3,2,128,128]{3,2,1,0:T(8,128)S(1)}, f32[3,2,128,128]{3,2,1,0:T(8,128)S(1)}, u32[]{:S(2)}, u32[]{:S(2)}) collective-permute-start(f32[3,2,128,128]{3,2,1,0:T(8,128)S(1)} %get-tuple-element.14), channel_id=1, source_target_pairs={{4,0},{5,1},{6,2},{7,3},{8,4},{9,5},{10,6},{11,7},{12,8},{13,9},{1... | collective-permute-start | bytes 1179656 | tf_op jit(solution)/shard_map/ppermute | solution.py:327
  20.6 7.4 %collective-permute-start.2 = (f32[3,32,2,128]{3,2,1,0:T(2,128)S(1)}, f32[3,32,2,128]{3,2,1,0:T(2,128)S(1)}, u32[]{:S(2)}, u32[]{:S(2)}) collective-permute-start(f32[3,32,2,128]{3,2,1,0:T(2,128)S(1)} %get-tuple-element.15), channel_id=1, source_target_pairs={{3,0},{0,1},{1,2},{2,3},{7,4},{4,5},{5,6},{6,7},{11,8},{8,9},{9,10... | collective-permute-start | bytes 294920 | tf_op jit(solution)/shard_map/ppermute | solution.py:327
  20.6 7.3 %collective-permute-start.3 = (f32[3,32,2,128]{3,2,1,0:T(2,128)S(1)}, f32[3,32,2,128]{3,2,1,0:T(2,128)S(1)}, u32[]{:S(2)}, u32[]{:S(2)}) collective-permute-start(f32[3,32,2,128]{3,2,1,0:T(2,128)S(1)} %get-tuple-element.16), channel_id=1, source_target_pairs={{1,0},{2,1},{3,2},{0,3},{5,4},{6,5},{7,6},{4,7},{9,8},{10,9},{11,1... | collective-permute-start | bytes 294920 | tf_op jit(solution)/shard_map/ppermute | solution.py:327
  22.4 5.6 %collective-permute-start.4 = (f32[128,128]{1,0:T(8,128)S(1)}, f32[128,128]{1,0:T(8,128)S(1)}, u32[]{:S(2)}, u32[]{:S(2)}) collective-permute-start(f32[128,128]{1,0:T(8,128)S(1)} %get-tuple-element.17), channel_id=1, source_target_pairs={{16,0},{17,1},{18,2},{19,3},{20,4},{21,5},{22,6},{23,7},{24,8},{25... | collective-permute-start | bytes 196616 | tf_op jit(solution)/shard_map/ppermute | solution.py:327
  28.3 7.5 %collective-permute-start.6 = (f32[8,128]{1,0:T(8,128)S(1)}, f32[8,128]{1,0:T(8,128)S(1)}, u32[]{:S(2)}, u32[]{:S(2)}) collective-permute-start(f32[8,128]{1,0:T(8,128)S(1)} %get-tuple-element.20._), channel_id=1, source_target_pairs={{4,0},{5,1},{6,2},{7,3},{8,4},{9,5},{10,6},{11,7},{12,8},{13,9},{1... | collective-permute-start | bytes 12296 | tf_op jit(solution)/shard_map/ppermute | solution.py:327
  30.8 6.3 %collective-permute-start.5 = (f32[8,128]{1,0:T(8,128)S(1)}, f32[8,128]{1,0:T(8,128)S(1)}, u32[]{:S(2)}, u32[]{:S(2)}) collective-permute-start(f32[8,128]{1,0:T(8,128)S(1)} %get-tuple-element.20._), channel_id=1, source_target_pairs={{28,0},{29,1},{30,2},{31,3},{0,4},{1,5},{2,6},{3,7},{4,8},{5,9},{6... | collective-permute-start | bytes 12296 | tf_op jit(solution)/shard_map/ppermute | solution.py:327
  37.1 6.3 %collective-permute-start.7 = (f32[8,128]{1,0:T(8,128)S(1)}, f32[8,128]{1,0:T(8,128)S(1)}, u32[]{:S(2)}, u32[]{:S(2)}) collective-permute-start(f32[8,128]{1,0:T(8,128)S(1)} %maximum_maximum_fusion), channel_id=1, source_target_pairs={{22,0},{23,1},{20,2},{21,3},{26,4},{27,5},{24,6},{25,7},{30,8},{31... | collective-permute-start | bytes 12296 | tf_op jit(solution)/shard_map/ppermute | solution.py:327
  43.4 5.7 %collective-permute-start.8 = (f32[8,128]{1,0:T(8,128)S(1)}, f32[8,128]{1,0:T(8,128)S(1)}, u32[]{:S(2)}, u32[]{:S(2)}) collective-permute-start(f32[8,128]{1,0:T(8,128)S(1)} %max.14), channel_id=1, source_target_pairs={{24,0},{25,1},{26,2},{27,3},{28,4},{29,5},{30,6},{31,7},{0,8},{1,9... | collective-permute-start | bytes 12296 | tf_op jit(solution)/shard_map/ppermute | solution.py:327

commit v3 on v2

--- a/solution.py
+++ b/solution.py
@@ -16,15 +16,14 @@
 
 PAD = 8
 HALO = 2
-GROUP = 4
 UNROLL = 4
 
 (
     WALL,
-    RATE_R,
     RATE_T,
     RADIAL_C,
     THETA_C,
+    CROSS_Z,
     SECOND_C,
     CENTRE_Z,
     CENTRE_T,
@@ -50,11 +49,11 @@
     nu = VISCOSITY
     rows = np.zeros((COUNT, radial))
     rows[WALL] = wall
-    rows[RATE_R] = wall / dr
     rows[RATE_T] = 1.0 / (centre * h)
     common = -2.0 * nu / dr**2 - 30.0 * nu / (12.0 * AXIAL_STEP**2)
     rows[RADIAL_C] = nu / (2.0 * dr * centre)
     rows[THETA_C] = -1.0 / (12.0 * h * centre)
+    rows[CROSS_Z] = 0.25 * rows[THETA_C]
     rows[SECOND_C] = nu / (12.0 * h * h * centre**2)
     rows[CENTRE_Z] = common - 30.0 * rows[SECOND_C]
     rows[CENTRE_T] = rows[CENTRE_Z] - nu / centre**2
@@ -88,72 +87,61 @@
     adv_z = -1.0 / (12.0 * AXIAL_STEP)
     vis_z = nu / (12.0 * AXIAL_STEP**2)
 
-    def pieces(component):
-        p1, m1, p2, m2 = (at(component, d, 0) for d in (1, -1, 2, -2))
-        first_t = 8.0 * (p1 - m1) - (p2 - m2)
-        second_t = 16.0 * (p1 + m1) - (p2 + m2)
-        p1, m1, p2, m2 = (at(component, 0, d) for d in (1, -1, 2, -2))
-        first_z = 8.0 * (p1 - m1) - (p2 - m2)
-        second_z = 16.0 * (p1 + m1) - (p2 + m2)
-        return first_t, second_t, first_z, second_z
-
-    a, b, c = (at(i, 0, 0) for i in range(3))
+    def differences(p1, m1, p2, m2):
+        return 8.0 * (p1 - m1) - (p2 - m2), 16.0 * (p1 + m1) - (p2 + m2)
+
+    def pieces(n):
+        over = [at(n, d, 0) for d in (1, -1, 2, -2)]
+        along = [at(n, 0, d) for d in (1, -1, 2, -2)]
+        return over, along, differences(*over), differences(*along)
+
+    a, b, c = (at(n, 0, 0) for n in range(3))
+    (a_side, *_), (a_next, *_), a_theta, a_axial = pieces(0)
+    (_, b_back, *_), (b_next, *_), b_theta, b_axial = pieces(1)
+    (c_side, *_), (_, c_back, *_), c_theta, c_axial = pieces(2)
     a_in = inn(a)
     pair_a = a + a_in
-    a_side = at(0, 1, 0)
     pair_side = a_side + inn(a_side)
-    a_next = at(0, 0, 1)
     pair_next = a_next + inn(a_next)
 
-    first_t, second_t, first_z, second_z = pieces(2)
     c_out = out(c)
     up = jnp.where(last_lane, -c, c_out)
     low = jnp.where(first_lane, ghost(2), inn(c))
     u_r = pair_a + pair_next
-    u_t = (at(1, -1, 0) + b) + (at(1, -1, 1) + at(1, 0, 1))
-    h_z = (up - low) * (coef(RADIAL_C) - u_r * (0.125 / dr)) + (up + low) * lap
-    h_z = h_z + first_t * (u_t * (0.25 * coef(THETA_C)))
-    h_z = h_z + second_t * coef(SECOND_C) + second_z * vis_z
-    h_z = h_z + c * (coef(CENTRE_Z) + first_z * adv_z)
-
-    first_t, second_t, first_z, second_z = pieces(1)
+    u_t = (b_back + b) + (at(1, -1, 1) + b_next)
+    h_z = (up - low) * (coef[RADIAL_C] - u_r * (0.125 / dr)) + (up + low) * lap
+    h_z = h_z + c_theta[0] * (u_t * coef[CROSS_Z])
+    h_z = h_z + (c_theta[1] * coef[SECOND_C] + c_axial[1] * vis_z)
+    h_z = h_z + c * (coef[CENTRE_Z] + c_axial[0] * adv_z)
+
     b_out = out(b)
     up = jnp.where(last_lane, -b, b_out)
     low = jnp.where(first_lane, ghost(1), inn(b))
     u_r = pair_a + pair_side
-    c_back = at(2, 0, -1)
-    u_z = (c_back + c) + (at(2, 1, -1) + at(2, 1, 0))
-    h_t = (up - low) * (coef(RADIAL_C) - u_r * (0.125 / dr)) + (up + low) * lap
-    h_t = h_t + b * (coef(CENTRE_T) + first_t * coef(THETA_C) - u_r * coef(CURVE_T))
-    h_t = h_t + second_t * coef(SECOND_C) + second_z * vis_z
-    h_t = h_t + first_z * (u_z * (0.25 * adv_z))
-    h_t = h_t + (pair_side - pair_a) * coef(TURN_T)
-
-    first_t, second_t, first_z, second_z = pieces(0)
+    u_z = (c_back + c) + (at(2, 1, -1) + c_side)
+    h_t = (up - low) * (coef[RADIAL_C] - u_r * (0.125 / dr)) + (up + low) * lap
+    h_t = h_t + b * (coef[CENTRE_T] + b_theta[0] * coef[THETA_C] - u_r * coef[CURVE_T])
+    h_t = h_t + (b_theta[1] * coef[SECOND_C] + b_axial[1] * vis_z)
+    h_t = h_t + b_axial[0] * (u_z * (0.25 * adv_z))
+    h_t = h_t + (pair_side - pair_a) * coef[TURN_T]
+
     up = out(a)
     low = jnp.where(first_lane, ghost(0), a_in)
-    b_back = at(1, -1, 0)
     pair_b = b + b_out
     pair_back = b_back + out(b_back)
     u_t = pair_b + pair_back
     u_z = (c + c_out) + (c_back + out(c_back))
-    h_r = (up - low) * (coef(RADIAL_F) - a * (0.5 / dr)) + (up + low) * lap
-    h_r = h_r + u_t * (u_t * coef(CURVE_R) + first_t * coef(THETA_F))
-    h_r = h_r + second_t * coef(SECOND_F) + second_z * vis_z
-    h_r = h_r + first_z * (u_z * (0.25 * adv_z)) + a * coef(CENTRE_R)
-    h_r = h_r + (pair_b - pair_back) * coef(TURN_R)
+    h_r = (up - low) * (coef[RADIAL_F] - a * (0.5 / dr)) + (up + low) * lap
+    h_r = h_r + u_t * (u_t * coef[CURVE_R] + a_theta[0] * coef[THETA_F])
+    h_r = h_r + (a_theta[1] * coef[SECOND_F] + a_axial[1] * vis_z)
+    h_r = h_r + (a_axial[0] * (u_z * (0.25 * adv_z)) + a * coef[CENTRE_R])
+    h_r = h_r + (pair_b - pair_back) * coef[TURN_R]
     return h_r, h_t, h_z
 
 
-def theta_edges(v_ref, head_ref, tail_ref):
-    count = v_ref.shape[1]
-    for n in range(3):
-        for q in range(HALO):
-            head_ref[n, q] = v_ref[n, q]
-            tail_ref[n, q] = v_ref[n, count - HALO + q]
-
-
-def first_pass(v_ref, coef_ref, vel_ref, low_ref, high_ref, inner_ref, pay_ref):
+def first_pass(
+    v_ref, coef_ref, vel_ref, head_ref, tail_ref, low_ref, high_ref, inner_ref, pay_ref
+):
     _, planes, axial, radial = v_ref.shape
     lane = lax.broadcasted_iota(jnp.int32, (8, radial), 1)
     sign = jnp.where(lane < 2 * planes, -1.0, 1.0).astype(jnp.float32)
@@ -161,28 +149,22 @@
     def rows(i, largest):
         k = pl.ds(pl.multiple_of(i * 8, 8), 8)
         padded = pl.ds(pl.multiple_of(i * 8 + PAD, 8), 8)
-
-        def group(g, carry):
-            largest, inner = carry
-            for q in range(GROUP):
-                j = g * GROUP + q
-                a, b, c = (v_ref[n, j, k, :] for n in range(3))
-                a = a * coef_ref[WALL]
-                rate = (
-                    jnp.abs(a) * float(radial)
-                    + jnp.abs(b) * coef_ref[RATE_T]
-                    + jnp.abs(c) * (1.0 / AXIAL_STEP)
-                )
-                largest = jnp.maximum(largest, rate)
-                for n, x in enumerate((a, b, c)):
-                    vel_ref[n, j + HALO, padded, :] = x
-                    place = n * planes + j
-                    inner = jnp.where(lane == place, pltpu.roll(x, place, 1), inner)
-            return largest, inner
-
-        zero = jnp.zeros((8, radial), jnp.float32)
-        largest, inner = lax.fori_loop(0, planes // GROUP, group, (largest, zero))
-        inner_ref[k, :] = inner * sign
+        wall, rate_t = coef_ref[WALL], coef_ref[RATE_T]
+        inner = [jnp.zeros((8, radial), jnp.float32)] * 3
+        for j in range(planes):
+            a, b, c = cells = [v_ref[n, j, k, :] for n in range(3)]
+            a = a * wall
+            rate = jnp.abs(a) * float(radial) + jnp.abs(b) * rate_t
+            largest = jnp.maximum(largest, rate + jnp.abs(c) * (1.0 / AXIAL_STEP))
+            for n, x in enumerate(cells):
+                vel_ref[n, j + HALO, padded, :] = a if n == 0 else x
+                place = n * planes + j
+                inner[n] = jnp.where(lane == place, pltpu.roll(x, place, 1), inner[n])
+                if j < HALO:
+                    head_ref[n, j, k, :] = x
+                if j >= planes - HALO:
+                    tail_ref[n, j - planes + HALO, k, :] = x
+        inner_ref[k, :] = (inner[0] + inner[1] + inner[2]) * sign
         return largest
 
     largest = lax.fori_loop(0, axial // 8, rows, jnp.zeros((8, radial), jnp.float32))
@@ -196,7 +178,7 @@
             high_ref[n, j] = v_ref[n, j, axial - 2 : axial, :]
         return carry
 
-    lax.fori_loop(0, planes, ends, 0)
+    lax.fori_loop(0, planes, ends, 0, unroll=8)
     last = lax.broadcasted_iota(jnp.int32, (2, radial), 1) == radial - 1
     for ref in (low_ref, high_ref):
         ref[0, 0] = jnp.where(last, top, ref[0, 0])
@@ -226,25 +208,34 @@
     lax.fori_loop(0, planes, plane, 0)
 
 
-def sweep(vel_ref, inner_ref, coef_ref, first, last, write):
+def sweep(vel_ref, inner_ref, coef_ref, first, last, write, beside=None, after=None):
     axial, radial = inner_ref.shape
     planes = vel_ref.shape[1] - 2 * HALO
 
     def plane(j, carry):
         def rows(i, carry):
-            k = pl.multiple_of(i * 8, 8)
-            inner = inner_ref[pl.ds(k, 8), :]
-
-            def ghost(component):
-                turn = lax.rem(2 * radial - component * planes - j, radial)
-                return pltpu.roll(inner, turn, 1)
-
-            found = terms(vel_ref, ghost, lambda n: coef_ref[n], j, k, 1.0 / radial)
-            for n, value in enumerate(found):
-                write(n, j, pl.ds(k, 8), value)
+            coef = [coef_ref[n] for n in range(COUNT)]
+            found = []
+            for u in range(UNROLL):
+                k = pl.multiple_of((i * UNROLL + u) * 8, 8)
+                inner = inner_ref[pl.ds(k, 8), :]
+
+                def ghost(component):
+                    turn = lax.rem(2 * radial - component * planes - j, radial)
+                    return pltpu.roll(inner, turn, 1)
+
+                found.append((k, terms(vel_ref, ghost, coef, j, k, 1.0 / radial)))
+            for k, values in found:
+                for n, value in enumerate(values):
+                    write(n, j, pl.ds(k, 8), value)
+                if beside is not None:
+                    beside(j, pl.ds(k, 8))
             return carry
 
-        return lax.fori_loop(0, axial // 8, rows, carry, unroll=UNROLL)
+        lax.fori_loop(0, axial // (8 * UNROLL), rows, 0)
+        if after is not None:
+            after(j)
+        return carry
 
     lax.fori_loop(first, last, plane, 0)
 
@@ -268,7 +259,7 @@
     coef_ref,
     *refs,
 ):
-    parts, (vel_in, out_ref, step_ref, vel_ref, res, sems) = refs[: len(spans)], refs[len(spans) :]
+    parts, (vel_in, out_ref, step_ref, vel_ref, res, sems) = refs[:-6], refs[-6:]
     del vel_in
     axial, radial = inner_ref.shape
     planes = res.shape[1]
@@ -277,29 +268,26 @@
     step_ref[0] = time_step
     scale = GAMMA * time_step
 
-    def store(first, last, n):
-        part = pl.ds(first, last - first)
-        return pltpu.make_async_copy(res.at[:, part], out_ref.at[:, part], sems.at[n])
+    def store(j):
+        return pltpu.make_async_copy(res.at[:, j], out_ref.at[:, j], sems.at[j])
 
     def write(n, j, k, value):
         factor = scale * coef_ref[WALL] if n == 0 else scale
         res[n, j, k, :] = value * factor
 
-    pending = []
-    for part, (first, last) in zip(parts, spans):
-
-        def plane(j, carry, part=part, first=first):
-            def rows(i, carry):
-                k = pl.ds(pl.multiple_of(i * 8, 8), 8)
-                for n in range(3):
-                    write(n, j, k, part[n, j - first, k, :])
-                return carry
-
-            return lax.fori_loop(0, axial // 8, rows, carry, unroll=UNROLL)
-
-        lax.fori_loop(first, last, plane, 0)
-        pending.append(store(first, last, len(pending)))
-        pending[-1].start()
+    (start, stop), others = spans[-1], spans[:-1]
+
+    def beside(j, k):
+        for part, (first, _) in zip(parts, others):
+            for n in range(3):
+                write(n, first + j - start, k, part[n, j - start, k, :])
+
+    def after(j):
+        store(j).start()
+        for first, _ in others:
+            store(first + j - start).start()
+
+    sweep(vel_ref, inner_ref, coef_ref, start, stop, write, beside, after)
 
     cells = pl.ds(PAD, axial)
     for q in range(HALO):
@@ -310,11 +298,21 @@
     vel_ref[1, HALO - 1, PAD + axial : PAD + axial + 1, :] = up_ref[1:2, :]
     vel_ref[2, HALO + planes, PAD - 1 : PAD, :] = down_ref[2:3, :]
     for first in (0, planes - HALO):
-        sweep(vel_ref, inner_ref, coef_ref, first, first + HALO, write)
-        pending.append(store(first, first + HALO, len(pending)))
-        pending[-1].start()
-    for copy in pending:
-        copy.wait()
+        sweep(
+            vel_ref,
+            inner_ref,
+            coef_ref,
+            first,
+            first + HALO,
+            write,
+            after=lambda j: store(j).start(),
+        )
+
+    def wait(j, carry):
+        store(j).wait()
+        return carry
+
+    lax.fori_loop(0, planes, wait, 0)
 
 
 def shifted(block, distance):
@@ -369,30 +367,21 @@
         )
 
     pair = shape(3, HALO, axial, radial)
-    head, tail = call(
-        theta_edges,
-        "theta_edges",
-        0,
-        out_shape=(pair, pair),
-        in_specs=[vmem],
-        out_specs=(vmem, vmem),
-    )(velocity)
-    below = shifted(tail, (1, 0))
-    above = shifted(head, (-1, 0))
-
     edge = shape(3, planes, 2, radial)
     padded = shape(3, planes + 2 * HALO, axial + 2 * PAD, radial)
-    vel, first, last, inner, pay = call(
+    vel, head, tail, first, last, inner, pay = call(
         first_pass,
         "first_pass",
         10 * velocity.size,
-        out_shape=(padded, edge, edge, shape(axial, radial), shape(8, radial)),
+        out_shape=(padded, pair, pair, edge, edge, shape(axial, radial), shape(8, radial)),
         in_specs=[vmem, vmem],
-        out_specs=(vmem,) * 5,
+        out_specs=(vmem,) * 7,
     )(velocity, coef)
     low = shifted(last, (0, 1))
     high = shifted(first, (0, -1))
     inner = shifted(inner, (sizes[0] // 2, 0))
+    below = shifted(tail, (1, 0))
+    above = shifted(head, (-1, 0))
     pay, vel = call(
         fold,
         "fold",
@@ -408,14 +397,15 @@
     known = {(0, 0), (0, 1), (0, sizes[1] - 1), (sizes[0] // 2, 0)}
     known = {((i + d) % sizes[0], k) for i, k in known for d in (-1, 0, 1)}
     plan = rounds(sizes, known)
-    count = len(plan) + 1
-    bounds = [
-        HALO + (planes - 2 * HALO) * n // count for n in range(count + 1)
-    ]
+    inside = planes - 2 * HALO
+    count = len(plan) + 2
+    while inside % count:
+        count += 1
+    bounds = range(HALO, planes - HALO + 1, inside // count)
     spans = list(zip(bounds[:-1], bounds[1:]))
     parts = []
     token = pay
-    for n, (first, last) in enumerate(spans):
+    for n, (first, last) in enumerate(spans[:-1]):
         parts.append(
             call(
                 functools.partial(interior, first, last),
@@ -429,10 +419,10 @@
         if n == 0:
             pay = jnp.maximum(pay, jnp.maximum(up, down))
             token = up
-        else:
-            pay = jnp.maximum(pay, far)
+        elif n <= len(plan):
             token = far
         if n < len(plan):
+            pay = pay if n == 0 else jnp.maximum(pay, far)
             far = shifted(pay, plan[n])
     increment, time_step, _ = call(
         functools.partial(finish, spans),
@@ -444,7 +434,7 @@
         out_specs=(anywhere, smem, vmem),
         scratch_shapes=[
             pltpu.VMEM(velocity.shape, f32),
-            pltpu.SemaphoreType.DMA((len(parts) + 2,)),
+            pltpu.SemaphoreType.DMA((planes,)),
         ],
         input_output_aliases={8 + len(parts): 2},
     )(below, above, up, down, pay, far, inner, coef, *parts, vel)

time: 54.9 us -> 53.4 us (0.973); the launches traced: 53.9 us -> 53.2 us
  Pallas kernels: 31.6 us -> 22.6 us
  waiting for transfers between devices: 7.3 us -> 15.2 us
  local copies, waits for them, and re-layouts: 2.78 us -> 3.62 us
    pallas_call x2 -> x1, Pallas kernels: 11 us -> 3.03 us  [per_device(): call(first_pass, 'first_pass', 10 * velocity.size, out_shape=(padded, pai...]
    ppermute x9, waiting for transfers between devices: 7.3 us -> 15.2 us  [shifted(): return lax.ppermute(block, ('az', 'ax'), route)]
    pallas_call x3, Pallas kernels: 15.5 us -> 11.4 us  [per_device(): call(functools.partial(interior, first, last), f'interior_{n}', 400 * (la...]
    pallas_call x1, Pallas kernels: 4.75 us -> 7.81 us  [per_device(): call(functools.partial(finish, spans), 'finish', 160 * velocity.size, scr...]
    unnamed x4, local copies, waits for them, and re-layouts: 2.78 us -> 3.62 us
  transfers between devices with their start and end apart: 9 -> 9, of which waited for: 3 -> 4; matrix products, arithmetic and copies ran while one was open for 0% -> 0% of each run, Pallas kernels for 50% -> 22%
where the time goes in v3:
time: 53.4 us; the launch traced here: 53.2 us
  Pallas kernels  22.6 us (42%)
  waiting for transfers between devices  15.2 us (28%)
  starting transfers between devices  11 us (21%)
  local copies, waits for them, and re-layouts  3.62 us (7%)
  between operations  0.7 us (1%)
    ppermute x9, waiting for transfers between devices, shifted(): return lax.ppermute(block, ('az', 'ax'), route)  15.2 us
    pallas_call x3, Pallas kernels, per_device(): call(functools.partial(interior, first, last), f'interior_{n}', 400 * (la...  11.4 us
    ppermute x9, starting transfers between devices, shifted(): return lax.ppermute(block, ('az', 'ax'), route)  11 us
    pallas_call x1, Pallas kernels, per_device(): call(functools.partial(finish, spans), 'finish', 160 * velocity.size, scr...  7.81 us
    unnamed x4, local copies, waits for them, and re-layouts  3.62 us
    pallas_call x1, Pallas kernels, per_device(): call(first_pass, 'first_pass', 10 * velocity.size, out_shape=(padded, pai...  3.03 us
  transfers between devices with their start and end apart: 9, of which 4 were waited for; matrix products, arithmetic and copies ran while one was open for 0% of the time, Pallas kernels for 22%

profile of v3, /device:TPU:0, one launch (start us, length us, event | category | flops | bytes accessed | tf_op | source)
XLA Modules:
  0.0 53.2 jit_solution(12304901314134048250)
XLA Ops:
  0.6 0.0 copy-start
  0.6 2.8 %copy-done = f32[3,32,128,128]{3,2,1,0:T(8,128)S(1)} copy-done((f32[3,32,128,128]{3,2,1,0:T(8,128)S(1)}, f32[3,32,128,128]{3,2,1,0:T(8,128)}, u32[]{:S(2)}) %copy-start) | copy-done | bytes 6291480
  3.4 0.0 copy-start.1
  3.4 0.8 %copy-done.1 = f32[16,8,128]{2,1,0:T(8,128)S(1)} copy-done((f32[16,8,128]{2,1,0:T(8,128)S(1)}, f32[16,8,128]{2,1,0:T(8,128)}, u32[]{:S(2)}) %copy-start.1) | copy-done | bytes 65560
  4.3 3.0 %first_pass.1 = (f32[3,36,144,128]{3,2,1,0:T(8,128)S(1)}, f32[3,2,128,128]{3,2,1,0:T(8,128)S(1)}, f32[3,2,128,128]{3,2,1,0:T(8,128)S(1)}, f32[3,32,2,128]{3,2,1,...) custom-call(f32[3,32,128,128]{3,2,1,0:T(8,128)S(1)} %copy-done, ...), custom_call_target="tpu_custom_call" | custom-call | flops 15728640 | bytes 6291456 | tf_op jit(solution)/shard_map/first_pass/pallas_call | solution.py:372
  7.3 3.0 %collective-permute-start = (f32[3,2,128,128]{3,2,1,0:T(8,128)S(1)}, f32[3,2,128,128]{3,2,1,0:T(8,128)S(1)}, u32[]{:S(2)}, u32[]{:S(2)}) collective-permute-start(f32[3,2,128,128]{3,2,1,0:T(8,128)S(1)} %get-tuple-element.13), channel_id=1, source_target_pairs={{28,0},{29,1},{30,2},{31,3},{0,4},{1,5},{2,6},{3,7},{4,8},{5,9},{6... | collective-permute-start | bytes 1179656 | tf_op jit(solution)/shard_map/ppermute | solution.py:325
  10.3 3.1 %collective-permute-start.1 = (f32[3,2,128,128]{3,2,1,0:T(8,128)S(1)}, f32[3,2,128,128]{3,2,1,0:T(8,128)S(1)}, u32[]{:S(2)}, u32[]{:S(2)}) collective-permute-start(f32[3,2,128,128]{3,2,1,0:T(8,128)S(1)} %get-tuple-element.14), channel_id=1, source_target_pairs={{4,0},{5,1},{6,2},{7,3},{8,4},{9,5},{10,6},{11,7},{12,8},{13,9},{1... | collective-permute-start | bytes 1179656 | tf_op jit(solution)/shard_map/ppermute | solution.py:325
  13.4 0.0 collective-permute-start.2
  13.4 1.7 %collective-permute-start.3 = (f32[3,32,2,128]{3,2,1,0:T(2,128)S(1)}, f32[3,32,2,128]{3,2,1,0:T(2,128)S(1)}, u32[]{:S(2)}, u32[]{:S(2)}) collective-permute-start(f32[3,32,2,128]{3,2,1,0:T(2,128)S(1)} %get-tuple-element.16), channel_id=1, source_target_pairs={{1,0},{2,1},{3,2},{0,3},{5,4},{6,5},{7,6},{4,7},{9,8},{10,9},{11,1... | collective-permute-start | bytes 294920 | tf_op jit(solution)/shard_map/ppermute | solution.py:325
  15.2 0.9 %collective-permute-start.4 = (f32[128,128]{1,0:T(8,128)S(1)}, f32[128,128]{1,0:T(8,128)S(1)}, u32[]{:S(2)}, u32[]{:S(2)}) collective-permute-start(f32[128,128]{1,0:T(8,128)S(1)} %get-tuple-element.17), channel_id=1, source_target_pairs={{16,0},{17,1},{18,2},{19,3},{20,4},{21,5},{22,6},{23,7},{24,8},{25... | collective-permute-start | bytes 196616 | tf_op jit(solution)/shard_map/ppermute | solution.py:325
  16.1 9.7 %collective-permute-done.4.inner_ref = f32[128,128]{1,0:T(8,128)S(1)} collective-permute-done((f32[128,128]{1,0:T(8,128)S(1)}, f32[128,128]{1,0:T(8,128)S(1)}, u32[]{:S(2)}, u32[]{:S(2)}) %collective-permute-start.4) | collective-permute-done | bytes 65568 | tf_op jit(solution)/shard_map/ppermute | solution.py:325
  25.7 0.0 collective-permute-done.2.low_ref
  25.7 0.0 collective-permute-done.3.high_ref
  25.7 0.4 fold.1
  26.1 1.2 %collective-permute-start.6 = (f32[8,128]{1,0:T(8,128)S(1)}, f32[8,128]{1,0:T(8,128)S(1)}, u32[]{:S(2)}, u32[]{:S(2)}) collective-permute-start(f32[8,128]{1,0:T(8,128)S(1)} %get-tuple-element.20._), channel_id=1, source_target_pairs={{4,0},{5,1},{6,2},{7,3},{8,4},{9,5},{10,6},{11,7},{12,8},{13,9},{1... | collective-permute-start | bytes 12296 | tf_op jit(solution)/shard_map/ppermute | solution.py:325
  27.3 0.8 %collective-permute-start.5 = (f32[8,128]{1,0:T(8,128)S(1)}, f32[8,128]{1,0:T(8,128)S(1)}, u32[]{:S(2)}, u32[]{:S(2)}) collective-permute-start(f32[8,128]{1,0:T(8,128)S(1)} %get-tuple-element.20._), channel_id=1, source_target_pairs={{28,0},{29,1},{30,2},{31,3},{0,4},{1,5},{2,6},{3,7},{4,8},{5,9},{6... | collective-permute-start | bytes 12296 | tf_op jit(solution)/shard_map/ppermute | solution.py:325
  28.2 3.8 %interior_0.1.refs_0_ = f32[3,7,128,128]{3,2,1,0:T(8,128)S(1)} custom-call(f32[3,36,144,128]{3,2,1,0:T(8,128)S(1)} %get-tuple-element.21.vel_ref.refs_3_, f32[128,128]{1,0:T(8,128)S(1)} %collective-permute-done.4.inner_ref, f32[16,8,128]{2,1,0:T(8,128)S(1)} %copy-done.1, f32[8,128]{1,0:T(8,128)S(1)} %get-tuple-element.20._), custom_call_target="tpu_custom_call" | custom-call | flops 45875200 | bytes 6291456 | tf_op jit(solution)/shard_map/interior_0/pallas_call | solution.py:410
  32.0 0.0 collective-permute-done.6.down_ref
  32.0 1.6 %collective-permute-done.5._.up_ref = f32[8,128]{1,0:T(8,128)S(1)} collective-permute-done((f32[8,128]{1,0:T(8,128)S(1)}, f32[8,128]{1,0:T(8,128)S(1)}, u32[]{:S(2)}, u32[]{:S(2)}) %collective-permute-start.5) | collective-permute-done | bytes 4128 | tf_op jit(solution)/shard_map/ppermute | solution.py:325
  33.6 0.0 collective-permute-start.7
  33.6 3.8 %interior_1.1.refs_1_ = f32[3,7,128,128]{3,2,1,0:T(8,128)S(1)} custom-call(f32[3,36,144,128]{3,2,1,0:T(8,128)S(1)} %get-tuple-element.21.vel_ref.refs_3_, f32[128,128]{1,0:T(8,128)S(1)} %collective-permute-done.4.inner_ref, f32[16,8,128]{2,1,0:T(8,128)S(1)} %copy-done.1, f32[8,128]{1,0:T(8,128)S(1)} %collective-permute-done.5._.up_ref), custom_call_target="tpu_custom_call" | custom-call | flops 45875200 | bytes 6291456 | tf_op jit(solution)/shard_map/interior_1/pallas_call | solution.py:410
  37.5 2.5 %collective-permute-done.7._ = f32[8,128]{1,0:T(8,128)S(1)} collective-permute-done((f32[8,128]{1,0:T(8,128)S(1)}, f32[8,128]{1,0:T(8,128)S(1)}, u32[]{:S(2)}, u32[]{:S(2)}) %collective-permute-start.7) | collective-permute-done | bytes 4128 | tf_op jit(solution)/shard_map/ppermute | solution.py:325
  39.9 0.2 collective-permute-start.8
  40.1 3.8 %interior_2.1.refs_2_ = f32[3,7,128,128]{3,2,1,0:T(8,128)S(1)} custom-call(f32[3,36,144,128]{3,2,1,0:T(8,128)S(1)} %get-tuple-element.21.vel_ref.refs_3_, f32[128,128]{1,0:T(8,128)S(1)} %collective-permute-done.4.inner_ref, f32[16,8,128]{2,1,0:T(8,128)S(1)} %copy-done.1, f32[8,128]{1,0:T(8,128)S(1)} %collective-permute-done.7._), custom_call_target="tpu_custom_call" | custom-call | flops 45875200 | bytes 6291456 | tf_op jit(solution)/shard_map/interior_2/pallas_call | solution.py:410
  43.9 1.4 %collective-permute-done.8.far_ref = f32[8,128]{1,0:T(8,128)S(1)} collective-permute-done((f32[8,128]{1,0:T(8,128)S(1)}, f32[8,128]{1,0:T(8,128)S(1)}, u32[]{:S(2)}, u32[]{:S(2)}) %collective-permute-start.8) | collective-permute-done | bytes 4128 | tf_op jit(solution)/shard_map/ppermute | solution.py:325
  45.3 0.0 collective-permute-done.below_ref
  45.3 0.0 collective-permute-done.1.above_ref
  45.3 7.8 %finish.1 = (f32[3,32,128,128]{3,2,1,0:T(8,128)}, f32[1]{0:T(128)}, f32[3,36,144,128]{3,2,1,0:T(8,128)S(1)}) custom-call(f32[3,2,128,128]{3,2,1,0:T(8,128)S(1)} %collective-permute-done.below_ref, f32[3,2,128,128]{3,2,1,0:T(8,128)S(1)} %collective-permute-done.1.above_ref, ...), custom_call_target="tpu_custom_call", output_to_operand_aliasing={{2}: (11, {})} | custom-call | flops 251658240 | bytes 6291456 | tf_op jit(solution)/shard_map/finish/pallas_call | solution.py:427
  (2 shorter events, 0.0 us)
Async XLA Ops:
  0.6 2.8 %copy-start = (f32[3,32,128,128]{3,2,1,0:T(8,128)S(1)}, f32[3,32,128,128]{3,2,1,0:T(8,128)}, u32[]{:S(2)}) copy-start(f32[3,32,128,128]{3,2,1,0:T(8,128)} %v_ref.1) | copy-start | bytes 18874372
  3.4 0.8 %copy-start.1 = (f32[16,8,128]{2,1,0:T(8,128)S(1)}, f32[16,8,128]{2,1,0:T(8,128)}, u32[]{:S(2)}) copy-start(f32[16,8,128]{2,1,0:T(8,128)} %constant.2.clone.coef_ref) | copy-start | bytes 196612
  7.3 38.0 %collective-permute-start = (f32[3,2,128,128]{3,2,1,0:T(8,128)S(1)}, f32[3,2,128,128]{3,2,1,0:T(8,128)S(1)}, u32[]{:S(2)}, u32[]{:S(2)}) collective-permute-start(f32[3,2,128,128]{3,2,1,0:T(8,128)S(1)} %get-tuple-element.13), channel_id=1, source_target_pairs={{28,0},{29,1},{30,2},{31,3},{0,4},{1,5},{2,6},{3,7},{4,8},{5,9},{6... | collective-permute-start | bytes 1179656 | tf_op jit(solution)/shard_map/ppermute | solution.py:325
  10.3 35.0 %collective-permute-start.1 = (f32[3,2,128,128]{3,2,1,0:T(8,128)S(1)}, f32[3,2,128,128]{3,2,1,0:T(8,128)S(1)}, u32[]{:S(2)}, u32[]{:S(2)}) collective-permute-start(f32[3,2,128,128]{3,2,1,0:T(8,128)S(1)} %get-tuple-element.14), channel_id=1, source_target_pairs={{4,0},{5,1},{6,2},{7,3},{8,4},{9,5},{10,6},{11,7},{12,8},{13,9},{1... | collective-permute-start | bytes 1179656 | tf_op jit(solution)/shard_map/ppermute | solution.py:325
  13.4 12.3 %collective-permute-start.2 = (f32[3,32,2,128]{3,2,1,0:T(2,128)S(1)}, f32[3,32,2,128]{3,2,1,0:T(2,128)S(1)}, u32[]{:S(2)}, u32[]{:S(2)}) collective-permute-start(f32[3,32,2,128]{3,2,1,0:T(2,128)S(1)} %get-tuple-element.15), channel_id=1, source_target_pairs={{3,0},{0,1},{1,2},{2,3},{7,4},{4,5},{5,6},{6,7},{11,8},{8,9},{9,10... | collective-permute-start | bytes 294920 | tf_op jit(solution)/shard_map/ppermute | solution.py:325
  13.4 12.3 %collective-permute-start.3 = (f32[3,32,2,128]{3,2,1,0:T(2,128)S(1)}, f32[3,32,2,128]{3,2,1,0:T(2,128)S(1)}, u32[]{:S(2)}, u32[]{:S(2)}) collective-permute-start(f32[3,32,2,128]{3,2,1,0:T(2,128)S(1)} %get-tuple-element.16), channel_id=1, source_target_pairs={{1,0},{2,1},{3,2},{0,3},{5,4},{6,5},{7,6},{4,7},{9,8},{10,9},{11,1... | collective-permute-start | bytes 294920 | tf_op jit(solution)/shard_map/ppermute | solution.py:325
  15.2 10.5 %collective-permute-start.4 = (f32[128,128]{1,0:T(8,128)S(1)}, f32[128,128]{1,0:T(8,128)S(1)}, u32[]{:S(2)}, u32[]{:S(2)}) collective-permute-start(f32[128,128]{1,0:T(8,128)S(1)} %get-tuple-element.17), channel_id=1, source_target_pairs={{16,0},{17,1},{18,2},{19,3},{20,4},{21,5},{22,6},{23,7},{24,8},{25... | collective-permute-start | bytes 196616 | tf_op jit(solution)/shard_map/ppermute | solution.py:325
  26.1 5.9 %collective-permute-start.6 = (f32[8,128]{1,0:T(8,128)S(1)}, f32[8,128]{1,0:T(8,128)S(1)}, u32[]{:S(2)}, u32[]{:S(2)}) collective-permute-start(f32[8,128]{1,0:T(8,128)S(1)} %get-tuple-element.20._), channel_id=1, source_target_pairs={{4,0},{5,1},{6,2},{7,3},{8,4},{9,5},{10,6},{11,7},{12,8},{13,9},{1... | collective-permute-start | bytes 12296 | tf_op jit(solution)/shard_map/ppermute | solution.py:325
  27.3 6.3 %collective-permute-start.5 = (f32[8,128]{1,0:T(8,128)S(1)}, f32[8,128]{1,0:T(8,128)S(1)}, u32[]{:S(2)}, u32[]{:S(2)}) collective-permute-start(f32[8,128]{1,0:T(8,128)S(1)} %get-tuple-element.20._), channel_id=1, source_target_pairs={{28,0},{29,1},{30,2},{31,3},{0,4},{1,5},{2,6},{3,7},{4,8},{5,9},{6... | collective-permute-start | bytes 12296 | tf_op jit(solution)/shard_map/ppermute | solution.py:325
  33.6 6.3 %collective-permute-start.7 = (f32[8,128]{1,0:T(8,128)S(1)}, f32[8,128]{1,0:T(8,128)S(1)}, u32[]{:S(2)}, u32[]{:S(2)}) collective-permute-start(f32[8,128]{1,0:T(8,128)S(1)} %maximum_maximum_fusion), channel_id=1, source_target_pairs={{22,0},{23,1},{20,2},{21,3},{26,4},{27,5},{24,6},{25,7},{30,8},{31... | collective-permute-start | bytes 12296 | tf_op jit(solution)/shard_map/ppermute | solution.py:325
  39.9 5.4 %collective-permute-start.8 = (f32[8,128]{1,0:T(8,128)S(1)}, f32[8,128]{1,0:T(8,128)S(1)}, u32[]{:S(2)}, u32[]{:S(2)}) collective-permute-start(f32[8,128]{1,0:T(8,128)S(1)} %max.11.pay_ref), channel_id=1, source_target_pairs={{24,0},{25,1},{26,2},{27,3},{28,4},{29,5},{30,6},{31,7},{0,8},{1,9... | collective-permute-start | bytes 12296 | tf_op jit(solution)/shard_map/ppermute | solution.py:325

commit v4 on v3

--- a/solution.py
+++ b/solution.py
@@ -20,7 +20,6 @@
 
 (
     WALL,
-    RATE_T,
     RADIAL_C,
     THETA_C,
     CROSS_Z,
@@ -36,7 +35,7 @@
     CURVE_R,
     TURN_R,
     COUNT,
-) = range(17)
+) = range(16)
 
 
 def coefficients(radial, theta_step):
@@ -49,7 +48,6 @@
     nu = VISCOSITY
     rows = np.zeros((COUNT, radial))
     rows[WALL] = wall
-    rows[RATE_T] = 1.0 / (centre * h)
     common = -2.0 * nu / dr**2 - 30.0 * nu / (12.0 * AXIAL_STEP**2)
     rows[RADIAL_C] = nu / (2.0 * dr * centre)
     rows[THETA_C] = -1.0 / (12.0 * h * centre)
@@ -68,19 +66,22 @@
     return np.broadcast_to(rows[:, None, :], (COUNT, 8, radial)).astype(np.float32)
 
 
-def terms(vel, ghost, coef, j, k, dr):
-    lane = lax.broadcasted_iota(jnp.int32, (8, 128), 1)
+def turned_in(x):
+    return pltpu.roll(x, 1, 1)
+
+
+def turned_out(x):
+    return pltpu.roll(x, x.shape[1] - 1, 1)
+
+
+def terms(vel, kept, ghost, coef, j, k, dr):
+    a_in, a_in_side, a_in_next, b_out, b_out_back, c_out, c_out_back = kept
+    lane = lax.broadcasted_iota(jnp.int32, a_in.shape, 1)
     first_lane = lane == 0
-    last_lane = lane == 127
+    last_lane = lane == a_in.shape[1] - 1
 
     def at(component, dj, dk):
         return vel[component, j + HALO + dj, pl.ds(k + PAD + dk, 8), :]
-
-    def out(x):
-        return pltpu.roll(x, 127, 1)
-
-    def inn(x):
-        return pltpu.roll(x, 1, 1)
 
     nu = VISCOSITY
     lap = nu / dr**2
@@ -95,18 +96,21 @@
         along = [at(n, 0, d) for d in (1, -1, 2, -2)]
         return over, along, differences(*over), differences(*along)
 
+    def below(n, x):
+        if ghost is not None:
+            return jnp.where(first_lane, ghost(n), x)
+        return x if n == 0 else jnp.where(first_lane, 0.0, x)
+
     a, b, c = (at(n, 0, 0) for n in range(3))
     (a_side, *_), (a_next, *_), a_theta, a_axial = pieces(0)
     (_, b_back, *_), (b_next, *_), b_theta, b_axial = pieces(1)
     (c_side, *_), (_, c_back, *_), c_theta, c_axial = pieces(2)
-    a_in = inn(a)
     pair_a = a + a_in
-    pair_side = a_side + inn(a_side)
-    pair_next = a_next + inn(a_next)
-
-    c_out = out(c)
+    pair_side = a_side + a_in_side
+    pair_next = a_next + a_in_next
+
     up = jnp.where(last_lane, -c, c_out)
-    low = jnp.where(first_lane, ghost(2), inn(c))
+    low = below(2, turned_in(c))
     u_r = pair_a + pair_next
     u_t = (b_back + b) + (at(1, -1, 1) + b_next)
     h_z = (up - low) * (coef[RADIAL_C] - u_r * (0.125 / dr)) + (up + low) * lap
@@ -114,9 +118,8 @@
     h_z = h_z + (c_theta[1] * coef[SECOND_C] + c_axial[1] * vis_z)
     h_z = h_z + c * (coef[CENTRE_Z] + c_axial[0] * adv_z)
 
-    b_out = out(b)
     up = jnp.where(last_lane, -b, b_out)
-    low = jnp.where(first_lane, ghost(1), inn(b))
+    low = below(1, turned_in(b))
     u_r = pair_a + pair_side
     u_z = (c_back + c) + (at(2, 1, -1) + c_side)
     h_t = (up - low) * (coef[RADIAL_C] - u_r * (0.125 / dr)) + (up + low) * lap
@@ -125,12 +128,12 @@
     h_t = h_t + b_axial[0] * (u_z * (0.25 * adv_z))
     h_t = h_t + (pair_side - pair_a) * coef[TURN_T]
 
-    up = out(a)
-    low = jnp.where(first_lane, ghost(0), a_in)
+    up = turned_out(a)
+    low = below(0, a_in)
     pair_b = b + b_out
-    pair_back = b_back + out(b_back)
+    pair_back = b_back + b_out_back
     u_t = pair_b + pair_back
-    u_z = (c + c_out) + (c_back + out(c_back))
+    u_z = (c + c_out) + (c_back + c_out_back)
     h_r = (up - low) * (coef[RADIAL_F] - a * (0.5 / dr)) + (up + low) * lap
     h_r = h_r + u_t * (u_t * coef[CURVE_R] + a_theta[0] * coef[THETA_F])
     h_r = h_r + (a_theta[1] * coef[SECOND_F] + a_axial[1] * vis_z)
@@ -139,17 +142,42 @@
     return h_r, h_t, h_z
 
 
-def first_pass(
-    v_ref, coef_ref, vel_ref, head_ref, tail_ref, low_ref, high_ref, inner_ref, pay_ref
-):
+def lane_zero_terms(vel, ghost, coef, j, k, dr):
+    def at(dj, dk):
+        return vel[0, j + HALO + dj, pl.ds(k + PAD + dk, 8), :]
+
+    lap = VISCOSITY / dr**2
+    a = at(0, 0)
+    first_lane = lax.broadcasted_iota(jnp.int32, a.shape, 1) == 0
+    add_r = ghost(0) * (lap - coef[RADIAL_F] + a * (0.5 / dr))
+    add_t = ghost(1) * (lap - coef[RADIAL_C] + (a + at(1, 0)) * (0.125 / dr))
+    add_z = ghost(2) * (lap - coef[RADIAL_C] + (a + at(0, 1)) * (0.125 / dr))
+    return tuple(jnp.where(first_lane, x, 0.0) for x in (add_r, add_t, add_z))
+
+
+def theta_edges(v_ref, head_ref, tail_ref):
+    count = v_ref.shape[1]
+    for n in range(3):
+        for q in range(HALO):
+            head_ref[n, q] = v_ref[n, q]
+            tail_ref[n, q] = v_ref[n, count - HALO + q]
+
+
+def wall_mask(rows, radial):
+    lane = lax.broadcasted_iota(jnp.int32, (rows, radial), 1)
+    return jnp.where(lane == radial - 1, 0.0, 1.0).astype(jnp.float32)
+
+
+def first_pass(theta_step, v_ref, _, vel_ref, low_ref, high_ref, inner_ref, pay_ref):
     _, planes, axial, radial = v_ref.shape
     lane = lax.broadcasted_iota(jnp.int32, (8, radial), 1)
     sign = jnp.where(lane < 2 * planes, -1.0, 1.0).astype(jnp.float32)
+    wall = wall_mask(8, radial)
+    rate_t = (radial / theta_step) / (lane.astype(jnp.float32) + 0.5)
 
     def rows(i, largest):
         k = pl.ds(pl.multiple_of(i * 8, 8), 8)
         padded = pl.ds(pl.multiple_of(i * 8 + PAD, 8), 8)
-        wall, rate_t = coef_ref[WALL], coef_ref[RATE_T]
         inner = [jnp.zeros((8, radial), jnp.float32)] * 3
         for j in range(planes):
             a, b, c = cells = [v_ref[n, j, k, :] for n in range(3)]
@@ -160,17 +188,14 @@
                 vel_ref[n, j + HALO, padded, :] = a if n == 0 else x
                 place = n * planes + j
                 inner[n] = jnp.where(lane == place, pltpu.roll(x, place, 1), inner[n])
-                if j < HALO:
-                    head_ref[n, j, k, :] = x
-                if j >= planes - HALO:
-                    tail_ref[n, j - planes + HALO, k, :] = x
         inner_ref[k, :] = (inner[0] + inner[1] + inner[2]) * sign
         return largest
 
     largest = lax.fori_loop(0, axial // 8, rows, jnp.zeros((8, radial), jnp.float32))
     top = jnp.max(largest, axis=(0, 1), keepdims=True)
     pay_ref[...] = jnp.broadcast_to(top, pay_ref.shape)
-    inner_ref[0:8, :] = jnp.where(lane == radial - 1, top, inner_ref[0:8, :])
+    pay_ref[1:2, :] = v_ref[1, planes - 1, 0:1, :]
+    pay_ref[2:3, :] = v_ref[2, 0, axial - 1 : axial, :]
 
     def ends(j, carry):
         for n in range(3):
@@ -184,19 +209,16 @@
         ref[0, 0] = jnp.where(last, top, ref[0, 0])
 
 
-def fold(low_ref, high_ref, inner_ref, pay_ref, coef_ref, vel_in, out_ref, vel_ref):
+def fold(low_ref, high_ref, up_ref, down_ref, pay_ref, vel_in, out_ref, vel_ref):
     del vel_in
     planes, radial = low_ref.shape[1], low_ref.shape[3]
-    axial = inner_ref.shape[0]
-    top = jnp.maximum(
-        jnp.maximum(low_ref[0, 0, 0:1, :], high_ref[0, 0, 0:1, :]), inner_ref[0:1, :]
-    )
+    axial = vel_ref.shape[2] - 2 * PAD
     lane = lax.broadcasted_iota(jnp.int32, (1, radial), 1)
+    top = jnp.maximum(low_ref[0, 0, 0:1, :], high_ref[0, 0, 0:1, :])
     top = jnp.max(jnp.where(lane == radial - 1, top, 0.0), axis=(0, 1), keepdims=True)
-    out_ref[...] = jnp.maximum(pay_ref[...], top)
-    out_ref[1:2, :] = high_ref[1, planes - 1, 0:1, :]
-    out_ref[2:3, :] = low_ref[2, 0, 1:2, :]
-    wall = coef_ref[WALL, 0:2, :]
+    top = jnp.maximum(top, jnp.maximum(up_ref[0:1, :], down_ref[0:1, :]))
+    out_ref[...] = jnp.broadcast_to(jnp.maximum(top, pay_ref[0:1, :]), out_ref.shape)
+    wall = wall_mask(2, radial)
 
     def plane(j, carry):
         for n in range(3):
@@ -205,34 +227,69 @@
             vel_ref[n, j + HALO, PAD + axial : PAD + axial + 2, :] = high_ref[n, j] * mask
         return carry
 
-    lax.fori_loop(0, planes, plane, 0)
-
-
-def sweep(vel_ref, inner_ref, coef_ref, first, last, write, beside=None, after=None):
-    axial, radial = inner_ref.shape
+    lax.fori_loop(0, planes, plane, 0, unroll=4)
+
+
+def ghosts(inner, planes, j):
+    radial = inner.shape[1]
+
+    def ghost(component):
+        turn = lax.rem(2 * radial - component * planes - j, radial)
+        return pltpu.roll(inner, turn, 1)
+
+    return ghost
+
+
+def sweep(vel_ref, inner_ref, coef_ref, kept_refs, first, last, write, beside=None, after=None):
+    a_kept, b_kept, c_kept = kept_refs
     planes = vel_ref.shape[1] - 2 * HALO
+    axial, radial = vel_ref.shape[2] - 2 * PAD, vel_ref.shape[3]
+
+    def padded(n, j, k):
+        return vel_ref[n, j + HALO, pl.ds(k + PAD, 8), :]
+
+    def fill(i, carry):
+        k = pl.multiple_of(i * 8, 8)
+        a_kept[pl.ds(k, 8), :] = turned_in(padded(0, first, k))
+        b_kept[pl.ds(k, 8), :] = turned_out(padded(1, first - 1, k))
+        return carry
+
+    lax.fori_loop(0, axial // 8, fill, 0, unroll=4)
+    a_kept[pl.ds(axial, 8), :] = turned_in(padded(0, first, axial))
 
     def plane(j, carry):
+        c_kept[0:PAD, :] = turned_out(padded(2, j, -PAD))
+
         def rows(i, carry):
             coef = [coef_ref[n] for n in range(COUNT)]
+            ks = [pl.multiple_of((i * UNROLL + u) * 8, 8) for u in range(UNROLL)]
+            a_in = [a_kept[pl.ds(k, 8), :] for k in ks]
+            a_in_next = [a_kept[pl.ds(k + 1, 8), :] for k in ks]
+            b_out_back = [b_kept[pl.ds(k, 8), :] for k in ks]
+            a_in_side = [turned_in(padded(0, j + 1, k)) for k in ks]
+            b_out = [turned_out(padded(1, j, k)) for k in ks]
+            c_out = [turned_out(padded(2, j, k)) for k in ks]
+            for u, k in enumerate(ks):
+                a_kept[pl.ds(k, 8), :] = a_in_side[u]
+                b_kept[pl.ds(k, 8), :] = b_out[u]
+                c_kept[pl.ds(k + PAD, 8), :] = c_out[u]
+            c_out_back = [c_kept[pl.ds(k + PAD - 1, 8), :] for k in ks]
+            kept = zip(a_in, a_in_side, a_in_next, b_out, b_out_back, c_out, c_out_back)
             found = []
-            for u in range(UNROLL):
-                k = pl.multiple_of((i * UNROLL + u) * 8, 8)
-                inner = inner_ref[pl.ds(k, 8), :]
-
-                def ghost(component):
-                    turn = lax.rem(2 * radial - component * planes - j, radial)
-                    return pltpu.roll(inner, turn, 1)
-
-                found.append((k, terms(vel_ref, ghost, coef, j, k, 1.0 / radial)))
-            for k, values in found:
+            for k, turned in zip(ks, kept):
+                ghost = None
+                if inner_ref is not None:
+                    ghost = ghosts(inner_ref[pl.ds(k, 8), :], planes, j)
+                found.append(terms(vel_ref, turned, ghost, coef, j, k, 1.0 / radial))
+            for k, values in zip(ks, found):
                 for n, value in enumerate(values):
                     write(n, j, pl.ds(k, 8), value)
                 if beside is not None:
-                    beside(j, pl.ds(k, 8))
+                    beside(j, k, coef)
             return carry
 
         lax.fori_loop(0, axial // (8 * UNROLL), rows, 0)
+        a_kept[pl.ds(axial, 8), :] = turned_in(padded(0, j + 1, axial))
         if after is not None:
             after(j)
         return carry
@@ -240,11 +297,13 @@
     lax.fori_loop(first, last, plane, 0)
 
 
-def interior(first, last, vel_ref, inner_ref, coef_ref, _, out_ref):
+def interior(first, last, vel_ref, coef_ref, _, out_ref, zero_ref, *kept_refs):
+    zero_ref[...] = jnp.zeros_like(zero_ref)
+
     def write(n, j, k, value):
         out_ref[n, j - first, k, :] = value
 
-    sweep(vel_ref, inner_ref, coef_ref, first, last, write)
+    sweep(vel_ref, None, coef_ref, kept_refs, first, last, write)
 
 
 def finish(
@@ -259,7 +318,8 @@
     coef_ref,
     *refs,
 ):
-    parts, (vel_in, out_ref, step_ref, vel_ref, res, sems) = refs[:-6], refs[-6:]
+    parts, refs = refs[: len(spans) - 1], refs[len(spans) - 1 :]
+    vel_in, out_ref, step_ref, vel_ref, res, sems, *kept_refs = refs
     del vel_in
     axial, radial = inner_ref.shape
     planes = res.shape[1]
@@ -277,17 +337,21 @@
 
     (start, stop), others = spans[-1], spans[:-1]
 
-    def beside(j, k):
+    def beside(j, k, coef):
+        inner = inner_ref[pl.ds(k, 8), :]
         for part, (first, _) in zip(parts, others):
-            for n in range(3):
-                write(n, first + j - start, k, part[n, j - start, k, :])
+            place = first + j - start
+            ghost = ghosts(inner, planes, place)
+            added = lane_zero_terms(vel_ref, ghost, coef, place, k, 1.0 / radial)
+            for n, value in enumerate(added):
+                write(n, place, pl.ds(k, 8), part[n, j - start, pl.ds(k, 8), :] + value)
 
     def after(j):
         store(j).start()
         for first, _ in others:
             store(first + j - start).start()
 
-    sweep(vel_ref, inner_ref, coef_ref, start, stop, write, beside, after)
+    sweep(vel_ref, inner_ref, coef_ref, kept_refs, start, stop, write, beside, after)
 
     cells = pl.ds(PAD, axial)
     for q in range(HALO):
@@ -302,6 +366,7 @@
             vel_ref,
             inner_ref,
             coef_ref,
+            kept_refs,
             first,
             first + HALO,
             write,
@@ -325,21 +390,27 @@
     return lax.ppermute(block, ("az", "ax"), route)
 
 
-def rounds(sizes, covered):
-    plan = []
+def rounds(sizes, covered, beam=16):
     shifts = [(i, k) for i in range(sizes[0]) for k in range(sizes[1])]
 
     def moved(cells, by):
         return {((i + by[0]) % sizes[0], (k + by[1]) % sizes[1]) for i, k in cells}
 
-    def hops(by):
-        return min(by[0], sizes[0] - by[0]) + min(by[1], sizes[1] - by[1])
-
-    while len(covered) < sizes[0] * sizes[1]:
-        best = max(shifts, key=lambda by: (len(covered | moved(covered, by)), -hops(by)))
-        covered = covered | moved(covered, best)
-        plan.append(best)
-    return plan
+    def hops(plan):
+        return sum(min(i, sizes[0] - i) + min(k, sizes[1] - k) for i, k in plan)
+
+    found = [(frozenset(covered), ())]
+    while len(found[0][0]) < len(shifts):
+        grown = {}
+        for cells, plan in found:
+            for by in shifts:
+                cover = cells | moved(cells, by)
+                longer = plan + (by,)
+                if cover not in grown or hops(longer) < hops(grown[cover]):
+                    grown[cover] = longer
+        ranked = sorted(grown.items(), key=lambda item: (-len(item[0]), hops(item[1]), item[1]))
+        found = ranked[:beam]
+    return found[0][1]
 
 
 def per_device(velocity):
@@ -367,21 +438,32 @@
         )
 
     pair = shape(3, HALO, axial, radial)
+    head, tail = call(
+        theta_edges,
+        "theta_edges",
+        0,
+        out_shape=(pair, pair),
+        in_specs=[vmem],
+        out_specs=(vmem, vmem),
+    )(velocity)
+    below = shifted(tail, (1, 0))
+    above = shifted(head, (-1, 0))
+
     edge = shape(3, planes, 2, radial)
     padded = shape(3, planes + 2 * HALO, axial + 2 * PAD, radial)
-    vel, head, tail, first, last, inner, pay = call(
-        first_pass,
+    vel, first, last, inner, pay = call(
+        functools.partial(first_pass, theta_step),
         "first_pass",
         10 * velocity.size,
-        out_shape=(padded, pair, pair, edge, edge, shape(axial, radial), shape(8, radial)),
+        out_shape=(padded, edge, edge, shape(axial, radial), shape(8, radial)),
         in_specs=[vmem, vmem],
-        out_specs=(vmem,) * 7,
-    )(velocity, coef)
+        out_specs=(vmem,) * 5,
+    )(velocity, head)
     low = shifted(last, (0, 1))
     high = shifted(first, (0, -1))
+    up = shifted(pay, (1, -1))
+    down = shifted(pay, (-1, 1))
     inner = shifted(inner, (sizes[0] // 2, 0))
-    below = shifted(tail, (1, 0))
-    above = shifted(head, (-1, 0))
     pay, vel = call(
         fold,
         "fold",
@@ -390,40 +472,40 @@
         in_specs=[vmem] * 6,
         out_specs=(vmem, vmem),
         input_output_aliases={5: 1},
-    )(low, high, inner, pay, coef, vel)
-    up = shifted(pay, (1, 0))
-    down = shifted(pay, (-1, 0))
-
-    known = {(0, 0), (0, 1), (0, sizes[1] - 1), (sizes[0] // 2, 0)}
-    known = {((i + d) % sizes[0], k) for i, k in known for d in (-1, 0, 1)}
+    )(low, high, up, down, pay, vel)
+
+    known = {(0, 0)}
+    for i, k in ((0, 1), (0, -1), (1, -1), (-1, 1)):
+        known.add((i % sizes[0], k % sizes[1]))
     plan = rounds(sizes, known)
     inside = planes - 2 * HALO
-    count = len(plan) + 2
+    count = len(plan) + 1
     while inside % count:
         count += 1
     bounds = range(HALO, planes - HALO + 1, inside // count)
     spans = list(zip(bounds[:-1], bounds[1:]))
+    kept = [
+        pltpu.VMEM((axial + 8, radial), f32),
+        pltpu.VMEM((axial, radial), f32),
+        pltpu.VMEM((axial + PAD, radial), f32),
+    ]
     parts = []
-    token = pay
+    far = zero = pay
     for n, (first, last) in enumerate(spans[:-1]):
-        parts.append(
-            call(
-                functools.partial(interior, first, last),
-                f"interior_{n}",
-                400 * (last - first) * axial * radial,
-                out_shape=shape(3, last - first, axial, radial),
-                in_specs=[vmem] * 4,
-                out_specs=vmem,
-            )(vel, inner, coef, token)
-        )
-        if n == 0:
-            pay = jnp.maximum(pay, jnp.maximum(up, down))
-            token = up
-        elif n <= len(plan):
-            token = far
+        before = far
         if n < len(plan):
-            pay = pay if n == 0 else jnp.maximum(pay, far)
+            pay = jnp.maximum(pay, jnp.maximum(far, zero)) if n else pay
             far = shifted(pay, plan[n])
+        part, zero = call(
+            functools.partial(interior, first, last),
+            f"interior_{n}",
+            400 * (last - first) * axial * radial,
+            out_shape=(shape(3, last - first, axial, radial), shape(8, radial)),
+            in_specs=[vmem] * 3,
+            out_specs=(vmem, vmem),
+            scratch_shapes=kept,
+        )(vel, coef, before)
+        parts.append(part)
     increment, time_step, _ = call(
         functools.partial(finish, spans),
         "finish",
@@ -435,6 +517,7 @@
         scratch_shapes=[
             pltpu.VMEM(velocity.shape, f32),
             pltpu.SemaphoreType.DMA((planes,)),
+            *kept,
         ],
         input_output_aliases={8 + len(parts): 2},
     )(below, above, up, down, pay, far, inner, coef, *parts, vel)

time: 53.4 us -> 53.5 us (level)
  waiting for transfers between devices: 15.2 us -> 2.08 us
  starting transfers between devices: 11 us -> 20.4 us
  Pallas kernels: 22.6 us -> 27.3 us
  local copies, waits for them, and re-layouts: 3.62 us -> 2.78 us
    ppermute x9 -> x10, waiting for transfers between devices: 15.2 us -> 2.08 us  [shifted(): return lax.ppermute(block, ('az', 'ax'), route)]
    ppermute x9 -> x10, starting transfers between devices: 11 us -> 20.4 us  [shifted(): return lax.ppermute(block, ('az', 'ax'), route)]
    pallas_call x1, Pallas kernels: 7.81 us -> 10.4 us  [per_device(): call(functools.partial(finish, spans), 'finish', 160 * velocity.size, scr...]
    pallas_call x3, Pallas kernels: 11.4 us -> 13.5 us  [per_device(): call(functools.partial(interior, first, last), f'interior_{n}', 400 * (la...]
    unnamed x4, local copies, waits for them, and re-layouts: 3.62 us -> 2.78 us
    pallas_call x1 -> x2, Pallas kernels: 3.03 us -> 3.21 us  [the longest x1 3.16 us: per_device(): call(functools.partial(first_pass, theta_step), 'first_pass', 10 * veloci...]
  transfers between devices with their start and end apart: 9 -> 10, of which waited for: 4 -> 1; matrix products, arithmetic and copies ran while one was open for 0% -> 0% of each run, Pallas kernels for 22% -> 26%
where the time goes in v4:
time: 53.5 us; the launch traced here: 53.2 us
  Pallas kernels  27.3 us (51%)
  starting transfers between devices  20.4 us (38%)
  local copies, waits for them, and re-layouts  2.78 us (5%)
  waiting for transfers between devices  2.08 us (4%)
  between operations  0.72 us (1%)
    ppermute x10, starting transfers between devices, shifted(): return lax.ppermute(block, ('az', 'ax'), route)  20.4 us
    pallas_call x3, Pallas kernels, per_device(): call(functools.partial(interior, first, last), f'interior_{n}', 400 * (la...  13.5 us
    pallas_call x1, Pallas kernels, per_device(): call(functools.partial(finish, spans), 'finish', 160 * velocity.size, scr...  10.4 us
    pallas_call x1, Pallas kernels, per_device(): call(functools.partial(first_pass, theta_step), 'first_pass', 10 * veloci...  3.16 us
    unnamed x4, local copies, waits for them, and re-layouts  2.78 us
    ppermute x10, waiting for transfers between devices, shifted(): return lax.ppermute(block, ('az', 'ax'), route)  2.08 us
  transfers between devices with their start and end apart: 10, of which 1 were waited for; matrix products, arithmetic and copies ran while one was open for 0% of the time, Pallas kernels for 26%

profile of v4, /device:TPU:0, one launch (start us, length us, event | category | flops | bytes accessed | tf_op | source)
XLA Modules:
  0.0 53.2 jit_solution(11882660604379157887)
XLA Ops:
  0.6 0.0 copy-start
  0.6 2.8 %copy-done = f32[3,32,128,128]{3,2,1,0:T(8,128)S(1)} copy-done((f32[3,32,128,128]{3,2,1,0:T(8,128)S(1)}, f32[3,32,128,128]{3,2,1,0:T(8,128)}, u32[]{:S(2)}) %copy-start) | copy-done | bytes 6291480
  3.4 0.1 theta_edges.1
  3.5 0.0 copy-start.1
  3.5 3.2 %first_pass.1 = (f32[3,36,144,128]{3,2,1,0:T(8,128)S(1)}, f32[3,32,2,128]{3,2,1,0:T(2,128)S(1)}, f32[3,32,2,128]{3,2,1,0:T(2,128)S(1)}, f32[128,128]{1,0:T(8,128)S(1)}, f32[8,128]{1,0:T(8,128)S(1)}) custom-call(f32[3,32,128,128]{3,2,1,0:T(8,128)S(1)} %copy-done, f32[3,2,128,128]{3,2,1,0:T(8,128)S(1)} %get-tuple-element.19._), custom_call_target="tpu_custom_call" | custom-call | flops 15728640 | bytes 6291456 | tf_op jit(solution)/shard_map/first_pass/pallas_call | solution.py:454
  6.6 0.5 collective-permute-start.4
  7.2 2.0 %collective-permute-start.5 = (f32[3,32,2,128]{3,2,1,0:T(2,128)S(1)}, f32[3,32,2,128]{3,2,1,0:T(2,128)S(1)}, u32[]{:S(2)}, u32[]{:S(2)}) collective-permute-start(f32[3,32,2,128]{3,2,1,0:T(2,128)S(1)} %get-tuple-element.22), channel_id=1, source_target_pairs={{1,0},{2,1},{3,2},{0,3},{5,4},{6,5},{7,6},{4,7},{9,8},{10,9},{11,1... | collective-permute-start | bytes 294920 | tf_op jit(solution)/shard_map/ppermute | solution.py:390
  9.1 4.8 %collective-permute-start.3 = (f32[8,128]{1,0:T(8,128)S(1)}, f32[8,128]{1,0:T(8,128)S(1)}, u32[]{:S(2)}, u32[]{:S(2)}) collective-permute-start(f32[8,128]{1,0:T(8,128)S(1)} %get-tuple-element.20.pay_ref), channel_id=1, source_target_pairs={{7,0},{4,1},{5,2},{6,3},{11,4},{8,5},{9,6},{10,7},{15,8},{12,9},{1... | collective-permute-start | bytes 12296 | tf_op jit(solution)/shard_map/ppermute | solution.py:390
  13.9 0.0 collective-permute-start.2
  13.9 5.9 %collective-permute-start.1 = (f32[3,2,128,128]{3,2,1,0:T(8,128)S(1)}, f32[3,2,128,128]{3,2,1,0:T(8,128)S(1)}, u32[]{:S(2)}, u32[]{:S(2)}) collective-permute-start(f32[3,2,128,128]{3,2,1,0:T(8,128)S(1)} %get-tuple-element.19._), channel_id=1, source_target_pairs={{4,0},{5,1},{6,2},{7,3},{8,4},{9,5},{10,6},{11,7},{12,8},{13,9},{1... | collective-permute-start | bytes 1179656 | tf_op jit(solution)/shard_map/ppermute | solution.py:390
  19.8 0.0 collective-permute-done.3.down_ref
  19.8 0.0 collective-permute-start
  19.8 0.0 collective-permute-done.2.up_ref
  19.8 0.1 collective-permute-start.9
  19.9 0.0 collective-permute-done.4.low_ref
  19.9 0.0 collective-permute-done.5.high_ref
  19.9 0.2 fold.1
  20.2 2.4 %collective-permute-start.6 = (f32[8,128]{1,0:T(8,128)S(1)}, f32[8,128]{1,0:T(8,128)S(1)}, u32[]{:S(2)}, u32[]{:S(2)}) collective-permute-start(f32[8,128]{1,0:T(8,128)S(1)} %get-tuple-element.24._), channel_id=1, source_target_pairs={{24,0},{25,1},{26,2},{27,3},{28,4},{29,5},{30,6},{31,7},{0,8},{1,9... | collective-permute-start | bytes 12296 | tf_op jit(solution)/shard_map/ppermute | solution.py:390
  22.5 0.0 copy-done.1
  22.5 4.3 %interior_0.1 = (f32[3,7,128,128]{3,2,1,0:T(8,128)S(1)}, f32[8,128]{1,0:T(8,128)S(1)}) custom-call(f32[3,36,144,128]{3,2,1,0:T(8,128)S(1)} %get-tuple-element.25.vel_ref.refs_3_, f32[15,8,128]{2,1,0:T(8,128)S(1)} %copy-done.1, f32[8,128]{1,0:T(8,128)S(1)} %get-tuple-element.24._), custom_call_target="tpu_custom_call" | custom-call | flops 45875200 | bytes 6291456 | tf_op jit(solution)/shard_map/interior_0/pallas_call | solution.py:499
  26.9 2.1 %collective-permute-done.6._ = f32[8,128]{1,0:T(8,128)S(1)} collective-permute-done((f32[8,128]{1,0:T(8,128)S(1)}, f32[8,128]{1,0:T(8,128)S(1)}, u32[]{:S(2)}, u32[]{:S(2)}) %collective-permute-start.6) | collective-permute-done | bytes 4128 | tf_op jit(solution)/shard_map/ppermute | solution.py:390
  28.9 4.7 %collective-permute-start.7 = (f32[8,128]{1,0:T(8,128)S(1)}, f32[8,128]{1,0:T(8,128)S(1)}, u32[]{:S(2)}, u32[]{:S(2)}) collective-permute-start(f32[8,128]{1,0:T(8,128)S(1)} %maximum_maximum_fusion.1), channel_id=1, source_target_pairs={{16,0},{17,1},{18,2},{19,3},{20,4},{21,5},{22,6},{23,7},{24,8},{25... | collective-permute-start | bytes 12296 | tf_op jit(solution)/shard_map/ppermute | solution.py:390
  33.7 4.3 %interior_1.1 = (f32[3,7,128,128]{3,2,1,0:T(8,128)S(1)}, f32[8,128]{1,0:T(8,128)S(1)}) custom-call(f32[3,36,144,128]{3,2,1,0:T(8,128)S(1)} %get-tuple-element.25.vel_ref.refs_3_, f32[15,8,128]{2,1,0:T(8,128)S(1)} %copy-done.1, f32[8,128]{1,0:T(8,128)S(1)} %collective-permute-done.6._), custom_call_target="tpu_custom_call" | custom-call | flops 45875200 | bytes 6291456 | tf_op jit(solution)/shard_map/interior_1/pallas_call | solution.py:499
  38.0 0.0 collective-permute-done.7._
  38.0 0.0 collective-permute-start.8
  38.0 4.8 %interior_2.1 = (f32[3,7,128,128]{3,2,1,0:T(8,128)S(1)}, f32[8,128]{1,0:T(8,128)}) custom-call(f32[3,36,144,128]{3,2,1,0:T(8,128)S(1)} %get-tuple-element.25.vel_ref.refs_3_, f32[15,8,128]{2,1,0:T(8,128)S(1)} %copy-done.1, f32[8,128]{1,0:T(8,128)S(1)} %collective-permute-done.7._), custom_call_target="tpu_custom_call" | custom-call | flops 45875200 | bytes 6291456 | tf_op jit(solution)/shard_map/interior_2/pallas_call | solution.py:499
  42.8 0.0 collective-permute-done.9.inner_ref
  42.8 0.0 collective-permute-done.8.far_ref
  42.9 0.0 collective-permute-done.below_ref
  42.9 0.0 collective-permute-done.1.above_ref
  42.9 10.4 %finish.1 = (f32[3,32,128,128]{3,2,1,0:T(8,128)}, f32[1]{0:T(128)}, f32[3,36,144,128]{3,2,1,0:T(8,128)S(1)}) custom-call(f32[3,2,128,128]{3,2,1,0:T(8,128)S(1)} %collective-permute-done.below_ref, f32[3,2,128,128]{3,2,1,0:T(8,128)S(1)} %collective-permute-done.1.above_ref, ...), custom_call_target="tpu_custom_call", output_to_operand_aliasing={{2}: (11, {})} | custom-call | flops 251658240 | bytes 6291456 | tf_op jit(solution)/shard_map/finish/pallas_call | solution.py:509
  (2 shorter events, 0.0 us)
Async XLA Ops:
  0.6 2.8 %copy-start = (f32[3,32,128,128]{3,2,1,0:T(8,128)S(1)}, f32[3,32,128,128]{3,2,1,0:T(8,128)}, u32[]{:S(2)}) copy-start(f32[3,32,128,128]{3,2,1,0:T(8,128)} %v_ref.3) | copy-start | bytes 18874372
  3.5 19.1 %copy-start.1 = (f32[15,8,128]{2,1,0:T(8,128)S(1)}, f32[15,8,128]{2,1,0:T(8,128)}, u32[]{:S(2)}) copy-start(f32[15,8,128]{2,1,0:T(8,128)} %constant.2.clone.coef_ref) | copy-start | bytes 184324
  6.6 13.2 %collective-permute-start.4 = (f32[3,32,2,128]{3,2,1,0:T(2,128)S(1)}, f32[3,32,2,128]{3,2,1,0:T(2,128)S(1)}, u32[]{:S(2)}, u32[]{:S(2)}) collective-permute-start(f32[3,32,2,128]{3,2,1,0:T(2,128)S(1)} %get-tuple-element.21), channel_id=1, source_target_pairs={{3,0},{0,1},{1,2},{2,3},{7,4},{4,5},{5,6},{6,7},{11,8},{8,9},{9,10... | collective-permute-start | bytes 294920 | tf_op jit(solution)/shard_map/ppermute | solution.py:390
  7.2 12.7 %collective-permute-start.5 = (f32[3,32,2,128]{3,2,1,0:T(2,128)S(1)}, f32[3,32,2,128]{3,2,1,0:T(2,128)S(1)}, u32[]{:S(2)}, u32[]{:S(2)}) collective-permute-start(f32[3,32,2,128]{3,2,1,0:T(2,128)S(1)} %get-tuple-element.22), channel_id=1, source_target_pairs={{1,0},{2,1},{3,2},{0,3},{5,4},{6,5},{7,6},{4,7},{9,8},{10,9},{11,1... | collective-permute-start | bytes 294920 | tf_op jit(solution)/shard_map/ppermute | solution.py:390
  9.1 10.7 %collective-permute-start.3 = (f32[8,128]{1,0:T(8,128)S(1)}, f32[8,128]{1,0:T(8,128)S(1)}, u32[]{:S(2)}, u32[]{:S(2)}) collective-permute-start(f32[8,128]{1,0:T(8,128)S(1)} %get-tuple-element.20.pay_ref), channel_id=1, source_target_pairs={{7,0},{4,1},{5,2},{6,3},{11,4},{8,5},{9,6},{10,7},{15,8},{12,9},{1... | collective-permute-start | bytes 12296 | tf_op jit(solution)/shard_map/ppermute | solution.py:390
  13.9 5.9 %collective-permute-start.2 = (f32[8,128]{1,0:T(8,128)S(1)}, f32[8,128]{1,0:T(8,128)S(1)}, u32[]{:S(2)}, u32[]{:S(2)}) collective-permute-start(f32[8,128]{1,0:T(8,128)S(1)} %get-tuple-element.20.pay_ref), channel_id=1, source_target_pairs={{29,0},{30,1},{31,2},{28,3},{1,4},{2,5},{3,6},{0,7},{5,8},{6,9},{7... | collective-permute-start | bytes 12296 | tf_op jit(solution)/shard_map/ppermute | solution.py:390
  13.9 28.9 %collective-permute-start.1 = (f32[3,2,128,128]{3,2,1,0:T(8,128)S(1)}, f32[3,2,128,128]{3,2,1,0:T(8,128)S(1)}, u32[]{:S(2)}, u32[]{:S(2)}) collective-permute-start(f32[3,2,128,128]{3,2,1,0:T(8,128)S(1)} %get-tuple-element.19._), channel_id=1, source_target_pairs={{4,0},{5,1},{6,2},{7,3},{8,4},{9,5},{10,6},{11,7},{12,8},{13,9},{1... | collective-permute-start | bytes 1179656 | tf_op jit(solution)/shard_map/ppermute | solution.py:390
  19.8 23.1 %collective-permute-start = (f32[3,2,128,128]{3,2,1,0:T(8,128)S(1)}, f32[3,2,128,128]{3,2,1,0:T(8,128)S(1)}, u32[]{:S(2)}, u32[]{:S(2)}) collective-permute-start(f32[3,2,128,128]{3,2,1,0:T(8,128)S(1)} %get-tuple-element.18), channel_id=1, source_target_pairs={{28,0},{29,1},{30,2},{31,3},{0,4},{1,5},{2,6},{3,7},{4,8},{5,9},{6... | collective-permute-start | bytes 1179656 | tf_op jit(solution)/shard_map/ppermute | solution.py:390
  19.8 23.0 %collective-permute-start.9 = (f32[128,128]{1,0:T(8,128)S(1)}, f32[128,128]{1,0:T(8,128)S(1)}, u32[]{:S(2)}, u32[]{:S(2)}) collective-permute-start(f32[128,128]{1,0:T(8,128)S(1)} %get-tuple-element.28), channel_id=1, source_target_pairs={{16,0},{17,1},{18,2},{19,3},{20,4},{21,5},{22,6},{23,7},{24,8},{25... | collective-permute-start | bytes 196616 | tf_op jit(solution)/shard_map/ppermute | solution.py:390
  20.2 8.8 %collective-permute-start.6 = (f32[8,128]{1,0:T(8,128)S(1)}, f32[8,128]{1,0:T(8,128)S(1)}, u32[]{:S(2)}, u32[]{:S(2)}) collective-permute-start(f32[8,128]{1,0:T(8,128)S(1)} %get-tuple-element.24._), channel_id=1, source_target_pairs={{24,0},{25,1},{26,2},{27,3},{28,4},{29,5},{30,6},{31,7},{0,8},{1,9... | collective-permute-start | bytes 12296 | tf_op jit(solution)/shard_map/ppermute | solution.py:390
  28.9 9.1 %collective-permute-start.7 = (f32[8,128]{1,0:T(8,128)S(1)}, f32[8,128]{1,0:T(8,128)S(1)}, u32[]{:S(2)}, u32[]{:S(2)}) collective-permute-start(f32[8,128]{1,0:T(8,128)S(1)} %maximum_maximum_fusion.1), channel_id=1, source_target_pairs={{16,0},{17,1},{18,2},{19,3},{20,4},{21,5},{22,6},{23,7},{24,8},{25... | collective-permute-start | bytes 12296 | tf_op jit(solution)/shard_map/ppermute | solution.py:390
  38.0 4.9 %collective-permute-start.8 = (f32[8,128]{1,0:T(8,128)S(1)}, f32[8,128]{1,0:T(8,128)S(1)}, u32[]{:S(2)}, u32[]{:S(2)}) collective-permute-start(f32[8,128]{1,0:T(8,128)S(1)} %maximum_maximum_fusion.pay_ref), channel_id=1, source_target_pairs={{3,0},{0,1},{1,2},{2,3},{7,4},{4,5},{5,6},{6,7},{11,8},{8,9},{9,10... | collective-permute-start | bytes 12296 | tf_op jit(solution)/shard_map/ppermute | solution.py:390

commit v5 on v4

--- a/solution.py
+++ b/solution.py
@@ -66,22 +66,19 @@
     return np.broadcast_to(rows[:, None, :], (COUNT, 8, radial)).astype(np.float32)
 
 
-def turned_in(x):
-    return pltpu.roll(x, 1, 1)
-
-
-def turned_out(x):
-    return pltpu.roll(x, x.shape[1] - 1, 1)
-
-
-def terms(vel, kept, ghost, coef, j, k, dr):
-    a_in, a_in_side, a_in_next, b_out, b_out_back, c_out, c_out_back = kept
-    lane = lax.broadcasted_iota(jnp.int32, a_in.shape, 1)
+def terms(vel, ghost, coef, j, k, dr):
+    lane = lax.broadcasted_iota(jnp.int32, (8, 128), 1)
     first_lane = lane == 0
-    last_lane = lane == a_in.shape[1] - 1
+    last_lane = lane == 127
 
     def at(component, dj, dk):
         return vel[component, j + HALO + dj, pl.ds(k + PAD + dk, 8), :]
+
+    def out(x):
+        return pltpu.roll(x, 127, 1)
+
+    def inn(x):
+        return pltpu.roll(x, 1, 1)
 
     nu = VISCOSITY
     lap = nu / dr**2
@@ -105,12 +102,14 @@
     (a_side, *_), (a_next, *_), a_theta, a_axial = pieces(0)
     (_, b_back, *_), (b_next, *_), b_theta, b_axial = pieces(1)
     (c_side, *_), (_, c_back, *_), c_theta, c_axial = pieces(2)
+    a_in = inn(a)
     pair_a = a + a_in
-    pair_side = a_side + a_in_side
-    pair_next = a_next + a_in_next
-
+    pair_side = a_side + inn(a_side)
+    pair_next = a_next + inn(a_next)
+
+    c_out = out(c)
     up = jnp.where(last_lane, -c, c_out)
-    low = below(2, turned_in(c))
+    low = below(2, inn(c))
     u_r = pair_a + pair_next
     u_t = (b_back + b) + (at(1, -1, 1) + b_next)
     h_z = (up - low) * (coef[RADIAL_C] - u_r * (0.125 / dr)) + (up + low) * lap
@@ -118,8 +117,9 @@
     h_z = h_z + (c_theta[1] * coef[SECOND_C] + c_axial[1] * vis_z)
     h_z = h_z + c * (coef[CENTRE_Z] + c_axial[0] * adv_z)
 
+    b_out = out(b)
     up = jnp.where(last_lane, -b, b_out)
-    low = below(1, turned_in(b))
+    low = below(1, inn(b))
     u_r = pair_a + pair_side
     u_z = (c_back + c) + (at(2, 1, -1) + c_side)
     h_t = (up - low) * (coef[RADIAL_C] - u_r * (0.125 / dr)) + (up + low) * lap
@@ -128,12 +128,12 @@
     h_t = h_t + b_axial[0] * (u_z * (0.25 * adv_z))
     h_t = h_t + (pair_side - pair_a) * coef[TURN_T]
 
-    up = turned_out(a)
+    up = out(a)
     low = below(0, a_in)
     pair_b = b + b_out
-    pair_back = b_back + b_out_back
+    pair_back = b_back + out(b_back)
     u_t = pair_b + pair_back
-    u_z = (c + c_out) + (c_back + c_out_back)
+    u_z = (c + c_out) + (c_back + out(c_back))
     h_r = (up - low) * (coef[RADIAL_F] - a * (0.5 / dr)) + (up + low) * lap
     h_r = h_r + u_t * (u_t * coef[CURVE_R] + a_theta[0] * coef[THETA_F])
     h_r = h_r + (a_theta[1] * coef[SECOND_F] + a_axial[1] * vis_z)
@@ -209,15 +209,16 @@
         ref[0, 0] = jnp.where(last, top, ref[0, 0])
 
 
-def fold(low_ref, high_ref, up_ref, down_ref, pay_ref, vel_in, out_ref, vel_ref):
+def fold(low_ref, high_ref, pay_ref, vel_in, out_ref, vel_ref):
     del vel_in
     planes, radial = low_ref.shape[1], low_ref.shape[3]
     axial = vel_ref.shape[2] - 2 * PAD
     lane = lax.broadcasted_iota(jnp.int32, (1, radial), 1)
     top = jnp.maximum(low_ref[0, 0, 0:1, :], high_ref[0, 0, 0:1, :])
     top = jnp.max(jnp.where(lane == radial - 1, top, 0.0), axis=(0, 1), keepdims=True)
-    top = jnp.maximum(top, jnp.maximum(up_ref[0:1, :], down_ref[0:1, :]))
-    out_ref[...] = jnp.broadcast_to(jnp.maximum(top, pay_ref[0:1, :]), out_ref.shape)
+    out_ref[...] = jnp.maximum(pay_ref[...], top)
+    out_ref[1:2, :] = high_ref[1, planes - 1, 0:1, :]
+    out_ref[2:3, :] = low_ref[2, 0, 1:2, :]
     wall = wall_mask(2, radial)
 
     def plane(j, carry):
@@ -230,6 +231,19 @@
     lax.fori_loop(0, planes, plane, 0, unroll=4)
 
 
+def late(pay_ref, *refs):
+    fars, (inner_in, tiles_ref, inner_ref) = refs[:-7], (refs[-7], *refs[-2:])
+    tile = pay_ref[...]
+    top = tile[0:1, :]
+    for far in fars:
+        top = jnp.maximum(top, far[0:1, :])
+    row = lax.broadcasted_iota(jnp.int32, tile.shape, 0)
+    tile = jnp.where(row == 0, top, tile)
+    for i in range(tiles_ref.shape[0]):
+        tiles_ref[i] = tile
+    inner_ref[...] = inner_in[...]
+
+
 def ghosts(inner, planes, j):
     radial = inner.shape[1]
 
@@ -240,47 +254,20 @@
     return ghost
 
 
-def sweep(vel_ref, inner_ref, coef_ref, kept_refs, first, last, write, beside=None, after=None):
-    a_kept, b_kept, c_kept = kept_refs
+def sweep(vel_ref, inner_ref, coef_ref, first, last, write, beside=None, after=None):
     planes = vel_ref.shape[1] - 2 * HALO
     axial, radial = vel_ref.shape[2] - 2 * PAD, vel_ref.shape[3]
 
-    def padded(n, j, k):
-        return vel_ref[n, j + HALO, pl.ds(k + PAD, 8), :]
-
-    def fill(i, carry):
-        k = pl.multiple_of(i * 8, 8)
-        a_kept[pl.ds(k, 8), :] = turned_in(padded(0, first, k))
-        b_kept[pl.ds(k, 8), :] = turned_out(padded(1, first - 1, k))
-        return carry
-
-    lax.fori_loop(0, axial // 8, fill, 0, unroll=4)
-    a_kept[pl.ds(axial, 8), :] = turned_in(padded(0, first, axial))
-
     def plane(j, carry):
-        c_kept[0:PAD, :] = turned_out(padded(2, j, -PAD))
-
         def rows(i, carry):
             coef = [coef_ref[n] for n in range(COUNT)]
             ks = [pl.multiple_of((i * UNROLL + u) * 8, 8) for u in range(UNROLL)]
-            a_in = [a_kept[pl.ds(k, 8), :] for k in ks]
-            a_in_next = [a_kept[pl.ds(k + 1, 8), :] for k in ks]
-            b_out_back = [b_kept[pl.ds(k, 8), :] for k in ks]
-            a_in_side = [turned_in(padded(0, j + 1, k)) for k in ks]
-            b_out = [turned_out(padded(1, j, k)) for k in ks]
-            c_out = [turned_out(padded(2, j, k)) for k in ks]
-            for u, k in enumerate(ks):
-                a_kept[pl.ds(k, 8), :] = a_in_side[u]
-                b_kept[pl.ds(k, 8), :] = b_out[u]
-                c_kept[pl.ds(k + PAD, 8), :] = c_out[u]
-            c_out_back = [c_kept[pl.ds(k + PAD - 1, 8), :] for k in ks]
-            kept = zip(a_in, a_in_side, a_in_next, b_out, b_out_back, c_out, c_out_back)
             found = []
-            for k, turned in zip(ks, kept):
+            for k in ks:
                 ghost = None
                 if inner_ref is not None:
                     ghost = ghosts(inner_ref[pl.ds(k, 8), :], planes, j)
-                found.append(terms(vel_ref, turned, ghost, coef, j, k, 1.0 / radial))
+                found.append(terms(vel_ref, ghost, coef, j, k, 1.0 / radial))
             for k, values in zip(ks, found):
                 for n, value in enumerate(values):
                     write(n, j, pl.ds(k, 8), value)
@@ -289,7 +276,6 @@
             return carry
 
         lax.fori_loop(0, axial // (8 * UNROLL), rows, 0)
-        a_kept[pl.ds(axial, 8), :] = turned_in(padded(0, j + 1, axial))
         if after is not None:
             after(j)
         return carry
@@ -297,33 +283,32 @@
     lax.fori_loop(first, last, plane, 0)
 
 
-def interior(first, last, vel_ref, coef_ref, _, out_ref, zero_ref, *kept_refs):
-    zero_ref[...] = jnp.zeros_like(zero_ref)
-
+def interior(first, last, vel_ref, coef_ref, _, out_ref):
     def write(n, j, k, value):
         out_ref[n, j - first, k, :] = value
 
-    sweep(vel_ref, None, coef_ref, kept_refs, first, last, write)
+    sweep(vel_ref, None, coef_ref, first, last, write)
 
 
 def finish(
     spans,
     below_ref,
     above_ref,
-    up_ref,
-    down_ref,
-    pay_ref,
-    far_ref,
+    tiles_ref,
     inner_ref,
     coef_ref,
     *refs,
 ):
     parts, refs = refs[: len(spans) - 1], refs[len(spans) - 1 :]
-    vel_in, out_ref, step_ref, vel_ref, res, sems, *kept_refs = refs
+    vel_in, out_ref, step_ref, vel_ref, res, sems = refs
     del vel_in
     axial, radial = inner_ref.shape
     planes = res.shape[1]
-    largest = jnp.max(jnp.maximum(pay_ref[0:1, :], far_ref[0:1, :]))
+    count = tiles_ref.shape[0]
+    top = tiles_ref[0, 0:1, :]
+    for i in range(1, count):
+        top = jnp.maximum(top, tiles_ref[i, 0:1, :])
+    largest = jnp.max(top)
     time_step = CFL_TARGET / (largest + 1e-06)
     step_ref[0] = time_step
     scale = GAMMA * time_step
@@ -351,7 +336,7 @@
         for first, _ in others:
             store(first + j - start).start()
 
-    sweep(vel_ref, inner_ref, coef_ref, kept_refs, start, stop, write, beside, after)
+    sweep(vel_ref, inner_ref, coef_ref, start, stop, write, beside, after)
 
     cells = pl.ds(PAD, axial)
     for q in range(HALO):
@@ -359,14 +344,15 @@
             vel_ref[0, place, cells, :] = ref[0, q] * coef_ref[WALL, 0:1, :]
             vel_ref[1, place, cells, :] = ref[1, q]
             vel_ref[2, place, cells, :] = ref[2, q]
-    vel_ref[1, HALO - 1, PAD + axial : PAD + axial + 1, :] = up_ref[1:2, :]
-    vel_ref[2, HALO + planes, PAD - 1 : PAD, :] = down_ref[2:3, :]
+    place = lax.axis_index("az")
+    lower, upper = lax.rem(place + count - 1, count), lax.rem(place + 1, count)
+    vel_ref[1, HALO - 1, PAD + axial : PAD + axial + 1, :] = tiles_ref[lower, 1:2, :]
+    vel_ref[2, HALO + planes, PAD - 1 : PAD, :] = tiles_ref[upper, 2:3, :]
     for first in (0, planes - HALO):
         sweep(
             vel_ref,
             inner_ref,
             coef_ref,
-            kept_refs,
             first,
             first + HALO,
             write,
@@ -390,27 +376,9 @@
     return lax.ppermute(block, ("az", "ax"), route)
 
 
-def rounds(sizes, covered, beam=16):
-    shifts = [(i, k) for i in range(sizes[0]) for k in range(sizes[1])]
-
-    def moved(cells, by):
-        return {((i + by[0]) % sizes[0], (k + by[1]) % sizes[1]) for i, k in cells}
-
-    def hops(plan):
-        return sum(min(i, sizes[0] - i) + min(k, sizes[1] - k) for i, k in plan)
-
-    found = [(frozenset(covered), ())]
-    while len(found[0][0]) < len(shifts):
-        grown = {}
-        for cells, plan in found:
-            for by in shifts:
-                cover = cells | moved(cells, by)
-                longer = plan + (by,)
-                if cover not in grown or hops(longer) < hops(grown[cover]):
-                    grown[cover] = longer
-        ranked = sorted(grown.items(), key=lambda item: (-len(item[0]), hops(item[1]), item[1]))
-        found = ranked[:beam]
-    return found[0][1]
+def quarters(planes):
+    step = (planes - 2 * HALO) // 4
+    return [(HALO + n * step, HALO + (n + 1) * step) for n in range(4)]
 
 
 def per_device(velocity):
@@ -431,9 +399,7 @@
             kernel,
             name=name,
             compiler_params=pltpu.CompilerParams(vmem_limit_bytes=(4 + scratch) * 2**20),
-            cost_estimate=pl.CostEstimate(
-                flops=work, bytes_accessed=velocity.size * 4, transcendentals=0
-            ),
+            cost_estimate=pl.CostEstimate(flops=work, bytes_accessed=work, transcendentals=0),
             **kwargs,
         )
 
@@ -454,73 +420,71 @@
     vel, first, last, inner, pay = call(
         functools.partial(first_pass, theta_step),
         "first_pass",
-        10 * velocity.size,
+        0,
         out_shape=(padded, edge, edge, shape(axial, radial), shape(8, radial)),
         in_specs=[vmem, vmem],
         out_specs=(vmem,) * 5,
     )(velocity, head)
     low = shifted(last, (0, 1))
     high = shifted(first, (0, -1))
-    up = shifted(pay, (1, -1))
-    down = shifted(pay, (-1, 1))
-    inner = shifted(inner, (sizes[0] // 2, 0))
     pay, vel = call(
         fold,
         "fold",
-        velocity.size // planes,
+        0,
         out_shape=(shape(8, radial), padded),
-        in_specs=[vmem] * 6,
+        in_specs=[vmem] * 4,
         out_specs=(vmem, vmem),
-        input_output_aliases={5: 1},
-    )(low, high, up, down, pay, vel)
-
-    known = {(0, 0)}
-    for i, k in ((0, 1), (0, -1), (1, -1), (-1, 1)):
-        known.add((i % sizes[0], k % sizes[1]))
-    plan = rounds(sizes, known)
-    inside = planes - 2 * HALO
-    count = len(plan) + 1
-    while inside % count:
-        count += 1
-    bounds = range(HALO, planes - HALO + 1, inside // count)
-    spans = list(zip(bounds[:-1], bounds[1:]))
-    kept = [
-        pltpu.VMEM((axial + 8, radial), f32),
-        pltpu.VMEM((axial, radial), f32),
-        pltpu.VMEM((axial + PAD, radial), f32),
-    ]
+        input_output_aliases={3: 1},
+    )(low, high, pay, vel)
+    top, fars, known = pay, [], 3
+    while known < sizes[1]:
+        step = min(known, sizes[1] - known)
+        fars.append(shifted(top, (0, step)))
+        top = jnp.maximum(top, fars[-1])
+        known += step
+
+    spans = quarters(planes)
     parts = []
-    far = zero = pay
-    for n, (first, last) in enumerate(spans[:-1]):
-        before = far
-        if n < len(plan):
-            pay = jnp.maximum(pay, jnp.maximum(far, zero)) if n else pay
-            far = shifted(pay, plan[n])
-        part, zero = call(
+
+    def inside(n, token):
+        first, last = spans[n]
+        part = call(
             functools.partial(interior, first, last),
             f"interior_{n}",
-            400 * (last - first) * axial * radial,
-            out_shape=(shape(3, last - first, axial, radial), shape(8, radial)),
+            velocity.size,
+            out_shape=shape(3, last - first, axial, radial),
             in_specs=[vmem] * 3,
-            out_specs=(vmem, vmem),
-            scratch_shapes=kept,
-        )(vel, coef, before)
+            out_specs=vmem,
+        )(vel, coef, token)
         parts.append(part)
+
+    inside(0, pay)
+    inside(1, pay)
+    tiles, inner = call(
+        late,
+        "late",
+        0,
+        out_shape=(shape(sizes[0], 8, radial), shape(axial, radial)),
+        in_specs=[vmem] * (6 + len(fars)),
+        out_specs=(vmem, vmem),
+    )(pay, *fars, inner, below, above, *parts)
+    inner = shifted(inner, (sizes[0] // 2, 0))
+    moved = lax.all_to_all(tiles, "az", 0, 0)
+    inside(2, tiles)
     increment, time_step, _ = call(
         functools.partial(finish, spans),
         "finish",
-        160 * velocity.size,
+        0,
         scratch=8,
         out_shape=(shape(*velocity.shape), shape(1), padded),
-        in_specs=[vmem] * (9 + len(parts)),
+        in_specs=[vmem] * (6 + len(parts)),
         out_specs=(anywhere, smem, vmem),
         scratch_shapes=[
             pltpu.VMEM(velocity.shape, f32),
             pltpu.SemaphoreType.DMA((planes,)),
-            *kept,
         ],
-        input_output_aliases={8 + len(parts): 2},
-    )(below, above, up, down, pay, far, inner, coef, *parts, vel)
+        input_output_aliases={5 + len(parts): 2},
+    )(below, above, moved, inner, coef, *parts, vel)
     return increment, time_step.reshape(())
 
 

time: 53.5 us -> 57.1 us (1.067)
  local copies, waits for them, and re-layouts: 2.78 us -> 14.1 us
  starting transfers between devices: 20.4 us -> 15.5 us
  Pallas kernels: 27.3 us -> 23.6 us
    unnamed x4 -> x22, local copies, waits for them, and re-layouts: 2.78 us -> 14.1 us
    ppermute x10 -> x6, starting transfers between devices: 20.4 us -> 11.6 us  [shifted(): return lax.ppermute(block, ('az', 'ax'), route)]
    all_to_all x0 -> x1, starting transfers between devices: none -> 3.95 us  [per_device(): moved = lax.all_to_all(tiles, 'az', 0, 0)]
    pallas_call x6 -> x7, Pallas kernels: 27.2 us -> 23.6 us  [the longest x3 10.1 us: inside(): call(functools.partial(interior, first, last), f'interior_{n}', velocity....]
    ppermute x10 -> x6, waiting for transfers between devices: 2.08 us -> 2.46 us  [shifted(): return lax.ppermute(block, ('az', 'ax'), route)]
  transfers between devices with their start and end apart: 10 -> 7, of which waited for: 1 -> 2; matrix products, arithmetic and copies ran while one was open for 0% -> 0% of each run, Pallas kernels for 26% -> 24%
where the time goes in v5:
time: 57.1 us; the launch traced here: 56.5 us
  Pallas kernels  23.6 us (41%)
  starting transfers between devices  15.5 us (27%)
  local copies, waits for them, and re-layouts  14.1 us (25%)
  waiting for transfers between devices  2.46 us (4%)
  between operations  0.77 us (1%)
    unnamed x22, local copies, waits for them, and re-layouts  14.1 us
    ppermute x6, starting transfers between devices, shifted(): return lax.ppermute(block, ('az', 'ax'), route)  11.6 us
    pallas_call x3, Pallas kernels, inside(): call(functools.partial(interior, first, last), f'interior_{n}', velocity....  10.1 us
    pallas_call x1, Pallas kernels, per_device(): call(functools.partial(finish, spans), 'finish', 0, scratch=8, out_shape=...  9.47 us
    all_to_all x1, starting transfers between devices, per_device(): moved = lax.all_to_all(tiles, 'az', 0, 0)  3.95 us
    pallas_call x1, Pallas kernels, per_device(): call(functools.partial(first_pass, theta_step), 'first_pass', 0, out_shap...  3.14 us
    ppermute x6, waiting for transfers between devices, shifted(): return lax.ppermute(block, ('az', 'ax'), route)  2.46 us
  transfers between devices with their start and end apart: 7, of which 2 were waited for; matrix products, arithmetic and copies ran while one was open for 0% of the time, Pallas kernels for 24%

profile of v5, /device:TPU:0, one launch (start us, length us, event | category | flops | bytes accessed | tf_op | source)
XLA Modules:
  0.0 56.5 jit_solution(5922477646984113116)
XLA Ops:
  0.6 0.0 copy-start.3
  0.6 2.8 %copy-done.3 = f32[3,32,128,128]{3,2,1,0:T(8,128)S(1)} copy-done((f32[3,32,128,128]{3,2,1,0:T(8,128)S(1)}, f32[3,32,128,128]{3,2,1,0:T(8,128)}, u32[]{:S(2)}) %copy-start.3) | copy-done | bytes 6291480
  3.4 0.1 theta_edges.1
  3.5 3.0 %collective-permute-start = (f32[3,2,128,128]{3,2,1,0:T(8,128)S(1)}, f32[3,2,128,128]{3,2,1,0:T(8,128)S(1)}, u32[]{:S(2)}, u32[]{:S(2)}) collective-permute-start(f32[3,2,128,128]{3,2,1,0:T(8,128)S(1)} %get-tuple-element.15), channel_id=1, source_target_pairs={{28,0},{29,1},{30,2},{31,3},{0,4},{1,5},{2,6},{3,7},{4,8},{5,9},{6... | collective-permute-start | bytes 1179656 | tf_op jit(solution)/shard_map/ppermute | solution.py:376
  6.5 0.0 copy-start.6
  6.5 3.1 %collective-permute-start.1 = (f32[3,2,128,128]{3,2,1,0:T(8,128)S(1)}, f32[3,2,128,128]{3,2,1,0:T(8,128)S(1)}, u32[]{:S(2)}, u32[]{:S(2)}) collective-permute-start(f32[3,2,128,128]{3,2,1,0:T(8,128)S(1)} %get-tuple-element.16._), channel_id=1, source_target_pairs={{4,0},{5,1},{6,2},{7,3},{8,4},{9,5},{10,6},{11,7},{12,8},{13,9},{1... | collective-permute-start | bytes 1179656 | tf_op jit(solution)/shard_map/ppermute | solution.py:376
  9.6 3.1 %first_pass.1 = (f32[3,36,144,128]{3,2,1,0:T(8,128)S(1)}, f32[3,32,2,128]{3,2,1,0:T(2,128)S(1)}, f32[3,32,2,128]{3,2,1,0:T(2,128)S(1)}, f32[128,128]{1,0:T(8,128)S(1)}, f32[8,128]{1,0:T(8,128)S(1)}) custom-call(f32[3,32,128,128]{3,2,1,0:T(8,128)S(1)} %copy-done.3, f32[3,2,128,128]{3,2,1,0:T(8,128)S(1)} %get-tuple-element.16._), custom_call_target="tpu_custom_call" | custom-call | tf_op jit(solution)/shard_map/first_pass/pallas_call | solution.py:420
  12.8 0.1 collective-permute-start.2
  12.8 1.7 %collective-permute-start.3 = (f32[3,32,2,128]{3,2,1,0:T(2,128)S(1)}, f32[3,32,2,128]{3,2,1,0:T(2,128)S(1)}, u32[]{:S(2)}, u32[]{:S(2)}) collective-permute-start(f32[3,32,2,128]{3,2,1,0:T(2,128)S(1)} %get-tuple-element.18), channel_id=1, source_target_pairs={{1,0},{2,1},{3,2},{0,3},{5,4},{6,5},{7,6},{4,7},{9,8},{10,9},{11,1... | collective-permute-start | bytes 294920 | tf_op jit(solution)/shard_map/ppermute | solution.py:376
  14.6 2.3 %collective-permute-done.2.low_ref = f32[3,32,2,128]{3,2,1,0:T(2,128)S(1)} collective-permute-done((f32[3,32,2,128]{3,2,1,0:T(2,128)S(1)}, f32[3,32,2,128]{3,2,1,0:T(2,128)S(1)}, u32[]{:S(2)}, u32[]{:S(2)}) %collective-permute-start.2) | collective-permute-done | bytes 98336 | tf_op jit(solution)/shard_map/ppermute | solution.py:376
  16.9 0.2 collective-permute-done.3.high_ref
  17.0 0.2 fold.1
  17.2 0.0 copy-start
  17.3 1.9 %collective-permute-start.4 = (f32[8,128]{1,0:T(8,128)S(1)}, f32[8,128]{1,0:T(8,128)S(1)}, u32[]{:S(2)}, u32[]{:S(2)}) collective-permute-start(f32[8,128]{1,0:T(8,128)S(1)} %get-tuple-element.21._.pay_ref), channel_id=1, source_target_pairs={{3,0},{0,1},{1,2},{2,3},{7,4},{4,5},{5,6},{6,7},{11,8},{8,9},{9,10... | collective-permute-start | bytes 12296 | tf_op jit(solution)/shard_map/ppermute | solution.py:376
  19.1 0.0 copy-done.6
  19.1 3.4 %interior_1.1.refs_5_.refs_1_ = f32[3,7,128,128]{3,2,1,0:T(8,128)S(1)} custom-call(f32[3,36,144,128]{3,2,1,0:T(8,128)S(1)} %get-tuple-element.23.vel_ref.refs_3_, f32[15,8,128]{2,1,0:T(8,128)S(1)} %copy-done.6, f32[8,128]{1,0:T(8,128)S(1)} %get-tuple-element.21._.pay_ref), custom_call_target="tpu_custom_call" | custom-call | flops 1572864 | bytes 1572864 | tf_op jit(solution)/shard_map/interior_1/pallas_call | solution.py:451
  22.5 3.4 %interior_0.1.refs_4_.refs_0_ = f32[3,7,128,128]{3,2,1,0:T(8,128)S(1)} custom-call(f32[3,36,144,128]{3,2,1,0:T(8,128)S(1)} %get-tuple-element.23.vel_ref.refs_3_, f32[15,8,128]{2,1,0:T(8,128)S(1)} %copy-done.6, f32[8,128]{1,0:T(8,128)S(1)} %get-tuple-element.21._.pay_ref), custom_call_target="tpu_custom_call" | custom-call | flops 1572864 | bytes 1572864 | tf_op jit(solution)/shard_map/interior_0/pallas_call | solution.py:451
  25.9 0.0 copy-done
  25.9 0.0 collective-permute-done.4.refs_0_
  25.9 0.0 collective-permute-done.refs_2_.below_ref
  26.0 0.0 collective-permute-done.1.refs_3_.above_ref
  26.0 0.6 %late.1 = (f32[8,8,128]{2,1,0:T(8,128)S(1)}, f32[128,128]{1,0:T(8,128)}) custom-call(f32[8,128]{1,0:T(8,128)S(1)} %get-tuple-element.21._.pay_ref, f32[8,128]{1,0:T(8,128)S(1)} %collective-permute-done.4.refs_0_, f32[128,128]{1,0:T(8,128)S(1)} %get-tuple-element.22.refs_1_, f32[3,2,128,128]{3,2,1,0:T(8,128)S(1)} %collective-permute-done.refs_2_.below_ref, ...), custom_call_target="tpu_custom_call" | custom-call | tf_op jit(solution)/shard_map/late/pallas_call | solution.py:463
  26.6 0.0 copy-start.9
  26.6 1.8 %collective-permute-start.5 = (f32[128,128]{1,0:T(8,128)}, f32[128,128]{1,0:T(8,128)}, u32[]{:S(2)}, u32[]{:S(2)}) collective-permute-start(f32[128,128]{1,0:T(8,128)} %get-tuple-element.25), channel_id=1, source_target_pairs={{16,0},{17,1},{18,2},{19,3},{20,4},{21,5},{22,6},{23,7},{24,8},{25... | collective-permute-start | bytes 196616 | tf_op jit(solution)/shard_map/ppermute | solution.py:376
  28.4 0.0 copy-done.9
  28.4 4.0 %all-to-all-start = ((f32[8,8,128]{2,1,0:T(8,128)}), f32[8,8,128]{2,1,0:T(8,128)}, u32[]{:S(2)}, u32[]{:S(2)}) async-start(f32[8,8,128]{2,1,0:T(8,128)} %copy-done.9), calls=%async_computation | async-start | bytes 65536 | tf_op jit(solution)/shard_map/all_to_all | solution.py:472
  32.3 0.0 copy-start.1
  32.3 3.3 %copy-done.1 = f32[3,36,144,128]{3,2,1,0:T(8,128)S(1)} copy-done((f32[3,36,144,128]{3,2,1,0:T(8,128)S(1)}, f32[3,36,144,128]{3,2,1,0:T(8,128)}, u32[]{:S(2)}) %copy-start.1) | copy-done | bytes 7962648
  35.6 0.0 copy-start.7
  35.6 0.8 %copy-done.7 = f32[15,8,128]{2,1,0:T(8,128)S(1)} copy-done((f32[15,8,128]{2,1,0:T(8,128)S(1)}, f32[15,8,128]{2,1,0:T(8,128)}, u32[]{:S(2)}) %copy-start.7) | copy-done | bytes 61464
  36.4 0.0 copy-start.10
  36.4 0.8 %copy-done.10 = f32[8,8,128]{2,1,0:T(8,128)S(1)} copy-done((f32[8,8,128]{2,1,0:T(8,128)S(1)}, f32[8,8,128]{2,1,0:T(8,128)}, u32[]{:S(2)}) %copy-start.10) | copy-done | bytes 32792
  37.2 3.4 %interior_2.1.refs_2_ = f32[3,7,128,128]{3,2,1,0:T(8,128)S(1)} custom-call(f32[3,36,144,128]{3,2,1,0:T(8,128)S(1)} %copy-done.1, f32[15,8,128]{2,1,0:T(8,128)S(1)} %copy-done.7, f32[8,8,128]{2,1,0:T(8,128)S(1)} %copy-done.10), custom_call_target="tpu_custom_call" | custom-call | flops 1572864 | bytes 1572864 | tf_op jit(solution)/shard_map/interior_2/pallas_call | solution.py:451
  40.6 0.0 copy-start.4
  40.6 1.1 %copy-done.4 = f32[3,7,128,128]{3,2,1,0:T(8,128)} copy-done((f32[3,7,128,128]{3,2,1,0:T(8,128)}, f32[3,7,128,128]{3,2,1,0:T(8,128)S(1)}, u32[]{:S(2)}) %copy-start.4) | copy-done | bytes 1376280
  41.6 0.0 all-to-all-done.tiles_ref
  41.6 0.0 collective-permute-done.5.inner_ref
  41.6 0.0 copy-start.2
  41.6 3.3 %copy-done.2 = f32[3,36,144,128]{3,2,1,0:T(8,128)S(1)} copy-done((f32[3,36,144,128]{3,2,1,0:T(8,128)S(1)}, f32[3,36,144,128]{3,2,1,0:T(8,128)}, u32[]{:S(2)}) %copy-start.2) | copy-done | bytes 7962648
  44.9 0.0 copy-start.5
  44.9 1.3 %copy-done.5 = f32[3,7,128,128]{3,2,1,0:T(8,128)S(1)} copy-done((f32[3,7,128,128]{3,2,1,0:T(8,128)S(1)}, f32[3,7,128,128]{3,2,1,0:T(8,128)}, u32[]{:S(2)}) %copy-start.5) | copy-done | bytes 1376280
  46.2 0.0 copy-start.8
  46.2 0.8 %copy-done.8 = f32[15,8,128]{2,1,0:T(8,128)S(1)} copy-done((f32[15,8,128]{2,1,0:T(8,128)S(1)}, f32[15,8,128]{2,1,0:T(8,128)}, u32[]{:S(2)}) %copy-start.8) | copy-done | bytes 61464
  47.1 9.5 %finish.1 = (f32[3,32,128,128]{3,2,1,0:T(8,128)}, f32[1]{0:T(128)}, f32[3,36,144,128]{3,2,1,0:T(8,128)S(1)}) custom-call(f32[3,2,128,128]{3,2,1,0:T(8,128)S(1)} %collective-permute-done.refs_2_.below_ref, f32[3,2,128,128]{3,2,1,0:T(8,128)S(1)} %collective-permute-done.1.refs_3_.above_ref, ...), custom_call_target="tpu_custom_call", output_to_operand_aliasing={{2}: (8, {})} | custom-call | tf_op jit(solution)/shard_map/finish/pallas_call | solution.py:474
Async XLA Ops:
  0.6 2.8 %copy-start.3 = (f32[3,32,128,128]{3,2,1,0:T(8,128)S(1)}, f32[3,32,128,128]{3,2,1,0:T(8,128)}, u32[]{:S(2)}) copy-start(f32[3,32,128,128]{3,2,1,0:T(8,128)} %v_ref.3) | copy-start | bytes 18874372
  3.5 22.5 %collective-permute-start = (f32[3,2,128,128]{3,2,1,0:T(8,128)S(1)}, f32[3,2,128,128]{3,2,1,0:T(8,128)S(1)}, u32[]{:S(2)}, u32[]{:S(2)}) collective-permute-start(f32[3,2,128,128]{3,2,1,0:T(8,128)S(1)} %get-tuple-element.15), channel_id=1, source_target_pairs={{28,0},{29,1},{30,2},{31,3},{0,4},{1,5},{2,6},{3,7},{4,8},{5,9},{6... | collective-permute-start | bytes 1179656 | tf_op jit(solution)/shard_map/ppermute | solution.py:376
  6.5 12.7 %copy-start.6 = (f32[15,8,128]{2,1,0:T(8,128)S(1)}, f32[15,8,128]{2,1,0:T(8,128)}, u32[]{:S(2)}) copy-start(f32[15,8,128]{2,1,0:T(8,128)} %constant.2.clone.coef_ref) | copy-start | bytes 184324
  6.5 19.5 %collective-permute-start.1 = (f32[3,2,128,128]{3,2,1,0:T(8,128)S(1)}, f32[3,2,128,128]{3,2,1,0:T(8,128)S(1)}, u32[]{:S(2)}, u32[]{:S(2)}) collective-permute-start(f32[3,2,128,128]{3,2,1,0:T(8,128)S(1)} %get-tuple-element.16._), channel_id=1, source_target_pairs={{4,0},{5,1},{6,2},{7,3},{8,4},{9,5},{10,6},{11,7},{12,8},{13,9},{1... | collective-permute-start | bytes 1179656 | tf_op jit(solution)/shard_map/ppermute | solution.py:376
  12.8 4.1 %collective-permute-start.2 = (f32[3,32,2,128]{3,2,1,0:T(2,128)S(1)}, f32[3,32,2,128]{3,2,1,0:T(2,128)S(1)}, u32[]{:S(2)}, u32[]{:S(2)}) collective-permute-start(f32[3,32,2,128]{3,2,1,0:T(2,128)S(1)} %get-tuple-element.17), channel_id=1, source_target_pairs={{3,0},{0,1},{1,2},{2,3},{7,4},{4,5},{5,6},{6,7},{11,8},{8,9},{9,10... | collective-permute-start | bytes 294920 | tf_op jit(solution)/shard_map/ppermute | solution.py:376
  12.8 4.2 %collective-permute-start.3 = (f32[3,32,2,128]{3,2,1,0:T(2,128)S(1)}, f32[3,32,2,128]{3,2,1,0:T(2,128)S(1)}, u32[]{:S(2)}, u32[]{:S(2)}) collective-permute-start(f32[3,32,2,128]{3,2,1,0:T(2,128)S(1)} %get-tuple-element.18), channel_id=1, source_target_pairs={{1,0},{2,1},{3,2},{0,3},{5,4},{6,5},{7,6},{4,7},{9,8},{10,9},{11,1... | collective-permute-start | bytes 294920 | tf_op jit(solution)/shard_map/ppermute | solution.py:376
  17.2 8.7 %copy-start = (f32[3,36,144,128]{3,2,1,0:T(8,128)}, f32[3,36,144,128]{3,2,1,0:T(8,128)S(1)}, u32[]{:S(2)}) copy-start(f32[3,36,144,128]{3,2,1,0:T(8,128)S(1)} %get-tuple-element.23.vel_ref.refs_3_) | copy-start | bytes 23887876
  17.3 8.7 %collective-permute-start.4 = (f32[8,128]{1,0:T(8,128)S(1)}, f32[8,128]{1,0:T(8,128)S(1)}, u32[]{:S(2)}, u32[]{:S(2)}) collective-permute-start(f32[8,128]{1,0:T(8,128)S(1)} %get-tuple-element.21._.pay_ref), channel_id=1, source_target_pairs={{3,0},{0,1},{1,2},{2,3},{7,4},{4,5},{5,6},{6,7},{11,8},{8,9},{9,10... | collective-permute-start | bytes 12296 | tf_op jit(solution)/shard_map/ppermute | solution.py:376
  26.6 1.8 %copy-start.9 = (f32[8,8,128]{2,1,0:T(8,128)}, f32[8,8,128]{2,1,0:T(8,128)S(1)}, u32[]{:S(2)}) copy-start(f32[8,8,128]{2,1,0:T(8,128)S(1)} %get-tuple-element.24._) | copy-start | bytes 98308
  26.6 15.0 %collective-permute-start.5 = (f32[128,128]{1,0:T(8,128)}, f32[128,128]{1,0:T(8,128)}, u32[]{:S(2)}, u32[]{:S(2)}) collective-permute-start(f32[128,128]{1,0:T(8,128)} %get-tuple-element.25), channel_id=1, source_target_pairs={{16,0},{17,1},{18,2},{19,3},{20,4},{21,5},{22,6},{23,7},{24,8},{25... | collective-permute-start | bytes 196616 | tf_op jit(solution)/shard_map/ppermute | solution.py:376
  28.4 13.3 %all-to-all-start = ((f32[8,8,128]{2,1,0:T(8,128)}), f32[8,8,128]{2,1,0:T(8,128)}, u32[]{:S(2)}, u32[]{:S(2)}) async-start(f32[8,8,128]{2,1,0:T(8,128)} %copy-done.9), calls=%async_computation | async-start | bytes 65536 | tf_op jit(solution)/shard_map/all_to_all | solution.py:472
  32.3 3.3 %copy-start.1 = (f32[3,36,144,128]{3,2,1,0:T(8,128)S(1)}, f32[3,36,144,128]{3,2,1,0:T(8,128)}, u32[]{:S(2)}) copy-start(f32[3,36,144,128]{3,2,1,0:T(8,128)} %copy-done) | copy-start | bytes 23887876
  35.6 0.8 %copy-start.7 = (f32[15,8,128]{2,1,0:T(8,128)S(1)}, f32[15,8,128]{2,1,0:T(8,128)}, u32[]{:S(2)}) copy-start(f32[15,8,128]{2,1,0:T(8,128)} %constant.2.clone.coef_ref) | copy-start | bytes 184324
  36.4 0.8 %copy-start.10 = (f32[8,8,128]{2,1,0:T(8,128)S(1)}, f32[8,8,128]{2,1,0:T(8,128)}, u32[]{:S(2)}) copy-start(f32[8,8,128]{2,1,0:T(8,128)} %copy-done.9) | copy-start | bytes 98308
  40.6 1.1 %copy-start.4 = (f32[3,7,128,128]{3,2,1,0:T(8,128)}, f32[3,7,128,128]{3,2,1,0:T(8,128)S(1)}, u32[]{:S(2)}) copy-start(f32[3,7,128,128]{3,2,1,0:T(8,128)S(1)} %interior_2.1.refs_2_) | copy-start | bytes 4128772
  41.6 3.3 %copy-start.2 = (f32[3,36,144,128]{3,2,1,0:T(8,128)S(1)}, f32[3,36,144,128]{3,2,1,0:T(8,128)}, u32[]{:S(2)}) copy-start(f32[3,36,144,128]{3,2,1,0:T(8,128)} %copy-done) | copy-start | bytes 23887876
  44.9 1.3 %copy-start.5 = (f32[3,7,128,128]{3,2,1,0:T(8,128)S(1)}, f32[3,7,128,128]{3,2,1,0:T(8,128)}, u32[]{:S(2)}) copy-start(f32[3,7,128,128]{3,2,1,0:T(8,128)} %copy-done.4) | copy-start | bytes 4128772
  46.2 0.8 %copy-start.8 = (f32[15,8,128]{2,1,0:T(8,128)S(1)}, f32[15,8,128]{2,1,0:T(8,128)}, u32[]{:S(2)}) copy-start(f32[15,8,128]{2,1,0:T(8,128)} %constant.2.clone.coef_ref) | copy-start | bytes 184324

commit v6 on v5

v6 whole, which is shorter than its diff:
```python
import functools
import math

import jax
import jax.numpy as jnp
import numpy as np
from jax import lax
from jax.experimental import pallas as pl
from jax.experimental.pallas import tpu as pltpu
from jax.sharding import PartitionSpec as P

AXIAL_STEP = 0.01
VISCOSITY = 0.001
CFL_TARGET = 1.2
GAMMA = 8.0 / 15.0

PAD = 8
HALO = 2
BLOCK = 4
GROUP = 4
UNROLL = 4

(
    WALL,
    RADIAL_C,
    THETA_C,
    CROSS_Z,
    SECOND_C,
    CENTRE_Z,
    CENTRE_T,
    CURVE_T,
    TURN_T,
    RADIAL_F,
    THETA_F,
    SECOND_F,
    CENTRE_R,
    CURVE_R,
    TURN_R,
    COUNT,
) = range(16)


def coefficients(radial, theta_step):
    dr = 1.0 / radial
    index = np.arange(radial, dtype=np.float64)
    centre = (index + 0.5) * dr
    face = (index + 1.0) * dr
    wall = np.where(index < radial - 1.5, 1.0, 0.0)
    h = theta_step
    nu = VISCOSITY
    rows = np.zeros((COUNT, radial))
    rows[WALL] = wall
    common = -2.0 * nu / dr**2 - 30.0 * nu / (12.0 * AXIAL_STEP**2)
    rows[RADIAL_C] = nu / (2.0 * dr * centre)
    rows[THETA_C] = -1.0 / (12.0 * h * centre)
    rows[CROSS_Z] = 0.25 * rows[THETA_C]
    rows[SECOND_C] = nu / (12.0 * h * h * centre**2)
    rows[CENTRE_Z] = common - 30.0 * rows[SECOND_C]
    rows[CENTRE_T] = rows[CENTRE_Z] - nu / centre**2
    rows[CURVE_T] = 0.25 / centre
    rows[TURN_T] = nu / (h * centre**2)
    rows[RADIAL_F] = nu / (2.0 * dr * face)
    rows[THETA_F] = -0.25 / (12.0 * h * face)
    rows[SECOND_F] = nu / (12.0 * h * h * face**2)
    rows[CENTRE_R] = common - 30.0 * rows[SECOND_F] - nu / face**2
    rows[CURVE_R] = 1.0 / (16.0 * face)
    rows[TURN_R] = -nu / (h * face**2)
    return np.broadcast_to(rows[:, None, :], (COUNT, 8, radial)).astype(np.float32)


class Cells:
    def __init__(self, vel, j, k):
        self.vel, self.j, self.k, self.known = vel, j, k, {}

    def once(self, key, make):
        if key not in self.known:
            self.known[key] = make()
        return self.known[key]

    def at(self, n, dj, dk=0):
        rows = pl.ds(self.k + PAD + dk, 8)
        return self.once((n, dj, dk), lambda: self.vel[n, self.j + HALO + dj, rows, :])

    def turned(self, by, n, dj, dk=0):
        return self.once(
            (by, n, dj, dk), lambda: pltpu.roll(self.at(n, dj, dk), by % self.vel.shape[3], 1)
        )

    def pair(self, by, n, dj, dk=0):
        return self.once(
            ("pair", n, dj, dk), lambda: self.at(n, dj, dk) + self.turned(by, n, dj, dk)
        )

    def beside(self, dj, dk):
        n = 1 if dk >= 0 else 2
        other = (1, dj - 1, dk) if n == 1 else (2, dj, dk)
        here = (1, dj, dk) if n == 1 else (2, dj, dk + 1)
        return self.once(("sum", n, dj, dk), lambda: self.at(*other) + self.at(*here))


def terms(cells, ghost, coef, q, dr):
    at, turned, pair = cells.at, cells.turned, cells.pair
    a, b, c = (at(n, q) for n in range(3))
    lane = lax.broadcasted_iota(jnp.int32, a.shape, 1)
    first_lane = lane == 0
    last_lane = lane == a.shape[1] - 1

    nu = VISCOSITY
    lap = nu / dr**2
    adv_z = -1.0 / (12.0 * AXIAL_STEP)
    vis_z = nu / (12.0 * AXIAL_STEP**2)

    def differences(p1, m1, p2, m2):
        return 8.0 * (p1 - m1) - (p2 - m2), 16.0 * (p1 + m1) - (p2 + m2)

    def pieces(n):
        over = differences(*(at(n, q + d) for d in (1, -1, 2, -2)))
        along = differences(*(at(n, q, d) for d in (1, -1, 2, -2)))
        return over, along

    def below(n):
        x = turned(1, n, q)
        if ghost is not None:
            return jnp.where(first_lane, ghost(n), x)
        return x if n == 0 else jnp.where(first_lane, 0.0, x)

    def above(n):
        return jnp.where(last_lane, -at(n, q), turned(-1, n, q))

    pair_a, pair_side, pair_next = pair(1, 0, q), pair(1, 0, q + 1), pair(1, 0, q, 1)
    pair_b, pair_back = pair(-1, 1, q), pair(-1, 1, q - 1)

    theta, axial = pieces(2)
    up, low = above(2), below(2)
    u_r = pair_a + pair_next
    u_t = cells.beside(q, 0) + cells.beside(q, 1)
    h_z = (up - low) * (coef[RADIAL_C] - u_r * (0.125 / dr)) + (up + low) * lap
    h_z = h_z + theta[0] * (u_t * coef[CROSS_Z])
    h_z = h_z + (theta[1] * coef[SECOND_C] + axial[1] * vis_z)
    h_z = h_z + c * (coef[CENTRE_Z] + axial[0] * adv_z)

    theta, axial = pieces(1)
    up, low = above(1), below(1)
    u_r = pair_a + pair_side
    u_z = cells.beside(q, -1) + cells.beside(q + 1, -1)
    h_t = (up - low) * (coef[RADIAL_C] - u_r * (0.125 / dr)) + (up + low) * lap
    h_t = h_t + b * (coef[CENTRE_T] + theta[0] * coef[THETA_C] - u_r * coef[CURVE_T])
    h_t = h_t + (theta[1] * coef[SECOND_C] + axial[1] * vis_z)
    h_t = h_t + axial[0] * (u_z * (0.25 * adv_z))
    h_t = h_t + (pair_side - pair_a) * coef[TURN_T]

    theta, axial = pieces(0)
    up, low = turned(-1, 0, q), below(0)
    u_t = pair_b + pair_back
    u_z = pair(-1, 2, q) + pair(-1, 2, q, -1)
    h_r = (up - low) * (coef[RADIAL_F] - a * (0.5 / dr)) + (up + low) * lap
    h_r = h_r + u_t * (u_t * coef[CURVE_R] + theta[0] * coef[THETA_F])
    h_r = h_r + (theta[1] * coef[SECOND_F] + axial[1] * vis_z)
    h_r = h_r + (axial[0] * (u_z * (0.25 * adv_z)) + a * coef[CENTRE_R])
    h_r = h_r + (pair_b - pair_back) * coef[TURN_R]
    return h_r, h_t, h_z


def lane_zero_terms(vel, ghost, coef, j, k, dr):
    def at(dj, dk):
        return vel[0, j + HALO + dj, pl.ds(k + PAD + dk, 8), :]

    lap = VISCOSITY / dr**2
    a = at(0, 0)
    first_lane = lax.broadcasted_iota(jnp.int32, a.shape, 1) == 0
    add_r = ghost(0) * (lap - coef[RADIAL_F] + a * (0.5 / dr))
    add_t = ghost(1) * (lap - coef[RADIAL_C] + (a + at(1, 0)) * (0.125 / dr))
    add_z = ghost(2) * (lap - coef[RADIAL_C] + (a + at(0, 1)) * (0.125 / dr))
    return tuple(jnp.where(first_lane, x, 0.0) for x in (add_r, add_t, add_z))


def wall_mask(rows, radial):
    lane = lax.broadcasted_iota(jnp.int32, (rows, radial), 1)
    return jnp.where(lane == radial - 1, 0.0, 1.0).astype(jnp.float32)


def first_pass(theta_step, v_ref, vel_ref, low_ref, high_ref, pay_ref, sems):
    _, planes, axial, radial = v_ref.shape
    lane = lax.broadcasted_iota(jnp.int32, (8, radial), 1)
    wall = wall_mask(8, radial)
    rate_t = (radial / theta_step) / (lane.astype(jnp.float32) + 0.5)

    def fetch(g):
        part = pl.ds(g * GROUP, GROUP)
        target = vel_ref.at[:, pl.ds(g * GROUP + HALO, GROUP), pl.ds(PAD, axial)]
        return pltpu.make_async_copy(v_ref.at[:, part], target, sems.at[g])

    for g in range(planes // GROUP):
        fetch(g).start()

    def group(g, largest):
        fetch(g).wait()

        def rows(i, largest):
            k = pl.ds(pl.multiple_of(i * 8, 8) + PAD, 8)
            largest = list(largest)
            for q in range(GROUP):
                j = g * GROUP + HALO + q
                a, b, c = (vel_ref[n, j, k, :] for n in range(3))
                a = a * wall
                vel_ref[0, j, k, :] = a
                rate = jnp.abs(a) * float(radial) + jnp.abs(b) * rate_t
                rate = rate + jnp.abs(c) * (1.0 / AXIAL_STEP)
                largest[q % 4] = jnp.maximum(largest[q % 4], rate)
            return tuple(largest)

        largest = lax.fori_loop(0, axial // 8, rows, largest, unroll=4)
        for q in range(GROUP):
            for n in range(3):
                j = g * GROUP + q
                low_ref[n, j] = vel_ref[n, j + HALO, PAD : PAD + 2, :]
                high_ref[n, j] = vel_ref[n, j + HALO, PAD + axial - 2 : PAD + axial, :]
        return largest

    zero = jnp.zeros((8, radial), jnp.float32)
    m = lax.fori_loop(0, planes // GROUP, group, (zero,) * 4)
    largest = jnp.maximum(jnp.maximum(m[0], m[1]), jnp.maximum(m[2], m[3]))
    top = jnp.max(largest, axis=(0, 1), keepdims=True)
    pay_ref[...] = jnp.broadcast_to(top, pay_ref.shape)
    last = lax.broadcasted_iota(jnp.int32, (2, radial), 1) == radial - 1
    for ref in (low_ref, high_ref):
        ref[0, 0] = jnp.where(last, top, ref[0, 0])


def pack(vel_ref, inner_ref):
    planes, (axial, radial) = vel_ref.shape[1] - 2 * HALO, inner_ref.shape
    lane = lax.broadcasted_iota(jnp.int32, (8, radial), 1)
    sign = jnp.where(lane < 2 * planes, -1.0, 1.0).astype(jnp.float32)

    def rows(i, carry):
        k = pl.multiple_of(i * 8, 8)
        inner = [jnp.zeros((8, radial), jnp.float32)] * 3
        for j in range(planes):
            for n in range(3):
                place = n * planes + j
                x = vel_ref[n, j + HALO, pl.ds(k + PAD, 8), :]
                x = pltpu.roll(x, place, 1)
                inner[n] = jnp.where(lane == place, x, inner[n])
        inner_ref[pl.ds(k, 8), :] = (inner[0] + inner[1] + inner[2]) * sign
        return carry

    lax.fori_loop(0, axial // 8, rows, 0)


def fold(low_ref, high_ref, pay_ref, vel_in, _, out_ref, vel_ref):
    del vel_in
    planes, radial = low_ref.shape[1], low_ref.shape[3]
    axial = vel_ref.shape[2] - 2 * PAD
    lane = lax.broadcasted_iota(jnp.int32, (1, radial), 1)
    top = jnp.maximum(low_ref[0, 0, 0:1, :], high_ref[0, 0, 0:1, :])
    top = jnp.max(jnp.where(lane == radial - 1, top, 0.0), axis=(0, 1), keepdims=True)
    out_ref[...] = jnp.maximum(pay_ref[...], top)
    out_ref[1:2, :] = high_ref[1, planes - 1, 0:1, :]
    out_ref[2:3, :] = low_ref[2, 0, 1:2, :]
    wall = wall_mask(2, radial)

    def plane(j, carry):
        for n in range(3):
            mask = wall if n == 0 else 1.0
            vel_ref[n, j + HALO, PAD - 2 : PAD, :] = low_ref[n, j] * mask
            vel_ref[n, j + HALO, PAD + axial : PAD + axial + 2, :] = high_ref[n, j] * mask
        return carry

    lax.fori_loop(0, planes, plane, 0, unroll=4)


def largest_along_ax(pay_ref, *refs):
    (inner_in, inner_ref), fars = (refs[-6], refs[-1]), refs[:-6]
    top = pay_ref[0:1, :]
    for far in fars:
        top = jnp.maximum(top, far[0:1, :])
    inner_ref[...] = inner_in[...]
    lane = lax.broadcasted_iota(jnp.int32, top.shape, 1)
    inner_ref[0:1, :] = jnp.where(lane == top.shape[1] - 1, top, inner_ref[0:1, :])


def largest_with_partner(pay_ref, mine_ref, inner_ref, _, out_ref):
    top = jnp.maximum(mine_ref[0:1, :], inner_ref[0:1, :])
    lane = lax.broadcasted_iota(jnp.int32, top.shape, 1)
    top = jnp.max(jnp.where(lane == top.shape[1] - 1, top, 0.0), axis=(0, 1), keepdims=True)
    row = lax.broadcasted_iota(jnp.int32, out_ref.shape, 0)
    out_ref[...] = jnp.where(row == 0, top, pay_ref[...])


def ghosts(inner, planes, j):
    radial = inner.shape[1]

    def ghost(component):
        turn = lax.rem(2 * radial - component * planes - j, radial)
        return pltpu.roll(inner, turn, 1)

    return ghost


def sweep(vel_ref, inner_ref, coef_ref, first, last, write):
    planes = vel_ref.shape[1] - 2 * HALO
    axial, radial = vel_ref.shape[2] - 2 * PAD, vel_ref.shape[3]
    size = math.gcd(BLOCK, last - first)

    def block(m, carry):
        j = first + m * size

        def rows(i, carry):
            k = pl.multiple_of(i * 8, 8)
            coef = [coef_ref[n] for n in range(COUNT)]
            cells = Cells(vel_ref, j, k)
            inner = None if inner_ref is None else inner_ref[pl.ds(k, 8), :]
            found = []
            for q in range(size):
                ghost = None if inner is None else ghosts(inner, planes, j + q)
                found.append(terms(cells, ghost, coef, q, 1.0 / radial))
            for q, values in enumerate(found):
                for n, value in enumerate(values):
                    write(n, j + q, pl.ds(k, 8), value)
            return carry

        return lax.fori_loop(0, axial // 8, rows, carry)

    lax.fori_loop(0, (last - first) // size, block, 0)


def interior(first, last, vel_ref, coef_ref, _, out_ref):
    def write(n, j, k, value):
        out_ref[n, j - first, k, :] = value

    sweep(vel_ref, None, coef_ref, first, last, write)


def finish(
    spans,
    below_ref,
    above_ref,
    up_ref,
    down_ref,
    pay_ref,
    far_refs,
    inner_ref,
    coef_ref,
    parts,
    out_ref,
    step_ref,
    vel_ref,
    res,
    sems,
):
    axial, radial = inner_ref.shape
    planes = res.shape[1]
    top = pay_ref[0:1, :]
    for ref in (up_ref, down_ref, *far_refs):
        top = jnp.maximum(top, ref[0:1, :])
    time_step = CFL_TARGET / (jnp.max(top) + 1e-06)
    step_ref[0] = time_step
    scale = GAMMA * time_step

    def store(j):
        return pltpu.make_async_copy(res.at[:, j], out_ref.at[:, j], sems.at[j])

    def send(first, last):
        def start(j, carry):
            store(j).start()
            return carry

        lax.fori_loop(first, last, start, 0)

    def write(n, j, k, value):
        factor = scale * coef_ref[WALL] if n == 0 else scale
        res[n, j, k, :] = value * factor

    for part, (first, last) in zip(parts, spans):

        def plane(j, carry, part=part, first=first):
            def rows(i, carry):
                k = pl.multiple_of(i * 8, 8)
                ghost = ghosts(inner_ref[pl.ds(k, 8), :], planes, j)
                added = lane_zero_terms(vel_ref, ghost, coef_ref, j, k, 1.0 / radial)
                for n, value in enumerate(added):
                    write(n, j, pl.ds(k, 8), part[n, j - first, pl.ds(k, 8), :] + value)
                return carry

            lax.fori_loop(0, axial // 8, rows, carry, unroll=UNROLL)
            store(j).start()
            return carry

        lax.fori_loop(first, last, plane, 0)

    sweep(vel_ref, inner_ref, coef_ref, *spans[-1], write)
    send(*spans[-1])

    cells = pl.ds(PAD, axial)
    for q in range(HALO):
        for ref, place in ((below_ref, q), (above_ref, HALO + planes + q)):
            vel_ref[0, place, cells, :] = ref[0, q] * coef_ref[WALL, 0:1, :]
            vel_ref[1, place, cells, :] = ref[1, q]
            vel_ref[2, place, cells, :] = ref[2, q]
    vel_ref[1, HALO - 1, PAD + axial : PAD + axial + 1, :] = up_ref[1:2, :]
    vel_ref[2, HALO + planes, PAD - 1 : PAD, :] = down_ref[2:3, :]
    for first in (0, planes - HALO):
        sweep(vel_ref, inner_ref, coef_ref, first, first + HALO, write)
        send(first, first + HALO)

    def wait(j, carry):
        store(j).wait()
        return carry

    lax.fori_loop(0, planes, wait, 0)


def shifted(block, distance):
    sizes = lax.axis_size("az"), lax.axis_size("ax")
    route = []
    for i in range(sizes[0]):
        for k in range(sizes[1]):
            source = (i - distance[0]) % sizes[0], (k - distance[1]) % sizes[1]
            route.append((source[0] * sizes[1] + source[1], i * sizes[1] + k))
    return lax.ppermute(block, ("az", "ax"), route)


def cuts(planes):
    blocks = (planes - 2 * HALO) // BLOCK
    ends = [blocks * n // 7 for n in (0, 2, 4, 5, 6)] + [blocks]
    return [(HALO + BLOCK * m, HALO + BLOCK * n) for m, n in zip(ends[:-1], ends[1:])]


def doublings(count, known):
    covered = {i % count for i in known}
    plan = []
    while len(covered) < count:
        best = max(range(1, count), key=lambda s: len(covered | {(i + s) % count for i in covered}))
        covered |= {(i + best) % count for i in covered}
        plan.append(best)
    return plan


def per_device(velocity):
    _, planes, axial, radial = velocity.shape
    sizes = lax.axis_size("az"), lax.axis_size("ax")
    theta_step = 2.0 * math.pi / (sizes[0] * planes)
    coef = jnp.asarray(coefficients(radial, theta_step))
    f32 = jnp.float32
    anywhere = pl.BlockSpec(memory_space=pl.ANY)
    vmem = pl.BlockSpec(memory_space=pltpu.VMEM)
    smem = pl.BlockSpec(memory_space=pltpu.SMEM)

    def shape(*sizes):
        return jax.ShapeDtypeStruct(sizes, f32)

    def call(kernel, name, work, scratch=0, **kwargs):
        return pl.pallas_call(
            kernel,
            name=name,
            compiler_params=pltpu.CompilerParams(vmem_limit_bytes=(4 + scratch) * 2**20),
            cost_estimate=pl.CostEstimate(flops=work, bytes_accessed=work, transcendentals=0),
            **kwargs,
        )

    below = shifted(velocity[:, planes - HALO :], (1, 0))
    above = shifted(velocity[:, :HALO], (-1, 0))

    edge = shape(3, planes, 2, radial)
    padded = shape(3, planes + 2 * HALO, axial + 2 * PAD, radial)
    tile = shape(8, radial)
    vel, first, last, pay = call(
        functools.partial(first_pass, theta_step),
        "first_pass",
        0,
        out_shape=(padded, edge, edge, tile),
        in_specs=[anywhere],
        out_specs=(vmem,) * 4,
        scratch_shapes=[pltpu.SemaphoreType.DMA((planes // GROUP,))],
    )(pltpu.with_memory_space_constraint(velocity, pltpu.HBM))
    low = shifted(last, (0, 1))
    high = shifted(first, (0, -1))
    inner = call(
        pack,
        "pack",
        velocity.size,
        out_shape=shape(axial, radial),
        in_specs=[vmem],
        out_specs=vmem,
    )(vel)
    pay, vel = call(
        fold,
        "fold",
        0,
        out_shape=(tile, padded),
        in_specs=[vmem] * 5,
        out_specs=(vmem, vmem),
        input_output_aliases={3: 1},
    )(low, high, pay, vel, inner)
    top, fars = pay, []
    for step in doublings(sizes[1], (0, 1, -1)):
        fars.append(shifted(top, (0, step)))
        top = jnp.maximum(top, fars[-1])

    spans = cuts(planes)
    parts = []

    def inside(n, token):
        first, last = spans[n]
        part = call(
            functools.partial(interior, first, last),
            f"interior_{n}",
            velocity.size,
            out_shape=shape(3, last - first, axial, radial),
            in_specs=[vmem] * 3,
            out_specs=vmem,
        )(vel, coef, token)
        parts.append(part)

    inside(0, pay)
    inside(1, pay)
    mine = call(
        largest_along_ax,
        "largest_along_ax",
        0,
        out_shape=shape(axial, radial),
        in_specs=[vmem] * (6 + len(fars)),
        out_specs=vmem,
    )(pay, *fars, inner, below, above, *parts)
    inner = shifted(mine, (sizes[0] // 2, 0))
    inside(2, mine)
    pay = call(
        largest_with_partner,
        "largest_with_partner",
        0,
        out_shape=tile,
        in_specs=[vmem] * 4,
        out_specs=vmem,
    )(pay, mine, inner, parts[2])
    up = shifted(pay, (1, 0))
    down = shifted(pay, (-1, 0))
    around = [(i, 0) for i in (0, sizes[0] // 2)]
    near = {(i + s) % sizes[0] for i, _ in around for s in (-1, 0, 1)}
    others = []
    while len(near) < sizes[0]:
        step = min(set(range(sizes[0])) - near)
        others.append(shifted(pay, (step, 0)))
        near |= {(i + step) % sizes[0] for i, _ in around}
    inside(3, pay)

    def last_kernel(*refs):
        ins, parts_in, rest = refs[:5], refs[5 : 5 + len(others)], refs[5 + len(others) :]
        inner_ref, coef_ref, *rest = rest
        parts_refs, rest = rest[: len(parts)], rest[len(parts) :]
        _, out_ref, step_ref, vel_ref, res, sems = rest
        finish(
            spans, *ins, parts_in, inner_ref, coef_ref, parts_refs, out_ref, step_ref, vel_ref,
            res, sems,
        )

    count = 7 + len(others) + len(parts)
    increment, time_step, _ = call(
        last_kernel,
        "finish",
        0,
        scratch=8,
        out_shape=(shape(*velocity.shape), shape(1), padded),
        in_specs=[vmem] * (count + 1),
        out_specs=(anywhere, smem, vmem),
        scratch_shapes=[
            pltpu.VMEM(velocity.shape, f32),
            pltpu.SemaphoreType.DMA((planes,)),
        ],
        input_output_aliases={count: 2},
    )(below, above, up, down, pay, *others, inner, coef, *parts, vel)
    return increment, time_step.reshape(())


def solution(mesh):
    return jax.shard_map(
        per_device,
        mesh=mesh,
        in_specs=(P(None, "az", "ax", None),),
        out_specs=(P(None, "az", "ax", None), P()),
        check_vma=False,
    )
```

time: 57.1 us -> 56.7 us (level)
  local copies, waits for them, and re-layouts: 14.1 us -> 1.18 us
  Pallas kernels: 23.6 us -> 32.6 us
  waiting for transfers between devices: 2.46 us -> 7.66 us
  starting transfers between devices: 15.5 us -> 14.4 us
    unnamed x22 -> x2, local copies, waits for them, and re-layouts: 14.1 us -> 0.01 us
    pallas_call x4 -> x5, Pallas kernels: 10.4 us -> 18.6 us  [the longest x1 15.5 us: per_device(): call(last_kernel, 'finish', 0, scratch=8, out_shape=(shape(*velocity.shap...]
    ppermute x6 -> x9, waiting for transfers between devices: 2.46 us -> 7.66 us  [shifted(): return lax.ppermute(block, ('az', 'ax'), route)]
    all_to_all x1 -> x0, starting transfers between devices: 3.95 us -> none  [per_device(): moved = lax.all_to_all(tiles, 'az', 0, 0)]
    ppermute x6 -> x9, starting transfers between devices: 11.6 us -> 14.4 us  [shifted(): return lax.ppermute(block, ('az', 'ax'), route)]
    slice x0 -> x1, local copies, waits for them, and re-layouts: none -> 1.17 us  [per_device(): above = shifted(velocity[:, :HALO], (-1, 0))]
    pallas_call x3 -> x4, Pallas kernels: 10.1 us -> 10.9 us  [inside(): call(functools.partial(interior, first, last), f'interior_{n}', velocity....]
  transfers between devices with their start and end apart: 7 -> 9, of which waited for: 2 -> 2; matrix products, arithmetic and copies ran while one was open for 0% -> 0% of each run, Pallas kernels for 24% -> 30%
where the time goes in v6:
time: 56.7 us; the launch traced here: 56.6 us
  Pallas kernels  32.6 us (57%)
  starting transfers between devices  14.4 us (25%)
  waiting for transfers between devices  7.66 us (14%)
  local copies, waits for them, and re-layouts  1.18 us (2%)
  between operations  0.78 us (1%)
    pallas_call x1, Pallas kernels, per_device(): call(last_kernel, 'finish', 0, scratch=8, out_shape=(shape(*velocity.shap...  15.5 us
    ppermute x9, starting transfers between devices, shifted(): return lax.ppermute(block, ('az', 'ax'), route)  14.4 us
    pallas_call x4, Pallas kernels, inside(): call(functools.partial(interior, first, last), f'interior_{n}', velocity....  10.9 us
    ppermute x9, waiting for transfers between devices, shifted(): return lax.ppermute(block, ('az', 'ax'), route)  7.66 us
    pallas_call x1, Pallas kernels, per_device(): call(functools.partial(first_pass, theta_step), 'first_pass', 0, out_shap...  3.1 us
    pallas_call x1, Pallas kernels, per_device(): call(pack, 'pack', velocity.size, out_shape=shape(axial, radial), in_spec...  2.73 us
    slice x1, local copies, waits for them, and re-layouts, per_device(): above = shifted(velocity[:, :HALO], (-1, 0))  1.17 us
  transfers between devices with their start and end apart: 9, of which 2 were waited for; matrix products, arithmetic and copies ran while one was open for 0% of the time, Pallas kernels for 30%

profile of v6, /device:TPU:0, one launch (start us, length us, event | category | flops | bytes accessed | tf_op | source)
XLA Modules:
  0.0 56.6 jit_solution(17269144825587568815)
XLA Ops:
  0.6 1.2 %fusion = (f32[3,2,128,128]{3,2,1,0:T(8,128)S(1)}, f32[3,2,128,128]{3,2,1,0:T(8,128)S(1)}) fusion(f32[3,32,128,128]{3,2,1,0:T(8,128)} %v_ref.1), kind=kLoop, calls=%fused_computation | loop fusion | bytes 1572864 | tf_op jit(solution)/shard_map/slice | solution.py:462
  1.8 6.1 %collective-permute-start.1 = (f32[3,2,128,128]{3,2,1,0:T(8,128)S(1)}, f32[3,2,128,128]{3,2,1,0:T(8,128)S(1)}, u32[]{:S(2)}, u32[]{:S(2)}) collective-permute-start(f32[3,2,128,128]{3,2,1,0:T(8,128)S(1)} %get-tuple-element.18), channel_id=1, source_target_pairs={{4,0},{5,1},{6,2},{7,3},{8,4},{9,5},{10,6},{11,7},{12,8},{13,9},{1... | collective-permute-start | bytes 1179656 | tf_op jit(solution)/shard_map/ppermute | solution.py:420
  7.9 0.0 collective-permute-start
  7.9 3.1 %first_pass.1 = (f32[3,36,144,128]{3,2,1,0:T(8,128)S(1)}, f32[3,32,2,128]{3,2,1,0:T(2,128)S(1)}, f32[3,32,2,128]{3,2,1,0:T(2,128)S(1)}, f32[8,128]{1,0:T(8,128)S(1)}) custom-call(f32[3,32,128,128]{3,2,1,0:T(8,128)} %v_ref.1), custom_call_target="tpu_custom_call" | custom-call | tf_op jit(solution)/shard_map/first_pass/pallas_call | solution.py:467
  11.0 0.1 collective-permute-start.2
  11.0 1.7 %collective-permute-start.3 = (f32[3,32,2,128]{3,2,1,0:T(2,128)S(1)}, f32[3,32,2,128]{3,2,1,0:T(2,128)S(1)}, u32[]{:S(2)}, u32[]{:S(2)}) collective-permute-start(f32[3,32,2,128]{3,2,1,0:T(2,128)S(1)} %get-tuple-element.11), channel_id=1, source_target_pairs={{1,0},{2,1},{3,2},{0,3},{5,4},{6,5},{7,6},{4,7},{9,8},{10,9},{11,1... | collective-permute-start | bytes 294920 | tf_op jit(solution)/shard_map/ppermute | solution.py:420
  12.8 0.0 copy-start
  12.8 2.7 %pack.1._.refs_1_ = f32[128,128]{1,0:T(8,128)S(1)} custom-call(f32[3,36,144,128]{3,2,1,0:T(8,128)S(1)} %get-tuple-element.13.vel_ref.vel_in), custom_call_target="tpu_custom_call" | custom-call | flops 1572864 | bytes 1572864 | tf_op jit(solution)/shard_map/pack/pallas_call | solution.py:478
  15.5 0.0 collective-permute-done.2.low_ref
  15.5 0.0 collective-permute-done.3.high_ref
  15.5 0.2 fold.1
  15.8 1.5 %collective-permute-start.4 = (f32[8,128]{1,0:T(8,128)S(1)}, f32[8,128]{1,0:T(8,128)S(1)}, u32[]{:S(2)}, u32[]{:S(2)}) collective-permute-start(f32[8,128]{1,0:T(8,128)S(1)} %get-tuple-element.14._.pay_ref), channel_id=1, source_target_pairs={{3,0},{0,1},{1,2},{2,3},{7,4},{4,5},{5,6},{6,7},{11,8},{8,9},{9,10... | collective-permute-start | bytes 12296 | tf_op jit(solution)/shard_map/ppermute | solution.py:420
  17.3 0.0 copy-done
  17.3 3.6 %interior_1.1.refs_5_.refs_9_ = f32[3,8,128,128]{3,2,1,0:T(8,128)S(1)} custom-call(f32[3,36,144,128]{3,2,1,0:T(8,128)S(1)} %get-tuple-element.15.vel_ref.refs_12_, f32[15,8,128]{2,1,0:T(8,128)S(1)} %copy-done, f32[8,128]{1,0:T(8,128)S(1)} %get-tuple-element.14._.pay_ref), custom_call_target="tpu_custom_call" | custom-call | flops 1572864 | bytes 1572864 | tf_op jit(solution)/shard_map/interior_1/pallas_call | solution.py:505
  20.9 3.6 %interior_0.1.refs_4_.refs_8_ = f32[3,8,128,128]{3,2,1,0:T(8,128)S(1)} custom-call(f32[3,36,144,128]{3,2,1,0:T(8,128)S(1)} %get-tuple-element.15.vel_ref.refs_12_, f32[15,8,128]{2,1,0:T(8,128)S(1)} %copy-done, f32[8,128]{1,0:T(8,128)S(1)} %get-tuple-element.14._.pay_ref), custom_call_target="tpu_custom_call" | custom-call | flops 1572864 | bytes 1572864 | tf_op jit(solution)/shard_map/interior_0/pallas_call | solution.py:505
  24.6 0.0 collective-permute-done.4.refs_0_
  24.6 0.0 collective-permute-done.1.refs_3_.refs_1_
  24.6 0.0 collective-permute-done.refs_2_.refs_0_
  24.6 0.7 %collective-permute-start.5 = (f32[128,128]{1,0:T(8,128)S(1)}, f32[128,128]{1,0:T(8,128)S(1)}, u32[]{:S(2)}, u32[]{:S(2)}) collective-permute-start(f32[128,128]{1,0:T(8,128)S(1)} %largest_along_ax.1._.mine_ref), channel_id=1, source_target_pairs={{16,0},{17,1},{18,2},{19,3},{20,4},{21,5},{22,6},{23,7},{24,8},{25... | collective-permute-start | bytes 196616 | tf_op jit(solution)/shard_map/ppermute | solution.py:420
  25.3 1.8 %interior_2.1._.refs_10_ = f32[3,4,128,128]{3,2,1,0:T(8,128)S(1)} custom-call(f32[3,36,144,128]{3,2,1,0:T(8,128)S(1)} %get-tuple-element.15.vel_ref.refs_12_, f32[15,8,128]{2,1,0:T(8,128)S(1)} %copy-done, f32[128,128]{1,0:T(8,128)S(1)} %largest_along_ax.1._.mine_ref), custom_call_target="tpu_custom_call" | custom-call | flops 1572864 | bytes 1572864 | tf_op jit(solution)/shard_map/interior_2/pallas_call | solution.py:505
  27.1 3.2 %collective-permute-done.5.inner_ref.refs_6_ = f32[128,128]{1,0:T(8,128)S(1)} collective-permute-done((f32[128,128]{1,0:T(8,128)S(1)}, f32[128,128]{1,0:T(8,128)S(1)}, u32[]{:S(2)}, u32[]{:S(2)}) %collective-permute-start.5) | collective-permute-done | bytes 65568 | tf_op jit(solution)/shard_map/ppermute | solution.py:420
  30.2 0.1 largest_with_partner.1._.refs_4_
  30.4 0.1 collective-permute-start.8
  30.4 4.4 %collective-permute-start.7 = (f32[8,128]{1,0:T(8,128)S(1)}, f32[8,128]{1,0:T(8,128)S(1)}, u32[]{:S(2)}, u32[]{:S(2)}) collective-permute-start(f32[8,128]{1,0:T(8,128)S(1)} %largest_with_partner.1._.refs_4_), channel_id=1, source_target_pairs={{4,0},{5,1},{6,2},{7,3},{8,4},{9,5},{10,6},{11,7},{12,8},{13,9},{1... | collective-permute-start | bytes 12296 | tf_op jit(solution)/shard_map/ppermute | solution.py:420
  34.8 0.0 collective-permute-start.6
  34.8 1.8 %interior_3.1.refs_11_ = f32[3,4,128,128]{3,2,1,0:T(8,128)S(1)} custom-call(f32[3,36,144,128]{3,2,1,0:T(8,128)S(1)} %get-tuple-element.15.vel_ref.refs_12_, f32[15,8,128]{2,1,0:T(8,128)S(1)} %copy-done, f32[8,128]{1,0:T(8,128)S(1)} %largest_with_partner.1._.refs_4_), custom_call_target="tpu_custom_call" | custom-call | flops 1572864 | bytes 1572864 | tf_op jit(solution)/shard_map/interior_3/pallas_call | solution.py:505
  36.6 0.0 collective-permute-done.8.refs_5_
  36.6 0.0 collective-permute-done.7.refs_3_
  36.6 4.5 %collective-permute-done.6.refs_2_ = f32[8,128]{1,0:T(8,128)S(1)} collective-permute-done((f32[8,128]{1,0:T(8,128)S(1)}, f32[8,128]{1,0:T(8,128)S(1)}, u32[]{:S(2)}, u32[]{:S(2)}) %collective-permute-start.6) | collective-permute-done | bytes 4128 | tf_op jit(solution)/shard_map/ppermute | solution.py:420
  41.1 15.5 %finish.1 = (f32[3,32,128,128]{3,2,1,0:T(8,128)}, f32[1]{0:T(128)}, f32[3,36,144,128]{3,2,1,0:T(8,128)S(1)}) custom-call(f32[3,2,128,128]{3,2,1,0:T(8,128)S(1)} %collective-permute-done.refs_2_.refs_0_, f32[3,2,128,128]{3,2,1,0:T(8,128)S(1)} %collective-permute-done.1.refs_3_.refs_1_, ...), custom_call_target="tpu_custom_call", output_to_operand_aliasing={{2}: (12, {})} | custom-call | tf_op jit(solution)/shard_map/finish/pallas_call | solution.py:557
  (1 shorter events, 0.0 us)
Async XLA Ops:
  1.8 22.8 %collective-permute-start.1 = (f32[3,2,128,128]{3,2,1,0:T(8,128)S(1)}, f32[3,2,128,128]{3,2,1,0:T(8,128)S(1)}, u32[]{:S(2)}, u32[]{:S(2)}) collective-permute-start(f32[3,2,128,128]{3,2,1,0:T(8,128)S(1)} %get-tuple-element.18), channel_id=1, source_target_pairs={{4,0},{5,1},{6,2},{7,3},{8,4},{9,5},{10,6},{11,7},{12,8},{13,9},{1... | collective-permute-start | bytes 1179656 | tf_op jit(solution)/shard_map/ppermute | solution.py:420
  7.9 16.7 %collective-permute-start = (f32[3,2,128,128]{3,2,1,0:T(8,128)S(1)}, f32[3,2,128,128]{3,2,1,0:T(8,128)S(1)}, u32[]{:S(2)}, u32[]{:S(2)}) collective-permute-start(f32[3,2,128,128]{3,2,1,0:T(8,128)S(1)} %get-tuple-element.19), channel_id=1, source_target_pairs={{28,0},{29,1},{30,2},{31,3},{0,4},{1,5},{2,6},{3,7},{4,8},{5,9},{6... | collective-permute-start | bytes 1179656 | tf_op jit(solution)/shard_map/ppermute | solution.py:420
  11.0 4.5 %collective-permute-start.2 = (f32[3,32,2,128]{3,2,1,0:T(2,128)S(1)}, f32[3,32,2,128]{3,2,1,0:T(2,128)S(1)}, u32[]{:S(2)}, u32[]{:S(2)}) collective-permute-start(f32[3,32,2,128]{3,2,1,0:T(2,128)S(1)} %get-tuple-element.10), channel_id=1, source_target_pairs={{3,0},{0,1},{1,2},{2,3},{7,4},{4,5},{5,6},{6,7},{11,8},{8,9},{9,10... | collective-permute-start | bytes 294920 | tf_op jit(solution)/shard_map/ppermute | solution.py:420
  11.0 4.5 %collective-permute-start.3 = (f32[3,32,2,128]{3,2,1,0:T(2,128)S(1)}, f32[3,32,2,128]{3,2,1,0:T(2,128)S(1)}, u32[]{:S(2)}, u32[]{:S(2)}) collective-permute-start(f32[3,32,2,128]{3,2,1,0:T(2,128)S(1)} %get-tuple-element.11), channel_id=1, source_target_pairs={{1,0},{2,1},{3,2},{0,3},{5,4},{6,5},{7,6},{4,7},{9,8},{10,9},{11,1... | collective-permute-start | bytes 294920 | tf_op jit(solution)/shard_map/ppermute | solution.py:420
  12.8 4.5 %copy-start = (f32[15,8,128]{2,1,0:T(8,128)S(1)}, f32[15,8,128]{2,1,0:T(8,128)}, u32[]{:S(2)}) copy-start(f32[15,8,128]{2,1,0:T(8,128)} %constant.2.clone.coef_ref.refs_7_) | copy-start | bytes 184324
  15.8 8.8 %collective-permute-start.4 = (f32[8,128]{1,0:T(8,128)S(1)}, f32[8,128]{1,0:T(8,128)S(1)}, u32[]{:S(2)}, u32[]{:S(2)}) collective-permute-start(f32[8,128]{1,0:T(8,128)S(1)} %get-tuple-element.14._.pay_ref), channel_id=1, source_target_pairs={{3,0},{0,1},{1,2},{2,3},{7,4},{4,5},{5,6},{6,7},{11,8},{8,9},{9,10... | collective-permute-start | bytes 12296 | tf_op jit(solution)/shard_map/ppermute | solution.py:420
  24.6 5.6 %collective-permute-start.5 = (f32[128,128]{1,0:T(8,128)S(1)}, f32[128,128]{1,0:T(8,128)S(1)}, u32[]{:S(2)}, u32[]{:S(2)}) collective-permute-start(f32[128,128]{1,0:T(8,128)S(1)} %largest_along_ax.1._.mine_ref), channel_id=1, source_target_pairs={{16,0},{17,1},{18,2},{19,3},{20,4},{21,5},{22,6},{23,7},{24,8},{25... | collective-permute-start | bytes 196616 | tf_op jit(solution)/shard_map/ppermute | solution.py:420
  30.4 6.2 %collective-permute-start.8 = (f32[8,128]{1,0:T(8,128)S(1)}, f32[8,128]{1,0:T(8,128)S(1)}, u32[]{:S(2)}, u32[]{:S(2)}) collective-permute-start(f32[8,128]{1,0:T(8,128)S(1)} %largest_with_partner.1._.refs_4_), channel_id=1, source_target_pairs={{24,0},{25,1},{26,2},{27,3},{28,4},{29,5},{30,6},{31,7},{0,8},{1,9... | collective-permute-start | bytes 12296 | tf_op jit(solution)/shard_map/ppermute | solution.py:420
  30.4 6.2 %collective-permute-start.7 = (f32[8,128]{1,0:T(8,128)S(1)}, f32[8,128]{1,0:T(8,128)S(1)}, u32[]{:S(2)}, u32[]{:S(2)}) collective-permute-start(f32[8,128]{1,0:T(8,128)S(1)} %largest_with_partner.1._.refs_4_), channel_id=1, source_target_pairs={{4,0},{5,1},{6,2},{7,3},{8,4},{9,5},{10,6},{11,7},{12,8},{13,9},{1... | collective-permute-start | bytes 12296 | tf_op jit(solution)/shard_map/ppermute | solution.py:420
  34.8 6.3 %collective-permute-start.6 = (f32[8,128]{1,0:T(8,128)S(1)}, f32[8,128]{1,0:T(8,128)S(1)}, u32[]{:S(2)}, u32[]{:S(2)}) collective-permute-start(f32[8,128]{1,0:T(8,128)S(1)} %largest_with_partner.1._.refs_4_), channel_id=1, source_target_pairs={{28,0},{29,1},{30,2},{31,3},{0,4},{1,5},{2,6},{3,7},{4,8},{5,9},{6... | collective-permute-start | bytes 12296 | tf_op jit(solution)/shard_map/ppermute | solution.py:420

commit v7 on v6

v7 whole, which is shorter than its diff:
```python
import functools
import math

import jax
import jax.numpy as jnp
import numpy as np
from jax import lax
from jax.experimental import pallas as pl
from jax.experimental.pallas import tpu as pltpu
from jax.sharding import PartitionSpec as P

AXIAL_STEP = 0.01
VISCOSITY = 0.001
CFL_TARGET = 1.2
GAMMA = 8.0 / 15.0

PAD = 8
HALO = 2
BLOCK = 4
GROUP = 4
UNROLL = 4

(
    WALL,
    RADIAL_C,
    THETA_C,
    CROSS_Z,
    SECOND_C,
    CENTRE_Z,
    CENTRE_T,
    CURVE_T,
    TURN_T,
    RADIAL_F,
    THETA_F,
    SECOND_F,
    CENTRE_R,
    CURVE_R,
    TURN_R,
    COUNT,
) = range(16)


def coefficients(radial, theta_step):
    dr = 1.0 / radial
    index = np.arange(radial, dtype=np.float64)
    centre = (index + 0.5) * dr
    face = (index + 1.0) * dr
    wall = np.where(index < radial - 1.5, 1.0, 0.0)
    h = theta_step
    nu = VISCOSITY
    rows = np.zeros((COUNT, radial))
    rows[WALL] = wall
    common = -2.0 * nu / dr**2 - 30.0 * nu / (12.0 * AXIAL_STEP**2)
    rows[RADIAL_C] = nu / (2.0 * dr * centre)
    rows[THETA_C] = -1.0 / (12.0 * h * centre)
    rows[CROSS_Z] = 0.25 * rows[THETA_C]
    rows[SECOND_C] = nu / (12.0 * h * h * centre**2)
    rows[CENTRE_Z] = common - 30.0 * rows[SECOND_C]
    rows[CENTRE_T] = rows[CENTRE_Z] - nu / centre**2
    rows[CURVE_T] = 0.25 / centre
    rows[TURN_T] = nu / (h * centre**2)
    rows[RADIAL_F] = nu / (2.0 * dr * face)
    rows[THETA_F] = -0.25 / (12.0 * h * face)
    rows[SECOND_F] = nu / (12.0 * h * h * face**2)
    rows[CENTRE_R] = common - 30.0 * rows[SECOND_F] - nu / face**2
    rows[CURVE_R] = 1.0 / (16.0 * face)
    rows[TURN_R] = -nu / (h * face**2)
    return np.broadcast_to(rows[:, None, :], (COUNT, 8, radial)).astype(np.float32)


class Cells:
    def __init__(self, vel, j, k):
        self.vel, self.j, self.k, self.known = vel, j, k, {}

    def once(self, key, make):
        if key not in self.known:
            self.known[key] = make()
        return self.known[key]

    def at(self, n, dj, dk=0):
        rows = pl.ds(self.k + PAD + dk, 8)
        return self.once((n, dj, dk), lambda: self.vel[n, self.j + HALO + dj, rows, :])

    def turned(self, by, n, dj, dk=0):
        return self.once(
            (by, n, dj, dk), lambda: pltpu.roll(self.at(n, dj, dk), by % self.vel.shape[3], 1)
        )

    def pair(self, by, n, dj, dk=0):
        return self.once(
            ("pair", n, dj, dk), lambda: self.at(n, dj, dk) + self.turned(by, n, dj, dk)
        )

    def beside(self, dj, dk):
        n = 1 if dk >= 0 else 2
        other = (1, dj - 1, dk) if n == 1 else (2, dj, dk)
        here = (1, dj, dk) if n == 1 else (2, dj, dk + 1)
        return self.once(("sum", n, dj, dk), lambda: self.at(*other) + self.at(*here))


def terms(cells, ghost, coef, q, dr):
    at, turned, pair = cells.at, cells.turned, cells.pair
    a, b, c = (at(n, q) for n in range(3))
    lane = lax.broadcasted_iota(jnp.int32, a.shape, 1)
    first_lane = lane == 0
    last_lane = lane == a.shape[1] - 1

    nu = VISCOSITY
    lap = nu / dr**2
    adv_z = -1.0 / (12.0 * AXIAL_STEP)
    vis_z = nu / (12.0 * AXIAL_STEP**2)

    def differences(p1, m1, p2, m2):
        return 8.0 * (p1 - m1) - (p2 - m2), 16.0 * (p1 + m1) - (p2 + m2)

    def pieces(n):
        over = differences(*(at(n, q + d) for d in (1, -1, 2, -2)))
        along = differences(*(at(n, q, d) for d in (1, -1, 2, -2)))
        return over, along

    def below(n):
        if ghost is not None and n > 0 and q % 2 == 0:
            x = jnp.where(last_lane, ghost(n, q + 1), at(n, q))
            return pltpu.roll(x, 1, 1)
        x = turned(1, n, q)
        if ghost is not None:
            return jnp.where(first_lane, ghost(n, q), x)
        return x if n == 0 else jnp.where(first_lane, 0.0, x)

    def above(n):
        return jnp.where(last_lane, -at(n, q), turned(-1, n, q))

    pair_a, pair_side, pair_next = pair(1, 0, q), pair(1, 0, q + 1), pair(1, 0, q, 1)
    pair_b, pair_back = pair(-1, 1, q), pair(-1, 1, q - 1)

    theta, axial = pieces(2)
    up, low = above(2), below(2)
    u_r = pair_a + pair_next
    u_t = cells.beside(q, 0) + cells.beside(q, 1)
    h_z = (up - low) * (coef[RADIAL_C] - u_r * (0.125 / dr)) + (up + low) * lap
    h_z = h_z + theta[0] * (u_t * coef[CROSS_Z])
    h_z = h_z + (theta[1] * coef[SECOND_C] + axial[1] * vis_z)
    h_z = h_z + c * (coef[CENTRE_Z] + axial[0] * adv_z)

    theta, axial = pieces(1)
    up, low = above(1), below(1)
    u_r = pair_a + pair_side
    u_z = cells.beside(q, -1) + cells.beside(q + 1, -1)
    h_t = (up - low) * (coef[RADIAL_C] - u_r * (0.125 / dr)) + (up + low) * lap
    h_t = h_t + b * (coef[CENTRE_T] + theta[0] * coef[THETA_C] - u_r * coef[CURVE_T])
    h_t = h_t + (theta[1] * coef[SECOND_C] + axial[1] * vis_z)
    h_t = h_t + axial[0] * (u_z * (0.25 * adv_z))
    h_t = h_t + (pair_side - pair_a) * coef[TURN_T]

    theta, axial = pieces(0)
    up, low = turned(-1, 0, q), below(0)
    u_t = pair_b + pair_back
    u_z = pair(-1, 2, q) + pair(-1, 2, q, -1)
    h_r = (up - low) * (coef[RADIAL_F] - a * (0.5 / dr)) + (up + low) * lap
    h_r = h_r + u_t * (u_t * coef[CURVE_R] + theta[0] * coef[THETA_F])
    h_r = h_r + (theta[1] * coef[SECOND_F] + axial[1] * vis_z)
    h_r = h_r + (axial[0] * (u_z * (0.25 * adv_z)) + a * coef[CENTRE_R])
    h_r = h_r + (pair_b - pair_back) * coef[TURN_R]
    return h_r, h_t, h_z


def lane_zero_terms(cells, ghost, coef, q, dr):
    lap = VISCOSITY / dr**2
    a = cells.at(0, q)
    first_lane = lax.broadcasted_iota(jnp.int32, a.shape, 1) == 0
    add_r = ghost(0, q) * (lap - coef[RADIAL_F] + a * (0.5 / dr))
    add_t = ghost(1, q) * (lap - coef[RADIAL_C] + (a + cells.at(0, q + 1)) * (0.125 / dr))
    add_z = ghost(2, q) * (lap - coef[RADIAL_C] + (a + cells.at(0, q, 1)) * (0.125 / dr))
    return tuple(jnp.where(first_lane, x, 0.0) for x in (add_r, add_t, add_z))


def wall_mask(rows, radial):
    lane = lax.broadcasted_iota(jnp.int32, (rows, radial), 1)
    return jnp.where(lane == radial - 1, 0.0, 1.0).astype(jnp.float32)


def first_pass(theta_step, v_ref, vel_ref, low_ref, high_ref, inner_ref, pay_ref, sems):
    _, planes, axial, radial = v_ref.shape
    lane = lax.broadcasted_iota(jnp.int32, (8, radial), 1)
    sign = jnp.where(lane < 2 * planes, -1.0, 1.0).astype(jnp.float32)
    wall = wall_mask(8, radial)
    rate_t = (radial / theta_step) / (lane.astype(jnp.float32) + 0.5)

    def fetch(g):
        part = pl.ds(g * GROUP, GROUP)
        target = vel_ref.at[:, pl.ds(g * GROUP + HALO, GROUP), pl.ds(PAD, axial)]
        return pltpu.make_async_copy(v_ref.at[:, part], target, sems.at[g])

    for g in range(planes // GROUP):
        fetch(g).start()

    zero = jnp.zeros((8, radial), jnp.float32)
    largest = (zero,) * 4
    for g in range(planes // GROUP):
        fetch(g).wait()

        def rows(i, largest, g=g):
            k = pl.multiple_of(i * 8, 8)
            largest = list(largest)
            inner = [zero] * 3
            for q in range(GROUP):
                j = g * GROUP + q
                cells = [vel_ref[n, j + HALO, pl.ds(k + PAD, 8), :] for n in range(3)]
                for n, x in enumerate(cells):
                    place = n * planes + j
                    x = pltpu.roll(x, place, 1) if place else x
                    inner[n] = jnp.where(lane == place, x, inner[n])
                a, b, c = cells
                a = a * wall
                vel_ref[0, j + HALO, pl.ds(k + PAD, 8), :] = a
                rate = jnp.abs(a) * float(radial) + jnp.abs(b) * rate_t
                rate = rate + jnp.abs(c) * (1.0 / AXIAL_STEP)
                largest[q % 4] = jnp.maximum(largest[q % 4], rate)
            inner = (inner[0] + inner[1] + inner[2]) * sign
            if g > 0:
                inner = inner_ref[pl.ds(k, 8), :] + inner
            inner_ref[pl.ds(k, 8), :] = inner
            return tuple(largest)

        largest = lax.fori_loop(0, axial // 8, rows, largest, unroll=UNROLL)
        for q in range(GROUP):
            for n in range(3):
                j = g * GROUP + q
                low_ref[n, j] = vel_ref[n, j + HALO, PAD : PAD + 2, :]
                high_ref[n, j] = vel_ref[n, j + HALO, PAD + axial - 2 : PAD + axial, :]

    largest = jnp.maximum(
        jnp.maximum(largest[0], largest[1]), jnp.maximum(largest[2], largest[3])
    )
    top = jnp.max(largest, axis=(0, 1), keepdims=True)
    pay_ref[...] = jnp.broadcast_to(top, pay_ref.shape)
    last = lax.broadcasted_iota(jnp.int32, (2, radial), 1) == radial - 1
    for ref in (low_ref, high_ref):
        ref[0, 0] = jnp.where(last, top, ref[0, 0])


def fold(low_ref, high_ref, pay_ref, inner_in, vel_in, *refs):
    del vel_in
    fars, (out_ref, inner_ref, vel_ref) = refs[2:-3], refs[-3:]
    planes = low_ref.shape[1]
    axial, radial = inner_in.shape
    lane = lax.broadcasted_iota(jnp.int32, (1, radial), 1)
    top = jnp.maximum(low_ref[0, 0, 0:1, :], high_ref[0, 0, 0:1, :])
    top = jnp.max(jnp.where(lane == radial - 1, top, 0.0), axis=(0, 1), keepdims=True)
    top = jnp.maximum(pay_ref[...], top)
    for far in fars:
        top = jnp.maximum(top, far[...])
    out_ref[...] = top
    out_ref[1:2, :] = high_ref[1, planes - 1, 0:1, :]
    out_ref[2:3, :] = low_ref[2, 0, 1:2, :]
    lane = lax.broadcasted_iota(jnp.int32, top.shape, 1)
    inner_ref[...] = inner_in[...]
    inner_ref[0:8, :] = jnp.where(lane == radial - 1, top, inner_in[0:8, :])
    wall = wall_mask(2, radial)

    def plane(j, carry):
        for n in range(3):
            mask = wall if n == 0 else 1.0
            vel_ref[n, j + HALO, PAD - 2 : PAD, :] = low_ref[n, j] * mask
            vel_ref[n, j + HALO, PAD + axial : PAD + axial + 2, :] = high_ref[n, j] * mask
        return carry

    lax.fori_loop(0, planes, plane, 0, unroll=4)


def with_partner(pay_ref, inner_ref, _, out_ref):
    lane = lax.broadcasted_iota(jnp.int32, (1, inner_ref.shape[1]), 1)
    top = jnp.where(lane == inner_ref.shape[1] - 1, inner_ref[0:1, :], 0.0)
    top = jnp.maximum(jnp.max(top, axis=(0, 1), keepdims=True), pay_ref[0:1, :])
    row = lax.broadcasted_iota(jnp.int32, out_ref.shape, 0)
    out_ref[...] = jnp.where(row == 0, top, pay_ref[...])


def theta_rest(vel_ref, *refs):
    head_ref, tail_ref = refs[-2:]
    planes, axial = vel_ref.shape[1] - 2 * HALO, head_ref.shape[2]
    for n in (1, 2):
        for q in range(HALO):
            head_ref[n - 1, q] = vel_ref[n, HALO + q, pl.ds(PAD, axial), :]
            tail_ref[n - 1, q] = vel_ref[n, planes + q, pl.ds(PAD, axial), :]


def ghosts(cells, inner, planes):
    radial = inner.shape[1]

    def ghost(n, q):
        turn = lax.rem(2 * radial - n * planes - q - cells.j, radial)
        return cells.once(("ghost", n, q), lambda: pltpu.roll(inner, turn, 1))

    return ghost


def sweep(vel_ref, inner_ref, coef_ref, first, last, write, after=None):
    planes = vel_ref.shape[1] - 2 * HALO
    axial, radial = vel_ref.shape[2] - 2 * PAD, vel_ref.shape[3]
    size = math.gcd(BLOCK, last - first)

    def block(m, carry):
        j = first + m * size

        def rows(i, carry):
            k = pl.multiple_of(i * 8, 8)
            coef = [coef_ref[n] for n in range(COUNT)]
            cells = Cells(vel_ref, j, k)
            ghost = None
            if inner_ref is not None:
                ghost = ghosts(cells, inner_ref[pl.ds(k, 8), :], planes)
            found = [terms(cells, ghost, coef, q, 1.0 / radial) for q in range(size)]
            for q, values in enumerate(found):
                for n, value in enumerate(values):
                    write(n, j + q, pl.ds(k, 8), value)
            return carry

        lax.fori_loop(0, axial // 8, rows, 0)
        if after is not None:
            after(j, size)
        return carry

    lax.fori_loop(0, (last - first) // size, block, 0)


def ahead(first, last, vel_ref, coef_ref, _, out_ref):
    def write(n, j, k, value):
        out_ref[n, j - first, k, :] = value

    sweep(vel_ref, None, coef_ref, first, last, write)


def ahead_with_ghosts(first, last, vel_ref, inner_ref, coef_ref, _, out_ref):
    def write(n, j, k, value):
        out_ref[n, j - first, k, :] = value

    sweep(vel_ref, inner_ref, coef_ref, first, last, write)


def stores(res, base, out_ref, sems):
    def copy(j):
        return pltpu.make_async_copy(res.at[:, j - base], out_ref.at[:, j], sems.at[j - base])

    def start(j, size):
        for q in range(size):
            copy(j + q).start()

    def wait(first, last):
        def one(j, carry):
            copy(j).wait()
            return carry

        lax.fori_loop(first, last, one, 0)

    return start, wait


def interior(
    spans, count, vel_ref, inner_ref, coef_ref, part_a, part_b, *refs
):
    tops, (out_ref, step_ref, res, sems) = refs[:count], refs[count:]
    axial, radial = inner_ref.shape
    planes = vel_ref.shape[1] - 2 * HALO
    top = tops[0][0:1, :]
    for ref in tops[1:]:
        top = jnp.maximum(top, ref[0:1, :])
    time_step = CFL_TARGET / (jnp.max(top) + 1e-06)
    step_ref[0] = time_step
    scale = GAMMA * time_step
    base = spans[0][0]
    start, wait = stores(res, base, out_ref, sems)

    def write(n, j, k, value):
        factor = scale * coef_ref[WALL] if n == 0 else scale
        res[n, j - base, k, :] = value * factor

    for part, (first, last), add in ((part_a, spans[0], True), (part_b, spans[1], False)):

        def block(m, carry, part=part, first=first, add=add):
            j = first + m * BLOCK

            def rows(i, carry):
                k = pl.multiple_of(i * 8, 8)
                cells = Cells(vel_ref, j, k)
                ghost = ghosts(cells, inner_ref[pl.ds(k, 8), :], planes)
                found = []
                for q in range(BLOCK):
                    values = [part[n, j + q - first, pl.ds(k, 8), :] for n in range(3)]
                    if add:
                        added = lane_zero_terms(cells, ghost, coef_ref, q, 1.0 / radial)
                        values = [x + y for x, y in zip(values, added)]
                    found.append(values)
                for q, values in enumerate(found):
                    for n, value in enumerate(values):
                        write(n, j + q, pl.ds(k, 8), value)
                return carry

            lax.fori_loop(0, axial // 8, rows, 0, unroll=2)
            start(j, BLOCK)
            return carry

        lax.fori_loop(0, (last - first) // BLOCK, block, 0)

    sweep(vel_ref, inner_ref, coef_ref, *spans[2], write, start)
    wait(spans[0][0], spans[2][1])


def edges(
    step_ref, below_r, above_r, below, above, up_ref, down_ref, inner_ref, coef_ref, vel_in, part,
    out_ref, vel_ref, res, sems,
):
    del vel_in, part
    axial, radial = inner_ref.shape
    planes = vel_ref.shape[1] - 2 * HALO
    scale = GAMMA * step_ref[0]
    cells = pl.ds(PAD, axial)
    for q in range(HALO):
        for first, rest, place in (
            (below_r, below, q),
            (above_r, above, HALO + planes + q),
        ):
            vel_ref[0, place, cells, :] = first[q] * coef_ref[WALL, 0:1, :]
            vel_ref[1, place, cells, :] = rest[0, q]
            vel_ref[2, place, cells, :] = rest[1, q]
    vel_ref[1, HALO - 1, PAD + axial : PAD + axial + 1, :] = up_ref[1:2, :]
    vel_ref[2, HALO + planes, PAD - 1 : PAD, :] = down_ref[2:3, :]
    for side, first in enumerate((0, planes - HALO)):
        base = first - side * HALO
        start, _ = stores(res, base, out_ref, sems)

        def write(n, j, k, value, base=base):
            factor = scale * coef_ref[WALL] if n == 0 else scale
            res[n, j - base, k, :] = value * factor

        sweep(vel_ref, inner_ref, coef_ref, first, first + HALO, write, start)
    for side, first in enumerate((0, planes - HALO)):
        stores(res, first - side * HALO, out_ref, sems)[1](first, first + HALO)


def shifted(block, distance):
    sizes = lax.axis_size("az"), lax.axis_size("ax")
    route = []
    for i in range(sizes[0]):
        for k in range(sizes[1]):
            source = (i - distance[0]) % sizes[0], (k - distance[1]) % sizes[1]
            route.append((source[0] * sizes[1] + source[1], i * sizes[1] + k))
    return lax.ppermute(block, ("az", "ax"), route)


def cuts(planes):
    ends = (HALO, HALO + BLOCK, HALO + 2 * BLOCK, planes - HALO)
    return list(zip(ends[:-1], ends[1:]))


def per_device(velocity):
    _, planes, axial, radial = velocity.shape
    sizes = lax.axis_size("az"), lax.axis_size("ax")
    theta_step = 2.0 * math.pi / (sizes[0] * planes)
    coef = jnp.asarray(coefficients(radial, theta_step))
    f32 = jnp.float32
    anywhere = pl.BlockSpec(memory_space=pl.ANY)
    vmem = pl.BlockSpec(memory_space=pltpu.VMEM)
    smem = pl.BlockSpec(memory_space=pltpu.SMEM)

    def shape(*sizes):
        return jax.ShapeDtypeStruct(sizes, f32)

    def call(kernel, name, work, scratch=0, **kwargs):
        return pl.pallas_call(
            kernel,
            name=name,
            compiler_params=pltpu.CompilerParams(vmem_limit_bytes=(4 + scratch) * 2**20),
            cost_estimate=pl.CostEstimate(flops=work, bytes_accessed=work, transcendentals=0),
            **kwargs,
        )

    below_r = shifted(velocity[0, planes - HALO :], (1, 0))
    above_r = shifted(velocity[0, :HALO], (-1, 0))

    edge = shape(3, planes, 2, radial)
    padded = shape(3, planes + 2 * HALO, axial + 2 * PAD, radial)
    row = shape(axial, radial)
    tile = shape(8, radial)
    vel, first, last, inner, pay = call(
        functools.partial(first_pass, theta_step),
        "first_pass",
        0,
        out_shape=(padded, edge, edge, row, tile),
        in_specs=[anywhere],
        out_specs=(vmem,) * 5,
        scratch_shapes=[pltpu.SemaphoreType.DMA((planes // GROUP,))],
    )(pltpu.with_memory_space_constraint(velocity, pltpu.HBM))
    low = shifted(last, (0, 1))
    high = shifted(first, (0, -1))
    fars = [shifted(pay, (0, step)) for step in range(2, sizes[1] - 1)]
    pay, inner, vel = call(
        fold,
        "fold",
        0,
        out_shape=(tile, row, padded),
        in_specs=[vmem] * (7 + len(fars)),
        out_specs=(vmem,) * 3,
        input_output_aliases={4: 2},
    )(low, high, pay, inner, vel, below_r, above_r, *fars)
    inner = shifted(inner, (sizes[0] // 2, 0))

    spans = cuts(planes)
    part_shape = shape(3, BLOCK, axial, radial)
    part_a = call(
        functools.partial(ahead, *spans[0]),
        "ahead",
        velocity.size,
        out_shape=part_shape,
        in_specs=[vmem] * 3,
        out_specs=vmem,
    )(vel, coef, pay)
    pay = call(
        with_partner,
        "with_partner",
        0,
        out_shape=tile,
        in_specs=[vmem] * 3,
        out_specs=vmem,
    )(pay, inner, part_a)
    up = shifted(pay, (1, 0))
    down = shifted(pay, (-1, 0))
    others, near = [], {(i + s) % sizes[0] for i in (0, sizes[0] // 2) for s in (-1, 0, 1)}
    while len(near) < sizes[0]:
        step = min(set(range(sizes[0])) - near)
        others.append(shifted(pay, (step, 0)))
        near |= {step, (step + sizes[0] // 2) % sizes[0]}
    part_b = call(
        functools.partial(ahead_with_ghosts, *spans[1]),
        "ahead_with_ghosts",
        velocity.size,
        out_shape=part_shape,
        in_specs=[vmem] * 4,
        out_specs=vmem,
    )(vel, inner, coef, pay)
    pair = shape(2, HALO, axial, radial)
    head, tail = call(
        theta_rest,
        "theta_rest",
        0,
        out_shape=(pair, pair),
        in_specs=[vmem] * (4 + len(others)),
        out_specs=(vmem, vmem),
    )(vel, up, down, *others, part_b)
    below = shifted(tail, (1, 0))
    above = shifted(head, (-1, 0))
    tops = (pay, up, down, *others)
    part, time_step = call(
        functools.partial(interior, spans, len(tops)),
        "interior",
        4 * velocity.size,
        scratch=6,
        out_shape=(shape(*velocity.shape), shape(1)),
        in_specs=[vmem] * (5 + len(tops)),
        out_specs=(anywhere, smem),
        scratch_shapes=[
            pltpu.VMEM((3, planes - 2 * HALO, axial, radial), f32),
            pltpu.SemaphoreType.DMA((planes - 2 * HALO,)),
        ],
    )(vel, inner, coef, part_a, part_b, *tops)
    increment, _ = call(
        edges,
        "edges",
        0,
        scratch=2,
        out_shape=(shape(*velocity.shape), padded),
        in_specs=[smem] + [vmem] * 9 + [anywhere],
        out_specs=(anywhere, vmem),
        scratch_shapes=[
            pltpu.VMEM((3, 2 * HALO, axial, radial), f32),
            pltpu.SemaphoreType.DMA((2 * HALO,)),
        ],
        input_output_aliases={9: 1, 10: 0},
    )(time_step, below_r, above_r, below, above, up, down, inner, coef, vel, part)
    return increment, time_step.reshape(())


def solution(mesh):
    return jax.shard_map(
        per_device,
        mesh=mesh,
        in_specs=(P(None, "az", "ax", None),),
        out_specs=(P(None, "az", "ax", None), P()),
        check_vma=False,
    )
```

time: 56.7 us -> 62 us (1.093)
  starting transfers between devices: 14.4 us -> 19 us
  waiting for transfers between devices: 7.66 us -> 9.97 us
  Pallas kernels: 32.6 us -> 31.1 us
    ppermute x9 -> x11, starting transfers between devices: 14.4 us -> 19 us  [shifted(): return lax.ppermute(block, ('az', 'ax'), route)]
    pallas_call x9 -> x7, Pallas kernels: 29.5 us -> 25.8 us  [the longest x1 15.1 us: per_device(): call(functools.partial(interior, spans, len(tops)), 'interior', 4 * veloc...]
    ppermute x9 -> x11, waiting for transfers between devices: 7.66 us -> 9.97 us  [shifted(): return lax.ppermute(block, ('az', 'ax'), route)]
    pallas_call x1, Pallas kernels: 3.1 us -> 5.23 us  [per_device(): call(functools.partial(first_pass, theta_step), 'first_pass', 0, out_shap...]
    slice x1 -> x0, local copies, waits for them, and re-layouts: 1.17 us -> none  [per_device(): above = shifted(velocity[:, :HALO], (-1, 0))]
    squeeze x0 -> x1, local copies, waits for them, and re-layouts: none -> 0.99 us  [per_device(): above_r = shifted(velocity[0, :HALO], (-1, 0))]
  transfers between devices with their start and end apart: 9 -> 11, of which waited for: 2 -> 3; matrix products, arithmetic and copies ran while one was open for 0% -> 0% of each run, Pallas kernels for 30% -> 40%
where the time goes in v7:
time: 62 us; the launch traced here: 61.8 us
  Pallas kernels  31.1 us (50%)
  starting transfers between devices  19 us (31%)
  waiting for transfers between devices  9.97 us (16%)
  local copies, waits for them, and re-layouts  0.99 us (2%)
  between operations  0.76 us (1%)
    ppermute x11, starting transfers between devices, shifted(): return lax.ppermute(block, ('az', 'ax'), route)  19 us
    pallas_call x1, Pallas kernels, per_device(): call(functools.partial(interior, spans, len(tops)), 'interior', 4 * veloc...  15.1 us
    ppermute x11, waiting for transfers between devices, shifted(): return lax.ppermute(block, ('az', 'ax'), route)  9.97 us
    pallas_call x1, Pallas kernels, per_device(): call(edges, 'edges', 0, scratch=2, out_shape=(shape(*velocity.shape), pad...  6.2 us
    pallas_call x1, Pallas kernels, per_device(): call(functools.partial(first_pass, theta_step), 'first_pass', 0, out_shap...  5.23 us
    pallas_call x1, Pallas kernels, per_device(): call(functools.partial(ahead_with_ghosts, *spans[1]), 'ahead_with_ghosts'...  2.36 us
    pallas_call x1, Pallas kernels, per_device(): call(functools.partial(ahead, *spans[0]), 'ahead', velocity.size, out_sha...  1.81 us
  transfers between devices with their start and end apart: 11, of which 3 were waited for; matrix products, arithmetic and copies ran while one was open for 0% of the time, Pallas kernels for 40%

profile of v7, /device:TPU:0, one launch (start us, length us, event | category | flops | bytes accessed | tf_op | source)
XLA Modules:
  0.0 61.8 jit_solution(4300050680980265097)
XLA Ops:
  0.6 1.0 %slice_bitcast_fusion = (f32[2,128,128]{2,1,0:T(8,128)S(1)}, f32[2,128,128]{2,1,0:T(8,128)S(1)}) fusion(f32[3,32,128,128]{3,2,1,0:T(8,128)} %v_ref.1), kind=kLoop, calls=%fused_computation | loop fusion | bytes 524288 | tf_op jit(solution)/shard_map/squeeze | solution.py:479
  1.6 6.1 %collective-permute-start.3 = (f32[2,128,128]{2,1,0:T(8,128)S(1)}, f32[2,128,128]{2,1,0:T(8,128)S(1)}, u32[]{:S(2)}, u32[]{:S(2)}) collective-permute-start(f32[2,128,128]{2,1,0:T(8,128)S(1)} %get-tuple-element.28), channel_id=1, source_target_pairs={{4,0},{5,1},{6,2},{7,3},{8,4},{9,5},{10,6},{11,7},{12,8},{13,9},{1... | collective-permute-start | bytes 393224 | tf_op jit(solution)/shard_map/ppermute | solution.py:448
  7.7 0.0 copy-start
  7.7 0.0 collective-permute-start.2
  7.7 5.2 %first_pass.1 = (f32[3,36,144,128]{3,2,1,0:T(8,128)S(1)}, f32[3,32,2,128]{3,2,1,0:T(2,128)S(1)}, f32[3,32,2,128]{3,2,1,0:T(2,128)S(1)}, f32[128,128]{1,0:T(8,128)S(1)}, f32[8,128]{1,0:T(8,128)S(1)}) custom-call(f32[3,32,128,128]{3,2,1,0:T(8,128)} %v_ref.1), custom_call_target="tpu_custom_call" | custom-call | tf_op jit(solution)/shard_map/first_pass/pallas_call | solution.py:485
  12.9 0.1 collective-permute-start
  13.0 1.7 %collective-permute-start.1 = (f32[3,32,2,128]{3,2,1,0:T(2,128)S(1)}, f32[3,32,2,128]{3,2,1,0:T(2,128)S(1)}, u32[]{:S(2)}, u32[]{:S(2)}) collective-permute-start(f32[3,32,2,128]{3,2,1,0:T(2,128)S(1)} %get-tuple-element.16), channel_id=1, source_target_pairs={{1,0},{2,1},{3,2},{0,3},{5,4},{6,5},{7,6},{4,7},{9,8},{10,9},{11,1... | collective-permute-start | bytes 294920 | tf_op jit(solution)/shard_map/ppermute | solution.py:448
  14.7 1.5 %collective-permute-start.4 = (f32[8,128]{1,0:T(8,128)S(1)}, f32[8,128]{1,0:T(8,128)S(1)}, u32[]{:S(2)}, u32[]{:S(2)}) collective-permute-start(f32[8,128]{1,0:T(8,128)S(1)} %get-tuple-element.17.pay_ref), channel_id=1, source_target_pairs={{2,0},{3,1},{0,2},{1,3},{6,4},{7,5},{4,6},{5,7},{10,8},{11,9},{8,1... | collective-permute-start | bytes 12296 | tf_op jit(solution)/shard_map/ppermute | solution.py:448
  16.2 2.6 %collective-permute-done.4.refs_2_ = f32[8,128]{1,0:T(8,128)S(1)} collective-permute-done((f32[8,128]{1,0:T(8,128)S(1)}, f32[8,128]{1,0:T(8,128)S(1)}, u32[]{:S(2)}, u32[]{:S(2)}) %collective-permute-start.4) | collective-permute-done | bytes 4128 | tf_op jit(solution)/shard_map/ppermute | solution.py:448
  18.8 0.0 collective-permute-done.low_ref
  18.8 0.0 collective-permute-done.1.high_ref
  18.8 0.0 collective-permute-done.3.refs_1_.above_r
  18.9 0.0 collective-permute-done.2.refs_0_.below_r
  18.9 0.2 fold.1
  19.1 0.1 collective-permute-start.5
  19.2 0.0 copy-done
  19.2 1.8 %ahead.1._.part_a = f32[3,4,128,128]{3,2,1,0:T(8,128)S(1)} custom-call(f32[3,36,144,128]{3,2,1,0:T(8,128)S(1)} %get-tuple-element.20.vel_ref.vel_in, f32[15,8,128]{2,1,0:T(8,128)S(1)} %copy-done, f32[8,128]{1,0:T(8,128)S(1)} %get-tuple-element.22._.pay_ref), custom_call_target="tpu_custom_call" | custom-call | flops 1572864 | bytes 1572864 | tf_op jit(solution)/shard_map/ahead/pallas_call | solution.py:510
  21.0 3.3 %collective-permute-done.5.inner_ref = f32[128,128]{1,0:T(8,128)S(1)} collective-permute-done((f32[128,128]{1,0:T(8,128)S(1)}, f32[128,128]{1,0:T(8,128)S(1)}, u32[]{:S(2)}, u32[]{:S(2)}) %collective-permute-start.5) | collective-permute-done | bytes 65568 | tf_op jit(solution)/shard_map/ppermute | solution.py:448
  24.3 0.1 with_partner.1._.refs_0_
  24.5 0.1 collective-permute-start.8
  24.5 4.8 %collective-permute-start.7 = (f32[8,128]{1,0:T(8,128)S(1)}, f32[8,128]{1,0:T(8,128)S(1)}, u32[]{:S(2)}, u32[]{:S(2)}) collective-permute-start(f32[8,128]{1,0:T(8,128)S(1)} %with_partner.1._.refs_0_), channel_id=1, source_target_pairs={{4,0},{5,1},{6,2},{7,3},{8,4},{9,5},{10,6},{11,7},{12,8},{13,9},{1... | collective-permute-start | bytes 12296 | tf_op jit(solution)/shard_map/ppermute | solution.py:448
  29.3 0.0 collective-permute-start.6
  29.3 2.4 %ahead_with_ghosts.1.part_b.refs_3_ = f32[3,4,128,128]{3,2,1,0:T(8,128)S(1)} custom-call(f32[3,36,144,128]{3,2,1,0:T(8,128)S(1)} %get-tuple-element.20.vel_ref.vel_in, f32[128,128]{1,0:T(8,128)S(1)} %collective-permute-done.5.inner_ref, f32[15,8,128]{2,1,0:T(8,128)S(1)} %copy-done, f32[8,128]{1,0:T(8,128)S(1)} %with_partner.1._.refs_0_), custom_call_target="tpu_custom_call" | custom-call | flops 1572864 | bytes 1572864 | tf_op jit(solution)/shard_map/ahead_with_ghosts/pallas_call | solution.py:533
  31.7 0.0 collective-permute-done.8.refs_3_.refs_2_
  31.7 0.0 collective-permute-done.7.refs_2_.refs_1_.down_ref
  31.7 4.0 %collective-permute-done.6.refs_1_.refs_0_.up_ref = f32[8,128]{1,0:T(8,128)S(1)} collective-permute-done((f32[8,128]{1,0:T(8,128)S(1)}, f32[8,128]{1,0:T(8,128)S(1)}, u32[]{:S(2)}, u32[]{:S(2)}) %collective-permute-start.6) | collective-permute-done | bytes 4128 | tf_op jit(solution)/shard_map/ppermute | solution.py:448
  35.7 0.1 collective-permute-start.9
  35.8 4.7 %collective-permute-start.10 = (f32[2,2,128,128]{3,2,1,0:T(8,128)S(1)}, f32[2,2,128,128]{3,2,1,0:T(8,128)S(1)}, u32[]{:S(2)}, u32[]{:S(2)}) collective-permute-start(f32[2,2,128,128]{3,2,1,0:T(8,128)S(1)} %get-tuple-element.25), channel_id=1, source_target_pairs={{4,0},{5,1},{6,2},{7,3},{8,4},{9,5},{10,6},{11,7},{12,8},{13,9},{1... | collective-permute-start | bytes 786440 | tf_op jit(solution)/shard_map/ppermute | solution.py:448
  40.5 15.1 %interior.1 = (f32[3,32,128,128]{3,2,1,0:T(8,128)}, f32[1]{0:T(128)}) custom-call(f32[3,36,144,128]{3,2,1,0:T(8,128)S(1)} %get-tuple-element.20.vel_ref.vel_in, f32[128,128]{1,0:T(8,128)S(1)} %collective-permute-done.5.inner_ref, f32[15,8,128]{2,1,0:T(8,128)S(1)} %copy-done, f32[3,4,128,128]{3,2,1,0:T(8,128)S(1)} %ahead.1._.part_a, ...), custom_call_target="tpu_custom_call" | custom-call | flops 6291456 | bytes 6291456 | tf_op jit(solution)/shard_map/interior/pallas_call | solution.py:553
  55.6 0.0 collective-permute-done.9.below
  55.6 0.0 collective-permute-done.10.above
  55.6 6.2 %edges.1 = (f32[3,32,128,128]{3,2,1,0:T(8,128)}, f32[3,36,144,128]{3,2,1,0:T(8,128)S(1)}) custom-call(f32[1]{0:T(128)} %get-tuple-element.23.step_ref, f32[2,128,128]{2,1,0:T(8,128)S(1)} %collective-permute-done.2.refs_0_.below_r, f32[2,128,128]{2,1,0:T(8,128)S(1)} %collective-permute-done.3.refs_1_.above_r, ...), custom_call_target="tpu_custom_call", output_to_operand_aliasing={{1}: (9, {}), {0}: (10, {})} | custom-call | tf_op jit(solution)/shard_map/edges/pallas_call | solution.py:566
  (1 shorter events, 0.0 us)
Async XLA Ops:
  1.6 17.2 %collective-permute-start.3 = (f32[2,128,128]{2,1,0:T(8,128)S(1)}, f32[2,128,128]{2,1,0:T(8,128)S(1)}, u32[]{:S(2)}, u32[]{:S(2)}) collective-permute-start(f32[2,128,128]{2,1,0:T(8,128)S(1)} %get-tuple-element.28), channel_id=1, source_target_pairs={{4,0},{5,1},{6,2},{7,3},{8,4},{9,5},{10,6},{11,7},{12,8},{13,9},{1... | collective-permute-start | bytes 393224 | tf_op jit(solution)/shard_map/ppermute | solution.py:448
  7.7 11.5 %copy-start = (f32[15,8,128]{2,1,0:T(8,128)S(1)}, f32[15,8,128]{2,1,0:T(8,128)}, u32[]{:S(2)}) copy-start(f32[15,8,128]{2,1,0:T(8,128)} %constant.2.clone.coef_ref) | copy-start | bytes 184324
  7.7 11.2 %collective-permute-start.2 = (f32[2,128,128]{2,1,0:T(8,128)S(1)}, f32[2,128,128]{2,1,0:T(8,128)S(1)}, u32[]{:S(2)}, u32[]{:S(2)}) collective-permute-start(f32[2,128,128]{2,1,0:T(8,128)S(1)} %get-tuple-element.29), channel_id=1, source_target_pairs={{28,0},{29,1},{30,2},{31,3},{0,4},{1,5},{2,6},{3,7},{4,8},{5,9},{6... | collective-permute-start | bytes 393224 | tf_op jit(solution)/shard_map/ppermute | solution.py:448
  12.9 5.9 %collective-permute-start = (f32[3,32,2,128]{3,2,1,0:T(2,128)S(1)}, f32[3,32,2,128]{3,2,1,0:T(2,128)S(1)}, u32[]{:S(2)}, u32[]{:S(2)}) collective-permute-start(f32[3,32,2,128]{3,2,1,0:T(2,128)S(1)} %get-tuple-element.15), channel_id=1, source_target_pairs={{3,0},{0,1},{1,2},{2,3},{7,4},{4,5},{5,6},{6,7},{11,8},{8,9},{9,10... | collective-permute-start | bytes 294920 | tf_op jit(solution)/shard_map/ppermute | solution.py:448
  13.0 5.9 %collective-permute-start.1 = (f32[3,32,2,128]{3,2,1,0:T(2,128)S(1)}, f32[3,32,2,128]{3,2,1,0:T(2,128)S(1)}, u32[]{:S(2)}, u32[]{:S(2)}) collective-permute-start(f32[3,32,2,128]{3,2,1,0:T(2,128)S(1)} %get-tuple-element.16), channel_id=1, source_target_pairs={{1,0},{2,1},{3,2},{0,3},{5,4},{6,5},{7,6},{4,7},{9,8},{10,9},{11,1... | collective-permute-start | bytes 294920 | tf_op jit(solution)/shard_map/ppermute | solution.py:448
  14.7 4.1 %collective-permute-start.4 = (f32[8,128]{1,0:T(8,128)S(1)}, f32[8,128]{1,0:T(8,128)S(1)}, u32[]{:S(2)}, u32[]{:S(2)}) collective-permute-start(f32[8,128]{1,0:T(8,128)S(1)} %get-tuple-element.17.pay_ref), channel_id=1, source_target_pairs={{2,0},{3,1},{0,2},{1,3},{6,4},{7,5},{4,6},{5,7},{10,8},{11,9},{8,1... | collective-permute-start | bytes 12296 | tf_op jit(solution)/shard_map/ppermute | solution.py:448
  19.1 5.2 %collective-permute-start.5 = (f32[128,128]{1,0:T(8,128)S(1)}, f32[128,128]{1,0:T(8,128)S(1)}, u32[]{:S(2)}, u32[]{:S(2)}) collective-permute-start(f32[128,128]{1,0:T(8,128)S(1)} %get-tuple-element.21), channel_id=1, source_target_pairs={{16,0},{17,1},{18,2},{19,3},{20,4},{21,5},{22,6},{23,7},{24,8},{25... | collective-permute-start | bytes 196616 | tf_op jit(solution)/shard_map/ppermute | solution.py:448
  24.5 7.2 %collective-permute-start.8 = (f32[8,128]{1,0:T(8,128)S(1)}, f32[8,128]{1,0:T(8,128)S(1)}, u32[]{:S(2)}, u32[]{:S(2)}) collective-permute-start(f32[8,128]{1,0:T(8,128)S(1)} %with_partner.1._.refs_0_), channel_id=1, source_target_pairs={{24,0},{25,1},{26,2},{27,3},{28,4},{29,5},{30,6},{31,7},{0,8},{1,9... | collective-permute-start | bytes 12296 | tf_op jit(solution)/shard_map/ppermute | solution.py:448
  24.5 7.1 %collective-permute-start.7 = (f32[8,128]{1,0:T(8,128)S(1)}, f32[8,128]{1,0:T(8,128)S(1)}, u32[]{:S(2)}, u32[]{:S(2)}) collective-permute-start(f32[8,128]{1,0:T(8,128)S(1)} %with_partner.1._.refs_0_), channel_id=1, source_target_pairs={{4,0},{5,1},{6,2},{7,3},{8,4},{9,5},{10,6},{11,7},{12,8},{13,9},{1... | collective-permute-start | bytes 12296 | tf_op jit(solution)/shard_map/ppermute | solution.py:448
  29.3 6.4 %collective-permute-start.6 = (f32[8,128]{1,0:T(8,128)S(1)}, f32[8,128]{1,0:T(8,128)S(1)}, u32[]{:S(2)}, u32[]{:S(2)}) collective-permute-start(f32[8,128]{1,0:T(8,128)S(1)} %with_partner.1._.refs_0_), channel_id=1, source_target_pairs={{28,0},{29,1},{30,2},{31,3},{0,4},{1,5},{2,6},{3,7},{4,8},{5,9},{6... | collective-permute-start | bytes 12296 | tf_op jit(solution)/shard_map/ppermute | solution.py:448
  35.7 19.9 %collective-permute-start.9 = (f32[2,2,128,128]{3,2,1,0:T(8,128)S(1)}, f32[2,2,128,128]{3,2,1,0:T(8,128)S(1)}, u32[]{:S(2)}, u32[]{:S(2)}) collective-permute-start(f32[2,2,128,128]{3,2,1,0:T(8,128)S(1)} %get-tuple-element.24), channel_id=1, source_target_pairs={{28,0},{29,1},{30,2},{31,3},{0,4},{1,5},{2,6},{3,7},{4,8},{5,9},{6... | collective-permute-start | bytes 786440 | tf_op jit(solution)/shard_map/ppermute | solution.py:448
  35.8 19.8 %collective-permute-start.10 = (f32[2,2,128,128]{3,2,1,0:T(8,128)S(1)}, f32[2,2,128,128]{3,2,1,0:T(8,128)S(1)}, u32[]{:S(2)}, u32[]{:S(2)}) collective-permute-start(f32[2,2,128,128]{3,2,1,0:T(8,128)S(1)} %get-tuple-element.25), channel_id=1, source_target_pairs={{4,0},{5,1},{6,2},{7,3},{8,4},{9,5},{10,6},{11,7},{12,8},{13,9},{1... | collective-permute-start | bytes 786440 | tf_op jit(solution)/shard_map/ppermute | solution.py:448

commit v8 on v6

--- a/solution.py
+++ b/solution.py
@@ -119,9 +119,12 @@
         return over, along
 
     def below(n):
+        if ghost is not None and n > 0 and q % 2 == 0:
+            x = jnp.where(last_lane, ghost(n, q + 1), at(n, q))
+            return pltpu.roll(x, 1, 1)
         x = turned(1, n, q)
         if ghost is not None:
-            return jnp.where(first_lane, ghost(n), x)
+            return jnp.where(first_lane, ghost(n, q), x)
         return x if n == 0 else jnp.where(first_lane, 0.0, x)
 
     def above(n):
@@ -161,16 +164,13 @@
     return h_r, h_t, h_z
 
 
-def lane_zero_terms(vel, ghost, coef, j, k, dr):
-    def at(dj, dk):
-        return vel[0, j + HALO + dj, pl.ds(k + PAD + dk, 8), :]
-
+def lane_zero_terms(cells, ghost, coef, q, dr):
     lap = VISCOSITY / dr**2
-    a = at(0, 0)
+    a = cells.at(0, q)
     first_lane = lax.broadcasted_iota(jnp.int32, a.shape, 1) == 0
-    add_r = ghost(0) * (lap - coef[RADIAL_F] + a * (0.5 / dr))
-    add_t = ghost(1) * (lap - coef[RADIAL_C] + (a + at(1, 0)) * (0.125 / dr))
-    add_z = ghost(2) * (lap - coef[RADIAL_C] + (a + at(0, 1)) * (0.125 / dr))
+    add_r = ghost(0, q) * (lap - coef[RADIAL_F] + a * (0.5 / dr))
+    add_t = ghost(1, q) * (lap - coef[RADIAL_C] + (a + cells.at(0, q + 1)) * (0.125 / dr))
+    add_z = ghost(2, q) * (lap - coef[RADIAL_C] + (a + cells.at(0, q, 1)) * (0.125 / dr))
     return tuple(jnp.where(first_lane, x, 0.0) for x in (add_r, add_t, add_z))
 
 
@@ -247,16 +247,20 @@
     lax.fori_loop(0, axial // 8, rows, 0)
 
 
-def fold(low_ref, high_ref, pay_ref, vel_in, _, out_ref, vel_ref):
+def fold(low_ref, high_ref, pay_ref, inner_in, vel_in, *refs):
     del vel_in
-    planes, radial = low_ref.shape[1], low_ref.shape[3]
-    axial = vel_ref.shape[2] - 2 * PAD
+    fars, (inner_ref, vel_ref) = refs[:-2], refs[-2:]
+    planes = low_ref.shape[1]
+    axial, radial = inner_in.shape
     lane = lax.broadcasted_iota(jnp.int32, (1, radial), 1)
     top = jnp.maximum(low_ref[0, 0, 0:1, :], high_ref[0, 0, 0:1, :])
     top = jnp.max(jnp.where(lane == radial - 1, top, 0.0), axis=(0, 1), keepdims=True)
-    out_ref[...] = jnp.maximum(pay_ref[...], top)
-    out_ref[1:2, :] = high_ref[1, planes - 1, 0:1, :]
-    out_ref[2:3, :] = low_ref[2, 0, 1:2, :]
+    top = jnp.maximum(pay_ref[...], top)
+    for far in fars:
+        top = jnp.maximum(top, far[...])
+    lane = lax.broadcasted_iota(jnp.int32, top.shape, 1)
+    inner_ref[...] = inner_in[...]
+    inner_ref[0:8, :] = jnp.where(lane == radial - 1, top, inner_in[0:8, :])
     wall = wall_mask(2, radial)
 
     def plane(j, carry):
@@ -269,145 +273,143 @@
     lax.fori_loop(0, planes, plane, 0, unroll=4)
 
 
-def largest_along_ax(pay_ref, *refs):
-    (inner_in, inner_ref), fars = (refs[-6], refs[-1]), refs[:-6]
-    top = pay_ref[0:1, :]
-    for far in fars:
-        top = jnp.maximum(top, far[0:1, :])
+def theta_in(below_ref, above_ref, inner_in, vel_in, _, tile_ref, inner_ref, vel_ref):
+    del vel_in
+    planes = vel_ref.shape[1] - 2 * HALO
+    axial, radial = inner_in.shape
+    cells = pl.ds(PAD, axial)
+    wall = wall_mask(1, radial)
+    for q in range(HALO):
+        for ref, place in ((below_ref, q), (above_ref, HALO + planes + q)):
+            vel_ref[0, place, cells, :] = ref[0, q] * wall
+            vel_ref[1, place, cells, :] = ref[1, q]
+            vel_ref[2, place, cells, :] = ref[2, q]
+    tile_ref[...] = jnp.zeros_like(tile_ref)
+    tile_ref[1:2, :] = below_ref[1, HALO - 1, 0:1, :]
+    tile_ref[2:3, :] = above_ref[2, 0, axial - 1 : axial, :]
     inner_ref[...] = inner_in[...]
-    lane = lax.broadcasted_iota(jnp.int32, top.shape, 1)
-    inner_ref[0:1, :] = jnp.where(lane == top.shape[1] - 1, top, inner_ref[0:1, :])
-
-
-def largest_with_partner(pay_ref, mine_ref, inner_ref, _, out_ref):
+
+
+def corners_in(mine_ref, inner_ref, next_ref, back_ref, vel_in, _, top_ref, vel_ref):
+    del vel_in
+    planes = vel_ref.shape[1] - 2 * HALO
+    axial, radial = inner_ref.shape
+    vel_ref[1, HALO - 1, PAD + axial : PAD + axial + 1, :] = next_ref[1:2, :]
+    vel_ref[2, HALO + planes, PAD - 1 : PAD, :] = back_ref[2:3, :]
+    lane = lax.broadcasted_iota(jnp.int32, (1, radial), 1)
     top = jnp.maximum(mine_ref[0:1, :], inner_ref[0:1, :])
-    lane = lax.broadcasted_iota(jnp.int32, top.shape, 1)
-    top = jnp.max(jnp.where(lane == top.shape[1] - 1, top, 0.0), axis=(0, 1), keepdims=True)
-    row = lax.broadcasted_iota(jnp.int32, out_ref.shape, 0)
-    out_ref[...] = jnp.where(row == 0, top, pay_ref[...])
-
-
-def ghosts(inner, planes, j):
+    top = jnp.max(jnp.where(lane == radial - 1, top, 0.0), axis=(0, 1), keepdims=True)
+    top_ref[...] = jnp.broadcast_to(top, top_ref.shape)
+
+
+def ghosts(cells, inner, planes):
     radial = inner.shape[1]
 
-    def ghost(component):
-        turn = lax.rem(2 * radial - component * planes - j, radial)
-        return pltpu.roll(inner, turn, 1)
+    def ghost(n, q):
+        turn = -(n * planes + q + cells.j) % radial
+        return cells.once(("ghost", n, q), lambda: pltpu.roll(inner, turn, 1) if turn else inner)
 
     return ghost
 
 
-def sweep(vel_ref, inner_ref, coef_ref, first, last, write):
+def block_terms(vel_ref, inner_ref, coef_ref, j, size, write):
     planes = vel_ref.shape[1] - 2 * HALO
     axial, radial = vel_ref.shape[2] - 2 * PAD, vel_ref.shape[3]
-    size = math.gcd(BLOCK, last - first)
-
-    def block(m, carry):
-        j = first + m * size
-
-        def rows(i, carry):
-            k = pl.multiple_of(i * 8, 8)
-            coef = [coef_ref[n] for n in range(COUNT)]
+    groups = 2 * BLOCK // size
+
+    def rows(i, carry):
+        coef = [coef_ref[n] for n in range(COUNT)]
+        found = []
+        for u in range(groups):
+            k = pl.multiple_of((i * groups + u) * 8, 8)
             cells = Cells(vel_ref, j, k)
-            inner = None if inner_ref is None else inner_ref[pl.ds(k, 8), :]
-            found = []
+            ghost = None
+            if inner_ref is not None:
+                ghost = ghosts(cells, inner_ref[pl.ds(k, 8), :], planes)
             for q in range(size):
-                ghost = None if inner is None else ghosts(inner, planes, j + q)
-                found.append(terms(cells, ghost, coef, q, 1.0 / radial))
-            for q, values in enumerate(found):
-                for n, value in enumerate(values):
-                    write(n, j + q, pl.ds(k, 8), value)
-            return carry
-
-        return lax.fori_loop(0, axial // 8, rows, carry)
-
-    lax.fori_loop(0, (last - first) // size, block, 0)
-
-
-def interior(first, last, vel_ref, coef_ref, _, out_ref):
+                found.append((q, k, terms(cells, ghost, coef, q, 1.0 / radial)))
+        for q, k, values in found:
+            for n, value in enumerate(values):
+                write(n, j + q, pl.ds(k, 8), value)
+        return carry
+
+    lax.fori_loop(0, axial // (8 * groups), rows, 0)
+
+
+def ahead(first, last, vel_ref, coef_ref, _, out_ref):
     def write(n, j, k, value):
         out_ref[n, j - first, k, :] = value
 
-    sweep(vel_ref, None, coef_ref, first, last, write)
-
-
-def finish(
-    spans,
-    below_ref,
-    above_ref,
-    up_ref,
-    down_ref,
-    pay_ref,
-    far_refs,
-    inner_ref,
-    coef_ref,
-    parts,
-    out_ref,
-    step_ref,
-    vel_ref,
-    res,
-    sems,
-):
+    def block(m, carry):
+        block_terms(vel_ref, None, coef_ref, first + m * BLOCK, BLOCK, write)
+        return carry
+
+    lax.fori_loop(0, (last - first) // BLOCK, block, 0)
+
+
+def rest(first, last, vel_ref, inner_ref, coef_ref, _, out_ref):
+    planes = vel_ref.shape[1] - 2 * HALO
+    runs = [(j, BLOCK, j - first) for j in range(first, last, BLOCK)]
+    runs += [(0, HALO, last - first), (planes - HALO, HALO, last - first + HALO)]
+    for j, size, place in runs:
+
+        def write(n, plane, k, value, shift=place - j):
+            out_ref[n, plane + shift, k, :] = value
+
+        block_terms(vel_ref, inner_ref, coef_ref, j, size, write)
+
+
+def finish(spans, count, vel_ref, inner_ref, coef_ref, part_a, part_b, part_c, *refs):
+    tops, (out_ref, step_ref, res, sems) = refs[:count], refs[count:]
     axial, radial = inner_ref.shape
-    planes = res.shape[1]
-    top = pay_ref[0:1, :]
-    for ref in (up_ref, down_ref, *far_refs):
+    planes = vel_ref.shape[1] - 2 * HALO
+    top = tops[0][0:1, :]
+    for ref in tops[1:]:
         top = jnp.maximum(top, ref[0:1, :])
     time_step = CFL_TARGET / (jnp.max(top) + 1e-06)
     step_ref[0] = time_step
     scale = GAMMA * time_step
-
-    def store(j):
-        return pltpu.make_async_copy(res.at[:, j], out_ref.at[:, j], sems.at[j])
-
-    def send(first, last):
-        def start(j, carry):
-            store(j).start()
+    factors = (scale * coef_ref[WALL], scale, scale)
+    pending = []
+
+    def complete(part, j, size, place, add):
+        groups = 2 * BLOCK // size
+
+        def rows(i, carry):
+            found = []
+            for u in range(groups):
+                k = pl.multiple_of((i * groups + u) * 8, 8)
+                cells = Cells(vel_ref, j, k)
+                ghost = ghosts(cells, inner_ref[pl.ds(k, 8), :], planes) if add else None
+                for q in range(size):
+                    values = [part[n, place + q, pl.ds(k, 8), :] for n in range(3)]
+                    if add:
+                        added = lane_zero_terms(cells, ghost, coef_ref, q, 1.0 / radial)
+                        values = [x + y for x, y in zip(values, added)]
+                    found.append((q, k, values))
+            for q, k, values in found:
+                for n, value in enumerate(values):
+                    res[n, j + q, pl.ds(k, 8), :] = value * factors[n]
             return carry
 
-        lax.fori_loop(first, last, start, 0)
-
-    def write(n, j, k, value):
-        factor = scale * coef_ref[WALL] if n == 0 else scale
-        res[n, j, k, :] = value * factor
-
-    for part, (first, last) in zip(parts, spans):
-
-        def plane(j, carry, part=part, first=first):
-            def rows(i, carry):
-                k = pl.multiple_of(i * 8, 8)
-                ghost = ghosts(inner_ref[pl.ds(k, 8), :], planes, j)
-                added = lane_zero_terms(vel_ref, ghost, coef_ref, j, k, 1.0 / radial)
-                for n, value in enumerate(added):
-                    write(n, j, pl.ds(k, 8), part[n, j - first, pl.ds(k, 8), :] + value)
-                return carry
-
-            lax.fori_loop(0, axial // 8, rows, carry, unroll=UNROLL)
-            store(j).start()
-            return carry
-
-        lax.fori_loop(first, last, plane, 0)
-
-    sweep(vel_ref, inner_ref, coef_ref, *spans[-1], write)
-    send(*spans[-1])
-
-    cells = pl.ds(PAD, axial)
-    for q in range(HALO):
-        for ref, place in ((below_ref, q), (above_ref, HALO + planes + q)):
-            vel_ref[0, place, cells, :] = ref[0, q] * coef_ref[WALL, 0:1, :]
-            vel_ref[1, place, cells, :] = ref[1, q]
-            vel_ref[2, place, cells, :] = ref[2, q]
-    vel_ref[1, HALO - 1, PAD + axial : PAD + axial + 1, :] = up_ref[1:2, :]
-    vel_ref[2, HALO + planes, PAD - 1 : PAD, :] = down_ref[2:3, :]
-    for first in (0, planes - HALO):
-        sweep(vel_ref, inner_ref, coef_ref, first, first + HALO, write)
-        send(first, first + HALO)
-
-    def wait(j, carry):
-        store(j).wait()
-        return carry
-
-    lax.fori_loop(0, planes, wait, 0)
+        lax.fori_loop(0, axial // (8 * groups), rows, 0)
+        part_of = pl.ds(j, size)
+        copy = pltpu.make_async_copy(
+            res.at[:, part_of], out_ref.at[:, part_of], sems.at[len(pending)]
+        )
+        copy.start()
+        pending.append(copy)
+
+    first, last = spans[2]
+    for j in range(first, last, BLOCK):
+        complete(part_c, j, BLOCK, j - first, False)
+    complete(part_c, 0, HALO, last - first, False)
+    complete(part_c, planes - HALO, HALO, last - first + HALO, False)
+    for part, (first, last) in ((part_a, spans[0]), (part_b, spans[1])):
+        for j in range(first, last, BLOCK):
+            complete(part, j, BLOCK, j - first, True)
+    for copy in pending:
+        copy.wait()
 
 
 def shifted(block, distance):
@@ -421,19 +423,17 @@
 
 
 def cuts(planes):
-    blocks = (planes - 2 * HALO) // BLOCK
-    ends = [blocks * n // 7 for n in (0, 2, 4, 5, 6)] + [blocks]
-    return [(HALO + BLOCK * m, HALO + BLOCK * n) for m, n in zip(ends[:-1], ends[1:])]
-
-
-def doublings(count, known):
-    covered = {i % count for i in known}
-    plan = []
-    while len(covered) < count:
-        best = max(range(1, count), key=lambda s: len(covered | {(i + s) % count for i in covered}))
-        covered |= {(i + best) % count for i in covered}
-        plan.append(best)
-    return plan
+    ends = (HALO, planes - HALO - 2 * BLOCK, planes - HALO - BLOCK, planes - HALO)
+    return list(zip(ends[:-1], ends[1:]))
+
+
+def exchanged(block, step):
+    sizes = lax.axis_size("az"), lax.axis_size("ax")
+    route = []
+    for i in range(sizes[0]):
+        for k in range(sizes[1]):
+            route.append(((i ^ step) * sizes[1] + k, i * sizes[1] + k))
+    return lax.ppermute(block, ("az", "ax"), route)
 
 
 def per_device(velocity):
@@ -463,6 +463,7 @@
 
     edge = shape(3, planes, 2, radial)
     padded = shape(3, planes + 2 * HALO, axial + 2 * PAD, radial)
+    row = shape(axial, radial)
     tile = shape(8, radial)
     vel, first, last, pay = call(
         functools.partial(first_pass, theta_step),
@@ -475,99 +476,85 @@
     )(pltpu.with_memory_space_constraint(velocity, pltpu.HBM))
     low = shifted(last, (0, 1))
     high = shifted(first, (0, -1))
+    fars = [shifted(pay, (0, step)) for step in range(2, sizes[1] - 1)]
     inner = call(
         pack,
         "pack",
         velocity.size,
-        out_shape=shape(axial, radial),
+        out_shape=row,
         in_specs=[vmem],
         out_specs=vmem,
     )(vel)
-    pay, vel = call(
+    mine, vel = call(
         fold,
         "fold",
         0,
-        out_shape=(tile, padded),
-        in_specs=[vmem] * 5,
-        out_specs=(vmem, vmem),
-        input_output_aliases={3: 1},
-    )(low, high, pay, vel, inner)
-    top, fars = pay, []
-    for step in doublings(sizes[1], (0, 1, -1)):
-        fars.append(shifted(top, (0, step)))
-        top = jnp.maximum(top, fars[-1])
+        out_shape=(row, padded),
+        in_specs=[vmem] * (5 + len(fars)),
+        out_specs=(vmem,) * 2,
+        input_output_aliases={4: 1},
+    )(low, high, pay, inner, vel, *fars)
 
     spans = cuts(planes)
-    parts = []
-
-    def inside(n, token):
+
+    def in_advance(n, vel, token):
         first, last = spans[n]
-        part = call(
-            functools.partial(interior, first, last),
-            f"interior_{n}",
-            velocity.size,
+        return call(
+            functools.partial(ahead, first, last),
+            f"ahead_{n}",
+            velocity.size * (2 - n),
             out_shape=shape(3, last - first, axial, radial),
             in_specs=[vmem] * 3,
             out_specs=vmem,
         )(vel, coef, token)
-        parts.append(part)
-
-    inside(0, pay)
-    inside(1, pay)
-    mine = call(
-        largest_along_ax,
-        "largest_along_ax",
+
+    part_a = in_advance(0, vel, mine)
+    tile_out, mine, vel = call(
+        theta_in,
+        "theta_in",
         0,
-        out_shape=shape(axial, radial),
-        in_specs=[vmem] * (6 + len(fars)),
-        out_specs=vmem,
-    )(pay, *fars, inner, below, above, *parts)
-    inner = shifted(mine, (sizes[0] // 2, 0))
-    inside(2, mine)
-    pay = call(
-        largest_with_partner,
-        "largest_with_partner",
+        out_shape=(tile, row, padded),
+        in_specs=[vmem] * 5,
+        out_specs=(vmem,) * 3,
+        input_output_aliases={3: 2},
+    )(below, above, mine, vel, part_a)
+    inner = exchanged(mine, sizes[0] // 2)
+    following = shifted(tile_out, (0, -1))
+    preceding = shifted(tile_out, (0, 1))
+    part_b = in_advance(1, vel, tile_out)
+    top, vel = call(
+        corners_in,
+        "corners_in",
         0,
-        out_shape=tile,
+        out_shape=(tile, padded),
+        in_specs=[vmem] * 6,
+        out_specs=(vmem,) * 2,
+        input_output_aliases={4: 1},
+    )(mine, inner, following, preceding, vel, part_b)
+    tops = (top, *(exchanged(top, step) for step in range(1, sizes[0] // 2)))
+    first, last = spans[2]
+    part_c = call(
+        functools.partial(rest, first, last),
+        "rest",
+        velocity.size,
+        out_shape=shape(3, last - first + 2 * HALO, axial, radial),
         in_specs=[vmem] * 4,
         out_specs=vmem,
-    )(pay, mine, inner, parts[2])
-    up = shifted(pay, (1, 0))
-    down = shifted(pay, (-1, 0))
-    around = [(i, 0) for i in (0, sizes[0] // 2)]
-    near = {(i + s) % sizes[0] for i, _ in around for s in (-1, 0, 1)}
-    others = []
-    while len(near) < sizes[0]:
-        step = min(set(range(sizes[0])) - near)
-        others.append(shifted(pay, (step, 0)))
-        near |= {(i + step) % sizes[0] for i, _ in around}
-    inside(3, pay)
-
-    def last_kernel(*refs):
-        ins, parts_in, rest = refs[:5], refs[5 : 5 + len(others)], refs[5 + len(others) :]
-        inner_ref, coef_ref, *rest = rest
-        parts_refs, rest = rest[: len(parts)], rest[len(parts) :]
-        _, out_ref, step_ref, vel_ref, res, sems = rest
-        finish(
-            spans, *ins, parts_in, inner_ref, coef_ref, parts_refs, out_ref, step_ref, vel_ref,
-            res, sems,
-        )
-
-    count = 7 + len(others) + len(parts)
-    increment, time_step, _ = call(
-        last_kernel,
+    )(vel, inner, coef, top)
+    return_shape = shape(*velocity.shape)
+    increment, time_step = call(
+        functools.partial(finish, spans, len(tops)),
         "finish",
         0,
         scratch=8,
-        out_shape=(shape(*velocity.shape), shape(1), padded),
-        in_specs=[vmem] * (count + 1),
-        out_specs=(anywhere, smem, vmem),
+        out_shape=(return_shape, shape(1)),
+        in_specs=[vmem] * (6 + len(tops)),
+        out_specs=(anywhere, smem),
         scratch_shapes=[
             pltpu.VMEM(velocity.shape, f32),
-            pltpu.SemaphoreType.DMA((planes,)),
+            pltpu.SemaphoreType.DMA(((planes - 2 * HALO) // BLOCK + 2,)),
         ],
-        input_output_aliases={count: 2},
-    )(below, above, up, down, pay, *others, inner, coef, *parts, vel)
+    )(vel, inner, coef, part_a, part_b, part_c, *tops)
     return increment, time_step.reshape(())
 
 

time: 56.7 us -> 43.6 us (0.77)
  Pallas kernels: 32.6 us -> 23.5 us
  waiting for transfers between devices: 7.66 us -> 1.82 us
  starting transfers between devices: 14.4 us -> 16.2 us
    pallas_call x9 -> x8, Pallas kernels: 29.5 us -> 20.4 us  [the longest x2 7.79 us: in_advance(): call(functools.partial(ahead, first, last), f'ahead_{n}', velocity.size *...]
    ppermute x9 -> x7, waiting for transfers between devices: 7.66 us -> 0.04 us  [shifted(): return lax.ppermute(block, ('az', 'ax'), route)]
    ppermute x0 -> x4, starting transfers between devices: none -> 5.06 us  [exchanged(): return lax.ppermute(block, ('az', 'ax'), route)]
    ppermute x9 -> x7, starting transfers between devices: 14.4 us -> 11.1 us  [shifted(): return lax.ppermute(block, ('az', 'ax'), route)]
    ppermute x0 -> x4, waiting for transfers between devices: none -> 1.79 us  [exchanged(): return lax.ppermute(block, ('az', 'ax'), route)]
  transfers between devices with their start and end apart: 9 -> 11, of which waited for: 2 -> 2; matrix products, arithmetic and copies ran while one was open for 0% -> 0% of each run, Pallas kernels for 30% -> 39%
where the time goes in v8:
time: 43.6 us; the launch traced here: 43.4 us
  Pallas kernels  23.5 us (54%)
  starting transfers between devices  16.2 us (37%)
  waiting for transfers between devices  1.82 us (4%)
  local copies, waits for them, and re-layouts  1.18 us (3%)
  between operations  0.78 us (2%)
    ppermute x7, starting transfers between devices, shifted(): return lax.ppermute(block, ('az', 'ax'), route)  11.1 us
    pallas_call x2, Pallas kernels, in_advance(): call(functools.partial(ahead, first, last), f'ahead_{n}', velocity.size *...  7.79 us
    pallas_call x1, Pallas kernels, per_device(): call(functools.partial(finish, spans, len(tops)), 'finish', 0, scratch=8,...  6.44 us
    ppermute x4, starting transfers between devices, exchanged(): return lax.ppermute(block, ('az', 'ax'), route)  5.06 us
    pallas_call x1, Pallas kernels, per_device(): call(functools.partial(first_pass, theta_step), 'first_pass', 0, out_shap...  3.1 us
    pallas_call x1, Pallas kernels, per_device(): call(functools.partial(rest, first, last), 'rest', velocity.size, out_sha...  3.01 us
    pallas_call x1, Pallas kernels, per_device(): call(pack, 'pack', velocity.size, out_shape=row, in_specs=[vmem], out_spe...  2.73 us
    ppermute x4, waiting for transfers between devices, exchanged(): return lax.ppermute(block, ('az', 'ax'), route)  1.79 us
  transfers between devices with their start and end apart: 11, of which 2 were waited for; matrix products, arithmetic and copies ran while one was open for 0% of the time, Pallas kernels for 39%

profile of v8, /device:TPU:0, one launch (start us, length us, event | category | flops | bytes accessed | tf_op | source)
XLA Modules:
  0.0 43.4 jit_solution(14759639600540089525)
XLA Ops:
  0.6 1.2 %fusion = (f32[3,2,128,128]{3,2,1,0:T(8,128)S(1)}, f32[3,2,128,128]{3,2,1,0:T(8,128)S(1)}) fusion(f32[3,32,128,128]{3,2,1,0:T(8,128)} %v_ref.1), kind=kLoop, calls=%fused_computation | loop fusion | bytes 1572864 | tf_op jit(solution)/shard_map/slice | solution.py:462
  1.8 6.1 %collective-permute-start.1 = (f32[3,2,128,128]{3,2,1,0:T(8,128)S(1)}, f32[3,2,128,128]{3,2,1,0:T(8,128)S(1)}, u32[]{:S(2)}, u32[]{:S(2)}) collective-permute-start(f32[3,2,128,128]{3,2,1,0:T(8,128)S(1)} %get-tuple-element.28), channel_id=1, source_target_pairs={{4,0},{5,1},{6,2},{7,3},{8,4},{9,5},{10,6},{11,7},{12,8},{13,9},{1... | collective-permute-start | bytes 1179656 | tf_op jit(solution)/shard_map/ppermute | solution.py:422
  7.9 0.0 collective-permute-start
  7.9 3.1 %first_pass.1 = (f32[3,36,144,128]{3,2,1,0:T(8,128)S(1)}, f32[3,32,2,128]{3,2,1,0:T(2,128)S(1)}, f32[3,32,2,128]{3,2,1,0:T(2,128)S(1)}, f32[8,128]{1,0:T(8,128)S(1)}) custom-call(f32[3,32,128,128]{3,2,1,0:T(8,128)} %v_ref.1), custom_call_target="tpu_custom_call" | custom-call | tf_op jit(solution)/shard_map/first_pass/pallas_call | solution.py:468
  11.0 0.1 collective-permute-start.2
  11.0 1.7 %collective-permute-start.3 = (f32[3,32,2,128]{3,2,1,0:T(2,128)S(1)}, f32[3,32,2,128]{3,2,1,0:T(2,128)S(1)}, u32[]{:S(2)}, u32[]{:S(2)}) collective-permute-start(f32[3,32,2,128]{3,2,1,0:T(2,128)S(1)} %get-tuple-element.16), channel_id=1, source_target_pairs={{1,0},{2,1},{3,2},{0,3},{5,4},{6,5},{7,6},{4,7},{9,8},{10,9},{11,1... | collective-permute-start | bytes 294920 | tf_op jit(solution)/shard_map/ppermute | solution.py:422
  12.8 1.5 %collective-permute-start.4 = (f32[8,128]{1,0:T(8,128)S(1)}, f32[8,128]{1,0:T(8,128)S(1)}, u32[]{:S(2)}, u32[]{:S(2)}) collective-permute-start(f32[8,128]{1,0:T(8,128)S(1)} %get-tuple-element.17.pay_ref), channel_id=1, source_target_pairs={{2,0},{3,1},{0,2},{1,3},{6,4},{7,5},{4,6},{5,7},{10,8},{11,9},{8,1... | collective-permute-start | bytes 12296 | tf_op jit(solution)/shard_map/ppermute | solution.py:422
  14.3 0.0 copy-start
  14.3 2.7 %pack.1.inner_in = f32[128,128]{1,0:T(8,128)S(1)} custom-call(f32[3,36,144,128]{3,2,1,0:T(8,128)S(1)} %get-tuple-element.18.vel_ref.vel_in), custom_call_target="tpu_custom_call" | custom-call | flops 1572864 | bytes 1572864 | tf_op jit(solution)/shard_map/pack/pallas_call | solution.py:480
  17.0 0.0 collective-permute-done.4.refs_0_
  17.0 0.0 collective-permute-done.2.low_ref
  17.0 0.0 collective-permute-done.3.high_ref
  17.0 0.2 fold.1
  17.3 0.0 copy-done
  17.3 6.5 %ahead_0.1._.part_a = f32[3,20,128,128]{3,2,1,0:T(8,128)S(1)} custom-call(f32[3,36,144,128]{3,2,1,0:T(8,128)S(1)} %get-tuple-element.20.vel_ref.vel_in, f32[15,8,128]{2,1,0:T(8,128)S(1)} %copy-done, f32[128,128]{1,0:T(8,128)S(1)} %get-tuple-element.19._.inner_in), custom_call_target="tpu_custom_call" | custom-call | flops 3145728 | bytes 3145728 | tf_op jit(solution)/shard_map/ahead_0/pallas_call | solution.py:502
  23.8 0.0 collective-permute-done.1.above_ref
  23.8 0.0 collective-permute-done.below_ref
  23.8 0.1 theta_in.1
  23.9 1.4 %collective-permute-start.5 = (f32[128,128]{1,0:T(8,128)S(1)}, f32[128,128]{1,0:T(8,128)S(1)}, u32[]{:S(2)}, u32[]{:S(2)}) collective-permute-start(f32[128,128]{1,0:T(8,128)S(1)} %get-tuple-element.21.mine_ref), channel_id=1, source_target_pairs={{16,0},{17,1},{18,2},{19,3},{20,4},{21,5},{22,6},{23,7},{24,8},{25... | collective-permute-start | bytes 196616 | tf_op jit(solution)/shard_map/ppermute | solution.py:436
  25.3 0.0 collective-permute-start.7
  25.3 1.7 %collective-permute-start.6 = (f32[8,128]{1,0:T(8,128)S(1)}, f32[8,128]{1,0:T(8,128)S(1)}, u32[]{:S(2)}, u32[]{:S(2)}) collective-permute-start(f32[8,128]{1,0:T(8,128)S(1)} %get-tuple-element.22._), channel_id=1, source_target_pairs={{1,0},{2,1},{3,2},{0,3},{5,4},{6,5},{7,6},{4,7},{9,8},{10,9},{11,1... | collective-permute-start | bytes 12296 | tf_op jit(solution)/shard_map/ppermute | solution.py:422
  27.1 1.3 %ahead_1.1._.part_b = f32[3,4,128,128]{3,2,1,0:T(8,128)S(1)} custom-call(f32[3,36,144,128]{3,2,1,0:T(8,128)S(1)} %get-tuple-element.23.vel_ref.vel_in, f32[15,8,128]{2,1,0:T(8,128)S(1)} %copy-done, f32[8,128]{1,0:T(8,128)S(1)} %get-tuple-element.22._), custom_call_target="tpu_custom_call" | custom-call | flops 1572864 | bytes 1572864 | tf_op jit(solution)/shard_map/ahead_1/pallas_call | solution.py:502
  28.4 0.0 collective-permute-done.7.back_ref
  28.4 0.0 collective-permute-done.6.next_ref
  28.4 1.2 %collective-permute-done.5.inner_ref = f32[128,128]{1,0:T(8,128)S(1)} collective-permute-done((f32[128,128]{1,0:T(8,128)S(1)}, f32[128,128]{1,0:T(8,128)S(1)}, u32[]{:S(2)}, u32[]{:S(2)}) %collective-permute-start.5) | collective-permute-done | bytes 65568 | tf_op jit(solution)/shard_map/ppermute | solution.py:436
  29.6 0.1 corners_in.1
  29.7 2.8 %collective-permute-start.10 = (f32[8,128]{1,0:T(8,128)S(1)}, f32[8,128]{1,0:T(8,128)S(1)}, u32[]{:S(2)}, u32[]{:S(2)}) collective-permute-start(f32[8,128]{1,0:T(8,128)S(1)} %get-tuple-element.25._.refs_0_), channel_id=1, source_target_pairs={{12,0},{13,1},{14,2},{15,3},{8,4},{9,5},{10,6},{11,7},{4,8},{5,9},... | collective-permute-start | bytes 12296 | tf_op jit(solution)/shard_map/ppermute | solution.py:436
  32.5 0.9 %collective-permute-start.9 = (f32[8,128]{1,0:T(8,128)S(1)}, f32[8,128]{1,0:T(8,128)S(1)}, u32[]{:S(2)}, u32[]{:S(2)}) collective-permute-start(f32[8,128]{1,0:T(8,128)S(1)} %get-tuple-element.25._.refs_0_), channel_id=1, source_target_pairs={{8,0},{9,1},{10,2},{11,3},{12,4},{13,5},{14,6},{15,7},{0,8},{1,9},... | collective-permute-start | bytes 12296 | tf_op jit(solution)/shard_map/ppermute | solution.py:436
  33.4 0.0 collective-permute-start.8
  33.4 3.0 %rest.1.part_c = f32[3,8,128,128]{3,2,1,0:T(8,128)S(1)} custom-call(f32[3,36,144,128]{3,2,1,0:T(8,128)S(1)} %get-tuple-element.24.vel_ref, f32[128,128]{1,0:T(8,128)S(1)} %collective-permute-done.5.inner_ref, f32[15,8,128]{2,1,0:T(8,128)S(1)} %copy-done, f32[8,128]{1,0:T(8,128)S(1)} %get-tuple-element.25._.refs_0_), custom_call_target="tpu_custom_call" | custom-call | flops 1572864 | bytes 1572864 | tf_op jit(solution)/shard_map/rest/pallas_call | solution.py:536
  36.4 0.0 collective-permute-done.10.refs_3_
  36.4 0.0 collective-permute-done.9.refs_2_
  36.4 0.6 %collective-permute-done.8.refs_1_ = f32[8,128]{1,0:T(8,128)S(1)} collective-permute-done((f32[8,128]{1,0:T(8,128)S(1)}, f32[8,128]{1,0:T(8,128)S(1)}, u32[]{:S(2)}, u32[]{:S(2)}) %collective-permute-start.8) | collective-permute-done | bytes 4128 | tf_op jit(solution)/shard_map/ppermute | solution.py:436
  37.0 6.4 %finish.1 = (f32[3,32,128,128]{3,2,1,0:T(8,128)}, f32[1]{0:T(128)}) custom-call(f32[3,36,144,128]{3,2,1,0:T(8,128)S(1)} %get-tuple-element.24.vel_ref, f32[128,128]{1,0:T(8,128)S(1)} %collective-permute-done.5.inner_ref, f32[15,8,128]{2,1,0:T(8,128)S(1)} %copy-done, f32[3,20,128,128]{3,2,1,0:T(8,128)S(1)} %ahead_0.1._.part_a, ...), custom_call_target="tpu_custom_call" | custom-call | tf_op jit(solution)/shard_map/finish/pallas_call | solution.py:545
Async XLA Ops:
  1.8 22.0 %collective-permute-start.1 = (f32[3,2,128,128]{3,2,1,0:T(8,128)S(1)}, f32[3,2,128,128]{3,2,1,0:T(8,128)S(1)}, u32[]{:S(2)}, u32[]{:S(2)}) collective-permute-start(f32[3,2,128,128]{3,2,1,0:T(8,128)S(1)} %get-tuple-element.28), channel_id=1, source_target_pairs={{4,0},{5,1},{6,2},{7,3},{8,4},{9,5},{10,6},{11,7},{12,8},{13,9},{1... | collective-permute-start | bytes 1179656 | tf_op jit(solution)/shard_map/ppermute | solution.py:422
  7.9 15.9 %collective-permute-start = (f32[3,2,128,128]{3,2,1,0:T(8,128)S(1)}, f32[3,2,128,128]{3,2,1,0:T(8,128)S(1)}, u32[]{:S(2)}, u32[]{:S(2)}) collective-permute-start(f32[3,2,128,128]{3,2,1,0:T(8,128)S(1)} %get-tuple-element.29), channel_id=1, source_target_pairs={{28,0},{29,1},{30,2},{31,3},{0,4},{1,5},{2,6},{3,7},{4,8},{5,9},{6... | collective-permute-start | bytes 1179656 | tf_op jit(solution)/shard_map/ppermute | solution.py:422
  11.0 6.0 %collective-permute-start.2 = (f32[3,32,2,128]{3,2,1,0:T(2,128)S(1)}, f32[3,32,2,128]{3,2,1,0:T(2,128)S(1)}, u32[]{:S(2)}, u32[]{:S(2)}) collective-permute-start(f32[3,32,2,128]{3,2,1,0:T(2,128)S(1)} %get-tuple-element.15), channel_id=1, source_target_pairs={{3,0},{0,1},{1,2},{2,3},{7,4},{4,5},{5,6},{6,7},{11,8},{8,9},{9,10... | collective-permute-start | bytes 294920 | tf_op jit(solution)/shard_map/ppermute | solution.py:422
  11.0 6.0 %collective-permute-start.3 = (f32[3,32,2,128]{3,2,1,0:T(2,128)S(1)}, f32[3,32,2,128]{3,2,1,0:T(2,128)S(1)}, u32[]{:S(2)}, u32[]{:S(2)}) collective-permute-start(f32[3,32,2,128]{3,2,1,0:T(2,128)S(1)} %get-tuple-element.16), channel_id=1, source_target_pairs={{1,0},{2,1},{3,2},{0,3},{5,4},{6,5},{7,6},{4,7},{9,8},{10,9},{11,1... | collective-permute-start | bytes 294920 | tf_op jit(solution)/shard_map/ppermute | solution.py:422
  12.8 4.2 %collective-permute-start.4 = (f32[8,128]{1,0:T(8,128)S(1)}, f32[8,128]{1,0:T(8,128)S(1)}, u32[]{:S(2)}, u32[]{:S(2)}) collective-permute-start(f32[8,128]{1,0:T(8,128)S(1)} %get-tuple-element.17.pay_ref), channel_id=1, source_target_pairs={{2,0},{3,1},{0,2},{1,3},{6,4},{7,5},{4,6},{5,7},{10,8},{11,9},{8,1... | collective-permute-start | bytes 12296 | tf_op jit(solution)/shard_map/ppermute | solution.py:422
  14.3 3.0 %copy-start = (f32[15,8,128]{2,1,0:T(8,128)S(1)}, f32[15,8,128]{2,1,0:T(8,128)}, u32[]{:S(2)}) copy-start(f32[15,8,128]{2,1,0:T(8,128)} %constant.2.clone.coef_ref) | copy-start | bytes 184324
  23.9 5.7 %collective-permute-start.5 = (f32[128,128]{1,0:T(8,128)S(1)}, f32[128,128]{1,0:T(8,128)S(1)}, u32[]{:S(2)}, u32[]{:S(2)}) collective-permute-start(f32[128,128]{1,0:T(8,128)S(1)} %get-tuple-element.21.mine_ref), channel_id=1, source_target_pairs={{16,0},{17,1},{18,2},{19,3},{20,4},{21,5},{22,6},{23,7},{24,8},{25... | collective-permute-start | bytes 196616 | tf_op jit(solution)/shard_map/ppermute | solution.py:436
  25.3 3.0 %collective-permute-start.7 = (f32[8,128]{1,0:T(8,128)S(1)}, f32[8,128]{1,0:T(8,128)S(1)}, u32[]{:S(2)}, u32[]{:S(2)}) collective-permute-start(f32[8,128]{1,0:T(8,128)S(1)} %get-tuple-element.22._), channel_id=1, source_target_pairs={{3,0},{0,1},{1,2},{2,3},{7,4},{4,5},{5,6},{6,7},{11,8},{8,9},{9,10... | collective-permute-start | bytes 12296 | tf_op jit(solution)/shard_map/ppermute | solution.py:422
  25.3 3.1 %collective-permute-start.6 = (f32[8,128]{1,0:T(8,128)S(1)}, f32[8,128]{1,0:T(8,128)S(1)}, u32[]{:S(2)}, u32[]{:S(2)}) collective-permute-start(f32[8,128]{1,0:T(8,128)S(1)} %get-tuple-element.22._), channel_id=1, source_target_pairs={{1,0},{2,1},{3,2},{0,3},{5,4},{6,5},{7,6},{4,7},{9,8},{10,9},{11,1... | collective-permute-start | bytes 12296 | tf_op jit(solution)/shard_map/ppermute | solution.py:422
  29.7 6.7 %collective-permute-start.10 = (f32[8,128]{1,0:T(8,128)S(1)}, f32[8,128]{1,0:T(8,128)S(1)}, u32[]{:S(2)}, u32[]{:S(2)}) collective-permute-start(f32[8,128]{1,0:T(8,128)S(1)} %get-tuple-element.25._.refs_0_), channel_id=1, source_target_pairs={{12,0},{13,1},{14,2},{15,3},{8,4},{9,5},{10,6},{11,7},{4,8},{5,9},... | collective-permute-start | bytes 12296 | tf_op jit(solution)/shard_map/ppermute | solution.py:436
  32.5 3.9 %collective-permute-start.9 = (f32[8,128]{1,0:T(8,128)S(1)}, f32[8,128]{1,0:T(8,128)S(1)}, u32[]{:S(2)}, u32[]{:S(2)}) collective-permute-start(f32[8,128]{1,0:T(8,128)S(1)} %get-tuple-element.25._.refs_0_), channel_id=1, source_target_pairs={{8,0},{9,1},{10,2},{11,3},{12,4},{13,5},{14,6},{15,7},{0,8},{1,9},... | collective-permute-start | bytes 12296 | tf_op jit(solution)/shard_map/ppermute | solution.py:436
  33.4 3.6 %collective-permute-start.8 = (f32[8,128]{1,0:T(8,128)S(1)}, f32[8,128]{1,0:T(8,128)S(1)}, u32[]{:S(2)}, u32[]{:S(2)}) collective-permute-start(f32[8,128]{1,0:T(8,128)S(1)} %get-tuple-element.25._.refs_0_), channel_id=1, source_target_pairs={{4,0},{5,1},{6,2},{7,3},{0,4},{1,5},{2,6},{3,7},{12,8},{13,9},{14,... | collective-permute-start | bytes 12296 | tf_op jit(solution)/shard_map/ppermute | solution.py:436

commit v9 on v8

--- a/solution.py
+++ b/solution.py
@@ -222,9 +222,6 @@
     largest = jnp.maximum(jnp.maximum(m[0], m[1]), jnp.maximum(m[2], m[3]))
     top = jnp.max(largest, axis=(0, 1), keepdims=True)
     pay_ref[...] = jnp.broadcast_to(top, pay_ref.shape)
-    last = lax.broadcasted_iota(jnp.int32, (2, radial), 1) == radial - 1
-    for ref in (low_ref, high_ref):
-        ref[0, 0] = jnp.where(last, top, ref[0, 0])
 
 
 def pack(vel_ref, inner_ref):
@@ -247,20 +244,10 @@
     lax.fori_loop(0, axial // 8, rows, 0)
 
 
-def fold(low_ref, high_ref, pay_ref, inner_in, vel_in, *refs):
+def fold(low_ref, high_ref, vel_in, _, vel_ref):
     del vel_in
-    fars, (inner_ref, vel_ref) = refs[:-2], refs[-2:]
-    planes = low_ref.shape[1]
-    axial, radial = inner_in.shape
-    lane = lax.broadcasted_iota(jnp.int32, (1, radial), 1)
-    top = jnp.maximum(low_ref[0, 0, 0:1, :], high_ref[0, 0, 0:1, :])
-    top = jnp.max(jnp.where(lane == radial - 1, top, 0.0), axis=(0, 1), keepdims=True)
-    top = jnp.maximum(pay_ref[...], top)
-    for far in fars:
-        top = jnp.maximum(top, far[...])
-    lane = lax.broadcasted_iota(jnp.int32, top.shape, 1)
-    inner_ref[...] = inner_in[...]
-    inner_ref[0:8, :] = jnp.where(lane == radial - 1, top, inner_in[0:8, :])
+    planes, radial = low_ref.shape[1], low_ref.shape[3]
+    axial = vel_ref.shape[2] - 2 * PAD
     wall = wall_mask(2, radial)
 
     def plane(j, carry):
@@ -273,8 +260,9 @@
     lax.fori_loop(0, planes, plane, 0, unroll=4)
 
 
-def theta_in(below_ref, above_ref, inner_in, vel_in, _, tile_ref, inner_ref, vel_ref):
+def theta_in(below_ref, above_ref, inner_in, vel_in, *refs):
     del vel_in
+    tile_ref, inner_ref, vel_ref = refs[-3:]
     planes = vel_ref.shape[1] - 2 * HALO
     axial, radial = inner_in.shape
     cells = pl.ds(PAD, axial)
@@ -290,16 +278,11 @@
     inner_ref[...] = inner_in[...]
 
 
-def corners_in(mine_ref, inner_ref, next_ref, back_ref, vel_in, _, top_ref, vel_ref):
+def corners_in(next_ref, back_ref, vel_in, _, vel_ref):
     del vel_in
-    planes = vel_ref.shape[1] - 2 * HALO
-    axial, radial = inner_ref.shape
+    planes, axial = vel_ref.shape[1] - 2 * HALO, vel_ref.shape[2] - 2 * PAD
     vel_ref[1, HALO - 1, PAD + axial : PAD + axial + 1, :] = next_ref[1:2, :]
     vel_ref[2, HALO + planes, PAD - 1 : PAD, :] = back_ref[2:3, :]
-    lane = lax.broadcasted_iota(jnp.int32, (1, radial), 1)
-    top = jnp.maximum(mine_ref[0:1, :], inner_ref[0:1, :])
-    top = jnp.max(jnp.where(lane == radial - 1, top, 0.0), axis=(0, 1), keepdims=True)
-    top_ref[...] = jnp.broadcast_to(top, top_ref.shape)
 
 
 def ghosts(cells, inner, planes):
@@ -359,21 +342,20 @@
         block_terms(vel_ref, inner_ref, coef_ref, j, size, write)
 
 
-def finish(spans, count, vel_ref, inner_ref, coef_ref, part_a, part_b, part_c, *refs):
-    tops, (out_ref, step_ref, res, sems) = refs[:count], refs[count:]
+def finish(
+    spans, vel_ref, inner_ref, coef_ref, part_a, part_b, part_c, top_ref, out_ref, step_ref, res,
+    sems,
+):
     axial, radial = inner_ref.shape
     planes = vel_ref.shape[1] - 2 * HALO
-    top = tops[0][0:1, :]
-    for ref in tops[1:]:
-        top = jnp.maximum(top, ref[0:1, :])
-    time_step = CFL_TARGET / (jnp.max(top) + 1e-06)
+    time_step = CFL_TARGET / (jnp.max(top_ref[0:8, :]) + 1e-06)
     step_ref[0] = time_step
     scale = GAMMA * time_step
     factors = (scale * coef_ref[WALL], scale, scale)
     pending = []
 
     def complete(part, j, size, place, add):
-        groups = 2 * BLOCK // size
+        groups = 4 * BLOCK // size
 
         def rows(i, carry):
             found = []
@@ -423,17 +405,8 @@
 
 
 def cuts(planes):
-    ends = (HALO, planes - HALO - 2 * BLOCK, planes - HALO - BLOCK, planes - HALO)
+    ends = (HALO, planes - HALO - 3 * BLOCK, planes - HALO - BLOCK, planes - HALO)
     return list(zip(ends[:-1], ends[1:]))
-
-
-def exchanged(block, step):
-    sizes = lax.axis_size("az"), lax.axis_size("ax")
-    route = []
-    for i in range(sizes[0]):
-        for k in range(sizes[1]):
-            route.append(((i ^ step) * sizes[1] + k, i * sizes[1] + k))
-    return lax.ppermute(block, ("az", "ax"), route)
 
 
 def per_device(velocity):
@@ -469,14 +442,14 @@
         functools.partial(first_pass, theta_step),
         "first_pass",
         0,
-        out_shape=(padded, edge, edge, tile),
+        out_shape=(padded, edge, edge, row),
         in_specs=[anywhere],
         out_specs=(vmem,) * 4,
         scratch_shapes=[pltpu.SemaphoreType.DMA((planes // GROUP,))],
     )(pltpu.with_memory_space_constraint(velocity, pltpu.HBM))
     low = shifted(last, (0, 1))
     high = shifted(first, (0, -1))
-    fars = [shifted(pay, (0, step)) for step in range(2, sizes[1] - 1)]
+    largest = lax.pmax(pay, ("az", "ax"))
     inner = call(
         pack,
         "pack",
@@ -485,15 +458,15 @@
         in_specs=[vmem],
         out_specs=vmem,
     )(vel)
-    mine, vel = call(
+    vel = call(
         fold,
         "fold",
         0,
-        out_shape=(row, padded),
-        in_specs=[vmem] * (5 + len(fars)),
-        out_specs=(vmem,) * 2,
-        input_output_aliases={4: 1},
-    )(low, high, pay, inner, vel, *fars)
+        out_shape=padded,
+        in_specs=[vmem] * 4,
+        out_specs=vmem,
+        input_output_aliases={2: 0},
+    )(low, high, vel, inner)
 
     spans = cuts(planes)
 
@@ -502,59 +475,58 @@
         return call(
             functools.partial(ahead, first, last),
             f"ahead_{n}",
-            velocity.size * (2 - n),
+            8 * velocity.size,
             out_shape=shape(3, last - first, axial, radial),
             in_specs=[vmem] * 3,
             out_specs=vmem,
         )(vel, coef, token)
 
-    part_a = in_advance(0, vel, mine)
+    part_a = in_advance(0, vel, inner)
     tile_out, mine, vel = call(
         theta_in,
         "theta_in",
         0,
         out_shape=(tile, row, padded),
-        in_specs=[vmem] * 5,
+        in_specs=[vmem] * 6,
         out_specs=(vmem,) * 3,
         input_output_aliases={3: 2},
-    )(below, above, mine, vel, part_a)
-    inner = exchanged(mine, sizes[0] // 2)
+    )(below, above, inner, vel, part_a, largest)
+    inner = shifted(mine, (sizes[0] // 2, 0))
     following = shifted(tile_out, (0, -1))
     preceding = shifted(tile_out, (0, 1))
     part_b = in_advance(1, vel, tile_out)
-    top, vel = call(
+    vel = call(
         corners_in,
         "corners_in",
         0,
-        out_shape=(tile, padded),
-        in_specs=[vmem] * 6,
-        out_specs=(vmem,) * 2,
-        input_output_aliases={4: 1},
-    )(mine, inner, following, preceding, vel, part_b)
-    tops = (top, *(exchanged(top, step) for step in range(1, sizes[0] // 2)))
+        out_shape=padded,
+        in_specs=[vmem] * 4,
+        out_specs=vmem,
+        input_output_aliases={2: 0},
+    )(following, preceding, vel, part_b)
     first, last = spans[2]
     part_c = call(
         functools.partial(rest, first, last),
         "rest",
-        velocity.size,
+        0,
         out_shape=shape(3, last - first + 2 * HALO, axial, radial),
         in_specs=[vmem] * 4,
         out_specs=vmem,
-    )(vel, inner, coef, top)
+    )(vel, inner, coef, part_b)
     return_shape = shape(*velocity.shape)
     increment, time_step = call(
-        functools.partial(finish, spans, len(tops)),
+        functools.partial(finish, spans),
         "finish",
         0,
         scratch=8,
         out_shape=(return_shape, shape(1)),
-        in_specs=[vmem] * (6 + len(tops)),
+        in_specs=[vmem] * 7,
         out_specs=(anywhere, smem),
         scratch_shapes=[
             pltpu.VMEM(velocity.shape, f32),
             pltpu.SemaphoreType.DMA(((planes - 2 * HALO) // BLOCK + 2,)),
         ],
-    )(vel, inner, coef, part_a, part_b, part_c, *tops)
+    )(vel, inner, coef, part_a, part_b, part_c, largest)
     return increment, time_step.reshape(())
 
 

time: 43.6 us -> 177 us (4.06)
  waiting for transfers between devices: 1.82 us -> 104 us
  local copies, waits for them, and re-layouts: 1.18 us -> 22.6 us
  between operations: 0.78 us -> 14.2 us
  starting transfers between devices: 16.2 us -> 12.7 us
    pmax x0 -> x1, waiting for transfers between devices: none -> 104 us  [per_device(): largest = lax.pmax(pay, ('az', 'ax'))]
    unnamed x2 -> x18, local copies, waits for them, and re-layouts: 0.01 us -> 20.5 us
    ppermute x4 -> x0, starting transfers between devices: 5.06 us -> none  [exchanged(): return lax.ppermute(block, ('az', 'ax'), route)]
    pallas_call x6, Pallas kernels: 17.6 us -> 15.7 us  [the longest x2 7.87 us: in_advance(): call(functools.partial(ahead, first, last), f'ahead_{n}', 8 * velocity.si...]
    ppermute x4 -> x0, waiting for transfers between devices: 1.79 us -> none  [exchanged(): return lax.ppermute(block, ('az', 'ax'), route)]
  transfers between devices with their start and end apart: 11 -> 8, of which waited for: 2 -> 1; matrix products, arithmetic and copies ran while one was open for 0% -> 0% of each run, Pallas kernels for 39% -> 8%
where the time goes in v9:
time: 177 us
  waiting for transfers between devices  104 us (59%)
  Pallas kernels  23.3 us (13%)
  local copies, waits for them, and re-layouts  22.6 us (13%)
  between operations  14.2 us (8%)
  starting transfers between devices  12.7 us (7%)
    pmax x1, waiting for transfers between devices, per_device(): largest = lax.pmax(pay, ('az', 'ax'))  104 us
    unnamed x18, local copies, waits for them, and re-layouts  20.5 us
    ppermute x7, starting transfers between devices, shifted(): return lax.ppermute(block, ('az', 'ax'), route)  12.7 us
    pallas_call x2, Pallas kernels, in_advance(): call(functools.partial(ahead, first, last), f'ahead_{n}', 8 * velocity.si...  7.87 us
    pallas_call x1, Pallas kernels, per_device(): call(functools.partial(finish, spans), 'finish', 0, scratch=8, out_shape=...  4.69 us
    pallas_call x1, Pallas kernels, per_device(): call(functools.partial(first_pass, theta_step), 'first_pass', 0, out_shap...  3.73 us
  transfers between devices with their start and end apart: 8, of which 1 were waited for; matrix products, arithmetic and copies ran while one was open for 0% of the time, Pallas kernels for 8%

profile of v9, /device:TPU:0, one launch (start us, length us, event | category | flops | bytes accessed | tf_op | source)
XLA Modules:
  0.0 177.0 jit_solution(4716288430776748422)
XLA Ops:
  7.2 0.0 all-reduce.2.cloned.1.call-start
  7.2 2.1 %fusion = (f32[3,2,128,128]{3,2,1,0:T(8,128)}, f32[3,2,128,128]{3,2,1,0:T(8,128)}) fusion(f32[3,32,128,128]{3,2,1,0:T(8,128)} %v_ref.1), kind=kLoop, calls=%fused_computation | loop fusion | bytes 1572864 | tf_op jit(solution)/shard_map/slice | solution.py:435
  9.3 6.0 %collective-permute-start.1 = (f32[3,2,128,128]{3,2,1,0:T(8,128)}, f32[3,2,128,128]{3,2,1,0:T(8,128)}, u32[]{:S(2)}, u32[]{:S(2)}) collective-permute-start(f32[3,2,128,128]{3,2,1,0:T(8,128)} %get-tuple-element.20), channel_id=1, source_target_pairs={{4,0},{5,1},{6,2},{7,3},{8,4},{9,5},{10,6},{11,7},{12,8},{13,9},{1... | collective-permute-start | bytes 1179656 | tf_op jit(solution)/shard_map/ppermute | solution.py:404
  15.3 0.0 collective-permute-start
  15.3 3.7 %first_pass.1 = (f32[3,36,144,128]{3,2,1,0:T(8,128)S(1)}, f32[3,32,2,128]{3,2,1,0:T(2,128)S(1)}, f32[3,32,2,128]{3,2,1,0:T(2,128)S(1)}, f32[128,128]{1,0:T(8,128)}) custom-call(f32[3,32,128,128]{3,2,1,0:T(8,128)} %v_ref.1), custom_call_target="tpu_custom_call" | custom-call | tf_op jit(solution)/shard_map/first_pass/pallas_call | solution.py:441
  19.0 0.0 copy-start
  19.1 3.1 %copy-done = f32[3,36,144,128]{3,2,1,0:T(8,128)} copy-done((f32[3,36,144,128]{3,2,1,0:T(8,128)}, f32[3,36,144,128]{3,2,1,0:T(8,128)S(1)}, u32[]{:S(2)}) %copy-start) | copy-done | bytes 7962648
  22.1 0.0 collective-permute-start.2
  22.1 1.7 collective-permute-start.3
  23.9 0.0 all-reduce.2.cloned.1.call-update
  23.9 0.0 copy-start.1
  23.9 3.3 %copy-done.1 = f32[3,36,144,128]{3,2,1,0:T(8,128)S(1)} copy-done((f32[3,36,144,128]{3,2,1,0:T(8,128)S(1)}, f32[3,36,144,128]{3,2,1,0:T(8,128)}, u32[]{:S(2)}) %copy-start.1) | copy-done | bytes 7962648
  27.2 2.7 %pack.1._.inner_in = f32[128,128]{1,0:T(8,128)S(1)} custom-call(f32[3,36,144,128]{3,2,1,0:T(8,128)S(1)} %copy-done.1), custom_call_target="tpu_custom_call" | custom-call | flops 1572864 | bytes 1572864 | tf_op jit(solution)/shard_map/pack/pallas_call | solution.py:453
  29.9 0.0 copy-start.6
  29.9 0.0 collective-permute-done.2.low_ref
  29.9 0.0 collective-permute-done.3.high_ref
  29.9 0.1 fold.1.vel_ref.vel_in
  30.1 0.7 copy-done.6
  30.7 5.2 %ahead_0.1.refs_0_.part_a = f32[3,16,128,128]{3,2,1,0:T(8,128)S(1)} custom-call(f32[3,36,144,128]{3,2,1,0:T(8,128)S(1)} %fold.1.vel_ref.vel_in, f32[15,8,128]{2,1,0:T(8,128)S(1)} %copy-done.6, f32[128,128]{1,0:T(8,128)S(1)} %pack.1._.inner_in), custom_call_target="tpu_custom_call" | custom-call | flops 12582912 | bytes 12582912 | tf_op jit(solution)/shard_map/ahead_0/pallas_call | solution.py:475
  36.0 0.0 copy-start.2
  36.0 3.1 %copy-done.2 = f32[3,36,144,128]{3,2,1,0:T(8,128)} copy-done((f32[3,36,144,128]{3,2,1,0:T(8,128)}, f32[3,36,144,128]{3,2,1,0:T(8,128)S(1)}, u32[]{:S(2)}) %copy-start.2) | copy-done | bytes 7962648
  39.1 104.1 %all-reduce.2.cloned.1.call-done.refs_1_.top_ref = f32[128,128]{1,0:T(8,128)} async-done(((f32[128,128]{1,0:T(8,128)}), f32[128,128]{1,0:T(8,128)}) %all-reduce.2.cloned.1.call-update) | async-done | bytes 65552 | tf_op jit(solution)/shard_map/pmax | solution.py:452
  143.2 0.0 collective-permute-done.1.above_ref
  143.2 0.0 collective-permute-done.below_ref
  143.2 0.0 copy-start.3
  143.2 3.3 %copy-done.3 = f32[3,36,144,128]{3,2,1,0:T(8,128)S(1)} copy-done((f32[3,36,144,128]{3,2,1,0:T(8,128)S(1)}, f32[3,36,144,128]{3,2,1,0:T(8,128)}, u32[]{:S(2)}) %copy-start.3) | copy-done | bytes 7962648
  146.5 0.0 copy-start.7
  146.5 0.8 copy-done.7
  147.3 1.2 theta_in.1
  148.5 3.2 %collective-permute-start.6 = (f32[128,128]{1,0:T(8,128)S(1)}, f32[128,128]{1,0:T(8,128)S(1)}, u32[]{:S(2)}, u32[]{:S(2)}) collective-permute-start(f32[128,128]{1,0:T(8,128)S(1)} %get-tuple-element.17), channel_id=1, source_target_pairs={{16,0},{17,1},{18,2},{19,3},{20,4},{21,5},{22,6},{23,7},{24,8},{25... | collective-permute-start | bytes 196616 | tf_op jit(solution)/shard_map/ppermute | solution.py:404
  151.6 0.0 collective-permute-start.5
  151.6 1.7 collective-permute-start.4
  153.4 2.6 %ahead_1.1._.part_b = f32[3,8,128,128]{3,2,1,0:T(8,128)S(1)} custom-call(f32[3,36,144,128]{3,2,1,0:T(8,128)S(1)} %get-tuple-element.16.vel_ref.vel_in, f32[15,8,128]{2,1,0:T(8,128)S(1)} %copy-done.6, f32[8,128]{1,0:T(8,128)S(1)} %get-tuple-element.15._), custom_call_target="tpu_custom_call" | custom-call | flops 12582912 | bytes 12582912 | tf_op jit(solution)/shard_map/ahead_1/pallas_call | solution.py:475
  156.0 0.0 collective-permute-done.5.back_ref
  156.0 0.0 collective-permute-done.4.next_ref
  156.0 0.0 copy-start.8
  156.0 0.0 collective-permute-done.6.inner_ref
  156.1 3.0 %rest.1.part_c = f32[3,8,128,128]{3,2,1,0:T(8,128)S(1)} custom-call(f32[3,36,144,128]{3,2,1,0:T(8,128)S(1)} %corners_in.1.vel_ref, f32[128,128]{1,0:T(8,128)S(1)} %collective-permute-done.6.inner_ref, f32[15,8,128]{2,1,0:T(8,128)S(1)} %copy-done.6, f32[3,8,128,128]{3,2,1,0:T(8,128)S(1)} %ahead_1.1._.part_b), custom_call_target="tpu_custom_call" | custom-call | tf_op jit(solution)/shard_map/rest/pallas_call | solution.py:508
  159.1 0.0 copy-start.4
  159.1 3.1 %copy-done.4 = f32[3,36,144,128]{3,2,1,0:T(8,128)} copy-done((f32[3,36,144,128]{3,2,1,0:T(8,128)}, f32[3,36,144,128]{3,2,1,0:T(8,128)S(1)}, u32[]{:S(2)}) %copy-start.4) | copy-done | bytes 7962648
  162.1 0.0 copy-done.8
  162.1 0.0 copy-start.5
  162.2 3.3 %copy-done.5 = f32[3,36,144,128]{3,2,1,0:T(8,128)S(1)} copy-done((f32[3,36,144,128]{3,2,1,0:T(8,128)S(1)}, f32[3,36,144,128]{3,2,1,0:T(8,128)}, u32[]{:S(2)}) %copy-start.5) | copy-done | bytes 7962648
  165.4 4.7 %finish.1 = (f32[3,32,128,128]{3,2,1,0:T(8,128)}, f32[1]{0:T(128)}) custom-call(f32[3,36,144,128]{3,2,1,0:T(8,128)S(1)} %copy-done.5, f32[128,128]{1,0:T(8,128)S(1)} %collective-permute-done.6.inner_ref, f32[15,8,128]{2,1,0:T(8,128)S(1)} %copy-done.6, f32[3,16,128,128]{3,2,1,0:T(8,128)S(1)} %ahead_0.1.refs_0_.part_a, ...), custom_call_target="tpu_custom_call" | custom-call | tf_op jit(solution)/shard_map/finish/pallas_call | solution.py:517
  (1 shorter events, 0.0 us)
Async XLA Ops:
  7.2 136.0 %all-reduce.2.cloned.1.call-start = ((), (), s32[]{:S(2)}) async-start(), calls=%async_computation | async-start | bytes 131072 | tf_op jit(solution)/shard_map/pmax | solution.py:452
  9.3 133.9 %collective-permute-start.1 = (f32[3,2,128,128]{3,2,1,0:T(8,128)}, f32[3,2,128,128]{3,2,1,0:T(8,128)}, u32[]{:S(2)}, u32[]{:S(2)}) collective-permute-start(f32[3,2,128,128]{3,2,1,0:T(8,128)} %get-tuple-element.20), channel_id=1, source_target_pairs={{4,0},{5,1},{6,2},{7,3},{8,4},{9,5},{10,6},{11,7},{12,8},{13,9},{1... | collective-permute-start | bytes 1179656 | tf_op jit(solution)/shard_map/ppermute | solution.py:404
  15.3 127.9 %collective-permute-start = (f32[3,2,128,128]{3,2,1,0:T(8,128)}, f32[3,2,128,128]{3,2,1,0:T(8,128)}, u32[]{:S(2)}, u32[]{:S(2)}) collective-permute-start(f32[3,2,128,128]{3,2,1,0:T(8,128)} %get-tuple-element.21), channel_id=1, source_target_pairs={{28,0},{29,1},{30,2},{31,3},{0,4},{1,5},{2,6},{3,7},{4,8},{5,9},{6... | collective-permute-start | bytes 1179656 | tf_op jit(solution)/shard_map/ppermute | solution.py:404
  19.0 3.1 %copy-start = (f32[3,36,144,128]{3,2,1,0:T(8,128)}, f32[3,36,144,128]{3,2,1,0:T(8,128)S(1)}, u32[]{:S(2)}) copy-start(f32[3,36,144,128]{3,2,1,0:T(8,128)S(1)} %get-tuple-element.11.vel_ref.vel_in) | copy-start | bytes 23887876
  22.1 7.8 %collective-permute-start.2 = (f32[3,32,2,128]{3,2,1,0:T(2,128)S(1)}, f32[3,32,2,128]{3,2,1,0:T(2,128)S(1)}, u32[]{:S(2)}, u32[]{:S(2)}) collective-permute-start(f32[3,32,2,128]{3,2,1,0:T(2,128)S(1)} %get-tuple-element.12), channel_id=1, source_target_pairs={{3,0},{0,1},{1,2},{2,3},{7,4},{4,5},{5,6},{6,7},{11,8},{8,9},{9,10... | collective-permute-start | bytes 294920 | tf_op jit(solution)/shard_map/ppermute | solution.py:404
  22.1 7.8 %collective-permute-start.3 = (f32[3,32,2,128]{3,2,1,0:T(2,128)S(1)}, f32[3,32,2,128]{3,2,1,0:T(2,128)S(1)}, u32[]{:S(2)}, u32[]{:S(2)}) collective-permute-start(f32[3,32,2,128]{3,2,1,0:T(2,128)S(1)} %get-tuple-element.13), channel_id=1, source_target_pairs={{1,0},{2,1},{3,2},{0,3},{5,4},{6,5},{7,6},{4,7},{9,8},{10,9},{11,1... | collective-permute-start | bytes 294920 | tf_op jit(solution)/shard_map/ppermute | solution.py:404
  23.9 3.3 %copy-start.1 = (f32[3,36,144,128]{3,2,1,0:T(8,128)S(1)}, f32[3,36,144,128]{3,2,1,0:T(8,128)}, u32[]{:S(2)}) copy-start(f32[3,36,144,128]{3,2,1,0:T(8,128)} %copy-done) | copy-start | bytes 23887876
  29.9 0.8 copy-start.6
  36.0 3.1 %copy-start.2 = (f32[3,36,144,128]{3,2,1,0:T(8,128)}, f32[3,36,144,128]{3,2,1,0:T(8,128)S(1)}, u32[]{:S(2)}) copy-start(f32[3,36,144,128]{3,2,1,0:T(8,128)S(1)} %fold.1.vel_ref.vel_in) | copy-start | bytes 23887876
  143.2 3.3 %copy-start.3 = (f32[3,36,144,128]{3,2,1,0:T(8,128)S(1)}, f32[3,36,144,128]{3,2,1,0:T(8,128)}, u32[]{:S(2)}) copy-start(f32[3,36,144,128]{3,2,1,0:T(8,128)} %copy-done.2) | copy-start | bytes 23887876
  146.5 0.8 copy-start.7
  148.5 7.6 %collective-permute-start.6 = (f32[128,128]{1,0:T(8,128)S(1)}, f32[128,128]{1,0:T(8,128)S(1)}, u32[]{:S(2)}, u32[]{:S(2)}) collective-permute-start(f32[128,128]{1,0:T(8,128)S(1)} %get-tuple-element.17), channel_id=1, source_target_pairs={{16,0},{17,1},{18,2},{19,3},{20,4},{21,5},{22,6},{23,7},{24,8},{25... | collective-permute-start | bytes 196616 | tf_op jit(solution)/shard_map/ppermute | solution.py:404
  151.6 4.4 %collective-permute-start.5 = (f32[8,128]{1,0:T(8,128)S(1)}, f32[8,128]{1,0:T(8,128)S(1)}, u32[]{:S(2)}, u32[]{:S(2)}) collective-permute-start(f32[8,128]{1,0:T(8,128)S(1)} %get-tuple-element.15._), channel_id=1, source_target_pairs={{3,0},{0,1},{1,2},{2,3},{7,4},{4,5},{5,6},{6,7},{11,8},{8,9},{9,10... | collective-permute-start | bytes 12296 | tf_op jit(solution)/shard_map/ppermute | solution.py:404
  151.6 4.4 %collective-permute-start.4 = (f32[8,128]{1,0:T(8,128)S(1)}, f32[8,128]{1,0:T(8,128)S(1)}, u32[]{:S(2)}, u32[]{:S(2)}) collective-permute-start(f32[8,128]{1,0:T(8,128)S(1)} %get-tuple-element.15._), channel_id=1, source_target_pairs={{1,0},{2,1},{3,2},{0,3},{5,4},{6,5},{7,6},{4,7},{9,8},{10,9},{11,1... | collective-permute-start | bytes 12296 | tf_op jit(solution)/shard_map/ppermute | solution.py:404
  156.0 6.1 %copy-start.8 = (f32[128,128]{1,0:T(8,128)S(1)}, f32[128,128]{1,0:T(8,128)}, u32[]{:S(2)}) copy-start(f32[128,128]{1,0:T(8,128)} %all-reduce.2.cloned.1.call-done.refs_1_.top_ref) | copy-start | bytes 196612
  159.1 3.1 %copy-start.4 = (f32[3,36,144,128]{3,2,1,0:T(8,128)}, f32[3,36,144,128]{3,2,1,0:T(8,128)S(1)}, u32[]{:S(2)}) copy-start(f32[3,36,144,128]{3,2,1,0:T(8,128)S(1)} %corners_in.1.vel_ref) | copy-start | bytes 23887876
  162.1 3.3 %copy-start.5 = (f32[3,36,144,128]{3,2,1,0:T(8,128)S(1)}, f32[3,36,144,128]{3,2,1,0:T(8,128)}, u32[]{:S(2)}) copy-start(f32[3,36,144,128]{3,2,1,0:T(8,128)} %copy-done.4) | copy-start | bytes 23887876
Sparse Core Ops, SparseCore 0:
  24.0 119.1 all-reduce.1

commit v10 on v8

--- a/solution.py
+++ b/solution.py
@@ -179,11 +179,13 @@
     return jnp.where(lane == radial - 1, 0.0, 1.0).astype(jnp.float32)
 
 
-def first_pass(theta_step, v_ref, vel_ref, low_ref, high_ref, pay_ref, sems):
+def first_pass(theta_step, v_ref, vel_ref, even_ref, odd_ref, pay_ref, sems):
     _, planes, axial, radial = v_ref.shape
     lane = lax.broadcasted_iota(jnp.int32, (8, radial), 1)
     wall = wall_mask(8, radial)
     rate_t = (radial / theta_step) / (lane.astype(jnp.float32) + 0.5)
+
+    odd = lax.rem(lax.axis_index("ax"), 2) == 1
 
     def fetch(g):
         part = pl.ds(g * GROUP, GROUP)
@@ -213,8 +215,10 @@
         for q in range(GROUP):
             for n in range(3):
                 j = g * GROUP + q
-                low_ref[n, j] = vel_ref[n, j + HALO, PAD : PAD + 2, :]
-                high_ref[n, j] = vel_ref[n, j + HALO, PAD + axial - 2 : PAD + axial, :]
+                first = vel_ref[n, j + HALO, PAD : PAD + 2, :]
+                last = vel_ref[n, j + HALO, PAD + axial - 2 : PAD + axial, :]
+                even_ref[n, j] = jnp.where(odd, first, last)
+                odd_ref[n, j] = jnp.where(odd, last, first)
         return largest
 
     zero = jnp.zeros((8, radial), jnp.float32)
@@ -223,7 +227,7 @@
     top = jnp.max(largest, axis=(0, 1), keepdims=True)
     pay_ref[...] = jnp.broadcast_to(top, pay_ref.shape)
     last = lax.broadcasted_iota(jnp.int32, (2, radial), 1) == radial - 1
-    for ref in (low_ref, high_ref):
+    for ref in (even_ref, odd_ref):
         ref[0, 0] = jnp.where(last, top, ref[0, 0])
 
 
@@ -247,13 +251,13 @@
     lax.fori_loop(0, axial // 8, rows, 0)
 
 
-def fold(low_ref, high_ref, pay_ref, inner_in, vel_in, *refs):
+def fold(even_ref, odd_ref, pay_ref, inner_in, vel_in, *refs):
     del vel_in
     fars, (inner_ref, vel_ref) = refs[:-2], refs[-2:]
-    planes = low_ref.shape[1]
+    planes = even_ref.shape[1]
     axial, radial = inner_in.shape
     lane = lax.broadcasted_iota(jnp.int32, (1, radial), 1)
-    top = jnp.maximum(low_ref[0, 0, 0:1, :], high_ref[0, 0, 0:1, :])
+    top = jnp.maximum(even_ref[0, 0, 0:1, :], odd_ref[0, 0, 0:1, :])
     top = jnp.max(jnp.where(lane == radial - 1, top, 0.0), axis=(0, 1), keepdims=True)
     top = jnp.maximum(pay_ref[...], top)
     for far in fars:
@@ -262,44 +266,49 @@
     inner_ref[...] = inner_in[...]
     inner_ref[0:8, :] = jnp.where(lane == radial - 1, top, inner_in[0:8, :])
     wall = wall_mask(2, radial)
+    odd = lax.rem(lax.axis_index("ax"), 2) == 1
 
     def plane(j, carry):
         for n in range(3):
             mask = wall if n == 0 else 1.0
-            vel_ref[n, j + HALO, PAD - 2 : PAD, :] = low_ref[n, j] * mask
-            vel_ref[n, j + HALO, PAD + axial : PAD + axial + 2, :] = high_ref[n, j] * mask
+            even, other = even_ref[n, j] * mask, odd_ref[n, j] * mask
+            low, high = jnp.where(odd, even, other), jnp.where(odd, other, even)
+            vel_ref[n, j + HALO, PAD - 2 : PAD, :] = low
+            vel_ref[n, j + HALO, PAD + axial : PAD + axial + 2, :] = high
         return carry
 
     lax.fori_loop(0, planes, plane, 0, unroll=4)
 
 
-def theta_in(below_ref, above_ref, inner_in, vel_in, _, tile_ref, inner_ref, vel_ref):
-    del vel_in
-    planes = vel_ref.shape[1] - 2 * HALO
-    axial, radial = inner_in.shape
-    cells = pl.ds(PAD, axial)
-    wall = wall_mask(1, radial)
-    for q in range(HALO):
-        for ref, place in ((below_ref, q), (above_ref, HALO + planes + q)):
-            vel_ref[0, place, cells, :] = ref[0, q] * wall
-            vel_ref[1, place, cells, :] = ref[1, q]
-            vel_ref[2, place, cells, :] = ref[2, q]
-    tile_ref[...] = jnp.zeros_like(tile_ref)
-    tile_ref[1:2, :] = below_ref[1, HALO - 1, 0:1, :]
-    tile_ref[2:3, :] = above_ref[2, 0, axial - 1 : axial, :]
-    inner_ref[...] = inner_in[...]
-
-
-def corners_in(mine_ref, inner_ref, next_ref, back_ref, vel_in, _, top_ref, vel_ref):
-    del vel_in
-    planes = vel_ref.shape[1] - 2 * HALO
-    axial, radial = inner_ref.shape
-    vel_ref[1, HALO - 1, PAD + axial : PAD + axial + 1, :] = next_ref[1:2, :]
-    vel_ref[2, HALO + planes, PAD - 1 : PAD, :] = back_ref[2:3, :]
+def with_partner(mine_ref, inner_ref, _, top_ref):
+    radial = inner_ref.shape[1]
     lane = lax.broadcasted_iota(jnp.int32, (1, radial), 1)
     top = jnp.maximum(mine_ref[0:1, :], inner_ref[0:1, :])
     top = jnp.max(jnp.where(lane == radial - 1, top, 0.0), axis=(0, 1), keepdims=True)
     top_ref[...] = jnp.broadcast_to(top, top_ref.shape)
+
+
+def theta_in(even_ref, odd_ref, vel_in, _, even_tile, odd_tile, vel_ref):
+    del vel_in
+    planes, axial = vel_ref.shape[1] - 2 * HALO, vel_ref.shape[2] - 2 * PAD
+    cells = pl.ds(PAD, axial)
+    wall = wall_mask(1, vel_ref.shape[3])
+    odd = lax.rem(lax.axis_index("az"), 2)
+    below, above = 0, HALO + planes
+    for ref, place in (
+        (even_ref, jnp.where(odd == 1, below, above)),
+        (odd_ref, jnp.where(odd == 1, above, below)),
+    ):
+        for q in range(HALO):
+            vel_ref[0, place + q, cells, :] = ref[0, q] * wall
+            vel_ref[1, place + q, cells, :] = ref[1, q]
+            vel_ref[2, place + q, cells, :] = ref[2, q]
+    first = vel_ref[1, below + HALO - 1, PAD : PAD + 1, :]
+    last = vel_ref[2, above, PAD + axial - 1 : PAD + axial, :]
+    odd = lax.rem(lax.axis_index("ax"), 2) == 1
+    shape = even_tile.shape
+    even_tile[...] = jnp.broadcast_to(jnp.where(odd, first, last), shape)
+    odd_tile[...] = jnp.broadcast_to(jnp.where(odd, last, first), shape)
 
 
 def ghosts(cells, inner, planes):
@@ -347,20 +356,16 @@
     lax.fori_loop(0, (last - first) // BLOCK, block, 0)
 
 
-def rest(first, last, vel_ref, inner_ref, coef_ref, _, out_ref):
-    planes = vel_ref.shape[1] - 2 * HALO
-    runs = [(j, BLOCK, j - first) for j in range(first, last, BLOCK)]
-    runs += [(0, HALO, last - first), (planes - HALO, HALO, last - first + HALO)]
-    for j, size, place in runs:
-
-        def write(n, plane, k, value, shift=place - j):
-            out_ref[n, plane + shift, k, :] = value
-
-        block_terms(vel_ref, inner_ref, coef_ref, j, size, write)
-
-
-def finish(spans, count, vel_ref, inner_ref, coef_ref, part_a, part_b, part_c, *refs):
-    tops, (out_ref, step_ref, res, sems) = refs[:count], refs[count:]
+def ahead_with_ghosts(first, last, vel_ref, inner_ref, coef_ref, _, out_ref):
+    def write(n, j, k, value):
+        out_ref[n, j - first, k, :] = value
+
+    for j in range(first, last, BLOCK):
+        block_terms(vel_ref, inner_ref, coef_ref, j, BLOCK, write)
+
+
+def interior(spans, count, vel_ref, inner_ref, coef_ref, part_a, part_b, *refs):
+    tops, (out_ref, step_ref, res, sems) = refs[:count], refs[-4:]
     axial, radial = inner_ref.shape
     planes = vel_ref.shape[1] - 2 * HALO
     top = tops[0][0:1, :]
@@ -372,8 +377,19 @@
     factors = (scale * coef_ref[WALL], scale, scale)
     pending = []
 
-    def complete(part, j, size, place, add):
-        groups = 2 * BLOCK // size
+    def send(j):
+        part_of = pl.ds(j, BLOCK)
+        copy = pltpu.make_async_copy(
+            res.at[:, pl.ds(j - HALO, BLOCK)], out_ref.at[:, part_of], sems.at[len(pending)]
+        )
+        copy.start()
+        pending.append(copy)
+
+    def write(n, j, k, value):
+        res[n, j - HALO, k, :] = value * factors[n]
+
+    def complete(part, j, place, add):
+        groups = 4
 
         def rows(i, carry):
             found = []
@@ -381,7 +397,7 @@
                 k = pl.multiple_of((i * groups + u) * 8, 8)
                 cells = Cells(vel_ref, j, k)
                 ghost = ghosts(cells, inner_ref[pl.ds(k, 8), :], planes) if add else None
-                for q in range(size):
+                for q in range(BLOCK):
                     values = [part[n, place + q, pl.ds(k, 8), :] for n in range(3)]
                     if add:
                         added = lane_zero_terms(cells, ghost, coef_ref, q, 1.0 / radial)
@@ -389,51 +405,74 @@
                     found.append((q, k, values))
             for q, k, values in found:
                 for n, value in enumerate(values):
-                    res[n, j + q, pl.ds(k, 8), :] = value * factors[n]
+                    write(n, j + q, pl.ds(k, 8), value)
             return carry
 
         lax.fori_loop(0, axial // (8 * groups), rows, 0)
-        part_of = pl.ds(j, size)
+        send(j)
+
+    for part, (first, last), add in ((part_a, spans[0], True), (part_b, spans[1], False)):
+        for j in range(first, last, BLOCK):
+            complete(part, j, j - first, add)
+    for j in range(*spans[2], BLOCK):
+        block_terms(vel_ref, inner_ref, coef_ref, j, BLOCK, write)
+        send(j)
+    for copy in pending:
+        copy.wait()
+
+
+def edges(
+    step_ref, even_ref, odd_ref, inner_ref, coef_ref, vel_in, part, out_ref, vel_ref, res, sems
+):
+    del vel_in, part
+    axial = inner_ref.shape[0]
+    planes = vel_ref.shape[1] - 2 * HALO
+    scale = GAMMA * step_ref[0]
+    factors = (scale * coef_ref[WALL], scale, scale)
+    odd = lax.rem(lax.axis_index("ax"), 2) == 1
+    even, other = even_ref[0:1, :], odd_ref[0:1, :]
+    following, preceding = jnp.where(odd, other, even), jnp.where(odd, even, other)
+    vel_ref[1, HALO - 1, PAD + axial : PAD + axial + 1, :] = following
+    vel_ref[2, HALO + planes, PAD - 1 : PAD, :] = preceding
+    pending = []
+    for side, first in enumerate((0, planes - HALO)):
+
+        def write(n, j, k, value, shift=side * HALO - first):
+            res[n, j + shift, k, :] = value * factors[n]
+
+        block_terms(vel_ref, inner_ref, coef_ref, first, HALO, write)
         copy = pltpu.make_async_copy(
-            res.at[:, part_of], out_ref.at[:, part_of], sems.at[len(pending)]
+            res.at[:, pl.ds(side * HALO, HALO)],
+            out_ref.at[:, pl.ds(first, HALO)],
+            sems.at[side],
         )
         copy.start()
         pending.append(copy)
-
-    first, last = spans[2]
-    for j in range(first, last, BLOCK):
-        complete(part_c, j, BLOCK, j - first, False)
-    complete(part_c, 0, HALO, last - first, False)
-    complete(part_c, planes - HALO, HALO, last - first + HALO, False)
-    for part, (first, last) in ((part_a, spans[0]), (part_b, spans[1])):
-        for j in range(first, last, BLOCK):
-            complete(part, j, BLOCK, j - first, True)
     for copy in pending:
         copy.wait()
 
 
-def shifted(block, distance):
-    sizes = lax.axis_size("az"), lax.axis_size("ax")
-    route = []
-    for i in range(sizes[0]):
-        for k in range(sizes[1]):
-            source = (i - distance[0]) % sizes[0], (k - distance[1]) % sizes[1]
-            route.append((source[0] * sizes[1] + source[1], i * sizes[1] + k))
-    return lax.ppermute(block, ("az", "ax"), route)
+def routed(block, axis, source):
+    count = lax.axis_size(axis)
+    return lax.ppermute(block, axis, [(source(i), i) for i in range(count)])
+
+
+def exchanged(block, axis, step):
+    return routed(block, axis, lambda i: i ^ step)
+
+
+def across_edges(even, odd, axis):
+    count = lax.axis_size(axis)
+
+    def source(i):
+        return (i + (1 if i % 2 else -1)) % count
+
+    return exchanged(even, axis, 1), routed(odd, axis, source)
 
 
 def cuts(planes):
-    ends = (HALO, planes - HALO - 2 * BLOCK, planes - HALO - BLOCK, planes - HALO)
+    ends = (HALO, HALO + 2 * BLOCK, HALO + 3 * BLOCK, planes - HALO)
     return list(zip(ends[:-1], ends[1:]))
-
-
-def exchanged(block, step):
-    sizes = lax.axis_size("az"), lax.axis_size("ax")
-    route = []
-    for i in range(sizes[0]):
-        for k in range(sizes[1]):
-            route.append(((i ^ step) * sizes[1] + k, i * sizes[1] + k))
-    return lax.ppermute(block, ("az", "ax"), route)
 
 
 def per_device(velocity):
@@ -458,14 +497,21 @@
             **kwargs,
         )
 
-    below = shifted(velocity[:, planes - HALO :], (1, 0))
-    above = shifted(velocity[:, :HALO], (-1, 0))
+    odd = lax.axis_index("az") % 2
+    ends = (planes - HALO, 0)
+    even_end = jnp.where(odd == 1, ends[1], ends[0])
+    odd_end = jnp.where(odd == 1, ends[0], ends[1])
+    theta_even, theta_odd = across_edges(
+        lax.dynamic_slice_in_dim(velocity, even_end, HALO, 1),
+        lax.dynamic_slice_in_dim(velocity, odd_end, HALO, 1),
+        "az",
+    )
 
     edge = shape(3, planes, 2, radial)
     padded = shape(3, planes + 2 * HALO, axial + 2 * PAD, radial)
     row = shape(axial, radial)
     tile = shape(8, radial)
-    vel, first, last, pay = call(
+    vel, edge_even, edge_odd, pay = call(
         functools.partial(first_pass, theta_step),
         "first_pass",
         0,
@@ -474,9 +520,11 @@
         out_specs=(vmem,) * 4,
         scratch_shapes=[pltpu.SemaphoreType.DMA((planes // GROUP,))],
     )(pltpu.with_memory_space_constraint(velocity, pltpu.HBM))
-    low = shifted(last, (0, 1))
-    high = shifted(first, (0, -1))
-    fars = [shifted(pay, (0, step)) for step in range(2, sizes[1] - 1)]
+    z_even, z_odd = across_edges(edge_even, edge_odd, "ax")
+    fars = [
+        routed(pay, "ax", lambda i, step=step: (i + step) % sizes[1])
+        for step in range(2, sizes[1] - 1)
+    ]
     inner = call(
         pack,
         "pack",
@@ -493,68 +541,76 @@
         in_specs=[vmem] * (5 + len(fars)),
         out_specs=(vmem,) * 2,
         input_output_aliases={4: 1},
-    )(low, high, pay, inner, vel, *fars)
+    )(z_even, z_odd, pay, inner, vel, *fars)
+    inner = exchanged(mine, "az", sizes[0] // 2)
 
     spans = cuts(planes)
 
-    def in_advance(n, vel, token):
-        first, last = spans[n]
-        return call(
-            functools.partial(ahead, first, last),
-            f"ahead_{n}",
-            velocity.size * (2 - n),
-            out_shape=shape(3, last - first, axial, radial),
-            in_specs=[vmem] * 3,
-            out_specs=vmem,
-        )(vel, coef, token)
-
-    part_a = in_advance(0, vel, mine)
-    tile_out, mine, vel = call(
+    def part_shape(n):
+        return shape(3, spans[n][1] - spans[n][0], axial, radial)
+
+    part_a = call(
+        functools.partial(ahead, *spans[0]),
+        "ahead",
+        velocity.size,
+        out_shape=part_shape(0),
+        in_specs=[vmem] * 3,
+        out_specs=vmem,
+    )(vel, coef, mine)
+    top = call(
+        with_partner,
+        "with_partner",
+        0,
+        out_shape=tile,
+        in_specs=[vmem] * 3,
+        out_specs=vmem,
+    )(mine, inner, part_a)
+    tops = (top, *(exchanged(top, "az", step) for step in range(1, sizes[0] // 2)))
+    part_b = call(
+        functools.partial(ahead_with_ghosts, *spans[1]),
+        "ahead_with_ghosts",
+        velocity.size,
+        out_shape=part_shape(1),
+        in_specs=[vmem] * 4,
+        out_specs=vmem,
+    )(vel, inner, coef, top)
+    tile_even, tile_odd, vel = call(
         theta_in,
         "theta_in",
         0,
-        out_shape=(tile, row, padded),
-        in_specs=[vmem] * 5,
+        out_shape=(tile, tile, padded),
+        in_specs=[vmem] * 4,
         out_specs=(vmem,) * 3,
-        input_output_aliases={3: 2},
-    )(below, above, mine, vel, part_a)
-    inner = exchanged(mine, sizes[0] // 2)
-    following = shifted(tile_out, (0, -1))
-    preceding = shifted(tile_out, (0, 1))
-    part_b = in_advance(1, vel, tile_out)
-    top, vel = call(
-        corners_in,
-        "corners_in",
-        0,
-        out_shape=(tile, padded),
-        in_specs=[vmem] * 6,
-        out_specs=(vmem,) * 2,
-        input_output_aliases={4: 1},
-    )(mine, inner, following, preceding, vel, part_b)
-    tops = (top, *(exchanged(top, step) for step in range(1, sizes[0] // 2)))
-    first, last = spans[2]
-    part_c = call(
-        functools.partial(rest, first, last),
-        "rest",
-        velocity.size,
-        out_shape=shape(3, last - first + 2 * HALO, axial, radial),
-        in_specs=[vmem] * 4,
-        out_specs=vmem,
-    )(vel, inner, coef, top)
-    return_shape = shape(*velocity.shape)
-    increment, time_step = call(
-        functools.partial(finish, spans, len(tops)),
-        "finish",
-        0,
-        scratch=8,
-        out_shape=(return_shape, shape(1)),
-        in_specs=[vmem] * (6 + len(tops)),
+        input_output_aliases={2: 2},
+    )(theta_even, theta_odd, vel, part_b)
+    corner_even, corner_odd = across_edges(tile_even, tile_odd, "ax")
+    part, time_step = call(
+        functools.partial(interior, spans, len(tops)),
+        "interior",
+        4 * velocity.size,
+        scratch=6,
+        out_shape=(shape(*velocity.shape), shape(1)),
+        in_specs=[vmem] * (5 + len(tops)),
         out_specs=(anywhere, smem),
         scratch_shapes=[
-            pltpu.VMEM(velocity.shape, f32),
-            pltpu.SemaphoreType.DMA(((planes - 2 * HALO) // BLOCK + 2,)),
+            pltpu.VMEM((3, planes - 2 * HALO, axial, radial), f32),
+            pltpu.SemaphoreType.DMA(((planes - 2 * HALO) // BLOCK,)),
         ],
-    )(vel, inner, coef, part_a, part_b, part_c, *tops)
+    )(vel, inner, coef, part_a, part_b, *tops)
+    increment, _ = call(
+        edges,
+        "edges",
+        0,
+        scratch=2,
+        out_shape=(shape(*velocity.shape), padded),
+        in_specs=[smem] + [vmem] * 5 + [anywhere],
+        out_specs=(anywhere, vmem),
+        scratch_shapes=[
+            pltpu.VMEM((3, 2 * HALO, axial, radial), f32),
+            pltpu.SemaphoreType.DMA((2,)),
+        ],
+        input_output_aliases={5: 1, 6: 0},
+    )(time_step, corner_even, corner_odd, inner, coef, vel, part)
     return increment, time_step.reshape(())
 
 

time: 43.6 us -> 41.8 us (0.959)
  starting transfers between devices: 16.2 us -> 14.6 us
  Pallas kernels: 23.5 us -> 22.5 us
  waiting for transfers between devices: 1.82 us -> 2.47 us
    ppermute x11, starting transfers between devices: 16.2 us -> 14.6 us  [routed(): return lax.ppermute(block, axis, [(source(i), i) for i in range(count)])]
    dynamic_slice x0 -> x1, local copies, waits for them, and re-layouts: none -> 1.18 us  [per_device(): lax.dynamic_slice_in_dim(velocity, odd_end, HALO, 1)]
    slice x1 -> x0, local copies, waits for them, and re-layouts: 1.17 us -> none  [per_device(): above = shifted(velocity[:, :HALO], (-1, 0))]
    pallas_call x6, Pallas kernels: 17.4 us -> 16.5 us  [the longest x1 9 us: per_device(): call(functools.partial(interior, spans, len(tops)), 'interior', 4 * veloc...]
    ppermute x11, waiting for transfers between devices: 1.82 us -> 2.47 us  [routed(): return lax.ppermute(block, axis, [(source(i), i) for i in range(count)])]
  transfers between devices with their start and end apart: 11 -> 11, of which waited for: 2 -> 2; matrix products, arithmetic and copies ran while one was open for 0% -> 0% of each run, Pallas kernels for 39% -> 47%
where the time goes in v10:
time: 41.8 us; the launch traced here: 41.6 us
  Pallas kernels  22.5 us (54%)
  starting transfers between devices  14.6 us (35%)
  waiting for transfers between devices  2.47 us (6%)
  local copies, waits for them, and re-layouts  1.18 us (3%)
  between operations  0.78 us (2%)
    ppermute x11, starting transfers between devices, routed(): return lax.ppermute(block, axis, [(source(i), i) for i in range(count)])  14.6 us
    pallas_call x1, Pallas kernels, per_device(): call(functools.partial(interior, spans, len(tops)), 'interior', 4 * veloc...  9 us
    pallas_call x1, Pallas kernels, per_device(): call(functools.partial(first_pass, theta_step), 'first_pass', 0, out_shap...  3.1 us
    pallas_call x1, Pallas kernels, per_device(): call(edges, 'edges', 0, scratch=2, out_shape=(shape(*velocity.shape), pad...  3.05 us
    pallas_call x1, Pallas kernels, per_device(): call(pack, 'pack', velocity.size, out_shape=row, in_specs=[vmem], out_spe...  2.73 us
    pallas_call x1, Pallas kernels, per_device(): call(functools.partial(ahead, *spans[0]), 'ahead', velocity.size, out_sha...  2.7 us
    ppermute x11, waiting for transfers between devices, routed(): return lax.ppermute(block, axis, [(source(i), i) for i in range(count)])  2.47 us
    pallas_call x1, Pallas kernels, per_device(): call(functools.partial(ahead_with_ghosts, *spans[1]), 'ahead_with_ghosts'...  1.55 us
  transfers between devices with their start and end apart: 11, of which 2 were waited for; matrix products, arithmetic and copies ran while one was open for 0% of the time, Pallas kernels for 47%

profile of v10, /device:TPU:0, one launch (start us, length us, event | category | flops | bytes accessed | tf_op | source)
XLA Modules:
  0.0 41.6 jit_solution(18335303914622937105)
XLA Ops:
  0.6 1.2 %constant_dynamic-slice_fusion = (f32[3,2,128,128]{3,2,1,0:T(8,128)S(1)}, f32[3,2,128,128]{3,2,1,0:T(8,128)S(1)}) fusion(f32[3,32,128,128]{3,2,1,0:T(8,128)} %v_ref.1, s32[]{:T(128)S(6)} %select_n.18, s32[]{:T(128)S(6)} %select_n.17), kind=kLoop, calls=%fused_computation | loop fusion | bytes 1572872 | tf_op jit(solution)/shard_map/dynamic_slice | solution.py:506
  1.8 6.1 %collective-permute-start.1 = (f32[3,2,128,128]{3,2,1,0:T(8,128)S(1)}, f32[3,2,128,128]{3,2,1,0:T(8,128)S(1)}, u32[]{:S(2)}, u32[]{:S(2)}) collective-permute-start(f32[3,2,128,128]{3,2,1,0:T(8,128)S(1)} %get-tuple-element.26), channel_id=1, source_target_pairs={{28,0},{8,4},{4,8},{16,12},{12,16},{24,20},{20,24},{0,28},{29,1},{... | collective-permute-start | bytes 1179656 | tf_op jit(solution)/shard_map/ppermute | solution.py:457
  7.9 0.0 collective-permute-start
  7.9 3.1 %first_pass.1 = (f32[3,36,144,128]{3,2,1,0:T(8,128)S(1)}, f32[3,32,2,128]{3,2,1,0:T(2,128)S(1)}, f32[3,32,2,128]{3,2,1,0:T(2,128)S(1)}, f32[8,128]{1,0:T(8,128)S(1)}) custom-call(f32[3,32,128,128]{3,2,1,0:T(8,128)} %v_ref.1), custom_call_target="tpu_custom_call" | custom-call | tf_op jit(solution)/shard_map/first_pass/pallas_call | solution.py:514
  11.0 0.1 collective-permute-start.2
  11.1 1.6 %collective-permute-start.3 = (f32[3,32,2,128]{3,2,1,0:T(2,128)S(1)}, f32[3,32,2,128]{3,2,1,0:T(2,128)S(1)}, u32[]{:S(2)}, u32[]{:S(2)}) collective-permute-start(f32[3,32,2,128]{3,2,1,0:T(2,128)S(1)} %get-tuple-element.15), channel_id=1, source_target_pairs={{3,0},{2,1},{1,2},{0,3},{7,4},{6,5},{5,6},{4,7},{11,8},{10,9},{9,1... | collective-permute-start | bytes 294920 | tf_op jit(solution)/shard_map/ppermute | solution.py:457
  12.7 0.5 %collective-permute-start.4 = (f32[8,128]{1,0:T(8,128)S(1)}, f32[8,128]{1,0:T(8,128)S(1)}, u32[]{:S(2)}, u32[]{:S(2)}) collective-permute-start(f32[8,128]{1,0:T(8,128)S(1)} %get-tuple-element.16.pay_ref), channel_id=1, source_target_pairs={{2,0},{3,1},{0,2},{1,3},{6,4},{7,5},{4,6},{5,7},{10,8},{11,9},{8,1... | collective-permute-start | bytes 12296 | tf_op jit(solution)/shard_map/ppermute | solution.py:457
  13.2 0.0 copy-start
  13.2 2.7 %pack.1.inner_in = f32[128,128]{1,0:T(8,128)S(1)} custom-call(f32[3,36,144,128]{3,2,1,0:T(8,128)S(1)} %get-tuple-element.17.vel_ref.vel_in), custom_call_target="tpu_custom_call" | custom-call | flops 1572864 | bytes 1572864 | tf_op jit(solution)/shard_map/pack/pallas_call | solution.py:528
  16.0 0.4 collective-permute-done.4.refs_0_
  16.3 0.0 collective-permute-done.2.even_ref
  16.3 0.0 collective-permute-done.3.odd_ref
  16.3 0.2 fold.1
  16.6 1.1 %collective-permute-start.5 = (f32[128,128]{1,0:T(8,128)S(1)}, f32[128,128]{1,0:T(8,128)S(1)}, u32[]{:S(2)}, u32[]{:S(2)}) collective-permute-start(f32[128,128]{1,0:T(8,128)S(1)} %get-tuple-element.19._.mine_ref), channel_id=1, source_target_pairs={{16,0},{20,4},{24,8},{28,12},{0,16},{4,20},{8,24},{12,28},{17,1},{... | collective-permute-start | bytes 196616 | tf_op jit(solution)/shard_map/ppermute | solution.py:457
  17.7 0.0 copy-done
  17.7 2.7 %ahead.1._.part_a = f32[3,8,128,128]{3,2,1,0:T(8,128)S(1)} custom-call(f32[3,36,144,128]{3,2,1,0:T(8,128)S(1)} %get-tuple-element.18.vel_ref.vel_in, f32[15,8,128]{2,1,0:T(8,128)S(1)} %copy-done, f32[128,128]{1,0:T(8,128)S(1)} %get-tuple-element.19._.mine_ref), custom_call_target="tpu_custom_call" | custom-call | flops 1572864 | bytes 1572864 | tf_op jit(solution)/shard_map/ahead/pallas_call | solution.py:552
  20.4 2.1 %collective-permute-done.5.inner_ref = f32[128,128]{1,0:T(8,128)S(1)} collective-permute-done((f32[128,128]{1,0:T(8,128)S(1)}, f32[128,128]{1,0:T(8,128)S(1)}, u32[]{:S(2)}, u32[]{:S(2)}) %collective-permute-start.5) | collective-permute-done | bytes 65568 | tf_op jit(solution)/shard_map/ppermute | solution.py:457
  22.5 0.1 with_partner.1._.refs_0_
  22.6 0.1 collective-permute-start.8
  22.7 2.8 %collective-permute-start.7 = (f32[8,128]{1,0:T(8,128)S(1)}, f32[8,128]{1,0:T(8,128)S(1)}, u32[]{:S(2)}, u32[]{:S(2)}) collective-permute-start(f32[8,128]{1,0:T(8,128)S(1)} %with_partner.1._.refs_0_), channel_id=1, source_target_pairs={{8,0},{12,4},{0,8},{4,12},{24,16},{28,20},{16,24},{20,28},{9,1},{1... | collective-permute-start | bytes 12296 | tf_op jit(solution)/shard_map/ppermute | solution.py:457
  25.5 0.7 %collective-permute-start.6 = (f32[8,128]{1,0:T(8,128)S(1)}, f32[8,128]{1,0:T(8,128)S(1)}, u32[]{:S(2)}, u32[]{:S(2)}) collective-permute-start(f32[8,128]{1,0:T(8,128)S(1)} %with_partner.1._.refs_0_), channel_id=1, source_target_pairs={{4,0},{0,4},{12,8},{8,12},{20,16},{16,20},{28,24},{24,28},{5,1},{1... | collective-permute-start | bytes 12296 | tf_op jit(solution)/shard_map/ppermute | solution.py:457
  26.2 1.5 %ahead_with_ghosts.1._.part_b = f32[3,4,128,128]{3,2,1,0:T(8,128)S(1)} custom-call(f32[3,36,144,128]{3,2,1,0:T(8,128)S(1)} %get-tuple-element.18.vel_ref.vel_in, f32[128,128]{1,0:T(8,128)S(1)} %collective-permute-done.5.inner_ref, f32[15,8,128]{2,1,0:T(8,128)S(1)} %copy-done, f32[8,128]{1,0:T(8,128)S(1)} %with_partner.1._.refs_0_), custom_call_target="tpu_custom_call" | custom-call | flops 1572864 | bytes 1572864 | tf_op jit(solution)/shard_map/ahead_with_ghosts/pallas_call | solution.py:569
  27.7 0.0 collective-permute-done.1.odd_ref
  27.7 0.0 collective-permute-done.even_ref
  27.8 0.1 theta_in.1
  27.8 0.1 collective-permute-start.9
  27.9 1.6 %collective-permute-start.10 = (f32[8,128]{1,0:T(8,128)S(1)}, f32[8,128]{1,0:T(8,128)S(1)}, u32[]{:S(2)}, u32[]{:S(2)}) collective-permute-start(f32[8,128]{1,0:T(8,128)S(1)} %get-tuple-element.23), channel_id=1, source_target_pairs={{3,0},{2,1},{1,2},{0,3},{7,4},{6,5},{5,6},{4,7},{11,8},{10,9},{9,1... | collective-permute-start | bytes 12296 | tf_op jit(solution)/shard_map/ppermute | solution.py:457
  29.5 0.0 collective-permute-done.8.refs_3_
  29.5 0.0 collective-permute-done.7.refs_2_
  29.5 0.0 collective-permute-done.6.refs_1_
  29.5 9.0 %interior.1 = (f32[3,32,128,128]{3,2,1,0:T(8,128)}, f32[1]{0:T(128)}) custom-call(f32[3,36,144,128]{3,2,1,0:T(8,128)S(1)} %get-tuple-element.20.vel_ref.vel_in, f32[128,128]{1,0:T(8,128)S(1)} %collective-permute-done.5.inner_ref, f32[15,8,128]{2,1,0:T(8,128)S(1)} %copy-done, f32[3,8,128,128]{3,2,1,0:T(8,128)S(1)} %ahead.1._.part_a, ...), custom_call_target="tpu_custom_call" | custom-call | flops 6291456 | bytes 6291456 | tf_op jit(solution)/shard_map/interior/pallas_call | solution.py:587
  38.5 0.0 collective-permute-done.9.even_ref
  38.6 0.0 collective-permute-done.10.odd_ref
  38.6 3.0 %edges.1 = (f32[3,32,128,128]{3,2,1,0:T(8,128)}, f32[3,36,144,128]{3,2,1,0:T(8,128)S(1)}) custom-call(f32[1]{0:T(128)} %get-tuple-element.21.step_ref, f32[8,128]{1,0:T(8,128)S(1)} %collective-permute-done.9.even_ref, f32[8,128]{1,0:T(8,128)S(1)} %collective-permute-done.10.odd_ref, ...), custom_call_target="tpu_custom_call", output_to_operand_aliasing={{1}: (5, {}), {0}: (6, {})} | custom-call | tf_op jit(solution)/shard_map/edges/pallas_call | solution.py:600
Async XLA Ops:
  1.8 25.9 %collective-permute-start.1 = (f32[3,2,128,128]{3,2,1,0:T(8,128)S(1)}, f32[3,2,128,128]{3,2,1,0:T(8,128)S(1)}, u32[]{:S(2)}, u32[]{:S(2)}) collective-permute-start(f32[3,2,128,128]{3,2,1,0:T(8,128)S(1)} %get-tuple-element.26), channel_id=1, source_target_pairs={{28,0},{8,4},{4,8},{16,12},{12,16},{24,20},{20,24},{0,28},{29,1},{... | collective-permute-start | bytes 1179656 | tf_op jit(solution)/shard_map/ppermute | solution.py:457
  7.9 19.9 %collective-permute-start = (f32[3,2,128,128]{3,2,1,0:T(8,128)S(1)}, f32[3,2,128,128]{3,2,1,0:T(8,128)S(1)}, u32[]{:S(2)}, u32[]{:S(2)}) collective-permute-start(f32[3,2,128,128]{3,2,1,0:T(8,128)S(1)} %get-tuple-element.27), channel_id=1, source_target_pairs={{4,0},{0,4},{12,8},{8,12},{20,16},{16,20},{28,24},{24,28},{5,1},{1... | collective-permute-start | bytes 1179656 | tf_op jit(solution)/shard_map/ppermute | solution.py:457
  11.0 5.3 %collective-permute-start.2 = (f32[3,32,2,128]{3,2,1,0:T(2,128)S(1)}, f32[3,32,2,128]{3,2,1,0:T(2,128)S(1)}, u32[]{:S(2)}, u32[]{:S(2)}) collective-permute-start(f32[3,32,2,128]{3,2,1,0:T(2,128)S(1)} %get-tuple-element.14), channel_id=1, source_target_pairs={{1,0},{0,1},{3,2},{2,3},{5,4},{4,5},{7,6},{6,7},{9,8},{8,9},{11,10... | collective-permute-start | bytes 294920 | tf_op jit(solution)/shard_map/ppermute | solution.py:457
  11.1 5.3 %collective-permute-start.3 = (f32[3,32,2,128]{3,2,1,0:T(2,128)S(1)}, f32[3,32,2,128]{3,2,1,0:T(2,128)S(1)}, u32[]{:S(2)}, u32[]{:S(2)}) collective-permute-start(f32[3,32,2,128]{3,2,1,0:T(2,128)S(1)} %get-tuple-element.15), channel_id=1, source_target_pairs={{3,0},{2,1},{1,2},{0,3},{7,4},{6,5},{5,6},{4,7},{11,8},{10,9},{9,1... | collective-permute-start | bytes 294920 | tf_op jit(solution)/shard_map/ppermute | solution.py:457
  12.7 3.6 %collective-permute-start.4 = (f32[8,128]{1,0:T(8,128)S(1)}, f32[8,128]{1,0:T(8,128)S(1)}, u32[]{:S(2)}, u32[]{:S(2)}) collective-permute-start(f32[8,128]{1,0:T(8,128)S(1)} %get-tuple-element.16.pay_ref), channel_id=1, source_target_pairs={{2,0},{3,1},{0,2},{1,3},{6,4},{7,5},{4,6},{5,7},{10,8},{11,9},{8,1... | collective-permute-start | bytes 12296 | tf_op jit(solution)/shard_map/ppermute | solution.py:457
  13.2 4.5 %copy-start = (f32[15,8,128]{2,1,0:T(8,128)S(1)}, f32[15,8,128]{2,1,0:T(8,128)}, u32[]{:S(2)}) copy-start(f32[15,8,128]{2,1,0:T(8,128)} %constant.28.clone.coef_ref) | copy-start | bytes 184324
  16.6 5.9 %collective-permute-start.5 = (f32[128,128]{1,0:T(8,128)S(1)}, f32[128,128]{1,0:T(8,128)S(1)}, u32[]{:S(2)}, u32[]{:S(2)}) collective-permute-start(f32[128,128]{1,0:T(8,128)S(1)} %get-tuple-element.19._.mine_ref), channel_id=1, source_target_pairs={{16,0},{20,4},{24,8},{28,12},{0,16},{4,20},{8,24},{12,28},{17,1},{... | collective-permute-start | bytes 196616 | tf_op jit(solution)/shard_map/ppermute | solution.py:457
  22.6 6.9 %collective-permute-start.8 = (f32[8,128]{1,0:T(8,128)S(1)}, f32[8,128]{1,0:T(8,128)S(1)}, u32[]{:S(2)}, u32[]{:S(2)}) collective-permute-start(f32[8,128]{1,0:T(8,128)S(1)} %with_partner.1._.refs_0_), channel_id=1, source_target_pairs={{12,0},{8,4},{4,8},{0,12},{28,16},{24,20},{20,24},{16,28},{13,1},{... | collective-permute-start | bytes 12296 | tf_op jit(solution)/shard_map/ppermute | solution.py:457
  22.7 6.8 %collective-permute-start.7 = (f32[8,128]{1,0:T(8,128)S(1)}, f32[8,128]{1,0:T(8,128)S(1)}, u32[]{:S(2)}, u32[]{:S(2)}) collective-permute-start(f32[8,128]{1,0:T(8,128)S(1)} %with_partner.1._.refs_0_), channel_id=1, source_target_pairs={{8,0},{12,4},{0,8},{4,12},{24,16},{28,20},{16,24},{20,28},{9,1},{1... | collective-permute-start | bytes 12296 | tf_op jit(solution)/shard_map/ppermute | solution.py:457
  25.5 4.0 %collective-permute-start.6 = (f32[8,128]{1,0:T(8,128)S(1)}, f32[8,128]{1,0:T(8,128)S(1)}, u32[]{:S(2)}, u32[]{:S(2)}) collective-permute-start(f32[8,128]{1,0:T(8,128)S(1)} %with_partner.1._.refs_0_), channel_id=1, source_target_pairs={{4,0},{0,4},{12,8},{8,12},{20,16},{16,20},{28,24},{24,28},{5,1},{1... | collective-permute-start | bytes 12296 | tf_op jit(solution)/shard_map/ppermute | solution.py:457
  27.8 10.7 %collective-permute-start.9 = (f32[8,128]{1,0:T(8,128)S(1)}, f32[8,128]{1,0:T(8,128)S(1)}, u32[]{:S(2)}, u32[]{:S(2)}) collective-permute-start(f32[8,128]{1,0:T(8,128)S(1)} %get-tuple-element.22), channel_id=1, source_target_pairs={{1,0},{0,1},{3,2},{2,3},{5,4},{4,5},{7,6},{6,7},{9,8},{8,9},{11,10... | collective-permute-start | bytes 12296 | tf_op jit(solution)/shard_map/ppermute | solution.py:457
  27.9 10.6 %collective-permute-start.10 = (f32[8,128]{1,0:T(8,128)S(1)}, f32[8,128]{1,0:T(8,128)S(1)}, u32[]{:S(2)}, u32[]{:S(2)}) collective-permute-start(f32[8,128]{1,0:T(8,128)S(1)} %get-tuple-element.23), channel_id=1, source_target_pairs={{3,0},{2,1},{1,2},{0,3},{7,4},{6,5},{5,6},{4,7},{11,8},{10,9},{9,1... | collective-permute-start | bytes 12296 | tf_op jit(solution)/shard_map/ppermute | solution.py:457

commit v11 on v10

--- a/solution.py
+++ b/solution.py
@@ -38,6 +38,9 @@
     TURN_R,
     COUNT,
 ) = range(16)
+
+
+UNIT = VISCOSITY / (12.0 * AXIAL_STEP**2)
 
 
 def coefficients(radial, theta_step):
@@ -65,6 +68,7 @@
     rows[CENTRE_R] = common - 30.0 * rows[SECOND_F] - nu / face**2
     rows[CURVE_R] = 1.0 / (16.0 * face)
     rows[TURN_R] = -nu / (h * face**2)
+    rows[RADIAL_C:] /= UNIT
     return np.broadcast_to(rows[:, None, :], (COUNT, 8, radial)).astype(np.float32)
 
 
@@ -105,10 +109,9 @@
     first_lane = lane == 0
     last_lane = lane == a.shape[1] - 1
 
-    nu = VISCOSITY
-    lap = nu / dr**2
-    adv_z = -1.0 / (12.0 * AXIAL_STEP)
-    vis_z = nu / (12.0 * AXIAL_STEP**2)
+    lap = VISCOSITY / dr**2 / UNIT
+    adv_z = -1.0 / (12.0 * AXIAL_STEP) / UNIT
+    by_dr = 1.0 / dr / UNIT
 
     def differences(p1, m1, p2, m2):
         return 8.0 * (p1 - m1) - (p2 - m2), 16.0 * (p1 + m1) - (p2 + m2)
@@ -137,18 +140,18 @@
     up, low = above(2), below(2)
     u_r = pair_a + pair_next
     u_t = cells.beside(q, 0) + cells.beside(q, 1)
-    h_z = (up - low) * (coef[RADIAL_C] - u_r * (0.125 / dr)) + (up + low) * lap
+    h_z = (up - low) * (coef[RADIAL_C] - u_r * (0.125 * by_dr)) + (up + low) * lap
     h_z = h_z + theta[0] * (u_t * coef[CROSS_Z])
-    h_z = h_z + (theta[1] * coef[SECOND_C] + axial[1] * vis_z)
+    h_z = h_z + (theta[1] * coef[SECOND_C] + axial[1])
     h_z = h_z + c * (coef[CENTRE_Z] + axial[0] * adv_z)
 
     theta, axial = pieces(1)
     up, low = above(1), below(1)
     u_r = pair_a + pair_side
     u_z = cells.beside(q, -1) + cells.beside(q + 1, -1)
-    h_t = (up - low) * (coef[RADIAL_C] - u_r * (0.125 / dr)) + (up + low) * lap
+    h_t = (up - low) * (coef[RADIAL_C] - u_r * (0.125 * by_dr)) + (up + low) * lap
     h_t = h_t + b * (coef[CENTRE_T] + theta[0] * coef[THETA_C] - u_r * coef[CURVE_T])
-    h_t = h_t + (theta[1] * coef[SECOND_C] + axial[1] * vis_z)
+    h_t = h_t + (theta[1] * coef[SECOND_C] + axial[1])
     h_t = h_t + axial[0] * (u_z * (0.25 * adv_z))
     h_t = h_t + (pair_side - pair_a) * coef[TURN_T]
 
@@ -156,21 +159,22 @@
     up, low = turned(-1, 0, q), below(0)
     u_t = pair_b + pair_back
     u_z = pair(-1, 2, q) + pair(-1, 2, q, -1)
-    h_r = (up - low) * (coef[RADIAL_F] - a * (0.5 / dr)) + (up + low) * lap
+    h_r = (up - low) * (coef[RADIAL_F] - a * (0.5 * by_dr)) + (up + low) * lap
     h_r = h_r + u_t * (u_t * coef[CURVE_R] + theta[0] * coef[THETA_F])
-    h_r = h_r + (theta[1] * coef[SECOND_F] + axial[1] * vis_z)
+    h_r = h_r + (theta[1] * coef[SECOND_F] + axial[1])
     h_r = h_r + (axial[0] * (u_z * (0.25 * adv_z)) + a * coef[CENTRE_R])
     h_r = h_r + (pair_b - pair_back) * coef[TURN_R]
     return h_r, h_t, h_z
 
 
 def lane_zero_terms(cells, ghost, coef, q, dr):
-    lap = VISCOSITY / dr**2
+    lap = VISCOSITY / dr**2 / UNIT
+    by_dr = 1.0 / dr / UNIT
     a = cells.at(0, q)
     first_lane = lax.broadcasted_iota(jnp.int32, a.shape, 1) == 0
-    add_r = ghost(0, q) * (lap - coef[RADIAL_F] + a * (0.5 / dr))
-    add_t = ghost(1, q) * (lap - coef[RADIAL_C] + (a + cells.at(0, q + 1)) * (0.125 / dr))
-    add_z = ghost(2, q) * (lap - coef[RADIAL_C] + (a + cells.at(0, q, 1)) * (0.125 / dr))
+    add_r = ghost(0, q) * (lap - coef[RADIAL_F] + a * (0.5 * by_dr))
+    add_t = ghost(1, q) * (lap - coef[RADIAL_C] + (a + cells.at(0, q + 1)) * (0.125 * by_dr))
+    add_z = ghost(2, q) * (lap - coef[RADIAL_C] + (a + cells.at(0, q, 1)) * (0.125 * by_dr))
     return tuple(jnp.where(first_lane, x, 0.0) for x in (add_r, add_t, add_z))
 
 
@@ -286,6 +290,10 @@
     top = jnp.maximum(mine_ref[0:1, :], inner_ref[0:1, :])
     top = jnp.max(jnp.where(lane == radial - 1, top, 0.0), axis=(0, 1), keepdims=True)
     top_ref[...] = jnp.broadcast_to(top, top_ref.shape)
+
+
+def merged(mine_ref, far_ref, _, top_ref):
+    top_ref[...] = jnp.maximum(mine_ref[...], far_ref[...])
 
 
 def theta_in(even_ref, odd_ref, vel_in, _, even_tile, odd_tile, vel_ref):
@@ -364,29 +372,28 @@
         block_terms(vel_ref, inner_ref, coef_ref, j, BLOCK, write)
 
 
-def interior(spans, count, vel_ref, inner_ref, coef_ref, part_a, part_b, *refs):
-    tops, (out_ref, step_ref, res, sems) = refs[:count], refs[-4:]
+def finish(spans, vel_in, inner_ref, coef_ref, part_a, part_b, part_c, top, far, even, odd, *refs):
+    del vel_in
+    out_ref, step_ref, vel_ref, res, sems = refs
     axial, radial = inner_ref.shape
     planes = vel_ref.shape[1] - 2 * HALO
-    top = tops[0][0:1, :]
-    for ref in tops[1:]:
-        top = jnp.maximum(top, ref[0:1, :])
-    time_step = CFL_TARGET / (jnp.max(top) + 1e-06)
+    largest = jnp.maximum(top[0:1, :], far[0:1, :])
+    time_step = CFL_TARGET / (jnp.max(largest) + 1e-06)
     step_ref[0] = time_step
-    scale = GAMMA * time_step
+    scale = GAMMA * UNIT * time_step
     factors = (scale * coef_ref[WALL], scale, scale)
     pending = []
 
-    def send(j):
-        part_of = pl.ds(j, BLOCK)
+    def send(j, size):
+        part_of = pl.ds(j, size)
         copy = pltpu.make_async_copy(
-            res.at[:, pl.ds(j - HALO, BLOCK)], out_ref.at[:, part_of], sems.at[len(pending)]
+            res.at[:, part_of], out_ref.at[:, part_of], sems.at[len(pending)]
         )
         copy.start()
         pending.append(copy)
 
     def write(n, j, k, value):
-        res[n, j - HALO, k, :] = value * factors[n]
+        res[n, j, k, :] = value * factors[n]
 
     def complete(part, j, place, add):
         groups = 4
@@ -409,45 +416,23 @@
             return carry
 
         lax.fori_loop(0, axial // (8 * groups), rows, 0)
-        send(j)
-
-    for part, (first, last), add in ((part_a, spans[0], True), (part_b, spans[1], False)):
+        send(j, BLOCK)
+
+    for part, (first, last), add in zip((part_a, part_b, part_c), spans, (True, False, False)):
         for j in range(first, last, BLOCK):
             complete(part, j, j - first, add)
-    for j in range(*spans[2], BLOCK):
+    for j in range(*spans[3], BLOCK):
         block_terms(vel_ref, inner_ref, coef_ref, j, BLOCK, write)
-        send(j)
-    for copy in pending:
-        copy.wait()
-
-
-def edges(
-    step_ref, even_ref, odd_ref, inner_ref, coef_ref, vel_in, part, out_ref, vel_ref, res, sems
-):
-    del vel_in, part
-    axial = inner_ref.shape[0]
-    planes = vel_ref.shape[1] - 2 * HALO
-    scale = GAMMA * step_ref[0]
-    factors = (scale * coef_ref[WALL], scale, scale)
-    odd = lax.rem(lax.axis_index("ax"), 2) == 1
-    even, other = even_ref[0:1, :], odd_ref[0:1, :]
-    following, preceding = jnp.where(odd, other, even), jnp.where(odd, even, other)
+        send(j, BLOCK)
+
+    second = lax.rem(lax.axis_index("ax"), 2) == 1
+    even, odd = even[0:1, :], odd[0:1, :]
+    following, preceding = jnp.where(second, odd, even), jnp.where(second, even, odd)
     vel_ref[1, HALO - 1, PAD + axial : PAD + axial + 1, :] = following
     vel_ref[2, HALO + planes, PAD - 1 : PAD, :] = preceding
-    pending = []
-    for side, first in enumerate((0, planes - HALO)):
-
-        def write(n, j, k, value, shift=side * HALO - first):
-            res[n, j + shift, k, :] = value * factors[n]
-
-        block_terms(vel_ref, inner_ref, coef_ref, first, HALO, write)
-        copy = pltpu.make_async_copy(
-            res.at[:, pl.ds(side * HALO, HALO)],
-            out_ref.at[:, pl.ds(first, HALO)],
-            sems.at[side],
-        )
-        copy.start()
-        pending.append(copy)
+    for j in (0, planes - HALO):
+        block_terms(vel_ref, inner_ref, coef_ref, j, HALO, write)
+        send(j, HALO)
     for copy in pending:
         copy.wait()
 
@@ -471,7 +456,8 @@
 
 
 def cuts(planes):
-    ends = (HALO, HALO + 2 * BLOCK, HALO + 3 * BLOCK, planes - HALO)
+    last = planes - HALO
+    ends = (HALO, last - 3 * BLOCK, last - 2 * BLOCK, last - BLOCK, last)
     return list(zip(ends[:-1], ends[1:]))
 
 
@@ -565,15 +551,30 @@
         in_specs=[vmem] * 3,
         out_specs=vmem,
     )(mine, inner, part_a)
-    tops = (top, *(exchanged(top, "az", step) for step in range(1, sizes[0] // 2)))
-    part_b = call(
-        functools.partial(ahead_with_ghosts, *spans[1]),
-        "ahead_with_ghosts",
-        velocity.size,
-        out_shape=part_shape(1),
-        in_specs=[vmem] * 4,
-        out_specs=vmem,
-    )(vel, inner, coef, top)
+    steps = [1 << n for n in range((sizes[0] // 2).bit_length() - 1)]
+    far = exchanged(top, "az", steps[0])
+
+    def with_ghosts(n, token):
+        return call(
+            functools.partial(ahead_with_ghosts, *spans[n]),
+            f"ahead_with_ghosts_{n}",
+            velocity.size,
+            out_shape=part_shape(n),
+            in_specs=[vmem] * 4,
+            out_specs=vmem,
+        )(vel, inner, coef, token)
+
+    part_b = with_ghosts(1, top)
+    for step in steps[1:]:
+        top = call(
+            merged,
+            "merged",
+            0,
+            out_shape=tile,
+            in_specs=[vmem] * 3,
+            out_specs=vmem,
+        )(top, far, part_b)
+        far = exchanged(top, "az", step)
     tile_even, tile_odd, vel = call(
         theta_in,
         "theta_in",
@@ -582,35 +583,23 @@
         in_specs=[vmem] * 4,
         out_specs=(vmem,) * 3,
         input_output_aliases={2: 2},
-    )(theta_even, theta_odd, vel, part_b)
+    )(theta_even, theta_odd, vel, top)
     corner_even, corner_odd = across_edges(tile_even, tile_odd, "ax")
-    part, time_step = call(
-        functools.partial(interior, spans, len(tops)),
-        "interior",
-        4 * velocity.size,
-        scratch=6,
-        out_shape=(shape(*velocity.shape), shape(1)),
-        in_specs=[vmem] * (5 + len(tops)),
-        out_specs=(anywhere, smem),
+    part_c = with_ghosts(2, tile_even)
+    increment, time_step, _ = call(
+        functools.partial(finish, spans),
+        "finish",
+        0,
+        scratch=8,
+        out_shape=(shape(*velocity.shape), shape(1), padded),
+        in_specs=[vmem] * 10,
+        out_specs=(anywhere, smem, vmem),
         scratch_shapes=[
-            pltpu.VMEM((3, planes - 2 * HALO, axial, radial), f32),
-            pltpu.SemaphoreType.DMA(((planes - 2 * HALO) // BLOCK,)),
+            pltpu.VMEM(velocity.shape, f32),
+            pltpu.SemaphoreType.DMA(((planes - 2 * HALO) // BLOCK + 2,)),
         ],
-    )(vel, inner, coef, part_a, part_b, *tops)
-    increment, _ = call(
-        edges,
-        "edges",
-        0,
-        scratch=2,
-        out_shape=(shape(*velocity.shape), padded),
-        in_specs=[smem] + [vmem] * 5 + [anywhere],
-        out_specs=(anywhere, vmem),
-        scratch_shapes=[
-            pltpu.VMEM((3, 2 * HALO, axial, radial), f32),
-            pltpu.SemaphoreType.DMA((2,)),
-        ],
-        input_output_aliases={5: 1, 6: 0},
-    )(time_step, corner_even, corner_odd, inner, coef, vel, part)
+        input_output_aliases={0: 2},
+    )(vel, inner, coef, part_a, part_b, part_c, top, far, corner_even, corner_odd)
     return increment, time_step.reshape(())
 
 

time: 41.8 us -> 37.1 us (0.89)
  starting transfers between devices: 14.6 us -> 12.4 us
  Pallas kernels: 22.5 us -> 21.1 us
  waiting for transfers between devices: 2.47 us -> 1.56 us
    pallas_call x3 -> x4, Pallas kernels: 13.6 us -> 9.69 us  [the longest x1 6.63 us: per_device(): call(functools.partial(finish, spans), 'finish', 0, scratch=8, out_shape=...]
    pallas_call x1, Pallas kernels: 2.7 us -> 5.17 us  [per_device(): call(functools.partial(ahead, *spans[0]), 'ahead', velocity.size, out_sha...]
    ppermute x11 -> x10, starting transfers between devices: 14.6 us -> 12.4 us  [routed(): return lax.ppermute(block, axis, [(source(i), i) for i in range(count)])]
    ppermute x11 -> x10, waiting for transfers between devices: 2.47 us -> 1.56 us  [routed(): return lax.ppermute(block, axis, [(source(i), i) for i in range(count)])]
  transfers between devices with their start and end apart: 11 -> 10, of which waited for: 2 -> 3; matrix products, arithmetic and copies ran while one was open for 0% -> 0% of each run, Pallas kernels for 47% -> 39%
where the time goes in v11:
time: 37.1 us; the launch traced here: 37 us
  Pallas kernels  21.1 us (57%)
  starting transfers between devices  12.4 us (33%)
  waiting for transfers between devices  1.56 us (4%)
  local copies, waits for them, and re-layouts  1.18 us (3%)
  between operations  0.74 us (2%)
    ppermute x10, starting transfers between devices, routed(): return lax.ppermute(block, axis, [(source(i), i) for i in range(count)])  12.4 us
    pallas_call x1, Pallas kernels, per_device(): call(functools.partial(finish, spans), 'finish', 0, scratch=8, out_shape=...  6.63 us
    pallas_call x1, Pallas kernels, per_device(): call(functools.partial(ahead, *spans[0]), 'ahead', velocity.size, out_sha...  5.17 us
    pallas_call x1, Pallas kernels, per_device(): call(functools.partial(first_pass, theta_step), 'first_pass', 0, out_shap...  3.1 us
    pallas_call x2, Pallas kernels, with_ghosts(): call(functools.partial(ahead_with_ghosts, *spans[n]), f'ahead_with_ghosts...  3.06 us
    pallas_call x1, Pallas kernels, per_device(): call(pack, 'pack', velocity.size, out_shape=row, in_specs=[vmem], out_spe...  2.73 us
    ppermute x10, waiting for transfers between devices, routed(): return lax.ppermute(block, axis, [(source(i), i) for i in range(count)])  1.56 us
    dynamic_slice x1, local copies, waits for them, and re-layouts, per_device(): lax.dynamic_slice_in_dim(velocity, odd_end, HALO, 1)  1.18 us
  transfers between devices with their start and end apart: 10, of which 3 were waited for; matrix products, arithmetic and copies ran while one was open for 0% of the time, Pallas kernels for 39%

profile of v11, /device:TPU:0, one launch (start us, length us, event | category | flops | bytes accessed | tf_op | source)
XLA Modules:
  0.0 37.0 jit_solution(6752488000849465426)
XLA Ops:
  0.6 1.2 %constant_dynamic-slice_fusion = (f32[3,2,128,128]{3,2,1,0:T(8,128)S(1)}, f32[3,2,128,128]{3,2,1,0:T(8,128)S(1)}) fusion(f32[3,32,128,128]{3,2,1,0:T(8,128)} %v_ref.1, s32[]{:T(128)S(6)} %select_n.18, s32[]{:T(128)S(6)} %select_n.17), kind=kLoop, calls=%fused_computation | loop fusion | bytes 1572872 | tf_op jit(solution)/shard_map/dynamic_slice | solution.py:492
  1.8 6.1 %collective-permute-start.1 = (f32[3,2,128,128]{3,2,1,0:T(8,128)S(1)}, f32[3,2,128,128]{3,2,1,0:T(8,128)S(1)}, u32[]{:S(2)}, u32[]{:S(2)}) collective-permute-start(f32[3,2,128,128]{3,2,1,0:T(8,128)S(1)} %get-tuple-element.24), channel_id=1, source_target_pairs={{28,0},{8,4},{4,8},{16,12},{12,16},{24,20},{20,24},{0,28},{29,1},{... | collective-permute-start | bytes 1179656 | tf_op jit(solution)/shard_map/ppermute | solution.py:442
  7.9 0.0 collective-permute-start
  7.9 3.1 %first_pass.1 = (f32[3,36,144,128]{3,2,1,0:T(8,128)S(1)}, f32[3,32,2,128]{3,2,1,0:T(2,128)S(1)}, f32[3,32,2,128]{3,2,1,0:T(2,128)S(1)}, f32[8,128]{1,0:T(8,128)S(1)}) custom-call(f32[3,32,128,128]{3,2,1,0:T(8,128)} %v_ref.1), custom_call_target="tpu_custom_call" | custom-call | tf_op jit(solution)/shard_map/first_pass/pallas_call | solution.py:500
  11.0 0.1 collective-permute-start.2
  11.1 1.6 %collective-permute-start.3 = (f32[3,32,2,128]{3,2,1,0:T(2,128)S(1)}, f32[3,32,2,128]{3,2,1,0:T(2,128)S(1)}, u32[]{:S(2)}, u32[]{:S(2)}) collective-permute-start(f32[3,32,2,128]{3,2,1,0:T(2,128)S(1)} %get-tuple-element.14), channel_id=1, source_target_pairs={{3,0},{2,1},{1,2},{0,3},{7,4},{6,5},{5,6},{4,7},{11,8},{10,9},{9,1... | collective-permute-start | bytes 294920 | tf_op jit(solution)/shard_map/ppermute | solution.py:442
  12.7 0.5 %collective-permute-start.4 = (f32[8,128]{1,0:T(8,128)S(1)}, f32[8,128]{1,0:T(8,128)S(1)}, u32[]{:S(2)}, u32[]{:S(2)}) collective-permute-start(f32[8,128]{1,0:T(8,128)S(1)} %get-tuple-element.15.pay_ref), channel_id=1, source_target_pairs={{2,0},{3,1},{0,2},{1,3},{6,4},{7,5},{4,6},{5,7},{10,8},{11,9},{8,1... | collective-permute-start | bytes 12296 | tf_op jit(solution)/shard_map/ppermute | solution.py:442
  13.2 0.0 copy-start
  13.2 2.7 %pack.1.inner_in = f32[128,128]{1,0:T(8,128)S(1)} custom-call(f32[3,36,144,128]{3,2,1,0:T(8,128)S(1)} %get-tuple-element.16.vel_ref.vel_in), custom_call_target="tpu_custom_call" | custom-call | flops 1572864 | bytes 1572864 | tf_op jit(solution)/shard_map/pack/pallas_call | solution.py:514
  16.0 0.4 collective-permute-done.4.refs_0_
  16.3 0.0 collective-permute-done.2.even_ref
  16.3 0.0 collective-permute-done.3.odd_ref
  16.3 0.2 fold.1
  16.6 1.1 %collective-permute-start.5 = (f32[128,128]{1,0:T(8,128)S(1)}, f32[128,128]{1,0:T(8,128)S(1)}, u32[]{:S(2)}, u32[]{:S(2)}) collective-permute-start(f32[128,128]{1,0:T(8,128)S(1)} %get-tuple-element.18._.mine_ref), channel_id=1, source_target_pairs={{16,0},{20,4},{24,8},{28,12},{0,16},{4,20},{8,24},{12,28},{17,1},{... | collective-permute-start | bytes 196616 | tf_op jit(solution)/shard_map/ppermute | solution.py:442
  17.7 0.0 copy-done
  17.7 5.2 %ahead.1._.part_a = f32[3,16,128,128]{3,2,1,0:T(8,128)S(1)} custom-call(f32[3,36,144,128]{3,2,1,0:T(8,128)S(1)} %get-tuple-element.17.vel_ref.vel_in, f32[15,8,128]{2,1,0:T(8,128)S(1)} %copy-done, f32[128,128]{1,0:T(8,128)S(1)} %get-tuple-element.18._.mine_ref), custom_call_target="tpu_custom_call" | custom-call | flops 1572864 | bytes 1572864 | tf_op jit(solution)/shard_map/ahead/pallas_call | solution.py:538
  22.9 0.0 collective-permute-done.5.inner_ref
  22.9 0.1 with_partner.1._.mine_ref
  23.0 1.0 %collective-permute-start.6 = (f32[8,128]{1,0:T(8,128)S(1)}, f32[8,128]{1,0:T(8,128)S(1)}, u32[]{:S(2)}, u32[]{:S(2)}) collective-permute-start(f32[8,128]{1,0:T(8,128)S(1)} %with_partner.1._.mine_ref), channel_id=1, source_target_pairs={{4,0},{0,4},{12,8},{8,12},{20,16},{16,20},{28,24},{24,28},{5,1},{1... | collective-permute-start | bytes 12296 | tf_op jit(solution)/shard_map/ppermute | solution.py:442
  24.1 1.5 %ahead_with_ghosts_1.1._.part_b = f32[3,4,128,128]{3,2,1,0:T(8,128)S(1)} custom-call(f32[3,36,144,128]{3,2,1,0:T(8,128)S(1)} %get-tuple-element.17.vel_ref.vel_in, f32[128,128]{1,0:T(8,128)S(1)} %collective-permute-done.5.inner_ref, f32[15,8,128]{2,1,0:T(8,128)S(1)} %copy-done, f32[8,128]{1,0:T(8,128)S(1)} %with_partner.1._.mine_ref), custom_call_target="tpu_custom_call" | custom-call | flops 1572864 | bytes 1572864 | tf_op jit(solution)/shard_map/ahead_with_ghosts_1/pallas_call | solution.py:558
  25.6 1.1 %collective-permute-done.6.far_ref = f32[8,128]{1,0:T(8,128)S(1)} collective-permute-done((f32[8,128]{1,0:T(8,128)S(1)}, f32[8,128]{1,0:T(8,128)S(1)}, u32[]{:S(2)}, u32[]{:S(2)}) %collective-permute-start.6) | collective-permute-done | bytes 4128 | tf_op jit(solution)/shard_map/ppermute | solution.py:442
  26.7 0.2 collective-permute-start.7
  26.9 0.0 collective-permute-done.1.odd_ref
  26.9 0.0 collective-permute-done.even_ref
  26.9 0.1 theta_in.1
  27.0 0.2 collective-permute-start.9
  27.2 1.5 %collective-permute-start.8 = (f32[8,128]{1,0:T(8,128)S(1)}, f32[8,128]{1,0:T(8,128)S(1)}, u32[]{:S(2)}, u32[]{:S(2)}) collective-permute-start(f32[8,128]{1,0:T(8,128)S(1)} %get-tuple-element.20._), channel_id=1, source_target_pairs={{1,0},{0,1},{3,2},{2,3},{5,4},{4,5},{7,6},{6,7},{9,8},{8,9},{11,10... | collective-permute-start | bytes 12296 | tf_op jit(solution)/shard_map/ppermute | solution.py:442
  28.7 1.5 %ahead_with_ghosts_2.1.part_c = f32[3,4,128,128]{3,2,1,0:T(8,128)S(1)} custom-call(f32[3,36,144,128]{3,2,1,0:T(8,128)S(1)} %get-tuple-element.19.vel_ref.vel_in, f32[128,128]{1,0:T(8,128)S(1)} %collective-permute-done.5.inner_ref, f32[15,8,128]{2,1,0:T(8,128)S(1)} %copy-done, f32[8,128]{1,0:T(8,128)S(1)} %get-tuple-element.20._), custom_call_target="tpu_custom_call" | custom-call | flops 1572864 | bytes 1572864 | tf_op jit(solution)/shard_map/ahead_with_ghosts_2/pallas_call | solution.py:558
  30.2 0.1 collective-permute-done.7.far
  30.3 0.0 collective-permute-done.9.odd
  30.3 0.0 collective-permute-done.8.even
  30.3 6.6 %finish.1 = (f32[3,32,128,128]{3,2,1,0:T(8,128)}, f32[1]{0:T(128)}, f32[3,36,144,128]{3,2,1,0:T(8,128)S(1)}) custom-call(f32[3,36,144,128]{3,2,1,0:T(8,128)S(1)} %get-tuple-element.19.vel_ref.vel_in, f32[128,128]{1,0:T(8,128)S(1)} %collective-permute-done.5.inner_ref, f32[15,8,128]{2,1,0:T(8,128)S(1)} %copy-done, ...), custom_call_target="tpu_custom_call", output_to_operand_aliasing={{2}: (0, {})} | custom-call | tf_op jit(solution)/shard_map/finish/pallas_call | solution.py:589
  (1 shorter events, 0.0 us)
Async XLA Ops:
  1.8 25.1 %collective-permute-start.1 = (f32[3,2,128,128]{3,2,1,0:T(8,128)S(1)}, f32[3,2,128,128]{3,2,1,0:T(8,128)S(1)}, u32[]{:S(2)}, u32[]{:S(2)}) collective-permute-start(f32[3,2,128,128]{3,2,1,0:T(8,128)S(1)} %get-tuple-element.24), channel_id=1, source_target_pairs={{28,0},{8,4},{4,8},{16,12},{12,16},{24,20},{20,24},{0,28},{29,1},{... | collective-permute-start | bytes 1179656 | tf_op jit(solution)/shard_map/ppermute | solution.py:442
  7.9 19.0 %collective-permute-start = (f32[3,2,128,128]{3,2,1,0:T(8,128)S(1)}, f32[3,2,128,128]{3,2,1,0:T(8,128)S(1)}, u32[]{:S(2)}, u32[]{:S(2)}) collective-permute-start(f32[3,2,128,128]{3,2,1,0:T(8,128)S(1)} %get-tuple-element.25), channel_id=1, source_target_pairs={{4,0},{0,4},{12,8},{8,12},{20,16},{16,20},{28,24},{24,28},{5,1},{1... | collective-permute-start | bytes 1179656 | tf_op jit(solution)/shard_map/ppermute | solution.py:442
  11.0 5.3 %collective-permute-start.2 = (f32[3,32,2,128]{3,2,1,0:T(2,128)S(1)}, f32[3,32,2,128]{3,2,1,0:T(2,128)S(1)}, u32[]{:S(2)}, u32[]{:S(2)}) collective-permute-start(f32[3,32,2,128]{3,2,1,0:T(2,128)S(1)} %get-tuple-element.13), channel_id=1, source_target_pairs={{1,0},{0,1},{3,2},{2,3},{5,4},{4,5},{7,6},{6,7},{9,8},{8,9},{11,10... | collective-permute-start | bytes 294920 | tf_op jit(solution)/shard_map/ppermute | solution.py:442
  11.1 5.3 %collective-permute-start.3 = (f32[3,32,2,128]{3,2,1,0:T(2,128)S(1)}, f32[3,32,2,128]{3,2,1,0:T(2,128)S(1)}, u32[]{:S(2)}, u32[]{:S(2)}) collective-permute-start(f32[3,32,2,128]{3,2,1,0:T(2,128)S(1)} %get-tuple-element.14), channel_id=1, source_target_pairs={{3,0},{2,1},{1,2},{0,3},{7,4},{6,5},{5,6},{4,7},{11,8},{10,9},{9,1... | collective-permute-start | bytes 294920 | tf_op jit(solution)/shard_map/ppermute | solution.py:442
  12.7 3.6 %collective-permute-start.4 = (f32[8,128]{1,0:T(8,128)S(1)}, f32[8,128]{1,0:T(8,128)S(1)}, u32[]{:S(2)}, u32[]{:S(2)}) collective-permute-start(f32[8,128]{1,0:T(8,128)S(1)} %get-tuple-element.15.pay_ref), channel_id=1, source_target_pairs={{2,0},{3,1},{0,2},{1,3},{6,4},{7,5},{4,6},{5,7},{10,8},{11,9},{8,1... | collective-permute-start | bytes 12296 | tf_op jit(solution)/shard_map/ppermute | solution.py:442
  13.2 4.5 %copy-start = (f32[15,8,128]{2,1,0:T(8,128)S(1)}, f32[15,8,128]{2,1,0:T(8,128)}, u32[]{:S(2)}) copy-start(f32[15,8,128]{2,1,0:T(8,128)} %constant.28.clone.coef_ref) | copy-start | bytes 184324
  16.6 6.3 %collective-permute-start.5 = (f32[128,128]{1,0:T(8,128)S(1)}, f32[128,128]{1,0:T(8,128)S(1)}, u32[]{:S(2)}, u32[]{:S(2)}) collective-permute-start(f32[128,128]{1,0:T(8,128)S(1)} %get-tuple-element.18._.mine_ref), channel_id=1, source_target_pairs={{16,0},{20,4},{24,8},{28,12},{0,16},{4,20},{8,24},{12,28},{17,1},{... | collective-permute-start | bytes 196616 | tf_op jit(solution)/shard_map/ppermute | solution.py:442
  23.0 3.7 %collective-permute-start.6 = (f32[8,128]{1,0:T(8,128)S(1)}, f32[8,128]{1,0:T(8,128)S(1)}, u32[]{:S(2)}, u32[]{:S(2)}) collective-permute-start(f32[8,128]{1,0:T(8,128)S(1)} %with_partner.1._.mine_ref), channel_id=1, source_target_pairs={{4,0},{0,4},{12,8},{8,12},{20,16},{16,20},{28,24},{24,28},{5,1},{1... | collective-permute-start | bytes 12296 | tf_op jit(solution)/shard_map/ppermute | solution.py:442
  26.7 3.6 %collective-permute-start.7 = (f32[8,128]{1,0:T(8,128)S(1)}, f32[8,128]{1,0:T(8,128)S(1)}, u32[]{:S(2)}, u32[]{:S(2)}) collective-permute-start(f32[8,128]{1,0:T(8,128)S(1)} %merged.1._.top), channel_id=1, source_target_pairs={{8,0},{12,4},{0,8},{4,12},{24,16},{28,20},{16,24},{20,28},{9,1},{1... | collective-permute-start | bytes 12296 | tf_op jit(solution)/shard_map/ppermute | solution.py:442
  27.0 3.3 %collective-permute-start.9 = (f32[8,128]{1,0:T(8,128)S(1)}, f32[8,128]{1,0:T(8,128)S(1)}, u32[]{:S(2)}, u32[]{:S(2)}) collective-permute-start(f32[8,128]{1,0:T(8,128)S(1)} %get-tuple-element.21), channel_id=1, source_target_pairs={{3,0},{2,1},{1,2},{0,3},{7,4},{6,5},{5,6},{4,7},{11,8},{10,9},{9,1... | collective-permute-start | bytes 12296 | tf_op jit(solution)/shard_map/ppermute | solution.py:442
  27.2 3.2 %collective-permute-start.8 = (f32[8,128]{1,0:T(8,128)S(1)}, f32[8,128]{1,0:T(8,128)S(1)}, u32[]{:S(2)}, u32[]{:S(2)}) collective-permute-start(f32[8,128]{1,0:T(8,128)S(1)} %get-tuple-element.20._), channel_id=1, source_target_pairs={{1,0},{0,1},{3,2},{2,3},{5,4},{4,5},{7,6},{6,7},{9,8},{8,9},{11,10... | collective-permute-start | bytes 12296 | tf_op jit(solution)/shard_map/ppermute | solution.py:442

commit v12 on v11

--- a/solution.py
+++ b/solution.py
@@ -183,12 +183,11 @@
     return jnp.where(lane == radial - 1, 0.0, 1.0).astype(jnp.float32)
 
 
-def first_pass(theta_step, v_ref, vel_ref, even_ref, odd_ref, pay_ref, sems):
+def first_pass(theta_step, v_ref, vel_ref, even_ref, odd_ref, inner_ref, pay_ref, sems):
     _, planes, axial, radial = v_ref.shape
     lane = lax.broadcasted_iota(jnp.int32, (8, radial), 1)
     wall = wall_mask(8, radial)
     rate_t = (radial / theta_step) / (lane.astype(jnp.float32) + 0.5)
-
     odd = lax.rem(lax.axis_index("ax"), 2) == 1
 
     def fetch(g):
@@ -199,23 +198,28 @@
     for g in range(planes // GROUP):
         fetch(g).start()
 
-    def group(g, largest):
+    zero = jnp.zeros((8, radial), jnp.float32)
+    largest = [zero] * 4
+    for g in range(planes // GROUP):
         fetch(g).wait()
-
-        def rows(i, largest):
-            k = pl.ds(pl.multiple_of(i * 8, 8) + PAD, 8)
-            largest = list(largest)
+        for i in range(axial // 8):
+            k = pl.ds(8 * i, 8)
+            padded = pl.ds(8 * i + PAD, 8)
+            inner = zero if g == 0 else inner_ref[k, :]
             for q in range(GROUP):
-                j = g * GROUP + HALO + q
-                a, b, c = (vel_ref[n, j, k, :] for n in range(3))
+                j = g * GROUP + q
+                cells = [vel_ref[n, j + HALO, padded, :] for n in range(3)]
+                for n, x in enumerate(cells):
+                    place = n * planes + j
+                    x = pltpu.roll(x, place, 1) if place else x
+                    inner = jnp.where(lane == place, x if n == 2 else -x, inner)
+                a, b, c = cells
                 a = a * wall
-                vel_ref[0, j, k, :] = a
+                vel_ref[0, j + HALO, padded, :] = a
                 rate = jnp.abs(a) * float(radial) + jnp.abs(b) * rate_t
                 rate = rate + jnp.abs(c) * (1.0 / AXIAL_STEP)
                 largest[q % 4] = jnp.maximum(largest[q % 4], rate)
-            return tuple(largest)
-
-        largest = lax.fori_loop(0, axial // 8, rows, largest, unroll=4)
+            inner_ref[k, :] = inner
         for q in range(GROUP):
             for n in range(3):
                 j = g * GROUP + q
@@ -223,52 +227,29 @@
                 last = vel_ref[n, j + HALO, PAD + axial - 2 : PAD + axial, :]
                 even_ref[n, j] = jnp.where(odd, first, last)
                 odd_ref[n, j] = jnp.where(odd, last, first)
-        return largest
-
-    zero = jnp.zeros((8, radial), jnp.float32)
-    m = lax.fori_loop(0, planes // GROUP, group, (zero,) * 4)
-    largest = jnp.maximum(jnp.maximum(m[0], m[1]), jnp.maximum(m[2], m[3]))
+
+    largest = jnp.maximum(
+        jnp.maximum(largest[0], largest[1]), jnp.maximum(largest[2], largest[3])
+    )
     top = jnp.max(largest, axis=(0, 1), keepdims=True)
     pay_ref[...] = jnp.broadcast_to(top, pay_ref.shape)
-    last = lax.broadcasted_iota(jnp.int32, (2, radial), 1) == radial - 1
+    end = lax.broadcasted_iota(jnp.int32, (2, radial), 1) == radial - 1
     for ref in (even_ref, odd_ref):
-        ref[0, 0] = jnp.where(last, top, ref[0, 0])
-
-
-def pack(vel_ref, inner_ref):
-    planes, (axial, radial) = vel_ref.shape[1] - 2 * HALO, inner_ref.shape
-    lane = lax.broadcasted_iota(jnp.int32, (8, radial), 1)
-    sign = jnp.where(lane < 2 * planes, -1.0, 1.0).astype(jnp.float32)
-
-    def rows(i, carry):
-        k = pl.multiple_of(i * 8, 8)
-        inner = [jnp.zeros((8, radial), jnp.float32)] * 3
-        for j in range(planes):
-            for n in range(3):
-                place = n * planes + j
-                x = vel_ref[n, j + HALO, pl.ds(k + PAD, 8), :]
-                x = pltpu.roll(x, place, 1)
-                inner[n] = jnp.where(lane == place, x, inner[n])
-        inner_ref[pl.ds(k, 8), :] = (inner[0] + inner[1] + inner[2]) * sign
-        return carry
-
-    lax.fori_loop(0, axial // 8, rows, 0)
-
-
-def fold(even_ref, odd_ref, pay_ref, inner_in, vel_in, *refs):
+        ref[0, 0] = jnp.where(end, top, ref[0, 0])
+
+
+def fold(even_ref, odd_ref, pay_ref, vel_in, *refs):
     del vel_in
-    fars, (inner_ref, vel_ref) = refs[:-2], refs[-2:]
-    planes = even_ref.shape[1]
-    axial, radial = inner_in.shape
+    fars, (top_ref, vel_ref) = refs[:-2], refs[-2:]
+    planes, radial = even_ref.shape[1], even_ref.shape[3]
+    axial = vel_ref.shape[2] - 2 * PAD
     lane = lax.broadcasted_iota(jnp.int32, (1, radial), 1)
     top = jnp.maximum(even_ref[0, 0, 0:1, :], odd_ref[0, 0, 0:1, :])
     top = jnp.max(jnp.where(lane == radial - 1, top, 0.0), axis=(0, 1), keepdims=True)
     top = jnp.maximum(pay_ref[...], top)
     for far in fars:
         top = jnp.maximum(top, far[...])
-    lane = lax.broadcasted_iota(jnp.int32, top.shape, 1)
-    inner_ref[...] = inner_in[...]
-    inner_ref[0:8, :] = jnp.where(lane == radial - 1, top, inner_in[0:8, :])
+    top_ref[...] = top
     wall = wall_mask(2, radial)
     odd = lax.rem(lax.axis_index("ax"), 2) == 1
 
@@ -282,14 +263,6 @@
         return carry
 
     lax.fori_loop(0, planes, plane, 0, unroll=4)
-
-
-def with_partner(mine_ref, inner_ref, _, top_ref):
-    radial = inner_ref.shape[1]
-    lane = lax.broadcasted_iota(jnp.int32, (1, radial), 1)
-    top = jnp.maximum(mine_ref[0:1, :], inner_ref[0:1, :])
-    top = jnp.max(jnp.where(lane == radial - 1, top, 0.0), axis=(0, 1), keepdims=True)
-    top_ref[...] = jnp.broadcast_to(top, top_ref.shape)
 
 
 def merged(mine_ref, far_ref, _, top_ref):
@@ -372,7 +345,8 @@
         block_terms(vel_ref, inner_ref, coef_ref, j, BLOCK, write)
 
 
-def finish(spans, vel_in, inner_ref, coef_ref, part_a, part_b, part_c, top, far, even, odd, *refs):
+def finish(spans, vel_in, inner_ref, coef_ref, top, far, even, odd, *refs):
+    parts, refs = refs[: len(spans)], refs[len(spans) :]
     del vel_in
     out_ref, step_ref, vel_ref, res, sems = refs
     axial, radial = inner_ref.shape
@@ -418,12 +392,9 @@
         lax.fori_loop(0, axial // (8 * groups), rows, 0)
         send(j, BLOCK)
 
-    for part, (first, last), add in zip((part_a, part_b, part_c), spans, (True, False, False)):
+    for n, (part, (first, last)) in enumerate(zip(parts, spans)):
         for j in range(first, last, BLOCK):
-            complete(part, j, j - first, add)
-    for j in range(*spans[3], BLOCK):
-        block_terms(vel_ref, inner_ref, coef_ref, j, BLOCK, write)
-        send(j, BLOCK)
+            complete(part, j, j - first, n == 0)
 
     second = lax.rem(lax.axis_index("ax"), 2) == 1
     even, odd = even[0:1, :], odd[0:1, :]
@@ -457,7 +428,7 @@
 
 def cuts(planes):
     last = planes - HALO
-    ends = (HALO, last - 3 * BLOCK, last - 2 * BLOCK, last - BLOCK, last)
+    ends = (HALO, last - 5 * BLOCK, last - 3 * BLOCK, last - BLOCK, last)
     return list(zip(ends[:-1], ends[1:]))
 
 
@@ -497,13 +468,13 @@
     padded = shape(3, planes + 2 * HALO, axial + 2 * PAD, radial)
     row = shape(axial, radial)
     tile = shape(8, radial)
-    vel, edge_even, edge_odd, pay = call(
+    vel, edge_even, edge_odd, mine, pay = call(
         functools.partial(first_pass, theta_step),
         "first_pass",
         0,
-        out_shape=(padded, edge, edge, tile),
+        out_shape=(padded, edge, edge, row, tile),
         in_specs=[anywhere],
-        out_specs=(vmem,) * 4,
+        out_specs=(vmem,) * 5,
         scratch_shapes=[pltpu.SemaphoreType.DMA((planes // GROUP,))],
     )(pltpu.with_memory_space_constraint(velocity, pltpu.HBM))
     z_even, z_odd = across_edges(edge_even, edge_odd, "ax")
@@ -511,70 +482,45 @@
         routed(pay, "ax", lambda i, step=step: (i + step) % sizes[1])
         for step in range(2, sizes[1] - 1)
     ]
-    inner = call(
-        pack,
-        "pack",
-        velocity.size,
-        out_shape=row,
-        in_specs=[vmem],
-        out_specs=vmem,
-    )(vel)
-    mine, vel = call(
+    inner = exchanged(mine, "az", sizes[0] // 2)
+    top, vel = call(
         fold,
         "fold",
         0,
-        out_shape=(row, padded),
-        in_specs=[vmem] * (5 + len(fars)),
+        out_shape=(tile, padded),
+        in_specs=[vmem] * (4 + len(fars)),
         out_specs=(vmem,) * 2,
-        input_output_aliases={4: 1},
-    )(z_even, z_odd, pay, inner, vel, *fars)
-    inner = exchanged(mine, "az", sizes[0] // 2)
+        input_output_aliases={3: 1},
+    )(z_even, z_odd, pay, vel, *fars)
 
     spans = cuts(planes)
 
-    def part_shape(n):
-        return shape(3, spans[n][1] - spans[n][0], axial, radial)
-
-    part_a = call(
-        functools.partial(ahead, *spans[0]),
-        "ahead",
-        velocity.size,
-        out_shape=part_shape(0),
-        in_specs=[vmem] * 3,
-        out_specs=vmem,
-    )(vel, coef, mine)
-    top = call(
-        with_partner,
-        "with_partner",
-        0,
-        out_shape=tile,
-        in_specs=[vmem] * 3,
-        out_specs=vmem,
-    )(mine, inner, part_a)
-    steps = [1 << n for n in range((sizes[0] // 2).bit_length() - 1)]
-    far = exchanged(top, "az", steps[0])
-
-    def with_ghosts(n, token):
+    def span(n, token):
+        kernel, given = (ahead, (vel, coef)) if n == 0 else (ahead_with_ghosts, (vel, inner, coef))
+        first, last = spans[n]
         return call(
-            functools.partial(ahead_with_ghosts, *spans[n]),
-            f"ahead_with_ghosts_{n}",
-            velocity.size,
-            out_shape=part_shape(n),
-            in_specs=[vmem] * 4,
+            functools.partial(kernel, first, last),
+            f"span_{n}",
+            velocity.size * 2,
+            out_shape=shape(3, last - first, axial, radial),
+            in_specs=[vmem] * (len(given) + 1),
             out_specs=vmem,
-        )(vel, inner, coef, token)
-
-    part_b = with_ghosts(1, top)
-    for step in steps[1:]:
-        top = call(
-            merged,
-            "merged",
-            0,
-            out_shape=tile,
-            in_specs=[vmem] * 3,
-            out_specs=vmem,
-        )(top, far, part_b)
-        far = exchanged(top, "az", step)
+        )(*given, token)
+
+    parts, token = [], top
+    for n in range(sizes[0].bit_length() - 1):
+        if n > 0:
+            top = token = call(
+                merged,
+                "merged",
+                0,
+                out_shape=tile,
+                in_specs=[vmem] * 3,
+                out_specs=vmem,
+            )(top, far, parts[-1])
+        far = exchanged(top, "az", 1 << n)
+        if n < 3:
+            parts.append(span(n, token))
     tile_even, tile_odd, vel = call(
         theta_in,
         "theta_in",
@@ -583,23 +529,23 @@
         in_specs=[vmem] * 4,
         out_specs=(vmem,) * 3,
         input_output_aliases={2: 2},
-    )(theta_even, theta_odd, vel, top)
+    )(theta_even, theta_odd, vel, parts[-1])
     corner_even, corner_odd = across_edges(tile_even, tile_odd, "ax")
-    part_c = with_ghosts(2, tile_even)
+    parts.append(span(3, tile_even))
     increment, time_step, _ = call(
         functools.partial(finish, spans),
         "finish",
         0,
         scratch=8,
         out_shape=(shape(*velocity.shape), shape(1), padded),
-        in_specs=[vmem] * 10,
+        in_specs=[vmem] * (7 + len(parts)),
         out_specs=(anywhere, smem, vmem),
         scratch_shapes=[
             pltpu.VMEM(velocity.shape, f32),
             pltpu.SemaphoreType.DMA(((planes - 2 * HALO) // BLOCK + 2,)),
         ],
         input_output_aliases={0: 2},
-    )(vel, inner, coef, part_a, part_b, part_c, top, far, corner_even, corner_odd)
+    )(vel, inner, coef, top, far, corner_even, corner_odd, *parts)
     return increment, time_step.reshape(())
 
 

time: 37.1 us -> 42 us (1.13)
  waiting for transfers between devices: 1.56 us -> 7.39 us
  Pallas kernels: 21.1 us -> 18.7 us
  starting transfers between devices: 12.4 us -> 13.9 us
    ppermute x10 -> x11, waiting for transfers between devices: 1.56 us -> 7.39 us  [routed(): return lax.ppermute(block, axis, [(source(i), i) for i in range(count)])]
    pallas_call x1, Pallas kernels: 6.63 us -> 4.45 us  [per_device(): call(functools.partial(finish, spans), 'finish', 0, scratch=8, out_shape=...]
    ppermute x10 -> x11, starting transfers between devices: 12.4 us -> 13.9 us  [routed(): return lax.ppermute(block, axis, [(source(i), i) for i in range(count)])]
    pallas_call x6 -> x5, Pallas kernels: 11.3 us -> 10.6 us  [the longest x4 10.4 us: span(): call(functools.partial(kernel, first, last), f'span_{n}', velocity.size *...]
  transfers between devices with their start and end apart: 10 -> 11, of which waited for: 3 -> 3; matrix products, arithmetic and copies ran while one was open for 0% -> 0% of each run, Pallas kernels for 39% -> 34%
where the time goes in v12:
time: 42 us; the launch traced here: 41.9 us
  Pallas kernels  18.7 us (45%)
  starting transfers between devices  13.9 us (33%)
  waiting for transfers between devices  7.39 us (18%)
  local copies, waits for them, and re-layouts  1.18 us (3%)
  between operations  0.77 us (2%)
    ppermute x11, starting transfers between devices, routed(): return lax.ppermute(block, axis, [(source(i), i) for i in range(count)])  13.9 us
    pallas_call x4, Pallas kernels, span(): call(functools.partial(kernel, first, last), f'span_{n}', velocity.size *...  10.4 us
    ppermute x11, waiting for transfers between devices, routed(): return lax.ppermute(block, axis, [(source(i), i) for i in range(count)])  7.39 us
    pallas_call x1, Pallas kernels, per_device(): call(functools.partial(finish, spans), 'finish', 0, scratch=8, out_shape=...  4.45 us
    pallas_call x1, Pallas kernels, per_device(): call(functools.partial(first_pass, theta_step), 'first_pass', 0, out_shap...  3.5 us
    dynamic_slice x1, local copies, waits for them, and re-layouts, per_device(): lax.dynamic_slice_in_dim(velocity, odd_end, HALO, 1)  1.18 us
  transfers between devices with their start and end apart: 11, of which 3 were waited for; matrix products, arithmetic and copies ran while one was open for 0% of the time, Pallas kernels for 34%

profile of v12, /device:TPU:0, one launch (start us, length us, event | category | flops | bytes accessed | tf_op | source)
XLA Modules:
  0.0 41.9 jit_solution(5401341691650887746)
XLA Ops:
  0.6 1.2 %constant_dynamic-slice_fusion = (f32[3,2,128,128]{3,2,1,0:T(8,128)S(1)}, f32[3,2,128,128]{3,2,1,0:T(8,128)S(1)}) fusion(f32[3,32,128,128]{3,2,1,0:T(8,128)} %v_ref.1, s32[]{:T(128)S(6)} %select_n.18, s32[]{:T(128)S(6)} %select_n.17), kind=kLoop, calls=%fused_computation | loop fusion | bytes 1572872 | tf_op jit(solution)/shard_map/dynamic_slice | solution.py:463
  1.8 6.1 %collective-permute-start.1 = (f32[3,2,128,128]{3,2,1,0:T(8,128)S(1)}, f32[3,2,128,128]{3,2,1,0:T(8,128)S(1)}, u32[]{:S(2)}, u32[]{:S(2)}) collective-permute-start(f32[3,2,128,128]{3,2,1,0:T(8,128)S(1)} %get-tuple-element.26), channel_id=1, source_target_pairs={{28,0},{8,4},{4,8},{16,12},{12,16},{24,20},{20,24},{0,28},{29,1},{... | collective-permute-start | bytes 1179656 | tf_op jit(solution)/shard_map/ppermute | solution.py:413
  7.9 0.0 copy-start
  7.9 0.0 collective-permute-start
  7.9 3.5 %first_pass.1 = (f32[3,36,144,128]{3,2,1,0:T(8,128)S(1)}, f32[3,32,2,128]{3,2,1,0:T(2,128)S(1)}, f32[3,32,2,128]{3,2,1,0:T(2,128)S(1)}, f32[128,128]{1,0:T(8,128)S(1)}, f32[8,128]{1,0:T(8,128)S(1)}) custom-call(f32[3,32,128,128]{3,2,1,0:T(8,128)} %v_ref.1), custom_call_target="tpu_custom_call" | custom-call | tf_op jit(solution)/shard_map/first_pass/pallas_call | solution.py:471
  11.4 0.1 collective-permute-start.2
  11.5 1.6 %collective-permute-start.3 = (f32[3,32,2,128]{3,2,1,0:T(2,128)S(1)}, f32[3,32,2,128]{3,2,1,0:T(2,128)S(1)}, u32[]{:S(2)}, u32[]{:S(2)}) collective-permute-start(f32[3,32,2,128]{3,2,1,0:T(2,128)S(1)} %get-tuple-element.15), channel_id=1, source_target_pairs={{3,0},{2,1},{1,2},{0,3},{7,4},{6,5},{5,6},{4,7},{11,8},{10,9},{9,1... | collective-permute-start | bytes 294920 | tf_op jit(solution)/shard_map/ppermute | solution.py:413
  13.1 0.5 %collective-permute-start.4 = (f32[8,128]{1,0:T(8,128)S(1)}, f32[8,128]{1,0:T(8,128)S(1)}, u32[]{:S(2)}, u32[]{:S(2)}) collective-permute-start(f32[8,128]{1,0:T(8,128)S(1)} %get-tuple-element.16.pay_ref), channel_id=1, source_target_pairs={{2,0},{3,1},{0,2},{1,3},{6,4},{7,5},{4,6},{5,7},{10,8},{11,9},{8,1... | collective-permute-start | bytes 12296 | tf_op jit(solution)/shard_map/ppermute | solution.py:413
  13.6 3.1 %collective-permute-done.4.refs_0_ = f32[8,128]{1,0:T(8,128)S(1)} collective-permute-done((f32[8,128]{1,0:T(8,128)S(1)}, f32[8,128]{1,0:T(8,128)S(1)}, u32[]{:S(2)}, u32[]{:S(2)}) %collective-permute-start.4) | collective-permute-done | bytes 4128 | tf_op jit(solution)/shard_map/ppermute | solution.py:413
  16.7 1.1 %collective-permute-start.5 = (f32[128,128]{1,0:T(8,128)S(1)}, f32[128,128]{1,0:T(8,128)S(1)}, u32[]{:S(2)}, u32[]{:S(2)}) collective-permute-start(f32[128,128]{1,0:T(8,128)S(1)} %get-tuple-element.19), channel_id=1, source_target_pairs={{16,0},{20,4},{24,8},{28,12},{0,16},{4,20},{8,24},{12,28},{17,1},{... | collective-permute-start | bytes 196616 | tf_op jit(solution)/shard_map/ppermute | solution.py:413
  17.8 0.0 collective-permute-done.2.even_ref
  17.8 0.0 collective-permute-done.3.odd_ref
  17.8 0.2 fold.1
  18.0 1.0 %collective-permute-start.6 = (f32[8,128]{1,0:T(8,128)S(1)}, f32[8,128]{1,0:T(8,128)S(1)}, u32[]{:S(2)}, u32[]{:S(2)}) collective-permute-start(f32[8,128]{1,0:T(8,128)S(1)} %get-tuple-element.20._.mine_ref), channel_id=1, source_target_pairs={{4,0},{0,4},{12,8},{8,12},{20,16},{16,20},{28,24},{24,28},{5,1},{1... | collective-permute-start | bytes 12296 | tf_op jit(solution)/shard_map/ppermute | solution.py:413
  19.1 0.0 copy-done
  19.1 2.7 %span_0.1._.refs_0_ = f32[3,8,128,128]{3,2,1,0:T(8,128)S(1)} custom-call(f32[3,36,144,128]{3,2,1,0:T(8,128)S(1)} %get-tuple-element.18.vel_ref.vel_in, f32[15,8,128]{2,1,0:T(8,128)S(1)} %copy-done, f32[8,128]{1,0:T(8,128)S(1)} %get-tuple-element.20._.mine_ref), custom_call_target="tpu_custom_call" | custom-call | flops 3145728 | bytes 3145728 | tf_op jit(solution)/shard_map/span_0/pallas_call | solution.py:501
  21.7 3.8 %collective-permute-done.6.far_ref = f32[8,128]{1,0:T(8,128)S(1)} collective-permute-done((f32[8,128]{1,0:T(8,128)S(1)}, f32[8,128]{1,0:T(8,128)S(1)}, u32[]{:S(2)}, u32[]{:S(2)}) %collective-permute-start.6) | collective-permute-done | bytes 4128 | tf_op jit(solution)/shard_map/ppermute | solution.py:413
  25.5 0.0 collective-permute-start.7
  25.5 0.0 collective-permute-done.5.inner_ref
  25.5 3.1 %span_1.1._.refs_1_ = f32[3,8,128,128]{3,2,1,0:T(8,128)S(1)} custom-call(f32[3,36,144,128]{3,2,1,0:T(8,128)S(1)} %get-tuple-element.18.vel_ref.vel_in, f32[128,128]{1,0:T(8,128)S(1)} %collective-permute-done.5.inner_ref, f32[15,8,128]{2,1,0:T(8,128)S(1)} %copy-done, f32[8,128]{1,0:T(8,128)S(1)} %merged.2._.mine_ref), custom_call_target="tpu_custom_call" | custom-call | flops 3145728 | bytes 3145728 | tf_op jit(solution)/shard_map/span_1/pallas_call | solution.py:501
  28.7 0.5 %collective-permute-done.7.far_ref = f32[8,128]{1,0:T(8,128)S(1)} collective-permute-done((f32[8,128]{1,0:T(8,128)S(1)}, f32[8,128]{1,0:T(8,128)S(1)}, u32[]{:S(2)}, u32[]{:S(2)}) %collective-permute-start.7) | collective-permute-done | bytes 4128 | tf_op jit(solution)/shard_map/ppermute | solution.py:413
  29.1 1.8 %collective-permute-start.8 = (f32[8,128]{1,0:T(8,128)S(1)}, f32[8,128]{1,0:T(8,128)S(1)}, u32[]{:S(2)}, u32[]{:S(2)}) collective-permute-start(f32[8,128]{1,0:T(8,128)S(1)} %merged.3._.top), channel_id=1, source_target_pairs={{16,0},{20,4},{24,8},{28,12},{0,16},{4,20},{8,24},{12,28},{17,1},{... | collective-permute-start | bytes 12296 | tf_op jit(solution)/shard_map/ppermute | solution.py:413
  31.0 3.1 %span_2.1._.refs_2_ = f32[3,8,128,128]{3,2,1,0:T(8,128)S(1)} custom-call(f32[3,36,144,128]{3,2,1,0:T(8,128)S(1)} %get-tuple-element.18.vel_ref.vel_in, f32[128,128]{1,0:T(8,128)S(1)} %collective-permute-done.5.inner_ref, f32[15,8,128]{2,1,0:T(8,128)S(1)} %copy-done, f32[8,128]{1,0:T(8,128)S(1)} %merged.3._.top), custom_call_target="tpu_custom_call" | custom-call | flops 3145728 | bytes 3145728 | tf_op jit(solution)/shard_map/span_2/pallas_call | solution.py:501
  34.1 0.0 collective-permute-done.1.odd_ref
  34.1 0.0 collective-permute-done.even_ref
  34.1 0.1 theta_in.1
  34.2 0.6 %collective-permute-start.10 = (f32[8,128]{1,0:T(8,128)S(1)}, f32[8,128]{1,0:T(8,128)S(1)}, u32[]{:S(2)}, u32[]{:S(2)}) collective-permute-start(f32[8,128]{1,0:T(8,128)S(1)} %get-tuple-element.23), channel_id=1, source_target_pairs={{3,0},{2,1},{1,2},{0,3},{7,4},{6,5},{5,6},{4,7},{11,8},{10,9},{9,1... | collective-permute-start | bytes 12296 | tf_op jit(solution)/shard_map/ppermute | solution.py:413
  34.8 1.1 %collective-permute-start.9 = (f32[8,128]{1,0:T(8,128)S(1)}, f32[8,128]{1,0:T(8,128)S(1)}, u32[]{:S(2)}, u32[]{:S(2)}) collective-permute-start(f32[8,128]{1,0:T(8,128)S(1)} %get-tuple-element.22._), channel_id=1, source_target_pairs={{1,0},{0,1},{3,2},{2,3},{5,4},{4,5},{7,6},{6,7},{9,8},{8,9},{11,10... | collective-permute-start | bytes 12296 | tf_op jit(solution)/shard_map/ppermute | solution.py:413
  35.9 1.5 %span_3.1.refs_3_ = f32[3,4,128,128]{3,2,1,0:T(8,128)S(1)} custom-call(f32[3,36,144,128]{3,2,1,0:T(8,128)S(1)} %get-tuple-element.21.vel_ref.vel_in, f32[128,128]{1,0:T(8,128)S(1)} %collective-permute-done.5.inner_ref, f32[15,8,128]{2,1,0:T(8,128)S(1)} %copy-done, f32[8,128]{1,0:T(8,128)S(1)} %get-tuple-element.22._), custom_call_target="tpu_custom_call" | custom-call | flops 3145728 | bytes 3145728 | tf_op jit(solution)/shard_map/span_3/pallas_call | solution.py:501
  37.4 0.0 collective-permute-done.8.far
  37.4 0.0 collective-permute-done.10.odd
  37.4 0.0 collective-permute-done.9.even
  37.5 4.4 %finish.1 = (f32[3,32,128,128]{3,2,1,0:T(8,128)}, f32[1]{0:T(128)}, f32[3,36,144,128]{3,2,1,0:T(8,128)S(1)}) custom-call(f32[3,36,144,128]{3,2,1,0:T(8,128)S(1)} %get-tuple-element.21.vel_ref.vel_in, f32[128,128]{1,0:T(8,128)S(1)} %collective-permute-done.5.inner_ref, f32[15,8,128]{2,1,0:T(8,128)S(1)} %copy-done, ...), custom_call_target="tpu_custom_call", output_to_operand_aliasing={{2}: (0, {})} | custom-call | tf_op jit(solution)/shard_map/finish/pallas_call | solution.py:535
  (2 shorter events, 0.0 us)
Async XLA Ops:
  1.8 32.3 %collective-permute-start.1 = (f32[3,2,128,128]{3,2,1,0:T(8,128)S(1)}, f32[3,2,128,128]{3,2,1,0:T(8,128)S(1)}, u32[]{:S(2)}, u32[]{:S(2)}) collective-permute-start(f32[3,2,128,128]{3,2,1,0:T(8,128)S(1)} %get-tuple-element.26), channel_id=1, source_target_pairs={{28,0},{8,4},{4,8},{16,12},{12,16},{24,20},{20,24},{0,28},{29,1},{... | collective-permute-start | bytes 1179656 | tf_op jit(solution)/shard_map/ppermute | solution.py:413
  7.9 11.2 %copy-start = (f32[15,8,128]{2,1,0:T(8,128)S(1)}, f32[15,8,128]{2,1,0:T(8,128)}, u32[]{:S(2)}) copy-start(f32[15,8,128]{2,1,0:T(8,128)} %constant.28.clone.coef_ref) | copy-start | bytes 184324
  7.9 26.2 %collective-permute-start = (f32[3,2,128,128]{3,2,1,0:T(8,128)S(1)}, f32[3,2,128,128]{3,2,1,0:T(8,128)S(1)}, u32[]{:S(2)}, u32[]{:S(2)}) collective-permute-start(f32[3,2,128,128]{3,2,1,0:T(8,128)S(1)} %get-tuple-element.27), channel_id=1, source_target_pairs={{4,0},{0,4},{12,8},{8,12},{20,16},{16,20},{28,24},{24,28},{5,1},{1... | collective-permute-start | bytes 1179656 | tf_op jit(solution)/shard_map/ppermute | solution.py:413
  11.4 6.4 %collective-permute-start.2 = (f32[3,32,2,128]{3,2,1,0:T(2,128)S(1)}, f32[3,32,2,128]{3,2,1,0:T(2,128)S(1)}, u32[]{:S(2)}, u32[]{:S(2)}) collective-permute-start(f32[3,32,2,128]{3,2,1,0:T(2,128)S(1)} %get-tuple-element.14), channel_id=1, source_target_pairs={{1,0},{0,1},{3,2},{2,3},{5,4},{4,5},{7,6},{6,7},{9,8},{8,9},{11,10... | collective-permute-start | bytes 294920 | tf_op jit(solution)/shard_map/ppermute | solution.py:413
  11.5 6.3 %collective-permute-start.3 = (f32[3,32,2,128]{3,2,1,0:T(2,128)S(1)}, f32[3,32,2,128]{3,2,1,0:T(2,128)S(1)}, u32[]{:S(2)}, u32[]{:S(2)}) collective-permute-start(f32[3,32,2,128]{3,2,1,0:T(2,128)S(1)} %get-tuple-element.15), channel_id=1, source_target_pairs={{3,0},{2,1},{1,2},{0,3},{7,4},{6,5},{5,6},{4,7},{11,8},{10,9},{9,1... | collective-permute-start | bytes 294920 | tf_op jit(solution)/shard_map/ppermute | solution.py:413
  13.1 3.6 %collective-permute-start.4 = (f32[8,128]{1,0:T(8,128)S(1)}, f32[8,128]{1,0:T(8,128)S(1)}, u32[]{:S(2)}, u32[]{:S(2)}) collective-permute-start(f32[8,128]{1,0:T(8,128)S(1)} %get-tuple-element.16.pay_ref), channel_id=1, source_target_pairs={{2,0},{3,1},{0,2},{1,3},{6,4},{7,5},{4,6},{5,7},{10,8},{11,9},{8,1... | collective-permute-start | bytes 12296 | tf_op jit(solution)/shard_map/ppermute | solution.py:413
  16.7 8.8 %collective-permute-start.5 = (f32[128,128]{1,0:T(8,128)S(1)}, f32[128,128]{1,0:T(8,128)S(1)}, u32[]{:S(2)}, u32[]{:S(2)}) collective-permute-start(f32[128,128]{1,0:T(8,128)S(1)} %get-tuple-element.19), channel_id=1, source_target_pairs={{16,0},{20,4},{24,8},{28,12},{0,16},{4,20},{8,24},{12,28},{17,1},{... | collective-permute-start | bytes 196616 | tf_op jit(solution)/shard_map/ppermute | solution.py:413
  18.0 7.5 %collective-permute-start.6 = (f32[8,128]{1,0:T(8,128)S(1)}, f32[8,128]{1,0:T(8,128)S(1)}, u32[]{:S(2)}, u32[]{:S(2)}) collective-permute-start(f32[8,128]{1,0:T(8,128)S(1)} %get-tuple-element.20._.mine_ref), channel_id=1, source_target_pairs={{4,0},{0,4},{12,8},{8,12},{20,16},{16,20},{28,24},{24,28},{5,1},{1... | collective-permute-start | bytes 12296 | tf_op jit(solution)/shard_map/ppermute | solution.py:413
  25.5 3.6 %collective-permute-start.7 = (f32[8,128]{1,0:T(8,128)S(1)}, f32[8,128]{1,0:T(8,128)S(1)}, u32[]{:S(2)}, u32[]{:S(2)}) collective-permute-start(f32[8,128]{1,0:T(8,128)S(1)} %merged.2._.mine_ref), channel_id=1, source_target_pairs={{8,0},{12,4},{0,8},{4,12},{24,16},{28,20},{16,24},{20,28},{9,1},{1... | collective-permute-start | bytes 12296 | tf_op jit(solution)/shard_map/ppermute | solution.py:413
  29.1 8.3 %collective-permute-start.8 = (f32[8,128]{1,0:T(8,128)S(1)}, f32[8,128]{1,0:T(8,128)S(1)}, u32[]{:S(2)}, u32[]{:S(2)}) collective-permute-start(f32[8,128]{1,0:T(8,128)S(1)} %merged.3._.top), channel_id=1, source_target_pairs={{16,0},{20,4},{24,8},{28,12},{0,16},{4,20},{8,24},{12,28},{17,1},{... | collective-permute-start | bytes 12296 | tf_op jit(solution)/shard_map/ppermute | solution.py:413
  34.2 3.2 %collective-permute-start.10 = (f32[8,128]{1,0:T(8,128)S(1)}, f32[8,128]{1,0:T(8,128)S(1)}, u32[]{:S(2)}, u32[]{:S(2)}) collective-permute-start(f32[8,128]{1,0:T(8,128)S(1)} %get-tuple-element.23), channel_id=1, source_target_pairs={{3,0},{2,1},{1,2},{0,3},{7,4},{6,5},{5,6},{4,7},{11,8},{10,9},{9,1... | collective-permute-start | bytes 12296 | tf_op jit(solution)/shard_map/ppermute | solution.py:413
  34.8 2.6 %collective-permute-start.9 = (f32[8,128]{1,0:T(8,128)S(1)}, f32[8,128]{1,0:T(8,128)S(1)}, u32[]{:S(2)}, u32[]{:S(2)}) collective-permute-start(f32[8,128]{1,0:T(8,128)S(1)} %get-tuple-element.22._), channel_id=1, source_target_pairs={{1,0},{0,1},{3,2},{2,3},{5,4},{4,5},{7,6},{6,7},{9,8},{8,9},{11,10... | collective-permute-start | bytes 12296 | tf_op jit(solution)/shard_map/ppermute | solution.py:413

commit v13 on v12

--- a/solution.py
+++ b/solution.py
@@ -238,18 +238,22 @@
         ref[0, 0] = jnp.where(end, top, ref[0, 0])
 
 
-def fold(even_ref, odd_ref, pay_ref, vel_in, *refs):
+def carried(even_ref, pay_ref, odd_in, odd_ref):
+    radial = even_ref.shape[3]
+    lane = lax.broadcasted_iota(jnp.int32, (2, radial), 1)
+    top = jnp.maximum(even_ref[0, 0], pay_ref[0:2, :])
+    odd_ref[0, 0] = jnp.where(lane == radial - 1, top, odd_in[0, 0])
+
+
+def fold(even_ref, odd_ref, pay_ref, vel_in, _, *refs):
     del vel_in
-    fars, (top_ref, vel_ref) = refs[:-2], refs[-2:]
+    top_ref, vel_ref = refs
     planes, radial = even_ref.shape[1], even_ref.shape[3]
     axial = vel_ref.shape[2] - 2 * PAD
     lane = lax.broadcasted_iota(jnp.int32, (1, radial), 1)
     top = jnp.maximum(even_ref[0, 0, 0:1, :], odd_ref[0, 0, 0:1, :])
     top = jnp.max(jnp.where(lane == radial - 1, top, 0.0), axis=(0, 1), keepdims=True)
-    top = jnp.maximum(pay_ref[...], top)
-    for far in fars:
-        top = jnp.maximum(top, far[...])
-    top_ref[...] = top
+    top_ref[...] = jnp.maximum(pay_ref[...], top)
     wall = wall_mask(2, radial)
     odd = lax.rem(lax.axis_index("ax"), 2) == 1
 
@@ -265,8 +269,8 @@
     lax.fori_loop(0, planes, plane, 0, unroll=4)
 
 
-def merged(mine_ref, far_ref, _, top_ref):
-    top_ref[...] = jnp.maximum(mine_ref[...], far_ref[...])
+def merged(mine_ref, far_ref, *refs):
+    refs[-1][...] = jnp.maximum(mine_ref[...], far_ref[...])
 
 
 def theta_in(even_ref, odd_ref, vel_in, _, even_tile, odd_tile, vel_ref):
@@ -302,16 +306,20 @@
     return ghost
 
 
-def block_terms(vel_ref, inner_ref, coef_ref, j, size, write):
+def block_terms(vel_ref, inner_ref, coef_ref, j, size, write, rounds=None):
     planes = vel_ref.shape[1] - 2 * HALO
     axial, radial = vel_ref.shape[2] - 2 * PAD, vel_ref.shape[3]
     groups = 2 * BLOCK // size
+    times, places = rounds or (
+        axial // (8 * groups),
+        lambda i: [(i * groups + u) * 8 for u in range(groups)],
+    )
 
     def rows(i, carry):
         coef = [coef_ref[n] for n in range(COUNT)]
         found = []
-        for u in range(groups):
-            k = pl.multiple_of((i * groups + u) * 8, 8)
+        for k in places(i):
+            k = pl.multiple_of(k, 8)
             cells = Cells(vel_ref, j, k)
             ghost = None
             if inner_ref is not None:
@@ -323,15 +331,17 @@
                 write(n, j + q, pl.ds(k, 8), value)
         return carry
 
-    lax.fori_loop(0, axial // (8 * groups), rows, 0)
-
-
-def ahead(first, last, vel_ref, coef_ref, _, out_ref):
+    lax.fori_loop(0, times, rows, 0)
+
+
+def ahead(first, last, rounds, vel_ref, coef_ref, *refs):
+    out_ref = refs[-1]
+
     def write(n, j, k, value):
         out_ref[n, j - first, k, :] = value
 
     def block(m, carry):
-        block_terms(vel_ref, None, coef_ref, first + m * BLOCK, BLOCK, write)
+        block_terms(vel_ref, None, coef_ref, first + m * BLOCK, BLOCK, write, rounds)
         return carry
 
     lax.fori_loop(0, (last - first) // BLOCK, block, 0)
@@ -394,7 +404,7 @@
 
     for n, (part, (first, last)) in enumerate(zip(parts, spans)):
         for j in range(first, last, BLOCK):
-            complete(part, j, j - first, n == 0)
+            complete(part, j, j - first, n < 2)
 
     second = lax.rem(lax.axis_index("ax"), 2) == 1
     even, odd = even[0:1, :], odd[0:1, :]
@@ -417,18 +427,18 @@
     return routed(block, axis, lambda i: i ^ step)
 
 
-def across_edges(even, odd, axis):
+def across_even(block, axis):
+    return exchanged(block, axis, 1)
+
+
+def across_odd(block, axis):
     count = lax.axis_size(axis)
-
-    def source(i):
-        return (i + (1 if i % 2 else -1)) % count
-
-    return exchanged(even, axis, 1), routed(odd, axis, source)
+    return routed(block, axis, lambda i: (i + (1 if i % 2 else -1)) % count)
 
 
 def cuts(planes):
     last = planes - HALO
-    ends = (HALO, last - 5 * BLOCK, last - 3 * BLOCK, last - BLOCK, last)
+    ends = (HALO, last - 5 * BLOCK, last - 4 * BLOCK, last - 2 * BLOCK, last - BLOCK, last)
     return list(zip(ends[:-1], ends[1:]))
 
 
@@ -458,11 +468,8 @@
     ends = (planes - HALO, 0)
     even_end = jnp.where(odd == 1, ends[1], ends[0])
     odd_end = jnp.where(odd == 1, ends[0], ends[1])
-    theta_even, theta_odd = across_edges(
-        lax.dynamic_slice_in_dim(velocity, even_end, HALO, 1),
-        lax.dynamic_slice_in_dim(velocity, odd_end, HALO, 1),
-        "az",
-    )
+    theta_even = across_even(lax.dynamic_slice_in_dim(velocity, even_end, HALO, 1), "az")
+    theta_odd = across_odd(lax.dynamic_slice_in_dim(velocity, odd_end, HALO, 1), "az")
 
     edge = shape(3, planes, 2, radial)
     padded = shape(3, planes + 2 * HALO, axial + 2 * PAD, radial)
@@ -477,50 +484,78 @@
         out_specs=(vmem,) * 5,
         scratch_shapes=[pltpu.SemaphoreType.DMA((planes // GROUP,))],
     )(pltpu.with_memory_space_constraint(velocity, pltpu.HBM))
-    z_even, z_odd = across_edges(edge_even, edge_odd, "ax")
-    fars = [
-        routed(pay, "ax", lambda i, step=step: (i + step) % sizes[1])
-        for step in range(2, sizes[1] - 1)
-    ]
     inner = exchanged(mine, "az", sizes[0] // 2)
+    z_even = across_even(edge_even, "ax")
+    edge_odd = call(
+        carried,
+        "carried",
+        0,
+        out_shape=edge,
+        in_specs=[vmem] * 3,
+        out_specs=vmem,
+        input_output_aliases={2: 0},
+    )(z_even, pay, edge_odd)
+    z_odd = across_odd(edge_odd, "ax")
+
+    spans = cuts(planes)
+
+    def part_shape(n):
+        return shape(3, spans[n][1] - spans[n][0], axial, radial)
+
+    def without_ghosts(n, name, rounds, vel, *tokens, **kwargs):
+        return call(
+            functools.partial(ahead, *spans[n], rounds),
+            name,
+            velocity.size * 2,
+            out_shape=part_shape(n),
+            in_specs=[vmem] * (2 + len(tokens)),
+            out_specs=vmem,
+            **kwargs,
+        )(vel, coef, *tokens)
+
+    def with_ghosts(n, token):
+        return call(
+            functools.partial(ahead_with_ghosts, *spans[n]),
+            f"span_{n}",
+            velocity.size * 2,
+            out_shape=part_shape(n),
+            in_specs=[vmem] * 4,
+            out_specs=vmem,
+        )(vel, inner, coef, token)
+
+    middle = (axial - 16) // 16, lambda i: [16 * i + 8, 16 * i + 16]
+    outer = 1, lambda i: [i * 8, i * 8 + axial - 8]
+    part = without_ghosts(0, "span_0_middle", middle, vel, pay)
     top, vel = call(
         fold,
         "fold",
         0,
         out_shape=(tile, padded),
-        in_specs=[vmem] * (4 + len(fars)),
+        in_specs=[vmem] * 5,
         out_specs=(vmem,) * 2,
         input_output_aliases={3: 1},
-    )(z_even, z_odd, pay, vel, *fars)
-
-    spans = cuts(planes)
-
-    def span(n, token):
-        kernel, given = (ahead, (vel, coef)) if n == 0 else (ahead_with_ghosts, (vel, inner, coef))
-        first, last = spans[n]
-        return call(
-            functools.partial(kernel, first, last),
-            f"span_{n}",
-            velocity.size * 2,
-            out_shape=shape(3, last - first, axial, radial),
-            in_specs=[vmem] * (len(given) + 1),
+    )(z_even, z_odd, pay, vel, part)
+    for step in (1 << n for n in range(2, sizes[1].bit_length() - 1)):
+        top = jnp.maximum(top, routed(top, "ax", lambda i, step=step: (i + step) % sizes[1]))
+
+    bits = [1 << n for n in range(1, sizes[0].bit_length() - 1)] + [1]
+    far = exchanged(top, "az", bits[0])
+    parts = [
+        without_ghosts(0, "span_0_outer", outer, vel, part, input_output_aliases={2: 0}),
+        without_ghosts(1, "span_1", None, vel, top),
+    ]
+    for n, bit in enumerate(bits[1:]):
+        top = call(
+            merged,
+            "merged",
+            0,
+            out_shape=tile,
+            in_specs=[vmem] * 4,
             out_specs=vmem,
-        )(*given, token)
-
-    parts, token = [], top
-    for n in range(sizes[0].bit_length() - 1):
-        if n > 0:
-            top = token = call(
-                merged,
-                "merged",
-                0,
-                out_shape=tile,
-                in_specs=[vmem] * 3,
-                out_specs=vmem,
-            )(top, far, parts[-1])
-        far = exchanged(top, "az", 1 << n)
-        if n < 3:
-            parts.append(span(n, token))
+        )(top, far, *parts[-2:])
+        far = exchanged(top, "az", bit)
+        if n < 2:
+            parts.append(with_ghosts(n + 2, top))
     tile_even, tile_odd, vel = call(
         theta_in,
         "theta_in",
@@ -530,8 +565,8 @@
         out_specs=(vmem,) * 3,
         input_output_aliases={2: 2},
     )(theta_even, theta_odd, vel, parts[-1])
-    corner_even, corner_odd = across_edges(tile_even, tile_odd, "ax")
-    parts.append(span(3, tile_even))
+    corner_even, corner_odd = across_even(tile_even, "ax"), across_odd(tile_odd, "ax")
+    parts.append(with_ghosts(4, tile_even))
     increment, time_step, _ = call(
         functools.partial(finish, spans),
         "finish",

time: 42 us -> 38.3 us (0.912)
  waiting for transfers between devices: 7.39 us -> 3.53 us
    ppermute x11 -> x10, waiting for transfers between devices: 7.39 us -> 3.53 us  [routed(): return lax.ppermute(block, axis, [(source(i), i) for i in range(count)])]
    pallas_call x1, Pallas kernels: 4.45 us -> 4.89 us  [per_device(): call(functools.partial(finish, spans), 'finish', 0, scratch=8, out_shape=...]
    pallas_call x7 -> x10, Pallas kernels: 10.7 us -> 10.5 us  [the longest x3 6.22 us: with_ghosts(): call(functools.partial(ahead_with_ghosts, *spans[n]), f'span_{n}', veloci...]
    ppermute x11 -> x10, starting transfers between devices: 13.9 us -> 13.7 us  [routed(): return lax.ppermute(block, axis, [(source(i), i) for i in range(count)])]
  transfers between devices with their start and end apart: 11 -> 10, of which waited for: 3 -> 4; matrix products, arithmetic and copies ran while one was open for 0% -> 0% of each run, Pallas kernels for 34% -> 37%
where the time goes in v13:
time: 38.3 us; the launch traced here: 38.2 us
  Pallas kernels  18.9 us (49%)
  starting transfers between devices  13.7 us (36%)
  waiting for transfers between devices  3.53 us (9%)
  local copies, waits for them, and re-layouts  1.18 us (3%)
  between operations  0.79 us (2%)
    ppermute x10, starting transfers between devices, routed(): return lax.ppermute(block, axis, [(source(i), i) for i in range(count)])  13.7 us
    pallas_call x3, Pallas kernels, with_ghosts(): call(functools.partial(ahead_with_ghosts, *spans[n]), f'span_{n}', veloci...  6.22 us
    pallas_call x1, Pallas kernels, per_device(): call(functools.partial(finish, spans), 'finish', 0, scratch=8, out_shape=...  4.89 us
    pallas_call x3, Pallas kernels, without_ghosts(): call(functools.partial(ahead, *spans[n], rounds), name, velocity.size * 2...  3.99 us
    ppermute x10, waiting for transfers between devices, routed(): return lax.ppermute(block, axis, [(source(i), i) for i in range(count)])  3.53 us
    pallas_call x1, Pallas kernels, per_device(): call(functools.partial(first_pass, theta_step), 'first_pass', 0, out_shap...  3.49 us
    dynamic_slice x1, local copies, waits for them, and re-layouts, per_device(): lax.dynamic_slice_in_dim(velocity, odd_end, HALO, 1)  1.18 us
  transfers between devices with their start and end apart: 10, of which 4 were waited for; matrix products, arithmetic and copies ran while one was open for 0% of the time, Pallas kernels for 37%

profile of v13, /device:TPU:0, one launch (start us, length us, event | category | flops | bytes accessed | tf_op | source)
XLA Modules:
  0.0 38.2 jit_solution(3917101935220578135)
XLA Ops:
  0.6 0.0 copy-start
  0.7 1.2 %constant_dynamic-slice_fusion = (f32[3,2,128,128]{3,2,1,0:T(8,128)S(1)}, f32[3,2,128,128]{3,2,1,0:T(8,128)S(1)}) fusion(f32[3,32,128,128]{3,2,1,0:T(8,128)} %v_ref.1, s32[]{:T(128)S(6)} %select_n.18, s32[]{:T(128)S(6)} %select_n.17), kind=kLoop, calls=%fused_computation | loop fusion | bytes 1572872 | tf_op jit(solution)/shard_map/dynamic_slice | solution.py:472
  1.8 6.1 %collective-permute-start.1 = (f32[3,2,128,128]{3,2,1,0:T(8,128)S(1)}, f32[3,2,128,128]{3,2,1,0:T(8,128)S(1)}, u32[]{:S(2)}, u32[]{:S(2)}) collective-permute-start(f32[3,2,128,128]{3,2,1,0:T(8,128)S(1)} %get-tuple-element.26), channel_id=1, source_target_pairs={{28,0},{8,4},{4,8},{16,12},{12,16},{24,20},{20,24},{0,28},{29,1},{... | collective-permute-start | bytes 1179656 | tf_op jit(solution)/shard_map/ppermute | solution.py:423
  7.9 0.0 collective-permute-start
  7.9 3.5 %first_pass.1 = (f32[3,36,144,128]{3,2,1,0:T(8,128)S(1)}, f32[3,32,2,128]{3,2,1,0:T(2,128)S(1)}, f32[3,32,2,128]{3,2,1,0:T(2,128)S(1)}, f32[128,128]{1,0:T(8,128)S(1)}, f32[8,128]{1,0:T(8,128)S(1)}) custom-call(f32[3,32,128,128]{3,2,1,0:T(8,128)} %v_ref.1), custom_call_target="tpu_custom_call" | custom-call | tf_op jit(solution)/shard_map/first_pass/pallas_call | solution.py:478
  11.4 0.1 collective-permute-start.2
  11.5 1.3 %collective-permute-done.2.even_ref = f32[3,32,2,128]{3,2,1,0:T(2,128)S(1)} collective-permute-done((f32[3,32,2,128]{3,2,1,0:T(2,128)S(1)}, f32[3,32,2,128]{3,2,1,0:T(2,128)S(1)}, u32[]{:S(2)}, u32[]{:S(2)}) %collective-permute-start.2) | collective-permute-done | bytes 98336 | tf_op jit(solution)/shard_map/ppermute | solution.py:423
  12.8 1.2 %collective-permute-start.3 = (f32[3,32,2,128]{3,2,1,0:T(2,128)S(1)}, f32[3,32,2,128]{3,2,1,0:T(2,128)S(1)}, u32[]{:S(2)}, u32[]{:S(2)}) collective-permute-start(f32[3,32,2,128]{3,2,1,0:T(2,128)S(1)} %carried.1), channel_id=1, source_target_pairs={{3,0},{2,1},{1,2},{0,3},{7,4},{6,5},{5,6},{4,7},{11,8},{10,9},{9,1... | collective-permute-start | bytes 294920 | tf_op jit(solution)/shard_map/ppermute | solution.py:423
  14.0 1.1 %collective-permute-start.4 = (f32[128,128]{1,0:T(8,128)S(1)}, f32[128,128]{1,0:T(8,128)S(1)}, u32[]{:S(2)}, u32[]{:S(2)}) collective-permute-start(f32[128,128]{1,0:T(8,128)S(1)} %get-tuple-element.19), channel_id=1, source_target_pairs={{16,0},{20,4},{24,8},{28,12},{0,16},{4,20},{8,24},{12,28},{17,1},{... | collective-permute-start | bytes 196616 | tf_op jit(solution)/shard_map/ppermute | solution.py:423
  15.1 0.0 copy-done
  15.1 2.4 %span_0_middle.1._.refs_0_ = f32[3,8,128,128]{3,2,1,0:T(8,128)S(1)} custom-call(f32[3,36,144,128]{3,2,1,0:T(8,128)S(1)} %get-tuple-element.17.vel_ref.vel_in, f32[15,8,128]{2,1,0:T(8,128)S(1)} %copy-done, f32[8,128]{1,0:T(8,128)S(1)} %get-tuple-element.15.pay_ref.refs_0_), custom_call_target="tpu_custom_call" | custom-call | flops 3145728 | bytes 3145728 | tf_op jit(solution)/shard_map/span_0_middle/pallas_call | solution.py:506
  17.5 0.1 collective-permute-done.3.odd_ref
  17.5 0.2 fold.1
  17.8 0.2 collective-permute-start.5
  18.0 0.3 span_0_outer.1.refs_0_
  18.3 1.3 %span_1.1.refs_1_.refs_0_ = f32[3,4,128,128]{3,2,1,0:T(8,128)S(1)} custom-call(f32[3,36,144,128]{3,2,1,0:T(8,128)S(1)} %get-tuple-element.18.vel_ref.vel_in, f32[15,8,128]{2,1,0:T(8,128)S(1)} %copy-done, f32[8,128]{1,0:T(8,128)S(1)} %get-tuple-element.20.refs_0_.mine_ref), custom_call_target="tpu_custom_call" | custom-call | flops 3145728 | bytes 3145728 | tf_op jit(solution)/shard_map/span_1/pallas_call | solution.py:506
  19.7 1.8 %collective-permute-done.5.far_ref = f32[8,128]{1,0:T(8,128)S(1)} collective-permute-done((f32[8,128]{1,0:T(8,128)S(1)}, f32[8,128]{1,0:T(8,128)S(1)}, u32[]{:S(2)}, u32[]{:S(2)}) %collective-permute-start.5) | collective-permute-done | bytes 4128 | tf_op jit(solution)/shard_map/ppermute | solution.py:423
  21.5 1.8 %collective-permute-start.6 = (f32[8,128]{1,0:T(8,128)S(1)}, f32[8,128]{1,0:T(8,128)S(1)}, u32[]{:S(2)}, u32[]{:S(2)}) collective-permute-start(f32[8,128]{1,0:T(8,128)S(1)} %merged.2._.mine_ref), channel_id=1, source_target_pairs={{16,0},{20,4},{24,8},{28,12},{0,16},{4,20},{8,24},{12,28},{17,1},{... | collective-permute-start | bytes 12296 | tf_op jit(solution)/shard_map/ppermute | solution.py:423
  23.3 0.0 collective-permute-done.4.inner_ref
  23.3 3.1 %span_2.1.refs_1_.refs_2_ = f32[3,8,128,128]{3,2,1,0:T(8,128)S(1)} custom-call(f32[3,36,144,128]{3,2,1,0:T(8,128)S(1)} %get-tuple-element.18.vel_ref.vel_in, f32[128,128]{1,0:T(8,128)S(1)} %collective-permute-done.4.inner_ref, f32[15,8,128]{2,1,0:T(8,128)S(1)} %copy-done, f32[8,128]{1,0:T(8,128)S(1)} %merged.2._.mine_ref), custom_call_target="tpu_custom_call" | custom-call | flops 3145728 | bytes 3145728 | tf_op jit(solution)/shard_map/span_2/pallas_call | solution.py:517
  26.4 0.0 collective-permute-done.6.far_ref
  26.4 2.1 %collective-permute-start.7 = (f32[8,128]{1,0:T(8,128)S(1)}, f32[8,128]{1,0:T(8,128)S(1)}, u32[]{:S(2)}, u32[]{:S(2)}) collective-permute-start(f32[8,128]{1,0:T(8,128)S(1)} %merged.3._.top), channel_id=1, source_target_pairs={{4,0},{0,4},{12,8},{8,12},{20,16},{16,20},{28,24},{24,28},{5,1},{1... | collective-permute-start | bytes 12296 | tf_op jit(solution)/shard_map/ppermute | solution.py:423
  28.5 1.6 %span_3.1._.refs_3_ = f32[3,4,128,128]{3,2,1,0:T(8,128)S(1)} custom-call(f32[3,36,144,128]{3,2,1,0:T(8,128)S(1)} %get-tuple-element.18.vel_ref.vel_in, f32[128,128]{1,0:T(8,128)S(1)} %collective-permute-done.4.inner_ref, f32[15,8,128]{2,1,0:T(8,128)S(1)} %copy-done, f32[8,128]{1,0:T(8,128)S(1)} %merged.3._.top), custom_call_target="tpu_custom_call" | custom-call | flops 3145728 | bytes 3145728 | tf_op jit(solution)/shard_map/span_3/pallas_call | solution.py:517
  30.1 0.0 collective-permute-done.1.odd_ref
  30.1 0.0 collective-permute-done.even_ref
  30.1 0.1 theta_in.1
  30.2 0.1 collective-permute-start.9
  30.2 1.1 %collective-permute-start.8 = (f32[8,128]{1,0:T(8,128)S(1)}, f32[8,128]{1,0:T(8,128)S(1)}, u32[]{:S(2)}, u32[]{:S(2)}) collective-permute-start(f32[8,128]{1,0:T(8,128)S(1)} %get-tuple-element.22._), channel_id=1, source_target_pairs={{1,0},{0,1},{3,2},{2,3},{5,4},{4,5},{7,6},{6,7},{9,8},{8,9},{11,10... | collective-permute-start | bytes 12296 | tf_op jit(solution)/shard_map/ppermute | solution.py:423
  31.3 1.6 %span_4.1.refs_4_ = f32[3,4,128,128]{3,2,1,0:T(8,128)S(1)} custom-call(f32[3,36,144,128]{3,2,1,0:T(8,128)S(1)} %get-tuple-element.21.vel_ref.vel_in, f32[128,128]{1,0:T(8,128)S(1)} %collective-permute-done.4.inner_ref, f32[15,8,128]{2,1,0:T(8,128)S(1)} %copy-done, f32[8,128]{1,0:T(8,128)S(1)} %get-tuple-element.22._), custom_call_target="tpu_custom_call" | custom-call | flops 3145728 | bytes 3145728 | tf_op jit(solution)/shard_map/span_4/pallas_call | solution.py:517
  32.9 0.0 collective-permute-done.7.far
  32.9 0.4 collective-permute-done.9.odd
  33.3 0.0 collective-permute-done.8.even
  33.3 4.9 %finish.1 = (f32[3,32,128,128]{3,2,1,0:T(8,128)}, f32[1]{0:T(128)}, f32[3,36,144,128]{3,2,1,0:T(8,128)S(1)}) custom-call(f32[3,36,144,128]{3,2,1,0:T(8,128)S(1)} %get-tuple-element.21.vel_ref.vel_in, f32[128,128]{1,0:T(8,128)S(1)} %collective-permute-done.4.inner_ref, f32[15,8,128]{2,1,0:T(8,128)S(1)} %copy-done, ...), custom_call_target="tpu_custom_call", output_to_operand_aliasing={{2}: (0, {})} | custom-call | tf_op jit(solution)/shard_map/finish/pallas_call | solution.py:570
  (3 shorter events, 0.0 us)
Async XLA Ops:
  0.6 14.5 %copy-start = (f32[15,8,128]{2,1,0:T(8,128)S(1)}, f32[15,8,128]{2,1,0:T(8,128)}, u32[]{:S(2)}) copy-start(f32[15,8,128]{2,1,0:T(8,128)} %constant.28.clone.coef_ref) | copy-start | bytes 184324
  1.8 28.2 %collective-permute-start.1 = (f32[3,2,128,128]{3,2,1,0:T(8,128)S(1)}, f32[3,2,128,128]{3,2,1,0:T(8,128)S(1)}, u32[]{:S(2)}, u32[]{:S(2)}) collective-permute-start(f32[3,2,128,128]{3,2,1,0:T(8,128)S(1)} %get-tuple-element.26), channel_id=1, source_target_pairs={{28,0},{8,4},{4,8},{16,12},{12,16},{24,20},{20,24},{0,28},{29,1},{... | collective-permute-start | bytes 1179656 | tf_op jit(solution)/shard_map/ppermute | solution.py:423
  7.9 22.2 %collective-permute-start = (f32[3,2,128,128]{3,2,1,0:T(8,128)S(1)}, f32[3,2,128,128]{3,2,1,0:T(8,128)S(1)}, u32[]{:S(2)}, u32[]{:S(2)}) collective-permute-start(f32[3,2,128,128]{3,2,1,0:T(8,128)S(1)} %get-tuple-element.27), channel_id=1, source_target_pairs={{4,0},{0,4},{12,8},{8,12},{20,16},{16,20},{28,24},{24,28},{5,1},{1... | collective-permute-start | bytes 1179656 | tf_op jit(solution)/shard_map/ppermute | solution.py:423
  11.4 1.4 %collective-permute-start.2 = (f32[3,32,2,128]{3,2,1,0:T(2,128)S(1)}, f32[3,32,2,128]{3,2,1,0:T(2,128)S(1)}, u32[]{:S(2)}, u32[]{:S(2)}) collective-permute-start(f32[3,32,2,128]{3,2,1,0:T(2,128)S(1)} %get-tuple-element.14), channel_id=1, source_target_pairs={{1,0},{0,1},{3,2},{2,3},{5,4},{4,5},{7,6},{6,7},{9,8},{8,9},{11,10... | collective-permute-start | bytes 294920 | tf_op jit(solution)/shard_map/ppermute | solution.py:423
  12.8 4.8 %collective-permute-start.3 = (f32[3,32,2,128]{3,2,1,0:T(2,128)S(1)}, f32[3,32,2,128]{3,2,1,0:T(2,128)S(1)}, u32[]{:S(2)}, u32[]{:S(2)}) collective-permute-start(f32[3,32,2,128]{3,2,1,0:T(2,128)S(1)} %carried.1), channel_id=1, source_target_pairs={{3,0},{2,1},{1,2},{0,3},{7,4},{6,5},{5,6},{4,7},{11,8},{10,9},{9,1... | collective-permute-start | bytes 294920 | tf_op jit(solution)/shard_map/ppermute | solution.py:423
  14.0 9.2 %collective-permute-start.4 = (f32[128,128]{1,0:T(8,128)S(1)}, f32[128,128]{1,0:T(8,128)S(1)}, u32[]{:S(2)}, u32[]{:S(2)}) collective-permute-start(f32[128,128]{1,0:T(8,128)S(1)} %get-tuple-element.19), channel_id=1, source_target_pairs={{16,0},{20,4},{24,8},{28,12},{0,16},{4,20},{8,24},{12,28},{17,1},{... | collective-permute-start | bytes 196616 | tf_op jit(solution)/shard_map/ppermute | solution.py:423
  17.8 3.7 %collective-permute-start.5 = (f32[8,128]{1,0:T(8,128)S(1)}, f32[8,128]{1,0:T(8,128)S(1)}, u32[]{:S(2)}, u32[]{:S(2)}) collective-permute-start(f32[8,128]{1,0:T(8,128)S(1)} %get-tuple-element.20.refs_0_.mine_ref), channel_id=1, source_target_pairs={{8,0},{12,4},{0,8},{4,12},{24,16},{28,20},{16,24},{20,28},{9,1},{1... | collective-permute-start | bytes 12296 | tf_op jit(solution)/shard_map/ppermute | solution.py:423
  21.5 4.9 %collective-permute-start.6 = (f32[8,128]{1,0:T(8,128)S(1)}, f32[8,128]{1,0:T(8,128)S(1)}, u32[]{:S(2)}, u32[]{:S(2)}) collective-permute-start(f32[8,128]{1,0:T(8,128)S(1)} %merged.2._.mine_ref), channel_id=1, source_target_pairs={{16,0},{20,4},{24,8},{28,12},{0,16},{4,20},{8,24},{12,28},{17,1},{... | collective-permute-start | bytes 12296 | tf_op jit(solution)/shard_map/ppermute | solution.py:423
  26.4 6.5 %collective-permute-start.7 = (f32[8,128]{1,0:T(8,128)S(1)}, f32[8,128]{1,0:T(8,128)S(1)}, u32[]{:S(2)}, u32[]{:S(2)}) collective-permute-start(f32[8,128]{1,0:T(8,128)S(1)} %merged.3._.top), channel_id=1, source_target_pairs={{4,0},{0,4},{12,8},{8,12},{20,16},{16,20},{28,24},{24,28},{5,1},{1... | collective-permute-start | bytes 12296 | tf_op jit(solution)/shard_map/ppermute | solution.py:423
  30.2 3.1 %collective-permute-start.9 = (f32[8,128]{1,0:T(8,128)S(1)}, f32[8,128]{1,0:T(8,128)S(1)}, u32[]{:S(2)}, u32[]{:S(2)}) collective-permute-start(f32[8,128]{1,0:T(8,128)S(1)} %get-tuple-element.23), channel_id=1, source_target_pairs={{3,0},{2,1},{1,2},{0,3},{7,4},{6,5},{5,6},{4,7},{11,8},{10,9},{9,1... | collective-permute-start | bytes 12296 | tf_op jit(solution)/shard_map/ppermute | solution.py:423
  30.2 3.0 %collective-permute-start.8 = (f32[8,128]{1,0:T(8,128)S(1)}, f32[8,128]{1,0:T(8,128)S(1)}, u32[]{:S(2)}, u32[]{:S(2)}) collective-permute-start(f32[8,128]{1,0:T(8,128)S(1)} %get-tuple-element.22._), channel_id=1, source_target_pairs={{1,0},{0,1},{3,2},{2,3},{5,4},{4,5},{7,6},{6,7},{9,8},{8,9},{11,10... | collective-permute-start | bytes 12296 | tf_op jit(solution)/shard_map/ppermute | solution.py:423

commit v14 on v13

--- a/solution.py
+++ b/solution.py
@@ -438,7 +438,7 @@
 
 def cuts(planes):
     last = planes - HALO
-    ends = (HALO, last - 5 * BLOCK, last - 4 * BLOCK, last - 2 * BLOCK, last - BLOCK, last)
+    ends = (HALO, last - 5 * BLOCK, last - 3 * BLOCK, last - BLOCK, last)
     return list(zip(ends[:-1], ends[1:]))
 
 
@@ -554,8 +554,8 @@
             out_specs=vmem,
         )(top, far, *parts[-2:])
         far = exchanged(top, "az", bit)
-        if n < 2:
-            parts.append(with_ghosts(n + 2, top))
+        if n == 0:
+            parts.append(with_ghosts(2, top))
     tile_even, tile_odd, vel = call(
         theta_in,
         "theta_in",
@@ -566,7 +566,7 @@
         input_output_aliases={2: 2},
     )(theta_even, theta_odd, vel, parts[-1])
     corner_even, corner_odd = across_even(tile_even, "ax"), across_odd(tile_odd, "ax")
-    parts.append(with_ghosts(4, tile_even))
+    parts.append(with_ghosts(3, tile_even))
     increment, time_step, _ = call(
         functools.partial(finish, spans),
         "finish",

time: 38.3 us -> 37.1 us (0.969)
  waiting for transfers between devices: 3.53 us -> 2.18 us
    pallas_call x3 -> x2, Pallas kernels: 6.22 us -> 4.66 us  [with_ghosts(): call(functools.partial(ahead_with_ghosts, *spans[n]), f'span_{n}', veloci...]
    ppermute x10, waiting for transfers between devices: 3.53 us -> 2.18 us  [routed(): return lax.ppermute(block, axis, [(source(i), i) for i in range(count)])]
    pallas_call x3, Pallas kernels: 3.99 us -> 5.33 us  [without_ghosts(): call(functools.partial(ahead, *spans[n], rounds), name, velocity.size * 2...]
    pallas_call x1, Pallas kernels: 4.89 us -> 5.31 us  [per_device(): call(functools.partial(finish, spans), 'finish', 0, scratch=8, out_shape=...]
where the time goes in v14:
time: 37.1 us; the launch traced here: 37 us
  Pallas kernels  19.1 us (51%)
  starting transfers between devices  13.8 us (37%)
  waiting for transfers between devices  2.18 us (6%)
  local copies, waits for them, and re-layouts  1.18 us (3%)
  between operations  0.76 us (2%)
    ppermute x10, starting transfers between devices, routed(): return lax.ppermute(block, axis, [(source(i), i) for i in range(count)])  13.8 us
    pallas_call x3, Pallas kernels, without_ghosts(): call(functools.partial(ahead, *spans[n], rounds), name, velocity.size * 2...  5.33 us
    pallas_call x1, Pallas kernels, per_device(): call(functools.partial(finish, spans), 'finish', 0, scratch=8, out_shape=...  5.31 us
    pallas_call x2, Pallas kernels, with_ghosts(): call(functools.partial(ahead_with_ghosts, *spans[n]), f'span_{n}', veloci...  4.66 us
    pallas_call x1, Pallas kernels, per_device(): call(functools.partial(first_pass, theta_step), 'first_pass', 0, out_shap...  3.49 us
    ppermute x10, waiting for transfers between devices, routed(): return lax.ppermute(block, axis, [(source(i), i) for i in range(count)])  2.18 us
    dynamic_slice x1, local copies, waits for them, and re-layouts, per_device(): lax.dynamic_slice_in_dim(velocity, odd_end, HALO, 1)  1.18 us
  transfers between devices with their start and end apart: 10, of which 4 were waited for; matrix products, arithmetic and copies ran while one was open for 0% of the time, Pallas kernels for 37%

profile of v14, /device:TPU:0, one launch (start us, length us, event | category | flops | bytes accessed | tf_op | source)
XLA Modules:
  0.0 37.0 jit_solution(2189108557187952094)
XLA Ops:
  0.6 0.0 copy-start
  0.7 1.2 %constant_dynamic-slice_fusion = (f32[3,2,128,128]{3,2,1,0:T(8,128)S(1)}, f32[3,2,128,128]{3,2,1,0:T(8,128)S(1)}) fusion(f32[3,32,128,128]{3,2,1,0:T(8,128)} %v_ref.1, s32[]{:T(128)S(6)} %select_n.18, s32[]{:T(128)S(6)} %select_n.17), kind=kLoop, calls=%fused_computation | loop fusion | bytes 1572872 | tf_op jit(solution)/shard_map/dynamic_slice | solution.py:472
  1.8 6.1 %collective-permute-start.1 = (f32[3,2,128,128]{3,2,1,0:T(8,128)S(1)}, f32[3,2,128,128]{3,2,1,0:T(8,128)S(1)}, u32[]{:S(2)}, u32[]{:S(2)}) collective-permute-start(f32[3,2,128,128]{3,2,1,0:T(8,128)S(1)} %get-tuple-element.26), channel_id=1, source_target_pairs={{28,0},{8,4},{4,8},{16,12},{12,16},{24,20},{20,24},{0,28},{29,1},{... | collective-permute-start | bytes 1179656 | tf_op jit(solution)/shard_map/ppermute | solution.py:423
  7.9 0.0 collective-permute-start
  7.9 3.5 %first_pass.1 = (f32[3,36,144,128]{3,2,1,0:T(8,128)S(1)}, f32[3,32,2,128]{3,2,1,0:T(2,128)S(1)}, f32[3,32,2,128]{3,2,1,0:T(2,128)S(1)}, f32[128,128]{1,0:T(8,128)S(1)}, f32[8,128]{1,0:T(8,128)S(1)}) custom-call(f32[3,32,128,128]{3,2,1,0:T(8,128)} %v_ref.1), custom_call_target="tpu_custom_call" | custom-call | tf_op jit(solution)/shard_map/first_pass/pallas_call | solution.py:478
  11.4 0.1 collective-permute-start.2
  11.5 1.3 %collective-permute-done.2.even_ref = f32[3,32,2,128]{3,2,1,0:T(2,128)S(1)} collective-permute-done((f32[3,32,2,128]{3,2,1,0:T(2,128)S(1)}, f32[3,32,2,128]{3,2,1,0:T(2,128)S(1)}, u32[]{:S(2)}, u32[]{:S(2)}) %collective-permute-start.2) | collective-permute-done | bytes 98336 | tf_op jit(solution)/shard_map/ppermute | solution.py:423
  12.8 1.2 %collective-permute-start.3 = (f32[3,32,2,128]{3,2,1,0:T(2,128)S(1)}, f32[3,32,2,128]{3,2,1,0:T(2,128)S(1)}, u32[]{:S(2)}, u32[]{:S(2)}) collective-permute-start(f32[3,32,2,128]{3,2,1,0:T(2,128)S(1)} %carried.1), channel_id=1, source_target_pairs={{3,0},{2,1},{1,2},{0,3},{7,4},{6,5},{5,6},{4,7},{11,8},{10,9},{9,1... | collective-permute-start | bytes 294920 | tf_op jit(solution)/shard_map/ppermute | solution.py:423
  14.0 1.1 %collective-permute-start.4 = (f32[128,128]{1,0:T(8,128)S(1)}, f32[128,128]{1,0:T(8,128)S(1)}, u32[]{:S(2)}, u32[]{:S(2)}) collective-permute-start(f32[128,128]{1,0:T(8,128)S(1)} %get-tuple-element.19), channel_id=1, source_target_pairs={{16,0},{20,4},{24,8},{28,12},{0,16},{4,20},{8,24},{12,28},{17,1},{... | collective-permute-start | bytes 196616 | tf_op jit(solution)/shard_map/ppermute | solution.py:423
  15.1 0.0 copy-done
  15.1 2.4 %span_0_middle.1._.refs_0_ = f32[3,8,128,128]{3,2,1,0:T(8,128)S(1)} custom-call(f32[3,36,144,128]{3,2,1,0:T(8,128)S(1)} %get-tuple-element.17.vel_ref.vel_in, f32[15,8,128]{2,1,0:T(8,128)S(1)} %copy-done, f32[8,128]{1,0:T(8,128)S(1)} %get-tuple-element.15.pay_ref.refs_0_), custom_call_target="tpu_custom_call" | custom-call | flops 3145728 | bytes 3145728 | tf_op jit(solution)/shard_map/span_0_middle/pallas_call | solution.py:506
  17.5 0.1 collective-permute-done.3.odd_ref
  17.5 0.2 fold.1
  17.8 0.2 collective-permute-start.5
  18.0 0.3 span_0_outer.1.refs_0_
  18.3 2.7 %span_1.1.refs_1_.refs_0_ = f32[3,8,128,128]{3,2,1,0:T(8,128)S(1)} custom-call(f32[3,36,144,128]{3,2,1,0:T(8,128)S(1)} %get-tuple-element.18.vel_ref.vel_in, f32[15,8,128]{2,1,0:T(8,128)S(1)} %copy-done, f32[8,128]{1,0:T(8,128)S(1)} %get-tuple-element.20.refs_0_.mine_ref), custom_call_target="tpu_custom_call" | custom-call | flops 3145728 | bytes 3145728 | tf_op jit(solution)/shard_map/span_1/pallas_call | solution.py:506
  21.0 0.4 %collective-permute-done.5.far_ref = f32[8,128]{1,0:T(8,128)S(1)} collective-permute-done((f32[8,128]{1,0:T(8,128)S(1)}, f32[8,128]{1,0:T(8,128)S(1)}, u32[]{:S(2)}, u32[]{:S(2)}) %collective-permute-start.5) | collective-permute-done | bytes 4128 | tf_op jit(solution)/shard_map/ppermute | solution.py:423
  21.5 1.8 %collective-permute-start.6 = (f32[8,128]{1,0:T(8,128)S(1)}, f32[8,128]{1,0:T(8,128)S(1)}, u32[]{:S(2)}, u32[]{:S(2)}) collective-permute-start(f32[8,128]{1,0:T(8,128)S(1)} %merged.2._.mine_ref), channel_id=1, source_target_pairs={{16,0},{20,4},{24,8},{28,12},{0,16},{4,20},{8,24},{12,28},{17,1},{... | collective-permute-start | bytes 12296 | tf_op jit(solution)/shard_map/ppermute | solution.py:423
  23.3 0.0 collective-permute-done.4.inner_ref
  23.3 3.1 %span_2.1._.refs_1_.refs_2_ = f32[3,8,128,128]{3,2,1,0:T(8,128)S(1)} custom-call(f32[3,36,144,128]{3,2,1,0:T(8,128)S(1)} %get-tuple-element.18.vel_ref.vel_in, f32[128,128]{1,0:T(8,128)S(1)} %collective-permute-done.4.inner_ref, f32[15,8,128]{2,1,0:T(8,128)S(1)} %copy-done, f32[8,128]{1,0:T(8,128)S(1)} %merged.2._.mine_ref), custom_call_target="tpu_custom_call" | custom-call | flops 3145728 | bytes 3145728 | tf_op jit(solution)/shard_map/span_2/pallas_call | solution.py:517
  26.4 0.0 collective-permute-done.6.far_ref
  26.4 2.1 %collective-permute-start.7 = (f32[8,128]{1,0:T(8,128)S(1)}, f32[8,128]{1,0:T(8,128)S(1)}, u32[]{:S(2)}, u32[]{:S(2)}) collective-permute-start(f32[8,128]{1,0:T(8,128)S(1)} %merged.3.top), channel_id=1, source_target_pairs={{4,0},{0,4},{12,8},{8,12},{20,16},{16,20},{28,24},{24,28},{5,1},{1... | collective-permute-start | bytes 12296 | tf_op jit(solution)/shard_map/ppermute | solution.py:423
  28.5 0.0 collective-permute-done.1.odd_ref
  28.5 0.0 collective-permute-done.even_ref
  28.5 0.1 theta_in.1
  28.6 0.1 collective-permute-start.9
  28.7 1.1 %collective-permute-start.8 = (f32[8,128]{1,0:T(8,128)S(1)}, f32[8,128]{1,0:T(8,128)S(1)}, u32[]{:S(2)}, u32[]{:S(2)}) collective-permute-start(f32[8,128]{1,0:T(8,128)S(1)} %get-tuple-element.22._), channel_id=1, source_target_pairs={{1,0},{0,1},{3,2},{2,3},{5,4},{4,5},{7,6},{6,7},{9,8},{8,9},{11,10... | collective-permute-start | bytes 12296 | tf_op jit(solution)/shard_map/ppermute | solution.py:423
  29.7 1.5 %span_3.1.refs_3_ = f32[3,4,128,128]{3,2,1,0:T(8,128)S(1)} custom-call(f32[3,36,144,128]{3,2,1,0:T(8,128)S(1)} %get-tuple-element.21.vel_ref.vel_in, f32[128,128]{1,0:T(8,128)S(1)} %collective-permute-done.4.inner_ref, f32[15,8,128]{2,1,0:T(8,128)S(1)} %copy-done, f32[8,128]{1,0:T(8,128)S(1)} %get-tuple-element.22._), custom_call_target="tpu_custom_call" | custom-call | flops 3145728 | bytes 3145728 | tf_op jit(solution)/shard_map/span_3/pallas_call | solution.py:517
  31.3 0.0 collective-permute-done.7.far
  31.3 0.4 collective-permute-done.9.odd
  31.7 0.0 collective-permute-done.8.even
  31.7 5.3 %finish.1 = (f32[3,32,128,128]{3,2,1,0:T(8,128)}, f32[1]{0:T(128)}, f32[3,36,144,128]{3,2,1,0:T(8,128)S(1)}) custom-call(f32[3,36,144,128]{3,2,1,0:T(8,128)S(1)} %get-tuple-element.21.vel_ref.vel_in, f32[128,128]{1,0:T(8,128)S(1)} %collective-permute-done.4.inner_ref, f32[15,8,128]{2,1,0:T(8,128)S(1)} %copy-done, ...), custom_call_target="tpu_custom_call", output_to_operand_aliasing={{2}: (0, {})} | custom-call | tf_op jit(solution)/shard_map/finish/pallas_call | solution.py:570
  (3 shorter events, 0.0 us)
Async XLA Ops:
  0.6 14.5 %copy-start = (f32[15,8,128]{2,1,0:T(8,128)S(1)}, f32[15,8,128]{2,1,0:T(8,128)}, u32[]{:S(2)}) copy-start(f32[15,8,128]{2,1,0:T(8,128)} %constant.28.clone.coef_ref) | copy-start | bytes 184324
  1.8 26.7 %collective-permute-start.1 = (f32[3,2,128,128]{3,2,1,0:T(8,128)S(1)}, f32[3,2,128,128]{3,2,1,0:T(8,128)S(1)}, u32[]{:S(2)}, u32[]{:S(2)}) collective-permute-start(f32[3,2,128,128]{3,2,1,0:T(8,128)S(1)} %get-tuple-element.26), channel_id=1, source_target_pairs={{28,0},{8,4},{4,8},{16,12},{12,16},{24,20},{20,24},{0,28},{29,1},{... | collective-permute-start | bytes 1179656 | tf_op jit(solution)/shard_map/ppermute | solution.py:423
  7.9 20.6 %collective-permute-start = (f32[3,2,128,128]{3,2,1,0:T(8,128)S(1)}, f32[3,2,128,128]{3,2,1,0:T(8,128)S(1)}, u32[]{:S(2)}, u32[]{:S(2)}) collective-permute-start(f32[3,2,128,128]{3,2,1,0:T(8,128)S(1)} %get-tuple-element.27), channel_id=1, source_target_pairs={{4,0},{0,4},{12,8},{8,12},{20,16},{16,20},{28,24},{24,28},{5,1},{1... | collective-permute-start | bytes 1179656 | tf_op jit(solution)/shard_map/ppermute | solution.py:423
  11.4 1.4 %collective-permute-start.2 = (f32[3,32,2,128]{3,2,1,0:T(2,128)S(1)}, f32[3,32,2,128]{3,2,1,0:T(2,128)S(1)}, u32[]{:S(2)}, u32[]{:S(2)}) collective-permute-start(f32[3,32,2,128]{3,2,1,0:T(2,128)S(1)} %get-tuple-element.14), channel_id=1, source_target_pairs={{1,0},{0,1},{3,2},{2,3},{5,4},{4,5},{7,6},{6,7},{9,8},{8,9},{11,10... | collective-permute-start | bytes 294920 | tf_op jit(solution)/shard_map/ppermute | solution.py:423
  12.8 4.8 %collective-permute-start.3 = (f32[3,32,2,128]{3,2,1,0:T(2,128)S(1)}, f32[3,32,2,128]{3,2,1,0:T(2,128)S(1)}, u32[]{:S(2)}, u32[]{:S(2)}) collective-permute-start(f32[3,32,2,128]{3,2,1,0:T(2,128)S(1)} %carried.1), channel_id=1, source_target_pairs={{3,0},{2,1},{1,2},{0,3},{7,4},{6,5},{5,6},{4,7},{11,8},{10,9},{9,1... | collective-permute-start | bytes 294920 | tf_op jit(solution)/shard_map/ppermute | solution.py:423
  14.0 9.2 %collective-permute-start.4 = (f32[128,128]{1,0:T(8,128)S(1)}, f32[128,128]{1,0:T(8,128)S(1)}, u32[]{:S(2)}, u32[]{:S(2)}) collective-permute-start(f32[128,128]{1,0:T(8,128)S(1)} %get-tuple-element.19), channel_id=1, source_target_pairs={{16,0},{20,4},{24,8},{28,12},{0,16},{4,20},{8,24},{12,28},{17,1},{... | collective-permute-start | bytes 196616 | tf_op jit(solution)/shard_map/ppermute | solution.py:423
  17.8 3.7 %collective-permute-start.5 = (f32[8,128]{1,0:T(8,128)S(1)}, f32[8,128]{1,0:T(8,128)S(1)}, u32[]{:S(2)}, u32[]{:S(2)}) collective-permute-start(f32[8,128]{1,0:T(8,128)S(1)} %get-tuple-element.20.refs_0_.mine_ref), channel_id=1, source_target_pairs={{8,0},{12,4},{0,8},{4,12},{24,16},{28,20},{16,24},{20,28},{9,1},{1... | collective-permute-start | bytes 12296 | tf_op jit(solution)/shard_map/ppermute | solution.py:423
  21.5 4.9 %collective-permute-start.6 = (f32[8,128]{1,0:T(8,128)S(1)}, f32[8,128]{1,0:T(8,128)S(1)}, u32[]{:S(2)}, u32[]{:S(2)}) collective-permute-start(f32[8,128]{1,0:T(8,128)S(1)} %merged.2._.mine_ref), channel_id=1, source_target_pairs={{16,0},{20,4},{24,8},{28,12},{0,16},{4,20},{8,24},{12,28},{17,1},{... | collective-permute-start | bytes 12296 | tf_op jit(solution)/shard_map/ppermute | solution.py:423
  26.4 4.9 %collective-permute-start.7 = (f32[8,128]{1,0:T(8,128)S(1)}, f32[8,128]{1,0:T(8,128)S(1)}, u32[]{:S(2)}, u32[]{:S(2)}) collective-permute-start(f32[8,128]{1,0:T(8,128)S(1)} %merged.3.top), channel_id=1, source_target_pairs={{4,0},{0,4},{12,8},{8,12},{20,16},{16,20},{28,24},{24,28},{5,1},{1... | collective-permute-start | bytes 12296 | tf_op jit(solution)/shard_map/ppermute | solution.py:423
  28.6 3.1 %collective-permute-start.9 = (f32[8,128]{1,0:T(8,128)S(1)}, f32[8,128]{1,0:T(8,128)S(1)}, u32[]{:S(2)}, u32[]{:S(2)}) collective-permute-start(f32[8,128]{1,0:T(8,128)S(1)} %get-tuple-element.23), channel_id=1, source_target_pairs={{3,0},{2,1},{1,2},{0,3},{7,4},{6,5},{5,6},{4,7},{11,8},{10,9},{9,1... | collective-permute-start | bytes 12296 | tf_op jit(solution)/shard_map/ppermute | solution.py:423
  28.7 3.0 %collective-permute-start.8 = (f32[8,128]{1,0:T(8,128)S(1)}, f32[8,128]{1,0:T(8,128)S(1)}, u32[]{:S(2)}, u32[]{:S(2)}) collective-permute-start(f32[8,128]{1,0:T(8,128)S(1)} %get-tuple-element.22._), channel_id=1, source_target_pairs={{1,0},{0,1},{3,2},{2,3},{5,4},{4,5},{7,6},{6,7},{9,8},{8,9},{11,10... | collective-permute-start | bytes 12296 | tf_op jit(solution)/shard_map/ppermute | solution.py:423

commit v15 on v14

--- a/solution.py
+++ b/solution.py
@@ -309,7 +309,7 @@
 def block_terms(vel_ref, inner_ref, coef_ref, j, size, write, rounds=None):
     planes = vel_ref.shape[1] - 2 * HALO
     axial, radial = vel_ref.shape[2] - 2 * PAD, vel_ref.shape[3]
-    groups = 2 * BLOCK // size
+    groups = 4 * BLOCK // size
     times, places = rounds or (
         axial // (8 * groups),
         lambda i: [(i * groups + u) * 8 for u in range(groups)],

time: 37.1 us -> 37.4 us (level)
  no operation moved by 1% of the time
where the time goes in v15:
time: 37.4 us; the launch traced here: 37.2 us
  Pallas kernels  19.3 us (52%)
  starting transfers between devices  13.7 us (37%)
  waiting for transfers between devices  2.31 us (6%)
  local copies, waits for them, and re-layouts  1.18 us (3%)
  between operations  0.76 us (2%)
    ppermute x10, starting transfers between devices, routed(): return lax.ppermute(block, axis, [(source(i), i) for i in range(count)])  13.7 us
    pallas_call x1, Pallas kernels, per_device(): call(functools.partial(finish, spans), 'finish', 0, scratch=8, out_shape=...  5.48 us
    pallas_call x3, Pallas kernels, without_ghosts(): call(functools.partial(ahead, *spans[n], rounds), name, velocity.size * 2...  5.21 us
    pallas_call x2, Pallas kernels, with_ghosts(): call(functools.partial(ahead_with_ghosts, *spans[n]), f'span_{n}', veloci...  4.79 us
    pallas_call x1, Pallas kernels, per_device(): call(functools.partial(first_pass, theta_step), 'first_pass', 0, out_shap...  3.49 us
    ppermute x10, waiting for transfers between devices, routed(): return lax.ppermute(block, axis, [(source(i), i) for i in range(count)])  2.31 us
    dynamic_slice x1, local copies, waits for them, and re-layouts, per_device(): lax.dynamic_slice_in_dim(velocity, odd_end, HALO, 1)  1.18 us
  transfers between devices with their start and end apart: 10, of which 4 were waited for; matrix products, arithmetic and copies ran while one was open for 0% of the time, Pallas kernels for 37%

profile of v15, /device:TPU:0, one launch (start us, length us, event | category | flops | bytes accessed | tf_op | source)
XLA Modules:
  0.0 37.2 jit_solution(8936005996527723442)
XLA Ops:
  0.6 0.0 copy-start
  0.7 1.2 %constant_dynamic-slice_fusion = (f32[3,2,128,128]{3,2,1,0:T(8,128)S(1)}, f32[3,2,128,128]{3,2,1,0:T(8,128)S(1)}) fusion(f32[3,32,128,128]{3,2,1,0:T(8,128)} %v_ref.1, s32[]{:T(128)S(6)} %select_n.18, s32[]{:T(128)S(6)} %select_n.17), kind=kLoop, calls=%fused_computation | loop fusion | bytes 1572872 | tf_op jit(solution)/shard_map/dynamic_slice | solution.py:472
  1.8 6.1 %collective-permute-start.1 = (f32[3,2,128,128]{3,2,1,0:T(8,128)S(1)}, f32[3,2,128,128]{3,2,1,0:T(8,128)S(1)}, u32[]{:S(2)}, u32[]{:S(2)}) collective-permute-start(f32[3,2,128,128]{3,2,1,0:T(8,128)S(1)} %get-tuple-element.26), channel_id=1, source_target_pairs={{28,0},{8,4},{4,8},{16,12},{12,16},{24,20},{20,24},{0,28},{29,1},{... | collective-permute-start | bytes 1179656 | tf_op jit(solution)/shard_map/ppermute | solution.py:423
  7.9 0.0 collective-permute-start
  7.9 3.5 %first_pass.1 = (f32[3,36,144,128]{3,2,1,0:T(8,128)S(1)}, f32[3,32,2,128]{3,2,1,0:T(2,128)S(1)}, f32[3,32,2,128]{3,2,1,0:T(2,128)S(1)}, f32[128,128]{1,0:T(8,128)S(1)}, f32[8,128]{1,0:T(8,128)S(1)}) custom-call(f32[3,32,128,128]{3,2,1,0:T(8,128)} %v_ref.1), custom_call_target="tpu_custom_call" | custom-call | tf_op jit(solution)/shard_map/first_pass/pallas_call | solution.py:478
  11.4 0.1 collective-permute-start.2
  11.5 1.3 %collective-permute-done.2.even_ref = f32[3,32,2,128]{3,2,1,0:T(2,128)S(1)} collective-permute-done((f32[3,32,2,128]{3,2,1,0:T(2,128)S(1)}, f32[3,32,2,128]{3,2,1,0:T(2,128)S(1)}, u32[]{:S(2)}, u32[]{:S(2)}) %collective-permute-start.2) | collective-permute-done | bytes 98336 | tf_op jit(solution)/shard_map/ppermute | solution.py:423
  12.8 1.2 %collective-permute-start.3 = (f32[3,32,2,128]{3,2,1,0:T(2,128)S(1)}, f32[3,32,2,128]{3,2,1,0:T(2,128)S(1)}, u32[]{:S(2)}, u32[]{:S(2)}) collective-permute-start(f32[3,32,2,128]{3,2,1,0:T(2,128)S(1)} %carried.1), channel_id=1, source_target_pairs={{3,0},{2,1},{1,2},{0,3},{7,4},{6,5},{5,6},{4,7},{11,8},{10,9},{9,1... | collective-permute-start | bytes 294920 | tf_op jit(solution)/shard_map/ppermute | solution.py:423
  14.0 1.1 %collective-permute-start.4 = (f32[128,128]{1,0:T(8,128)S(1)}, f32[128,128]{1,0:T(8,128)S(1)}, u32[]{:S(2)}, u32[]{:S(2)}) collective-permute-start(f32[128,128]{1,0:T(8,128)S(1)} %get-tuple-element.19), channel_id=1, source_target_pairs={{16,0},{20,4},{24,8},{28,12},{0,16},{4,20},{8,24},{12,28},{17,1},{... | collective-permute-start | bytes 196616 | tf_op jit(solution)/shard_map/ppermute | solution.py:423
  15.1 0.0 copy-done
  15.1 2.4 %span_0_middle.1._.refs_0_ = f32[3,8,128,128]{3,2,1,0:T(8,128)S(1)} custom-call(f32[3,36,144,128]{3,2,1,0:T(8,128)S(1)} %get-tuple-element.17.vel_ref.vel_in, f32[15,8,128]{2,1,0:T(8,128)S(1)} %copy-done, f32[8,128]{1,0:T(8,128)S(1)} %get-tuple-element.15.pay_ref.refs_0_), custom_call_target="tpu_custom_call" | custom-call | flops 3145728 | bytes 3145728 | tf_op jit(solution)/shard_map/span_0_middle/pallas_call | solution.py:506
  17.5 0.1 collective-permute-done.3.odd_ref
  17.5 0.2 fold.1
  17.8 0.2 collective-permute-start.5
  18.0 0.3 span_0_outer.1.refs_0_
  18.3 2.5 %span_1.1.refs_1_.refs_0_ = f32[3,8,128,128]{3,2,1,0:T(8,128)S(1)} custom-call(f32[3,36,144,128]{3,2,1,0:T(8,128)S(1)} %get-tuple-element.18.vel_ref.vel_in, f32[15,8,128]{2,1,0:T(8,128)S(1)} %copy-done, f32[8,128]{1,0:T(8,128)S(1)} %get-tuple-element.20.refs_0_.mine_ref), custom_call_target="tpu_custom_call" | custom-call | flops 3145728 | bytes 3145728 | tf_op jit(solution)/shard_map/span_1/pallas_call | solution.py:506
  20.9 0.6 %collective-permute-done.5.far_ref = f32[8,128]{1,0:T(8,128)S(1)} collective-permute-done((f32[8,128]{1,0:T(8,128)S(1)}, f32[8,128]{1,0:T(8,128)S(1)}, u32[]{:S(2)}, u32[]{:S(2)}) %collective-permute-start.5) | collective-permute-done | bytes 4128 | tf_op jit(solution)/shard_map/ppermute | solution.py:423
  21.5 1.8 %collective-permute-start.6 = (f32[8,128]{1,0:T(8,128)S(1)}, f32[8,128]{1,0:T(8,128)S(1)}, u32[]{:S(2)}, u32[]{:S(2)}) collective-permute-start(f32[8,128]{1,0:T(8,128)S(1)} %merged.2._.mine_ref), channel_id=1, source_target_pairs={{16,0},{20,4},{24,8},{28,12},{0,16},{4,20},{8,24},{12,28},{17,1},{... | collective-permute-start | bytes 12296 | tf_op jit(solution)/shard_map/ppermute | solution.py:423
  23.3 0.0 collective-permute-done.4.inner_ref
  23.3 3.2 %span_2.1._.refs_1_.refs_2_ = f32[3,8,128,128]{3,2,1,0:T(8,128)S(1)} custom-call(f32[3,36,144,128]{3,2,1,0:T(8,128)S(1)} %get-tuple-element.18.vel_ref.vel_in, f32[128,128]{1,0:T(8,128)S(1)} %collective-permute-done.4.inner_ref, f32[15,8,128]{2,1,0:T(8,128)S(1)} %copy-done, f32[8,128]{1,0:T(8,128)S(1)} %merged.2._.mine_ref), custom_call_target="tpu_custom_call" | custom-call | flops 3145728 | bytes 3145728 | tf_op jit(solution)/shard_map/span_2/pallas_call | solution.py:517
  26.5 0.0 collective-permute-done.6.far_ref
  26.5 2.1 %collective-permute-start.7 = (f32[8,128]{1,0:T(8,128)S(1)}, f32[8,128]{1,0:T(8,128)S(1)}, u32[]{:S(2)}, u32[]{:S(2)}) collective-permute-start(f32[8,128]{1,0:T(8,128)S(1)} %merged.3.top), channel_id=1, source_target_pairs={{4,0},{0,4},{12,8},{8,12},{20,16},{16,20},{28,24},{24,28},{5,1},{1... | collective-permute-start | bytes 12296 | tf_op jit(solution)/shard_map/ppermute | solution.py:423
  28.6 0.0 collective-permute-done.1.odd_ref
  28.6 0.0 collective-permute-done.even_ref
  28.6 0.1 theta_in.1
  28.7 0.1 collective-permute-start.9
  28.7 1.0 %collective-permute-start.8 = (f32[8,128]{1,0:T(8,128)S(1)}, f32[8,128]{1,0:T(8,128)S(1)}, u32[]{:S(2)}, u32[]{:S(2)}) collective-permute-start(f32[8,128]{1,0:T(8,128)S(1)} %get-tuple-element.22._), channel_id=1, source_target_pairs={{1,0},{0,1},{3,2},{2,3},{5,4},{4,5},{7,6},{6,7},{9,8},{8,9},{11,10... | collective-permute-start | bytes 12296 | tf_op jit(solution)/shard_map/ppermute | solution.py:423
  29.8 1.6 %span_3.1.refs_3_ = f32[3,4,128,128]{3,2,1,0:T(8,128)S(1)} custom-call(f32[3,36,144,128]{3,2,1,0:T(8,128)S(1)} %get-tuple-element.21.vel_ref.vel_in, f32[128,128]{1,0:T(8,128)S(1)} %collective-permute-done.4.inner_ref, f32[15,8,128]{2,1,0:T(8,128)S(1)} %copy-done, f32[8,128]{1,0:T(8,128)S(1)} %get-tuple-element.22._), custom_call_target="tpu_custom_call" | custom-call | flops 3145728 | bytes 3145728 | tf_op jit(solution)/shard_map/span_3/pallas_call | solution.py:517
  31.4 0.0 collective-permute-done.7.far
  31.4 0.4 %collective-permute-done.9.odd = f32[8,128]{1,0:T(8,128)S(1)} collective-permute-done((f32[8,128]{1,0:T(8,128)S(1)}, f32[8,128]{1,0:T(8,128)S(1)}, u32[]{:S(2)}, u32[]{:S(2)}) %collective-permute-start.9) | collective-permute-done | bytes 4128 | tf_op jit(solution)/shard_map/ppermute | solution.py:423
  31.7 0.0 collective-permute-done.8.even
  31.8 5.5 %finish.1 = (f32[3,32,128,128]{3,2,1,0:T(8,128)}, f32[1]{0:T(128)}, f32[3,36,144,128]{3,2,1,0:T(8,128)S(1)}) custom-call(f32[3,36,144,128]{3,2,1,0:T(8,128)S(1)} %get-tuple-element.21.vel_ref.vel_in, f32[128,128]{1,0:T(8,128)S(1)} %collective-permute-done.4.inner_ref, f32[15,8,128]{2,1,0:T(8,128)S(1)} %copy-done, ...), custom_call_target="tpu_custom_call", output_to_operand_aliasing={{2}: (0, {})} | custom-call | tf_op jit(solution)/shard_map/finish/pallas_call | solution.py:570
  (3 shorter events, 0.0 us)
Async XLA Ops:
  0.6 14.5 %copy-start = (f32[15,8,128]{2,1,0:T(8,128)S(1)}, f32[15,8,128]{2,1,0:T(8,128)}, u32[]{:S(2)}) copy-start(f32[15,8,128]{2,1,0:T(8,128)} %constant.28.clone.coef_ref) | copy-start | bytes 184324
  1.8 26.7 %collective-permute-start.1 = (f32[3,2,128,128]{3,2,1,0:T(8,128)S(1)}, f32[3,2,128,128]{3,2,1,0:T(8,128)S(1)}, u32[]{:S(2)}, u32[]{:S(2)}) collective-permute-start(f32[3,2,128,128]{3,2,1,0:T(8,128)S(1)} %get-tuple-element.26), channel_id=1, source_target_pairs={{28,0},{8,4},{4,8},{16,12},{12,16},{24,20},{20,24},{0,28},{29,1},{... | collective-permute-start | bytes 1179656 | tf_op jit(solution)/shard_map/ppermute | solution.py:423
  7.9 20.7 %collective-permute-start = (f32[3,2,128,128]{3,2,1,0:T(8,128)S(1)}, f32[3,2,128,128]{3,2,1,0:T(8,128)S(1)}, u32[]{:S(2)}, u32[]{:S(2)}) collective-permute-start(f32[3,2,128,128]{3,2,1,0:T(8,128)S(1)} %get-tuple-element.27), channel_id=1, source_target_pairs={{4,0},{0,4},{12,8},{8,12},{20,16},{16,20},{28,24},{24,28},{5,1},{1... | collective-permute-start | bytes 1179656 | tf_op jit(solution)/shard_map/ppermute | solution.py:423
  11.4 1.4 %collective-permute-start.2 = (f32[3,32,2,128]{3,2,1,0:T(2,128)S(1)}, f32[3,32,2,128]{3,2,1,0:T(2,128)S(1)}, u32[]{:S(2)}, u32[]{:S(2)}) collective-permute-start(f32[3,32,2,128]{3,2,1,0:T(2,128)S(1)} %get-tuple-element.14), channel_id=1, source_target_pairs={{1,0},{0,1},{3,2},{2,3},{5,4},{4,5},{7,6},{6,7},{9,8},{8,9},{11,10... | collective-permute-start | bytes 294920 | tf_op jit(solution)/shard_map/ppermute | solution.py:423
  12.8 4.8 %collective-permute-start.3 = (f32[3,32,2,128]{3,2,1,0:T(2,128)S(1)}, f32[3,32,2,128]{3,2,1,0:T(2,128)S(1)}, u32[]{:S(2)}, u32[]{:S(2)}) collective-permute-start(f32[3,32,2,128]{3,2,1,0:T(2,128)S(1)} %carried.1), channel_id=1, source_target_pairs={{3,0},{2,1},{1,2},{0,3},{7,4},{6,5},{5,6},{4,7},{11,8},{10,9},{9,1... | collective-permute-start | bytes 294920 | tf_op jit(solution)/shard_map/ppermute | solution.py:423
  14.0 9.2 %collective-permute-start.4 = (f32[128,128]{1,0:T(8,128)S(1)}, f32[128,128]{1,0:T(8,128)S(1)}, u32[]{:S(2)}, u32[]{:S(2)}) collective-permute-start(f32[128,128]{1,0:T(8,128)S(1)} %get-tuple-element.19), channel_id=1, source_target_pairs={{16,0},{20,4},{24,8},{28,12},{0,16},{4,20},{8,24},{12,28},{17,1},{... | collective-permute-start | bytes 196616 | tf_op jit(solution)/shard_map/ppermute | solution.py:423
  17.8 3.7 %collective-permute-start.5 = (f32[8,128]{1,0:T(8,128)S(1)}, f32[8,128]{1,0:T(8,128)S(1)}, u32[]{:S(2)}, u32[]{:S(2)}) collective-permute-start(f32[8,128]{1,0:T(8,128)S(1)} %get-tuple-element.20.refs_0_.mine_ref), channel_id=1, source_target_pairs={{8,0},{12,4},{0,8},{4,12},{24,16},{28,20},{16,24},{20,28},{9,1},{1... | collective-permute-start | bytes 12296 | tf_op jit(solution)/shard_map/ppermute | solution.py:423
  21.5 5.0 %collective-permute-start.6 = (f32[8,128]{1,0:T(8,128)S(1)}, f32[8,128]{1,0:T(8,128)S(1)}, u32[]{:S(2)}, u32[]{:S(2)}) collective-permute-start(f32[8,128]{1,0:T(8,128)S(1)} %merged.2._.mine_ref), channel_id=1, source_target_pairs={{16,0},{20,4},{24,8},{28,12},{0,16},{4,20},{8,24},{12,28},{17,1},{... | collective-permute-start | bytes 12296 | tf_op jit(solution)/shard_map/ppermute | solution.py:423
  26.5 4.9 %collective-permute-start.7 = (f32[8,128]{1,0:T(8,128)S(1)}, f32[8,128]{1,0:T(8,128)S(1)}, u32[]{:S(2)}, u32[]{:S(2)}) collective-permute-start(f32[8,128]{1,0:T(8,128)S(1)} %merged.3.top), channel_id=1, source_target_pairs={{4,0},{0,4},{12,8},{8,12},{20,16},{16,20},{28,24},{24,28},{5,1},{1... | collective-permute-start | bytes 12296 | tf_op jit(solution)/shard_map/ppermute | solution.py:423
  28.7 3.1 %collective-permute-start.9 = (f32[8,128]{1,0:T(8,128)S(1)}, f32[8,128]{1,0:T(8,128)S(1)}, u32[]{:S(2)}, u32[]{:S(2)}) collective-permute-start(f32[8,128]{1,0:T(8,128)S(1)} %get-tuple-element.23), channel_id=1, source_target_pairs={{3,0},{2,1},{1,2},{0,3},{7,4},{6,5},{5,6},{4,7},{11,8},{10,9},{9,1... | collective-permute-start | bytes 12296 | tf_op jit(solution)/shard_map/ppermute | solution.py:423
  28.7 3.0 %collective-permute-start.8 = (f32[8,128]{1,0:T(8,128)S(1)}, f32[8,128]{1,0:T(8,128)S(1)}, u32[]{:S(2)}, u32[]{:S(2)}) collective-permute-start(f32[8,128]{1,0:T(8,128)S(1)} %get-tuple-element.22._), channel_id=1, source_target_pairs={{1,0},{0,1},{3,2},{2,3},{5,4},{4,5},{7,6},{6,7},{9,8},{8,9},{11,10... | collective-permute-start | bytes 12296 | tf_op jit(solution)/shard_map/ppermute | solution.py:423

commit v16 on v15

--- a/solution.py
+++ b/solution.py
@@ -306,21 +306,45 @@
     return ghost
 
 
-def block_terms(vel_ref, inner_ref, coef_ref, j, size, write, rounds=None):
+def block_terms(vel_ref, inner_ref, coef_ref, kept, j, size, write, rounds=None):
     planes = vel_ref.shape[1] - 2 * HALO
     axial, radial = vel_ref.shape[2] - 2 * PAD, vel_ref.shape[3]
+    a_kept, c_kept = kept
     groups = 4 * BLOCK // size
-    times, places = rounds or (
+    start, times, places = rounds or (
+        0,
         axial // (8 * groups),
         lambda i: [(i * groups + u) * 8 for u in range(groups)],
     )
 
+    def keep_c(cells, q):
+        value = cells.pair(-1, 2, q)
+        c_kept[q, pl.ds(cells.k + PAD, 8), :] = value
+
+    if start is not None:
+        before = Cells(vel_ref, j, start - 8)
+        for q in range(size):
+            keep_c(before, q)
+
     def rows(i, carry):
         coef = [coef_ref[n] for n in range(COUNT)]
+        ks = [pl.multiple_of(k, 8) for k in places(i)]
+        all_cells = [Cells(vel_ref, j, k) for k in ks]
+        if start is not None:
+            for cells in all_cells + [Cells(vel_ref, j, ks[-1] + 8)]:
+                for q in range(size):
+                    a_kept[q, pl.ds(cells.k + PAD, 8), :] = cells.pair(1, 0, q)
+            for cells in all_cells:
+                for q in range(size):
+                    keep_c(cells, q)
+            for cells in all_cells:
+                for q in range(size):
+                    ahead_row = pl.ds(cells.k + PAD + 1, 8)
+                    cells.known["pair", 0, q, 1] = a_kept[q, ahead_row, :]
+                    back_row = pl.ds(cells.k + PAD - 1, 8)
+                    cells.known["pair", 2, q, -1] = c_kept[q, back_row, :]
         found = []
-        for k in places(i):
-            k = pl.multiple_of(k, 8)
-            cells = Cells(vel_ref, j, k)
+        for k, cells in zip(ks, all_cells):
             ghost = None
             if inner_ref is not None:
                 ghost = ghosts(cells, inner_ref[pl.ds(k, 8), :], planes)
@@ -335,30 +359,30 @@
 
 
 def ahead(first, last, rounds, vel_ref, coef_ref, *refs):
-    out_ref = refs[-1]
+    out_ref, *kept = refs[-3:]
 
     def write(n, j, k, value):
         out_ref[n, j - first, k, :] = value
 
     def block(m, carry):
-        block_terms(vel_ref, None, coef_ref, first + m * BLOCK, BLOCK, write, rounds)
+        block_terms(vel_ref, None, coef_ref, kept, first + m * BLOCK, BLOCK, write, rounds)
         return carry
 
     lax.fori_loop(0, (last - first) // BLOCK, block, 0)
 
 
-def ahead_with_ghosts(first, last, vel_ref, inner_ref, coef_ref, _, out_ref):
+def ahead_with_ghosts(first, last, vel_ref, inner_ref, coef_ref, _, out_ref, *kept):
     def write(n, j, k, value):
         out_ref[n, j - first, k, :] = value
 
     for j in range(first, last, BLOCK):
-        block_terms(vel_ref, inner_ref, coef_ref, j, BLOCK, write)
+        block_terms(vel_ref, inner_ref, coef_ref, kept, j, BLOCK, write)
 
 
 def finish(spans, vel_in, inner_ref, coef_ref, top, far, even, odd, *refs):
     parts, refs = refs[: len(spans)], refs[len(spans) :]
     del vel_in
-    out_ref, step_ref, vel_ref, res, sems = refs
+    out_ref, step_ref, vel_ref, res, sems, *kept = refs
     axial, radial = inner_ref.shape
     planes = vel_ref.shape[1] - 2 * HALO
     largest = jnp.maximum(top[0:1, :], far[0:1, :])
@@ -412,7 +436,7 @@
     vel_ref[1, HALO - 1, PAD + axial : PAD + axial + 1, :] = following
     vel_ref[2, HALO + planes, PAD - 1 : PAD, :] = preceding
     for j in (0, planes - HALO):
-        block_terms(vel_ref, inner_ref, coef_ref, j, HALO, write)
+        block_terms(vel_ref, inner_ref, coef_ref, kept, j, HALO, write)
         send(j, HALO)
     for copy in pending:
         copy.wait()
@@ -502,6 +526,8 @@
     def part_shape(n):
         return shape(3, spans[n][1] - spans[n][0], axial, radial)
 
+    kept = [pltpu.VMEM((BLOCK, axial + 2 * PAD, radial), f32)] * 2
+
     def without_ghosts(n, name, rounds, vel, *tokens, **kwargs):
         return call(
             functools.partial(ahead, *spans[n], rounds),
@@ -510,6 +536,7 @@
             out_shape=part_shape(n),
             in_specs=[vmem] * (2 + len(tokens)),
             out_specs=vmem,
+            scratch_shapes=kept,
             **kwargs,
         )(vel, coef, *tokens)
 
@@ -521,10 +548,11 @@
             out_shape=part_shape(n),
             in_specs=[vmem] * 4,
             out_specs=vmem,
+            scratch_shapes=kept,
         )(vel, inner, coef, token)
 
-    middle = (axial - 16) // 16, lambda i: [16 * i + 8, 16 * i + 16]
-    outer = 1, lambda i: [i * 8, i * 8 + axial - 8]
+    middle = 8, (axial - 16) // 16, lambda i: [16 * i + 8, 16 * i + 16]
+    outer = None, 1, lambda i: [i * 8, i * 8 + axial - 8]
     part = without_ghosts(0, "span_0_middle", middle, vel, pay)
     top, vel = call(
         fold,
@@ -578,6 +606,7 @@
         scratch_shapes=[
             pltpu.VMEM(velocity.shape, f32),
             pltpu.SemaphoreType.DMA(((planes - 2 * HALO) // BLOCK + 2,)),
+            *kept,
         ],
         input_output_aliases={0: 2},
     )(vel, inner, coef, top, far, corner_even, corner_odd, *parts)

time: 37.4 us -> 37.8 us (1.011)
  Pallas kernels: 19.3 us -> 20.1 us
    pallas_call x3, Pallas kernels: 5.21 us -> 5.82 us  [without_ghosts(): call(functools.partial(ahead, *spans[n], rounds), name, velocity.size * 2...]
  transfers between devices with their start and end apart: 10 -> 10, of which waited for: 4 -> 3; matrix products, arithmetic and copies ran while one was open for 0% -> 0% of each run, Pallas kernels for 37% -> 39%
where the time goes in v16:
time: 37.8 us; the launch traced here: 37.6 us
  Pallas kernels  20.1 us (53%)
  starting transfers between devices  13.4 us (35%)
  waiting for transfers between devices  2.13 us (6%)
  local copies, waits for them, and re-layouts  1.18 us (3%)
  between operations  0.77 us (2%)
    ppermute x10, starting transfers between devices, routed(): return lax.ppermute(block, axis, [(source(i), i) for i in range(count)])  13.4 us
    pallas_call x3, Pallas kernels, without_ghosts(): call(functools.partial(ahead, *spans[n], rounds), name, velocity.size * 2...  5.82 us
    pallas_call x1, Pallas kernels, per_device(): call(functools.partial(finish, spans), 'finish', 0, scratch=8, out_shape=...  5.4 us
    pallas_call x2, Pallas kernels, with_ghosts(): call(functools.partial(ahead_with_ghosts, *spans[n]), f'span_{n}', veloci...  5.13 us
    pallas_call x1, Pallas kernels, per_device(): call(functools.partial(first_pass, theta_step), 'first_pass', 0, out_shap...  3.49 us
    ppermute x10, waiting for transfers between devices, routed(): return lax.ppermute(block, axis, [(source(i), i) for i in range(count)])  2.13 us
    dynamic_slice x1, local copies, waits for them, and re-layouts, per_device(): lax.dynamic_slice_in_dim(velocity, odd_end, HALO, 1)  1.18 us
  transfers between devices with their start and end apart: 10, of which 3 were waited for; matrix products, arithmetic and copies ran while one was open for 0% of the time, Pallas kernels for 39%

profile of v16, /device:TPU:0, one launch (start us, length us, event | category | flops | bytes accessed | tf_op | source)
XLA Modules:
  0.0 37.6 jit_solution(8502740531511071979)
XLA Ops:
  0.6 0.0 copy-start
  0.7 1.2 %constant_dynamic-slice_fusion = (f32[3,2,128,128]{3,2,1,0:T(8,128)S(1)}, f32[3,2,128,128]{3,2,1,0:T(8,128)S(1)}) fusion(f32[3,32,128,128]{3,2,1,0:T(8,128)} %v_ref.1, s32[]{:T(128)S(6)} %select_n.18, s32[]{:T(128)S(6)} %select_n.17), kind=kLoop, calls=%fused_computation | loop fusion | bytes 1572872 | tf_op jit(solution)/shard_map/dynamic_slice | solution.py:496
  1.8 6.1 %collective-permute-start.1 = (f32[3,2,128,128]{3,2,1,0:T(8,128)S(1)}, f32[3,2,128,128]{3,2,1,0:T(8,128)S(1)}, u32[]{:S(2)}, u32[]{:S(2)}) collective-permute-start(f32[3,2,128,128]{3,2,1,0:T(8,128)S(1)} %get-tuple-element.26), channel_id=1, source_target_pairs={{28,0},{8,4},{4,8},{16,12},{12,16},{24,20},{20,24},{0,28},{29,1},{... | collective-permute-start | bytes 1179656 | tf_op jit(solution)/shard_map/ppermute | solution.py:447
  7.9 0.0 collective-permute-start
  7.9 3.5 %first_pass.1 = (f32[3,36,144,128]{3,2,1,0:T(8,128)S(1)}, f32[3,32,2,128]{3,2,1,0:T(2,128)S(1)}, f32[3,32,2,128]{3,2,1,0:T(2,128)S(1)}, f32[128,128]{1,0:T(8,128)S(1)}, f32[8,128]{1,0:T(8,128)S(1)}) custom-call(f32[3,32,128,128]{3,2,1,0:T(8,128)} %v_ref.1), custom_call_target="tpu_custom_call" | custom-call | tf_op jit(solution)/shard_map/first_pass/pallas_call | solution.py:502
  11.4 0.1 collective-permute-start.2
  11.5 1.3 %collective-permute-done.2.even_ref = f32[3,32,2,128]{3,2,1,0:T(2,128)S(1)} collective-permute-done((f32[3,32,2,128]{3,2,1,0:T(2,128)S(1)}, f32[3,32,2,128]{3,2,1,0:T(2,128)S(1)}, u32[]{:S(2)}, u32[]{:S(2)}) %collective-permute-start.2) | collective-permute-done | bytes 98336 | tf_op jit(solution)/shard_map/ppermute | solution.py:447
  12.8 1.2 %collective-permute-start.3 = (f32[3,32,2,128]{3,2,1,0:T(2,128)S(1)}, f32[3,32,2,128]{3,2,1,0:T(2,128)S(1)}, u32[]{:S(2)}, u32[]{:S(2)}) collective-permute-start(f32[3,32,2,128]{3,2,1,0:T(2,128)S(1)} %carried.1), channel_id=1, source_target_pairs={{3,0},{2,1},{1,2},{0,3},{7,4},{6,5},{5,6},{4,7},{11,8},{10,9},{9,1... | collective-permute-start | bytes 294920 | tf_op jit(solution)/shard_map/ppermute | solution.py:447
  14.0 1.1 %collective-permute-start.4 = (f32[128,128]{1,0:T(8,128)S(1)}, f32[128,128]{1,0:T(8,128)S(1)}, u32[]{:S(2)}, u32[]{:S(2)}) collective-permute-start(f32[128,128]{1,0:T(8,128)S(1)} %get-tuple-element.19), channel_id=1, source_target_pairs={{16,0},{20,4},{24,8},{28,12},{0,16},{4,20},{8,24},{12,28},{17,1},{... | collective-permute-start | bytes 196616 | tf_op jit(solution)/shard_map/ppermute | solution.py:447
  15.1 0.0 copy-done
  15.1 2.6 %span_0_middle.1._.refs_0_ = f32[3,8,128,128]{3,2,1,0:T(8,128)S(1)} custom-call(f32[3,36,144,128]{3,2,1,0:T(8,128)S(1)} %get-tuple-element.17.vel_ref.vel_in, f32[15,8,128]{2,1,0:T(8,128)S(1)} %copy-done, f32[8,128]{1,0:T(8,128)S(1)} %get-tuple-element.15.pay_ref.refs_0_), custom_call_target="tpu_custom_call" | custom-call | flops 3145728 | bytes 3145728 | tf_op jit(solution)/shard_map/span_0_middle/pallas_call | solution.py:532
  17.7 0.0 collective-permute-done.3.odd_ref
  17.7 0.2 fold.1
  18.0 0.3 collective-permute-start.5
  18.3 0.3 span_0_outer.1.refs_0_
  18.6 2.9 %span_1.1.refs_1_.refs_0_ = f32[3,8,128,128]{3,2,1,0:T(8,128)S(1)} custom-call(f32[3,36,144,128]{3,2,1,0:T(8,128)S(1)} %get-tuple-element.18.vel_ref.vel_in, f32[15,8,128]{2,1,0:T(8,128)S(1)} %copy-done, f32[8,128]{1,0:T(8,128)S(1)} %get-tuple-element.20.refs_0_.mine_ref), custom_call_target="tpu_custom_call" | custom-call | flops 3145728 | bytes 3145728 | tf_op jit(solution)/shard_map/span_1/pallas_call | solution.py:532
  21.5 0.2 collective-permute-done.5.far_ref
  21.7 1.9 %collective-permute-start.6 = (f32[8,128]{1,0:T(8,128)S(1)}, f32[8,128]{1,0:T(8,128)S(1)}, u32[]{:S(2)}, u32[]{:S(2)}) collective-permute-start(f32[8,128]{1,0:T(8,128)S(1)} %merged.2._.mine_ref), channel_id=1, source_target_pairs={{16,0},{20,4},{24,8},{28,12},{0,16},{4,20},{8,24},{12,28},{17,1},{... | collective-permute-start | bytes 12296 | tf_op jit(solution)/shard_map/ppermute | solution.py:447
  23.5 0.0 collective-permute-done.4.inner_ref
  23.5 3.4 %span_2.1._.refs_1_.refs_2_ = f32[3,8,128,128]{3,2,1,0:T(8,128)S(1)} custom-call(f32[3,36,144,128]{3,2,1,0:T(8,128)S(1)} %get-tuple-element.18.vel_ref.vel_in, f32[128,128]{1,0:T(8,128)S(1)} %collective-permute-done.4.inner_ref, f32[15,8,128]{2,1,0:T(8,128)S(1)} %copy-done, f32[8,128]{1,0:T(8,128)S(1)} %merged.2._.mine_ref), custom_call_target="tpu_custom_call" | custom-call | flops 3145728 | bytes 3145728 | tf_op jit(solution)/shard_map/span_2/pallas_call | solution.py:544
  26.9 0.0 collective-permute-done.6.far_ref
  27.0 2.1 %collective-permute-start.7 = (f32[8,128]{1,0:T(8,128)S(1)}, f32[8,128]{1,0:T(8,128)S(1)}, u32[]{:S(2)}, u32[]{:S(2)}) collective-permute-start(f32[8,128]{1,0:T(8,128)S(1)} %merged.3.top), channel_id=1, source_target_pairs={{4,0},{0,4},{12,8},{8,12},{20,16},{16,20},{28,24},{24,28},{5,1},{1... | collective-permute-start | bytes 12296 | tf_op jit(solution)/shard_map/ppermute | solution.py:447
  29.1 0.0 collective-permute-done.1.odd_ref
  29.1 0.0 collective-permute-done.even_ref
  29.1 0.1 theta_in.1
  29.1 0.1 collective-permute-start.9
  29.2 0.6 %collective-permute-start.8 = (f32[8,128]{1,0:T(8,128)S(1)}, f32[8,128]{1,0:T(8,128)S(1)}, u32[]{:S(2)}, u32[]{:S(2)}) collective-permute-start(f32[8,128]{1,0:T(8,128)S(1)} %get-tuple-element.22._), channel_id=1, source_target_pairs={{1,0},{0,1},{3,2},{2,3},{5,4},{4,5},{7,6},{6,7},{9,8},{8,9},{11,10... | collective-permute-start | bytes 12296 | tf_op jit(solution)/shard_map/ppermute | solution.py:447
  29.9 1.7 %span_3.1.refs_3_ = f32[3,4,128,128]{3,2,1,0:T(8,128)S(1)} custom-call(f32[3,36,144,128]{3,2,1,0:T(8,128)S(1)} %get-tuple-element.21.vel_ref.vel_in, f32[128,128]{1,0:T(8,128)S(1)} %collective-permute-done.4.inner_ref, f32[15,8,128]{2,1,0:T(8,128)S(1)} %copy-done, f32[8,128]{1,0:T(8,128)S(1)} %get-tuple-element.22._), custom_call_target="tpu_custom_call" | custom-call | flops 3145728 | bytes 3145728 | tf_op jit(solution)/shard_map/span_3/pallas_call | solution.py:544
  31.6 0.0 collective-permute-done.7.far
  31.6 0.7 %collective-permute-done.9.odd = f32[8,128]{1,0:T(8,128)S(1)} collective-permute-done((f32[8,128]{1,0:T(8,128)S(1)}, f32[8,128]{1,0:T(8,128)S(1)}, u32[]{:S(2)}, u32[]{:S(2)}) %collective-permute-start.9) | collective-permute-done | bytes 4128 | tf_op jit(solution)/shard_map/ppermute | solution.py:447
  32.2 0.0 collective-permute-done.8.even
  32.2 5.4 %finish.1 = (f32[3,32,128,128]{3,2,1,0:T(8,128)}, f32[1]{0:T(128)}, f32[3,36,144,128]{3,2,1,0:T(8,128)S(1)}) custom-call(f32[3,36,144,128]{3,2,1,0:T(8,128)S(1)} %get-tuple-element.21.vel_ref.vel_in, f32[128,128]{1,0:T(8,128)S(1)} %collective-permute-done.4.inner_ref, f32[15,8,128]{2,1,0:T(8,128)S(1)} %copy-done, ...), custom_call_target="tpu_custom_call", output_to_operand_aliasing={{2}: (0, {})} | custom-call | tf_op jit(solution)/shard_map/finish/pallas_call | solution.py:598
  (3 shorter events, 0.0 us)
Async XLA Ops:
  0.6 14.5 %copy-start = (f32[15,8,128]{2,1,0:T(8,128)S(1)}, f32[15,8,128]{2,1,0:T(8,128)}, u32[]{:S(2)}) copy-start(f32[15,8,128]{2,1,0:T(8,128)} %constant.28.clone.coef_ref) | copy-start | bytes 184324
  1.8 27.2 %collective-permute-start.1 = (f32[3,2,128,128]{3,2,1,0:T(8,128)S(1)}, f32[3,2,128,128]{3,2,1,0:T(8,128)S(1)}, u32[]{:S(2)}, u32[]{:S(2)}) collective-permute-start(f32[3,2,128,128]{3,2,1,0:T(8,128)S(1)} %get-tuple-element.26), channel_id=1, source_target_pairs={{28,0},{8,4},{4,8},{16,12},{12,16},{24,20},{20,24},{0,28},{29,1},{... | collective-permute-start | bytes 1179656 | tf_op jit(solution)/shard_map/ppermute | solution.py:447
  7.9 21.2 %collective-permute-start = (f32[3,2,128,128]{3,2,1,0:T(8,128)S(1)}, f32[3,2,128,128]{3,2,1,0:T(8,128)S(1)}, u32[]{:S(2)}, u32[]{:S(2)}) collective-permute-start(f32[3,2,128,128]{3,2,1,0:T(8,128)S(1)} %get-tuple-element.27), channel_id=1, source_target_pairs={{4,0},{0,4},{12,8},{8,12},{20,16},{16,20},{28,24},{24,28},{5,1},{1... | collective-permute-start | bytes 1179656 | tf_op jit(solution)/shard_map/ppermute | solution.py:447
  11.4 1.4 %collective-permute-start.2 = (f32[3,32,2,128]{3,2,1,0:T(2,128)S(1)}, f32[3,32,2,128]{3,2,1,0:T(2,128)S(1)}, u32[]{:S(2)}, u32[]{:S(2)}) collective-permute-start(f32[3,32,2,128]{3,2,1,0:T(2,128)S(1)} %get-tuple-element.14), channel_id=1, source_target_pairs={{1,0},{0,1},{3,2},{2,3},{5,4},{4,5},{7,6},{6,7},{9,8},{8,9},{11,10... | collective-permute-start | bytes 294920 | tf_op jit(solution)/shard_map/ppermute | solution.py:447
  12.8 5.0 %collective-permute-start.3 = (f32[3,32,2,128]{3,2,1,0:T(2,128)S(1)}, f32[3,32,2,128]{3,2,1,0:T(2,128)S(1)}, u32[]{:S(2)}, u32[]{:S(2)}) collective-permute-start(f32[3,32,2,128]{3,2,1,0:T(2,128)S(1)} %carried.1), channel_id=1, source_target_pairs={{3,0},{2,1},{1,2},{0,3},{7,4},{6,5},{5,6},{4,7},{11,8},{10,9},{9,1... | collective-permute-start | bytes 294920 | tf_op jit(solution)/shard_map/ppermute | solution.py:447
  14.0 9.5 %collective-permute-start.4 = (f32[128,128]{1,0:T(8,128)S(1)}, f32[128,128]{1,0:T(8,128)S(1)}, u32[]{:S(2)}, u32[]{:S(2)}) collective-permute-start(f32[128,128]{1,0:T(8,128)S(1)} %get-tuple-element.19), channel_id=1, source_target_pairs={{16,0},{20,4},{24,8},{28,12},{0,16},{4,20},{8,24},{12,28},{17,1},{... | collective-permute-start | bytes 196616 | tf_op jit(solution)/shard_map/ppermute | solution.py:447
  18.0 3.7 %collective-permute-start.5 = (f32[8,128]{1,0:T(8,128)S(1)}, f32[8,128]{1,0:T(8,128)S(1)}, u32[]{:S(2)}, u32[]{:S(2)}) collective-permute-start(f32[8,128]{1,0:T(8,128)S(1)} %get-tuple-element.20.refs_0_.mine_ref), channel_id=1, source_target_pairs={{8,0},{12,4},{0,8},{4,12},{24,16},{28,20},{16,24},{20,28},{9,1},{1... | collective-permute-start | bytes 12296 | tf_op jit(solution)/shard_map/ppermute | solution.py:447
  21.7 5.3 %collective-permute-start.6 = (f32[8,128]{1,0:T(8,128)S(1)}, f32[8,128]{1,0:T(8,128)S(1)}, u32[]{:S(2)}, u32[]{:S(2)}) collective-permute-start(f32[8,128]{1,0:T(8,128)S(1)} %merged.2._.mine_ref), channel_id=1, source_target_pairs={{16,0},{20,4},{24,8},{28,12},{0,16},{4,20},{8,24},{12,28},{17,1},{... | collective-permute-start | bytes 12296 | tf_op jit(solution)/shard_map/ppermute | solution.py:447
  27.0 4.6 %collective-permute-start.7 = (f32[8,128]{1,0:T(8,128)S(1)}, f32[8,128]{1,0:T(8,128)S(1)}, u32[]{:S(2)}, u32[]{:S(2)}) collective-permute-start(f32[8,128]{1,0:T(8,128)S(1)} %merged.3.top), channel_id=1, source_target_pairs={{4,0},{0,4},{12,8},{8,12},{20,16},{16,20},{28,24},{24,28},{5,1},{1... | collective-permute-start | bytes 12296 | tf_op jit(solution)/shard_map/ppermute | solution.py:447
  29.1 3.1 %collective-permute-start.9 = (f32[8,128]{1,0:T(8,128)S(1)}, f32[8,128]{1,0:T(8,128)S(1)}, u32[]{:S(2)}, u32[]{:S(2)}) collective-permute-start(f32[8,128]{1,0:T(8,128)S(1)} %get-tuple-element.23), channel_id=1, source_target_pairs={{3,0},{2,1},{1,2},{0,3},{7,4},{6,5},{5,6},{4,7},{11,8},{10,9},{9,1... | collective-permute-start | bytes 12296 | tf_op jit(solution)/shard_map/ppermute | solution.py:447
  29.2 3.0 %collective-permute-start.8 = (f32[8,128]{1,0:T(8,128)S(1)}, f32[8,128]{1,0:T(8,128)S(1)}, u32[]{:S(2)}, u32[]{:S(2)}) collective-permute-start(f32[8,128]{1,0:T(8,128)S(1)} %get-tuple-element.22._), channel_id=1, source_target_pairs={{1,0},{0,1},{3,2},{2,3},{5,4},{4,5},{7,6},{6,7},{9,8},{8,9},{11,10... | collective-permute-start | bytes 12296 | tf_op jit(solution)/shard_map/ppermute | solution.py:447

commit v17 on v15

--- a/solution.py
+++ b/solution.py
@@ -317,7 +317,6 @@
 
     def rows(i, carry):
         coef = [coef_ref[n] for n in range(COUNT)]
-        found = []
         for k in places(i):
             k = pl.multiple_of(k, 8)
             cells = Cells(vel_ref, j, k)
@@ -325,10 +324,8 @@
             if inner_ref is not None:
                 ghost = ghosts(cells, inner_ref[pl.ds(k, 8), :], planes)
             for q in range(size):
-                found.append((q, k, terms(cells, ghost, coef, q, 1.0 / radial)))
-        for q, k, values in found:
-            for n, value in enumerate(values):
-                write(n, j + q, pl.ds(k, 8), value)
+                for n, value in enumerate(terms(cells, ghost, coef, q, 1.0 / radial)):
+                    write(n, j + q, pl.ds(k, 8), value)
         return carry
 
     lax.fori_loop(0, times, rows, 0)

time: 37.4 us -> 37.4 us (level)
  no operation moved by 1% of the time
where the time goes in v17:
time: 37.4 us; the launch traced here: 37.2 us
  Pallas kernels  19.3 us (52%)
  starting transfers between devices  13.7 us (37%)
  waiting for transfers between devices  2.31 us (6%)
  local copies, waits for them, and re-layouts  1.18 us (3%)
  between operations  0.76 us (2%)
    ppermute x10, starting transfers between devices, routed(): return lax.ppermute(block, axis, [(source(i), i) for i in range(count)])  13.7 us
    pallas_call x1, Pallas kernels, per_device(): call(functools.partial(finish, spans), 'finish', 0, scratch=8, out_shape=...  5.48 us
    pallas_call x3, Pallas kernels, without_ghosts(): call(functools.partial(ahead, *spans[n], rounds), name, velocity.size * 2...  5.21 us
    pallas_call x2, Pallas kernels, with_ghosts(): call(functools.partial(ahead_with_ghosts, *spans[n]), f'span_{n}', veloci...  4.79 us
    pallas_call x1, Pallas kernels, per_device(): call(functools.partial(first_pass, theta_step), 'first_pass', 0, out_shap...  3.49 us
    ppermute x10, waiting for transfers between devices, routed(): return lax.ppermute(block, axis, [(source(i), i) for i in range(count)])  2.31 us
    dynamic_slice x1, local copies, waits for them, and re-layouts, per_device(): lax.dynamic_slice_in_dim(velocity, odd_end, HALO, 1)  1.18 us
  transfers between devices with their start and end apart: 10, of which 4 were waited for; matrix products, arithmetic and copies ran while one was open for 0% of the time, Pallas kernels for 37%

profile of v17, /device:TPU:0, one launch (start us, length us, event | category | flops | bytes accessed | tf_op | source)
XLA Modules:
  0.0 37.2 jit_solution(8936005996527723442)
XLA Ops:
  0.6 0.0 copy-start
  0.7 1.2 %constant_dynamic-slice_fusion = (f32[3,2,128,128]{3,2,1,0:T(8,128)S(1)}, f32[3,2,128,128]{3,2,1,0:T(8,128)S(1)}) fusion(f32[3,32,128,128]{3,2,1,0:T(8,128)} %v_ref.1, s32[]{:T(128)S(6)} %select_n.18, s32[]{:T(128)S(6)} %select_n.17), kind=kLoop, calls=%fused_computation | loop fusion | bytes 1572872 | tf_op jit(solution)/shard_map/dynamic_slice | solution.py:469
  1.8 6.1 %collective-permute-start.1 = (f32[3,2,128,128]{3,2,1,0:T(8,128)S(1)}, f32[3,2,128,128]{3,2,1,0:T(8,128)S(1)}, u32[]{:S(2)}, u32[]{:S(2)}) collective-permute-start(f32[3,2,128,128]{3,2,1,0:T(8,128)S(1)} %get-tuple-element.26), channel_id=1, source_target_pairs={{28,0},{8,4},{4,8},{16,12},{12,16},{24,20},{20,24},{0,28},{29,1},{... | collective-permute-start | bytes 1179656 | tf_op jit(solution)/shard_map/ppermute | solution.py:420
  7.9 0.0 collective-permute-start
  7.9 3.5 %first_pass.1 = (f32[3,36,144,128]{3,2,1,0:T(8,128)S(1)}, f32[3,32,2,128]{3,2,1,0:T(2,128)S(1)}, f32[3,32,2,128]{3,2,1,0:T(2,128)S(1)}, f32[128,128]{1,0:T(8,128)S(1)}, f32[8,128]{1,0:T(8,128)S(1)}) custom-call(f32[3,32,128,128]{3,2,1,0:T(8,128)} %v_ref.1), custom_call_target="tpu_custom_call" | custom-call | tf_op jit(solution)/shard_map/first_pass/pallas_call | solution.py:475
  11.4 0.1 collective-permute-start.2
  11.5 1.3 %collective-permute-done.2.even_ref = f32[3,32,2,128]{3,2,1,0:T(2,128)S(1)} collective-permute-done((f32[3,32,2,128]{3,2,1,0:T(2,128)S(1)}, f32[3,32,2,128]{3,2,1,0:T(2,128)S(1)}, u32[]{:S(2)}, u32[]{:S(2)}) %collective-permute-start.2) | collective-permute-done | bytes 98336 | tf_op jit(solution)/shard_map/ppermute | solution.py:420
  12.8 1.2 %collective-permute-start.3 = (f32[3,32,2,128]{3,2,1,0:T(2,128)S(1)}, f32[3,32,2,128]{3,2,1,0:T(2,128)S(1)}, u32[]{:S(2)}, u32[]{:S(2)}) collective-permute-start(f32[3,32,2,128]{3,2,1,0:T(2,128)S(1)} %carried.1), channel_id=1, source_target_pairs={{3,0},{2,1},{1,2},{0,3},{7,4},{6,5},{5,6},{4,7},{11,8},{10,9},{9,1... | collective-permute-start | bytes 294920 | tf_op jit(solution)/shard_map/ppermute | solution.py:420
  14.0 1.1 %collective-permute-start.4 = (f32[128,128]{1,0:T(8,128)S(1)}, f32[128,128]{1,0:T(8,128)S(1)}, u32[]{:S(2)}, u32[]{:S(2)}) collective-permute-start(f32[128,128]{1,0:T(8,128)S(1)} %get-tuple-element.19), channel_id=1, source_target_pairs={{16,0},{20,4},{24,8},{28,12},{0,16},{4,20},{8,24},{12,28},{17,1},{... | collective-permute-start | bytes 196616 | tf_op jit(solution)/shard_map/ppermute | solution.py:420
  15.1 0.0 copy-done
  15.1 2.4 %span_0_middle.1._.refs_0_ = f32[3,8,128,128]{3,2,1,0:T(8,128)S(1)} custom-call(f32[3,36,144,128]{3,2,1,0:T(8,128)S(1)} %get-tuple-element.17.vel_ref.vel_in, f32[15,8,128]{2,1,0:T(8,128)S(1)} %copy-done, f32[8,128]{1,0:T(8,128)S(1)} %get-tuple-element.15.pay_ref.refs_0_), custom_call_target="tpu_custom_call" | custom-call | flops 3145728 | bytes 3145728 | tf_op jit(solution)/shard_map/span_0_middle/pallas_call | solution.py:503
  17.5 0.1 collective-permute-done.3.odd_ref
  17.5 0.2 fold.1
  17.8 0.2 collective-permute-start.5
  18.0 0.3 span_0_outer.1.refs_0_
  18.3 2.5 %span_1.1.refs_1_.refs_0_ = f32[3,8,128,128]{3,2,1,0:T(8,128)S(1)} custom-call(f32[3,36,144,128]{3,2,1,0:T(8,128)S(1)} %get-tuple-element.18.vel_ref.vel_in, f32[15,8,128]{2,1,0:T(8,128)S(1)} %copy-done, f32[8,128]{1,0:T(8,128)S(1)} %get-tuple-element.20.refs_0_.mine_ref), custom_call_target="tpu_custom_call" | custom-call | flops 3145728 | bytes 3145728 | tf_op jit(solution)/shard_map/span_1/pallas_call | solution.py:503
  20.9 0.6 %collective-permute-done.5.far_ref = f32[8,128]{1,0:T(8,128)S(1)} collective-permute-done((f32[8,128]{1,0:T(8,128)S(1)}, f32[8,128]{1,0:T(8,128)S(1)}, u32[]{:S(2)}, u32[]{:S(2)}) %collective-permute-start.5) | collective-permute-done | bytes 4128 | tf_op jit(solution)/shard_map/ppermute | solution.py:420
  21.5 1.8 %collective-permute-start.6 = (f32[8,128]{1,0:T(8,128)S(1)}, f32[8,128]{1,0:T(8,128)S(1)}, u32[]{:S(2)}, u32[]{:S(2)}) collective-permute-start(f32[8,128]{1,0:T(8,128)S(1)} %merged.2._.mine_ref), channel_id=1, source_target_pairs={{16,0},{20,4},{24,8},{28,12},{0,16},{4,20},{8,24},{12,28},{17,1},{... | collective-permute-start | bytes 12296 | tf_op jit(solution)/shard_map/ppermute | solution.py:420
  23.3 0.0 collective-permute-done.4.inner_ref
  23.3 3.2 %span_2.1._.refs_1_.refs_2_ = f32[3,8,128,128]{3,2,1,0:T(8,128)S(1)} custom-call(f32[3,36,144,128]{3,2,1,0:T(8,128)S(1)} %get-tuple-element.18.vel_ref.vel_in, f32[128,128]{1,0:T(8,128)S(1)} %collective-permute-done.4.inner_ref, f32[15,8,128]{2,1,0:T(8,128)S(1)} %copy-done, f32[8,128]{1,0:T(8,128)S(1)} %merged.2._.mine_ref), custom_call_target="tpu_custom_call" | custom-call | flops 3145728 | bytes 3145728 | tf_op jit(solution)/shard_map/span_2/pallas_call | solution.py:514
  26.5 0.0 collective-permute-done.6.far_ref
  26.5 2.1 %collective-permute-start.7 = (f32[8,128]{1,0:T(8,128)S(1)}, f32[8,128]{1,0:T(8,128)S(1)}, u32[]{:S(2)}, u32[]{:S(2)}) collective-permute-start(f32[8,128]{1,0:T(8,128)S(1)} %merged.3.top), channel_id=1, source_target_pairs={{4,0},{0,4},{12,8},{8,12},{20,16},{16,20},{28,24},{24,28},{5,1},{1... | collective-permute-start | bytes 12296 | tf_op jit(solution)/shard_map/ppermute | solution.py:420
  28.6 0.0 collective-permute-done.1.odd_ref
  28.6 0.0 collective-permute-done.even_ref
  28.6 0.1 theta_in.1
  28.7 0.1 collective-permute-start.9
  28.7 1.0 %collective-permute-start.8 = (f32[8,128]{1,0:T(8,128)S(1)}, f32[8,128]{1,0:T(8,128)S(1)}, u32[]{:S(2)}, u32[]{:S(2)}) collective-permute-start(f32[8,128]{1,0:T(8,128)S(1)} %get-tuple-element.22._), channel_id=1, source_target_pairs={{1,0},{0,1},{3,2},{2,3},{5,4},{4,5},{7,6},{6,7},{9,8},{8,9},{11,10... | collective-permute-start | bytes 12296 | tf_op jit(solution)/shard_map/ppermute | solution.py:420
  29.8 1.6 %span_3.1.refs_3_ = f32[3,4,128,128]{3,2,1,0:T(8,128)S(1)} custom-call(f32[3,36,144,128]{3,2,1,0:T(8,128)S(1)} %get-tuple-element.21.vel_ref.vel_in, f32[128,128]{1,0:T(8,128)S(1)} %collective-permute-done.4.inner_ref, f32[15,8,128]{2,1,0:T(8,128)S(1)} %copy-done, f32[8,128]{1,0:T(8,128)S(1)} %get-tuple-element.22._), custom_call_target="tpu_custom_call" | custom-call | flops 3145728 | bytes 3145728 | tf_op jit(solution)/shard_map/span_3/pallas_call | solution.py:514
  31.4 0.0 collective-permute-done.7.far
  31.4 0.4 %collective-permute-done.9.odd = f32[8,128]{1,0:T(8,128)S(1)} collective-permute-done((f32[8,128]{1,0:T(8,128)S(1)}, f32[8,128]{1,0:T(8,128)S(1)}, u32[]{:S(2)}, u32[]{:S(2)}) %collective-permute-start.9) | collective-permute-done | bytes 4128 | tf_op jit(solution)/shard_map/ppermute | solution.py:420
  31.7 0.0 collective-permute-done.8.even
  31.8 5.5 %finish.1 = (f32[3,32,128,128]{3,2,1,0:T(8,128)}, f32[1]{0:T(128)}, f32[3,36,144,128]{3,2,1,0:T(8,128)S(1)}) custom-call(f32[3,36,144,128]{3,2,1,0:T(8,128)S(1)} %get-tuple-element.21.vel_ref.vel_in, f32[128,128]{1,0:T(8,128)S(1)} %collective-permute-done.4.inner_ref, f32[15,8,128]{2,1,0:T(8,128)S(1)} %copy-done, ...), custom_call_target="tpu_custom_call", output_to_operand_aliasing={{2}: (0, {})} | custom-call | tf_op jit(solution)/shard_map/finish/pallas_call | solution.py:567
  (3 shorter events, 0.0 us)
Async XLA Ops:
  0.6 14.5 %copy-start = (f32[15,8,128]{2,1,0:T(8,128)S(1)}, f32[15,8,128]{2,1,0:T(8,128)}, u32[]{:S(2)}) copy-start(f32[15,8,128]{2,1,0:T(8,128)} %constant.28.clone.coef_ref) | copy-start | bytes 184324
  1.8 26.7 %collective-permute-start.1 = (f32[3,2,128,128]{3,2,1,0:T(8,128)S(1)}, f32[3,2,128,128]{3,2,1,0:T(8,128)S(1)}, u32[]{:S(2)}, u32[]{:S(2)}) collective-permute-start(f32[3,2,128,128]{3,2,1,0:T(8,128)S(1)} %get-tuple-element.26), channel_id=1, source_target_pairs={{28,0},{8,4},{4,8},{16,12},{12,16},{24,20},{20,24},{0,28},{29,1},{... | collective-permute-start | bytes 1179656 | tf_op jit(solution)/shard_map/ppermute | solution.py:420
  7.9 20.7 %collective-permute-start = (f32[3,2,128,128]{3,2,1,0:T(8,128)S(1)}, f32[3,2,128,128]{3,2,1,0:T(8,128)S(1)}, u32[]{:S(2)}, u32[]{:S(2)}) collective-permute-start(f32[3,2,128,128]{3,2,1,0:T(8,128)S(1)} %get-tuple-element.27), channel_id=1, source_target_pairs={{4,0},{0,4},{12,8},{8,12},{20,16},{16,20},{28,24},{24,28},{5,1},{1... | collective-permute-start | bytes 1179656 | tf_op jit(solution)/shard_map/ppermute | solution.py:420
  11.4 1.4 %collective-permute-start.2 = (f32[3,32,2,128]{3,2,1,0:T(2,128)S(1)}, f32[3,32,2,128]{3,2,1,0:T(2,128)S(1)}, u32[]{:S(2)}, u32[]{:S(2)}) collective-permute-start(f32[3,32,2,128]{3,2,1,0:T(2,128)S(1)} %get-tuple-element.14), channel_id=1, source_target_pairs={{1,0},{0,1},{3,2},{2,3},{5,4},{4,5},{7,6},{6,7},{9,8},{8,9},{11,10... | collective-permute-start | bytes 294920 | tf_op jit(solution)/shard_map/ppermute | solution.py:420
  12.8 4.8 %collective-permute-start.3 = (f32[3,32,2,128]{3,2,1,0:T(2,128)S(1)}, f32[3,32,2,128]{3,2,1,0:T(2,128)S(1)}, u32[]{:S(2)}, u32[]{:S(2)}) collective-permute-start(f32[3,32,2,128]{3,2,1,0:T(2,128)S(1)} %carried.1), channel_id=1, source_target_pairs={{3,0},{2,1},{1,2},{0,3},{7,4},{6,5},{5,6},{4,7},{11,8},{10,9},{9,1... | collective-permute-start | bytes 294920 | tf_op jit(solution)/shard_map/ppermute | solution.py:420
  14.0 9.2 %collective-permute-start.4 = (f32[128,128]{1,0:T(8,128)S(1)}, f32[128,128]{1,0:T(8,128)S(1)}, u32[]{:S(2)}, u32[]{:S(2)}) collective-permute-start(f32[128,128]{1,0:T(8,128)S(1)} %get-tuple-element.19), channel_id=1, source_target_pairs={{16,0},{20,4},{24,8},{28,12},{0,16},{4,20},{8,24},{12,28},{17,1},{... | collective-permute-start | bytes 196616 | tf_op jit(solution)/shard_map/ppermute | solution.py:420
  17.8 3.7 %collective-permute-start.5 = (f32[8,128]{1,0:T(8,128)S(1)}, f32[8,128]{1,0:T(8,128)S(1)}, u32[]{:S(2)}, u32[]{:S(2)}) collective-permute-start(f32[8,128]{1,0:T(8,128)S(1)} %get-tuple-element.20.refs_0_.mine_ref), channel_id=1, source_target_pairs={{8,0},{12,4},{0,8},{4,12},{24,16},{28,20},{16,24},{20,28},{9,1},{1... | collective-permute-start | bytes 12296 | tf_op jit(solution)/shard_map/ppermute | solution.py:420
  21.5 5.0 %collective-permute-start.6 = (f32[8,128]{1,0:T(8,128)S(1)}, f32[8,128]{1,0:T(8,128)S(1)}, u32[]{:S(2)}, u32[]{:S(2)}) collective-permute-start(f32[8,128]{1,0:T(8,128)S(1)} %merged.2._.mine_ref), channel_id=1, source_target_pairs={{16,0},{20,4},{24,8},{28,12},{0,16},{4,20},{8,24},{12,28},{17,1},{... | collective-permute-start | bytes 12296 | tf_op jit(solution)/shard_map/ppermute | solution.py:420
  26.5 4.9 %collective-permute-start.7 = (f32[8,128]{1,0:T(8,128)S(1)}, f32[8,128]{1,0:T(8,128)S(1)}, u32[]{:S(2)}, u32[]{:S(2)}) collective-permute-start(f32[8,128]{1,0:T(8,128)S(1)} %merged.3.top), channel_id=1, source_target_pairs={{4,0},{0,4},{12,8},{8,12},{20,16},{16,20},{28,24},{24,28},{5,1},{1... | collective-permute-start | bytes 12296 | tf_op jit(solution)/shard_map/ppermute | solution.py:420
  28.7 3.1 %collective-permute-start.9 = (f32[8,128]{1,0:T(8,128)S(1)}, f32[8,128]{1,0:T(8,128)S(1)}, u32[]{:S(2)}, u32[]{:S(2)}) collective-permute-start(f32[8,128]{1,0:T(8,128)S(1)} %get-tuple-element.23), channel_id=1, source_target_pairs={{3,0},{2,1},{1,2},{0,3},{7,4},{6,5},{5,6},{4,7},{11,8},{10,9},{9,1... | collective-permute-start | bytes 12296 | tf_op jit(solution)/shard_map/ppermute | solution.py:420
  28.7 3.0 %collective-permute-start.8 = (f32[8,128]{1,0:T(8,128)S(1)}, f32[8,128]{1,0:T(8,128)S(1)}, u32[]{:S(2)}, u32[]{:S(2)}) collective-permute-start(f32[8,128]{1,0:T(8,128)S(1)} %get-tuple-element.22._), channel_id=1, source_target_pairs={{1,0},{0,1},{3,2},{2,3},{5,4},{4,5},{7,6},{6,7},{9,8},{8,9},{11,10... | collective-permute-start | bytes 12296 | tf_op jit(solution)/shard_map/ppermute | solution.py:420

commit v18 on v15

--- a/solution.py
+++ b/solution.py
@@ -238,7 +238,7 @@
         ref[0, 0] = jnp.where(end, top, ref[0, 0])
 
 
-def carried(even_ref, pay_ref, odd_in, odd_ref):
+def carried(even_ref, pay_ref, odd_in, _, odd_ref):
     radial = even_ref.shape[3]
     lane = lax.broadcasted_iota(jnp.int32, (2, radial), 1)
     top = jnp.maximum(even_ref[0, 0], pay_ref[0:2, :])
@@ -404,7 +404,7 @@
 
     for n, (part, (first, last)) in enumerate(zip(parts, spans)):
         for j in range(first, last, BLOCK):
-            complete(part, j, j - first, n < 2)
+            complete(part, j, j - first, n < 3)
 
     second = lax.rem(lax.axis_index("ax"), 2) == 1
     even, odd = even[0:1, :], odd[0:1, :]
@@ -438,7 +438,7 @@
 
 def cuts(planes):
     last = planes - HALO
-    ends = (HALO, last - 5 * BLOCK, last - 3 * BLOCK, last - BLOCK, last)
+    ends = (HALO, HALO + BLOCK, last - 5 * BLOCK, last - 3 * BLOCK, last - BLOCK, last)
     return list(zip(ends[:-1], ends[1:]))
 
 
@@ -486,17 +486,6 @@
     )(pltpu.with_memory_space_constraint(velocity, pltpu.HBM))
     inner = exchanged(mine, "az", sizes[0] // 2)
     z_even = across_even(edge_even, "ax")
-    edge_odd = call(
-        carried,
-        "carried",
-        0,
-        out_shape=edge,
-        in_specs=[vmem] * 3,
-        out_specs=vmem,
-        input_output_aliases={2: 0},
-    )(z_even, pay, edge_odd)
-    z_odd = across_odd(edge_odd, "ax")
-
     spans = cuts(planes)
 
     def part_shape(n):
@@ -525,7 +514,19 @@
 
     middle = (axial - 16) // 16, lambda i: [16 * i + 8, 16 * i + 16]
     outer = 1, lambda i: [i * 8, i * 8 + axial - 8]
-    part = without_ghosts(0, "span_0_middle", middle, vel, pay)
+    part_0 = without_ghosts(0, "span_0_middle", middle, vel, pay)
+    edge_odd = call(
+        carried,
+        "carried",
+        0,
+        out_shape=edge,
+        in_specs=[vmem] * 4,
+        out_specs=vmem,
+        input_output_aliases={2: 0},
+    )(z_even, pay, edge_odd, part_0)
+    z_odd = across_odd(edge_odd, "ax")
+
+    part_1 = without_ghosts(1, "span_1_middle", middle, vel, edge_odd)
     top, vel = call(
         fold,
         "fold",
@@ -534,15 +535,16 @@
         in_specs=[vmem] * 5,
         out_specs=(vmem,) * 2,
         input_output_aliases={3: 1},
-    )(z_even, z_odd, pay, vel, part)
+    )(z_even, z_odd, pay, vel, part_1)
     for step in (1 << n for n in range(2, sizes[1].bit_length() - 1)):
         top = jnp.maximum(top, routed(top, "ax", lambda i, step=step: (i + step) % sizes[1]))
 
     bits = [1 << n for n in range(1, sizes[0].bit_length() - 1)] + [1]
     far = exchanged(top, "az", bits[0])
     parts = [
-        without_ghosts(0, "span_0_outer", outer, vel, part, input_output_aliases={2: 0}),
-        without_ghosts(1, "span_1", None, vel, top),
+        without_ghosts(0, "span_0_outer", outer, vel, part_0, input_output_aliases={2: 0}),
+        without_ghosts(1, "span_1_outer", outer, vel, part_1, input_output_aliases={2: 0}),
+        without_ghosts(2, "span_2", None, vel, top),
     ]
     for n, bit in enumerate(bits[1:]):
         top = call(
@@ -550,12 +552,12 @@
             "merged",
             0,
             out_shape=tile,
-            in_specs=[vmem] * 4,
+            in_specs=[vmem] * 5,
             out_specs=vmem,
-        )(top, far, *parts[-2:])
+        )(top, far, *parts[-3:])
         far = exchanged(top, "az", bit)
         if n == 0:
-            parts.append(with_ghosts(2, top))
+            parts.append(with_ghosts(3, top))
     tile_even, tile_odd, vel = call(
         theta_in,
         "theta_in",
@@ -566,7 +568,7 @@
         input_output_aliases={2: 2},
     )(theta_even, theta_odd, vel, parts[-1])
     corner_even, corner_odd = across_even(tile_even, "ax"), across_odd(tile_odd, "ax")
-    parts.append(with_ghosts(3, tile_even))
+    parts.append(with_ghosts(4, tile_even))
     increment, time_step, _ = call(
         functools.partial(finish, spans),
         "finish",

time: 37.4 us -> 36.7 us (0.981)
  waiting for transfers between devices: 2.31 us -> 1.72 us
    ppermute x10, waiting for transfers between devices: 2.31 us -> 1.72 us  [routed(): return lax.ppermute(block, axis, [(source(i), i) for i in range(count)])]
    pallas_call x3 -> x5, Pallas kernels: 5.21 us -> 5.19 us  [without_ghosts(): call(functools.partial(ahead, *spans[n], rounds), name, velocity.size * 2...]
  transfers between devices with their start and end apart: 10 -> 10, of which waited for: 4 -> 4; matrix products, arithmetic and copies ran while one was open for 0% -> 0% of each run, Pallas kernels for 37% -> 38%
where the time goes in v18:
time: 36.7 us; the launch traced here: 36.6 us
  Pallas kernels  19.2 us (52%)
  starting transfers between devices  13.7 us (37%)
  waiting for transfers between devices  1.72 us (5%)
  local copies, waits for them, and re-layouts  1.18 us (3%)
  between operations  0.77 us (2%)
    ppermute x10, starting transfers between devices, routed(): return lax.ppermute(block, axis, [(source(i), i) for i in range(count)])  13.7 us
    pallas_call x1, Pallas kernels, per_device(): call(functools.partial(finish, spans), 'finish', 0, scratch=8, out_shape=...  5.47 us
    pallas_call x5, Pallas kernels, without_ghosts(): call(functools.partial(ahead, *spans[n], rounds), name, velocity.size * 2...  5.19 us
    pallas_call x2, Pallas kernels, with_ghosts(): call(functools.partial(ahead_with_ghosts, *spans[n]), f'span_{n}', veloci...  4.76 us
    pallas_call x1, Pallas kernels, per_device(): call(functools.partial(first_pass, theta_step), 'first_pass', 0, out_shap...  3.47 us
    ppermute x10, waiting for transfers between devices, routed(): return lax.ppermute(block, axis, [(source(i), i) for i in range(count)])  1.72 us
    dynamic_slice x1, local copies, waits for them, and re-layouts, per_device(): lax.dynamic_slice_in_dim(velocity, odd_end, HALO, 1)  1.18 us
  transfers between devices with their start and end apart: 10, of which 4 were waited for; matrix products, arithmetic and copies ran while one was open for 0% of the time, Pallas kernels for 38%

profile of v18, /device:TPU:0, one launch (start us, length us, event | category | flops | bytes accessed | tf_op | source)
XLA Modules:
  0.0 36.6 jit_solution(17938787885226622956)
XLA Ops:
  0.6 0.0 copy-start
  0.7 1.2 %constant_dynamic-slice_fusion = (f32[3,2,128,128]{3,2,1,0:T(8,128)S(1)}, f32[3,2,128,128]{3,2,1,0:T(8,128)S(1)}) fusion(f32[3,32,128,128]{3,2,1,0:T(8,128)} %v_ref.1, s32[]{:T(128)S(6)} %select_n.18, s32[]{:T(128)S(6)} %select_n.17), kind=kLoop, calls=%fused_computation | loop fusion | bytes 1572872 | tf_op jit(solution)/shard_map/dynamic_slice | solution.py:472
  1.8 6.1 %collective-permute-start.1 = (f32[3,2,128,128]{3,2,1,0:T(8,128)S(1)}, f32[3,2,128,128]{3,2,1,0:T(8,128)S(1)}, u32[]{:S(2)}, u32[]{:S(2)}) collective-permute-start(f32[3,2,128,128]{3,2,1,0:T(8,128)S(1)} %get-tuple-element.26), channel_id=1, source_target_pairs={{28,0},{8,4},{4,8},{16,12},{12,16},{24,20},{20,24},{0,28},{29,1},{... | collective-permute-start | bytes 1179656 | tf_op jit(solution)/shard_map/ppermute | solution.py:423
  7.9 0.0 collective-permute-start
  7.9 3.5 %first_pass.1 = (f32[3,36,144,128]{3,2,1,0:T(8,128)S(1)}, f32[3,32,2,128]{3,2,1,0:T(2,128)S(1)}, f32[3,32,2,128]{3,2,1,0:T(2,128)S(1)}, f32[128,128]{1,0:T(8,128)S(1)}, f32[8,128]{1,0:T(8,128)S(1)}) custom-call(f32[3,32,128,128]{3,2,1,0:T(8,128)} %v_ref.1), custom_call_target="tpu_custom_call" | custom-call | tf_op jit(solution)/shard_map/first_pass/pallas_call | solution.py:478
  11.4 0.1 collective-permute-start.2
  11.5 0.0 copy-done
  11.5 1.2 %span_0_middle.1._.refs_0_ = f32[3,4,128,128]{3,2,1,0:T(8,128)S(1)} custom-call(f32[3,36,144,128]{3,2,1,0:T(8,128)S(1)} %get-tuple-element.17.vel_ref.vel_in, f32[15,8,128]{2,1,0:T(8,128)S(1)} %copy-done, f32[8,128]{1,0:T(8,128)S(1)} %get-tuple-element.15.refs_0_.pay_ref), custom_call_target="tpu_custom_call" | custom-call | flops 3145728 | bytes 3145728 | tf_op jit(solution)/shard_map/span_0_middle/pallas_call | solution.py:495
  12.6 0.1 collective-permute-done.2.even_ref
  12.8 1.5 %collective-permute-start.3 = (f32[3,32,2,128]{3,2,1,0:T(2,128)S(1)}, f32[3,32,2,128]{3,2,1,0:T(2,128)S(1)}, u32[]{:S(2)}, u32[]{:S(2)}) collective-permute-start(f32[3,32,2,128]{3,2,1,0:T(2,128)S(1)} %carried.1.refs_0_), channel_id=1, source_target_pairs={{3,0},{2,1},{1,2},{0,3},{7,4},{6,5},{5,6},{4,7},{11,8},{10,9},{9,1... | collective-permute-start | bytes 294920 | tf_op jit(solution)/shard_map/ppermute | solution.py:423
  14.3 1.1 %collective-permute-start.4 = (f32[128,128]{1,0:T(8,128)S(1)}, f32[128,128]{1,0:T(8,128)S(1)}, u32[]{:S(2)}, u32[]{:S(2)}) collective-permute-start(f32[128,128]{1,0:T(8,128)S(1)} %get-tuple-element.19), channel_id=1, source_target_pairs={{16,0},{20,4},{24,8},{28,12},{0,16},{4,20},{8,24},{12,28},{17,1},{... | collective-permute-start | bytes 196616 | tf_op jit(solution)/shard_map/ppermute | solution.py:423
  15.4 1.1 %span_1_middle.1._.refs_0_ = f32[3,4,128,128]{3,2,1,0:T(8,128)S(1)} custom-call(f32[3,36,144,128]{3,2,1,0:T(8,128)S(1)} %get-tuple-element.17.vel_ref.vel_in, f32[15,8,128]{2,1,0:T(8,128)S(1)} %copy-done, f32[3,32,2,128]{3,2,1,0:T(2,128)S(1)} %carried.1.refs_0_), custom_call_target="tpu_custom_call" | custom-call | flops 3145728 | bytes 3145728 | tf_op jit(solution)/shard_map/span_1_middle/pallas_call | solution.py:495
  16.5 0.7 %collective-permute-done.3.odd_ref = f32[3,32,2,128]{3,2,1,0:T(2,128)S(1)} collective-permute-done((f32[3,32,2,128]{3,2,1,0:T(2,128)S(1)}, f32[3,32,2,128]{3,2,1,0:T(2,128)S(1)}, u32[]{:S(2)}, u32[]{:S(2)}) %collective-permute-start.3) | collective-permute-done | bytes 98336 | tf_op jit(solution)/shard_map/ppermute | solution.py:423
  17.3 0.2 fold.1
  17.5 0.1 collective-permute-start.5
  17.6 0.2 span_1_outer.1.refs_1_.refs_0_
  17.8 0.2 span_0_outer.1.refs_0_
  18.0 2.6 %span_2.1.refs_2_.refs_1_ = f32[3,8,128,128]{3,2,1,0:T(8,128)S(1)} custom-call(f32[3,36,144,128]{3,2,1,0:T(8,128)S(1)} %get-tuple-element.18.vel_ref.vel_in, f32[15,8,128]{2,1,0:T(8,128)S(1)} %copy-done, f32[8,128]{1,0:T(8,128)S(1)} %get-tuple-element.20.refs_0_.mine_ref), custom_call_target="tpu_custom_call" | custom-call | flops 3145728 | bytes 3145728 | tf_op jit(solution)/shard_map/span_2/pallas_call | solution.py:495
  20.5 0.7 %collective-permute-done.5.far_ref = f32[8,128]{1,0:T(8,128)S(1)} collective-permute-done((f32[8,128]{1,0:T(8,128)S(1)}, f32[8,128]{1,0:T(8,128)S(1)}, u32[]{:S(2)}, u32[]{:S(2)}) %collective-permute-start.5) | collective-permute-done | bytes 4128 | tf_op jit(solution)/shard_map/ppermute | solution.py:423
  21.2 1.1 %collective-permute-start.6 = (f32[8,128]{1,0:T(8,128)S(1)}, f32[8,128]{1,0:T(8,128)S(1)}, u32[]{:S(2)}, u32[]{:S(2)}) collective-permute-start(f32[8,128]{1,0:T(8,128)S(1)} %merged.2._.mine_ref), channel_id=1, source_target_pairs={{16,0},{20,4},{24,8},{28,12},{0,16},{4,20},{8,24},{12,28},{17,1},{... | collective-permute-start | bytes 12296 | tf_op jit(solution)/shard_map/ppermute | solution.py:423
  22.3 0.0 collective-permute-done.4.inner_ref
  22.3 3.2 %span_3.1._.refs_2_.refs_3_ = f32[3,8,128,128]{3,2,1,0:T(8,128)S(1)} custom-call(f32[3,36,144,128]{3,2,1,0:T(8,128)S(1)} %get-tuple-element.18.vel_ref.vel_in, f32[128,128]{1,0:T(8,128)S(1)} %collective-permute-done.4.inner_ref, f32[15,8,128]{2,1,0:T(8,128)S(1)} %copy-done, f32[8,128]{1,0:T(8,128)S(1)} %merged.2._.mine_ref), custom_call_target="tpu_custom_call" | custom-call | flops 3145728 | bytes 3145728 | tf_op jit(solution)/shard_map/span_3/pallas_call | solution.py:506
  25.5 0.2 collective-permute-done.6.far_ref
  25.7 2.0 %collective-permute-start.7 = (f32[8,128]{1,0:T(8,128)S(1)}, f32[8,128]{1,0:T(8,128)S(1)}, u32[]{:S(2)}, u32[]{:S(2)}) collective-permute-start(f32[8,128]{1,0:T(8,128)S(1)} %merged.3.top), channel_id=1, source_target_pairs={{4,0},{0,4},{12,8},{8,12},{20,16},{16,20},{28,24},{24,28},{5,1},{1... | collective-permute-start | bytes 12296 | tf_op jit(solution)/shard_map/ppermute | solution.py:423
  27.7 0.0 collective-permute-done.1.odd_ref
  27.7 0.0 collective-permute-done.even_ref
  27.7 0.1 theta_in.1
  27.8 0.2 collective-permute-start.9
  28.0 1.5 %collective-permute-start.8 = (f32[8,128]{1,0:T(8,128)S(1)}, f32[8,128]{1,0:T(8,128)S(1)}, u32[]{:S(2)}, u32[]{:S(2)}) collective-permute-start(f32[8,128]{1,0:T(8,128)S(1)} %get-tuple-element.22._), channel_id=1, source_target_pairs={{1,0},{0,1},{3,2},{2,3},{5,4},{4,5},{7,6},{6,7},{9,8},{8,9},{11,10... | collective-permute-start | bytes 12296 | tf_op jit(solution)/shard_map/ppermute | solution.py:423
  29.5 1.6 %span_4.1.refs_4_ = f32[3,4,128,128]{3,2,1,0:T(8,128)S(1)} custom-call(f32[3,36,144,128]{3,2,1,0:T(8,128)S(1)} %get-tuple-element.21.vel_ref.vel_in, f32[128,128]{1,0:T(8,128)S(1)} %collective-permute-done.4.inner_ref, f32[15,8,128]{2,1,0:T(8,128)S(1)} %copy-done, f32[8,128]{1,0:T(8,128)S(1)} %get-tuple-element.22._), custom_call_target="tpu_custom_call" | custom-call | flops 3145728 | bytes 3145728 | tf_op jit(solution)/shard_map/span_4/pallas_call | solution.py:506
  31.1 0.0 collective-permute-done.7.far
  31.1 0.0 collective-permute-done.9.odd
  31.1 0.0 collective-permute-done.8.even
  31.1 5.5 %finish.1 = (f32[3,32,128,128]{3,2,1,0:T(8,128)}, f32[1]{0:T(128)}, f32[3,36,144,128]{3,2,1,0:T(8,128)S(1)}) custom-call(f32[3,36,144,128]{3,2,1,0:T(8,128)S(1)} %get-tuple-element.21.vel_ref.vel_in, f32[128,128]{1,0:T(8,128)S(1)} %collective-permute-done.4.inner_ref, f32[15,8,128]{2,1,0:T(8,128)S(1)} %copy-done, ...), custom_call_target="tpu_custom_call", output_to_operand_aliasing={{2}: (0, {})} | custom-call | tf_op jit(solution)/shard_map/finish/pallas_call | solution.py:572
  (3 shorter events, 0.0 us)
Async XLA Ops:
  0.6 10.8 %copy-start = (f32[15,8,128]{2,1,0:T(8,128)S(1)}, f32[15,8,128]{2,1,0:T(8,128)}, u32[]{:S(2)}) copy-start(f32[15,8,128]{2,1,0:T(8,128)} %constant.28.clone.coef_ref) | copy-start | bytes 184324
  1.8 25.9 %collective-permute-start.1 = (f32[3,2,128,128]{3,2,1,0:T(8,128)S(1)}, f32[3,2,128,128]{3,2,1,0:T(8,128)S(1)}, u32[]{:S(2)}, u32[]{:S(2)}) collective-permute-start(f32[3,2,128,128]{3,2,1,0:T(8,128)S(1)} %get-tuple-element.26), channel_id=1, source_target_pairs={{28,0},{8,4},{4,8},{16,12},{12,16},{24,20},{20,24},{0,28},{29,1},{... | collective-permute-start | bytes 1179656 | tf_op jit(solution)/shard_map/ppermute | solution.py:423
  7.9 19.8 %collective-permute-start = (f32[3,2,128,128]{3,2,1,0:T(8,128)S(1)}, f32[3,2,128,128]{3,2,1,0:T(8,128)S(1)}, u32[]{:S(2)}, u32[]{:S(2)}) collective-permute-start(f32[3,2,128,128]{3,2,1,0:T(8,128)S(1)} %get-tuple-element.27), channel_id=1, source_target_pairs={{4,0},{0,4},{12,8},{8,12},{20,16},{16,20},{28,24},{24,28},{5,1},{1... | collective-permute-start | bytes 1179656 | tf_op jit(solution)/shard_map/ppermute | solution.py:423
  11.4 1.4 %collective-permute-start.2 = (f32[3,32,2,128]{3,2,1,0:T(2,128)S(1)}, f32[3,32,2,128]{3,2,1,0:T(2,128)S(1)}, u32[]{:S(2)}, u32[]{:S(2)}) collective-permute-start(f32[3,32,2,128]{3,2,1,0:T(2,128)S(1)} %get-tuple-element.14), channel_id=1, source_target_pairs={{1,0},{0,1},{3,2},{2,3},{5,4},{4,5},{7,6},{6,7},{9,8},{8,9},{11,10... | collective-permute-start | bytes 294920 | tf_op jit(solution)/shard_map/ppermute | solution.py:423
  12.8 4.5 %collective-permute-start.3 = (f32[3,32,2,128]{3,2,1,0:T(2,128)S(1)}, f32[3,32,2,128]{3,2,1,0:T(2,128)S(1)}, u32[]{:S(2)}, u32[]{:S(2)}) collective-permute-start(f32[3,32,2,128]{3,2,1,0:T(2,128)S(1)} %carried.1.refs_0_), channel_id=1, source_target_pairs={{3,0},{2,1},{1,2},{0,3},{7,4},{6,5},{5,6},{4,7},{11,8},{10,9},{9,1... | collective-permute-start | bytes 294920 | tf_op jit(solution)/shard_map/ppermute | solution.py:423
  14.3 8.0 %collective-permute-start.4 = (f32[128,128]{1,0:T(8,128)S(1)}, f32[128,128]{1,0:T(8,128)S(1)}, u32[]{:S(2)}, u32[]{:S(2)}) collective-permute-start(f32[128,128]{1,0:T(8,128)S(1)} %get-tuple-element.19), channel_id=1, source_target_pairs={{16,0},{20,4},{24,8},{28,12},{0,16},{4,20},{8,24},{12,28},{17,1},{... | collective-permute-start | bytes 196616 | tf_op jit(solution)/shard_map/ppermute | solution.py:423
  17.5 3.7 %collective-permute-start.5 = (f32[8,128]{1,0:T(8,128)S(1)}, f32[8,128]{1,0:T(8,128)S(1)}, u32[]{:S(2)}, u32[]{:S(2)}) collective-permute-start(f32[8,128]{1,0:T(8,128)S(1)} %get-tuple-element.20.refs_0_.mine_ref), channel_id=1, source_target_pairs={{8,0},{12,4},{0,8},{4,12},{24,16},{28,20},{16,24},{20,28},{9,1},{1... | collective-permute-start | bytes 12296 | tf_op jit(solution)/shard_map/ppermute | solution.py:423
  21.2 4.5 %collective-permute-start.6 = (f32[8,128]{1,0:T(8,128)S(1)}, f32[8,128]{1,0:T(8,128)S(1)}, u32[]{:S(2)}, u32[]{:S(2)}) collective-permute-start(f32[8,128]{1,0:T(8,128)S(1)} %merged.2._.mine_ref), channel_id=1, source_target_pairs={{16,0},{20,4},{24,8},{28,12},{0,16},{4,20},{8,24},{12,28},{17,1},{... | collective-permute-start | bytes 12296 | tf_op jit(solution)/shard_map/ppermute | solution.py:423
  25.7 5.4 %collective-permute-start.7 = (f32[8,128]{1,0:T(8,128)S(1)}, f32[8,128]{1,0:T(8,128)S(1)}, u32[]{:S(2)}, u32[]{:S(2)}) collective-permute-start(f32[8,128]{1,0:T(8,128)S(1)} %merged.3.top), channel_id=1, source_target_pairs={{4,0},{0,4},{12,8},{8,12},{20,16},{16,20},{28,24},{24,28},{5,1},{1... | collective-permute-start | bytes 12296 | tf_op jit(solution)/shard_map/ppermute | solution.py:423
  27.8 3.3 %collective-permute-start.9 = (f32[8,128]{1,0:T(8,128)S(1)}, f32[8,128]{1,0:T(8,128)S(1)}, u32[]{:S(2)}, u32[]{:S(2)}) collective-permute-start(f32[8,128]{1,0:T(8,128)S(1)} %get-tuple-element.23), channel_id=1, source_target_pairs={{3,0},{2,1},{1,2},{0,3},{7,4},{6,5},{5,6},{4,7},{11,8},{10,9},{9,1... | collective-permute-start | bytes 12296 | tf_op jit(solution)/shard_map/ppermute | solution.py:423
  28.0 3.1 %collective-permute-start.8 = (f32[8,128]{1,0:T(8,128)S(1)}, f32[8,128]{1,0:T(8,128)S(1)}, u32[]{:S(2)}, u32[]{:S(2)}) collective-permute-start(f32[8,128]{1,0:T(8,128)S(1)} %get-tuple-element.22._), channel_id=1, source_target_pairs={{1,0},{0,1},{3,2},{2,3},{5,4},{4,5},{7,6},{6,7},{9,8},{8,9},{11,10... | collective-permute-start | bytes 12296 | tf_op jit(solution)/shard_map/ppermute | solution.py:423

commit v19 on v18

--- a/solution.py
+++ b/solution.py
@@ -309,7 +309,7 @@
 def block_terms(vel_ref, inner_ref, coef_ref, j, size, write, rounds=None):
     planes = vel_ref.shape[1] - 2 * HALO
     axial, radial = vel_ref.shape[2] - 2 * PAD, vel_ref.shape[3]
-    groups = 4 * BLOCK // size
+    groups = (4 if inner_ref is None else 2) * BLOCK // size
     times, places = rounds or (
         axial // (8 * groups),
         lambda i: [(i * groups + u) * 8 for u in range(groups)],
@@ -468,8 +468,8 @@
     ends = (planes - HALO, 0)
     even_end = jnp.where(odd == 1, ends[1], ends[0])
     odd_end = jnp.where(odd == 1, ends[0], ends[1])
+    theta_odd = across_odd(lax.dynamic_slice_in_dim(velocity, odd_end, HALO, 1), "az")
     theta_even = across_even(lax.dynamic_slice_in_dim(velocity, even_end, HALO, 1), "az")
-    theta_odd = across_odd(lax.dynamic_slice_in_dim(velocity, odd_end, HALO, 1), "az")
 
     edge = shape(3, planes, 2, radial)
     padded = shape(3, planes + 2 * HALO, axial + 2 * PAD, radial)

time: 36.7 us -> 36.5 us (level)
  transfers between devices with their start and end apart: 10 -> 10, of which waited for: 4 -> 4; matrix products, arithmetic and copies ran while one was open for 0% -> 0% of each run, Pallas kernels for 38% -> 37%
where the time goes in v19:
time: 36.5 us; the launch traced here: 36.4 us
  Pallas kernels  18.9 us (52%)
  starting transfers between devices  13.7 us (38%)
  waiting for transfers between devices  1.8 us (5%)
  local copies, waits for them, and re-layouts  1.18 us (3%)
  between operations  0.77 us (2%)
    ppermute x10, starting transfers between devices, routed(): return lax.ppermute(block, axis, [(source(i), i) for i in range(count)])  13.7 us
    pallas_call x1, Pallas kernels, per_device(): call(functools.partial(finish, spans), 'finish', 0, scratch=8, out_shape=...  5.28 us
    pallas_call x5, Pallas kernels, without_ghosts(): call(functools.partial(ahead, *spans[n], rounds), name, velocity.size * 2...  5.19 us
    pallas_call x2, Pallas kernels, with_ghosts(): call(functools.partial(ahead_with_ghosts, *spans[n]), f'span_{n}', veloci...  4.65 us
    pallas_call x1, Pallas kernels, per_device(): call(functools.partial(first_pass, theta_step), 'first_pass', 0, out_shap...  3.47 us
    ppermute x10, waiting for transfers between devices, routed(): return lax.ppermute(block, axis, [(source(i), i) for i in range(count)])  1.8 us
    dynamic_slice x1, local copies, waits for them, and re-layouts, per_device(): lax.dynamic_slice_in_dim(velocity, odd_end, HALO, 1)  1.18 us
  transfers between devices with their start and end apart: 10, of which 4 were waited for; matrix products, arithmetic and copies ran while one was open for 0% of the time, Pallas kernels for 37%

profile of v19, /device:TPU:0, one launch (start us, length us, event | category | flops | bytes accessed | tf_op | source)
XLA Modules:
  0.0 36.4 jit_solution(12243093356703648014)
XLA Ops:
  0.6 0.0 copy-start
  0.7 1.2 %constant_dynamic-slice_fusion = (f32[3,2,128,128]{3,2,1,0:T(8,128)S(1)}, f32[3,2,128,128]{3,2,1,0:T(8,128)S(1)}) fusion(f32[3,32,128,128]{3,2,1,0:T(8,128)} %v_ref.1, s32[]{:T(128)S(6)} %select_n.18, s32[]{:T(128)S(6)} %select_n.17), kind=kLoop, calls=%fused_computation | loop fusion | bytes 1572872 | tf_op jit(solution)/shard_map/dynamic_slice | solution.py:471
  1.8 6.1 %collective-permute-start.1 = (f32[3,2,128,128]{3,2,1,0:T(8,128)S(1)}, f32[3,2,128,128]{3,2,1,0:T(8,128)S(1)}, u32[]{:S(2)}, u32[]{:S(2)}) collective-permute-start(f32[3,2,128,128]{3,2,1,0:T(8,128)S(1)} %get-tuple-element.26), channel_id=1, source_target_pairs={{28,0},{8,4},{4,8},{16,12},{12,16},{24,20},{20,24},{0,28},{29,1},{... | collective-permute-start | bytes 1179656 | tf_op jit(solution)/shard_map/ppermute | solution.py:423
  7.9 0.0 collective-permute-start
  7.9 3.5 %first_pass.1 = (f32[3,36,144,128]{3,2,1,0:T(8,128)S(1)}, f32[3,32,2,128]{3,2,1,0:T(2,128)S(1)}, f32[3,32,2,128]{3,2,1,0:T(2,128)S(1)}, f32[128,128]{1,0:T(8,128)S(1)}, f32[8,128]{1,0:T(8,128)S(1)}) custom-call(f32[3,32,128,128]{3,2,1,0:T(8,128)} %v_ref.1), custom_call_target="tpu_custom_call" | custom-call | tf_op jit(solution)/shard_map/first_pass/pallas_call | solution.py:478
  11.4 0.1 collective-permute-start.2
  11.5 0.0 copy-done
  11.5 1.2 %span_0_middle.1._.refs_0_ = f32[3,4,128,128]{3,2,1,0:T(8,128)S(1)} custom-call(f32[3,36,144,128]{3,2,1,0:T(8,128)S(1)} %get-tuple-element.17.vel_ref.vel_in, f32[15,8,128]{2,1,0:T(8,128)S(1)} %copy-done, f32[8,128]{1,0:T(8,128)S(1)} %get-tuple-element.15.refs_0_.pay_ref), custom_call_target="tpu_custom_call" | custom-call | flops 3145728 | bytes 3145728 | tf_op jit(solution)/shard_map/span_0_middle/pallas_call | solution.py:495
  12.6 0.1 collective-permute-done.2.even_ref
  12.8 1.5 %collective-permute-start.3 = (f32[3,32,2,128]{3,2,1,0:T(2,128)S(1)}, f32[3,32,2,128]{3,2,1,0:T(2,128)S(1)}, u32[]{:S(2)}, u32[]{:S(2)}) collective-permute-start(f32[3,32,2,128]{3,2,1,0:T(2,128)S(1)} %carried.1.refs_0_), channel_id=1, source_target_pairs={{3,0},{2,1},{1,2},{0,3},{7,4},{6,5},{5,6},{4,7},{11,8},{10,9},{9,1... | collective-permute-start | bytes 294920 | tf_op jit(solution)/shard_map/ppermute | solution.py:423
  14.3 1.1 %collective-permute-start.4 = (f32[128,128]{1,0:T(8,128)S(1)}, f32[128,128]{1,0:T(8,128)S(1)}, u32[]{:S(2)}, u32[]{:S(2)}) collective-permute-start(f32[128,128]{1,0:T(8,128)S(1)} %get-tuple-element.19), channel_id=1, source_target_pairs={{16,0},{20,4},{24,8},{28,12},{0,16},{4,20},{8,24},{12,28},{17,1},{... | collective-permute-start | bytes 196616 | tf_op jit(solution)/shard_map/ppermute | solution.py:423
  15.4 1.1 %span_1_middle.1._.refs_0_ = f32[3,4,128,128]{3,2,1,0:T(8,128)S(1)} custom-call(f32[3,36,144,128]{3,2,1,0:T(8,128)S(1)} %get-tuple-element.17.vel_ref.vel_in, f32[15,8,128]{2,1,0:T(8,128)S(1)} %copy-done, f32[3,32,2,128]{3,2,1,0:T(2,128)S(1)} %carried.1.refs_0_), custom_call_target="tpu_custom_call" | custom-call | flops 3145728 | bytes 3145728 | tf_op jit(solution)/shard_map/span_1_middle/pallas_call | solution.py:495
  16.5 0.7 %collective-permute-done.3.odd_ref = f32[3,32,2,128]{3,2,1,0:T(2,128)S(1)} collective-permute-done((f32[3,32,2,128]{3,2,1,0:T(2,128)S(1)}, f32[3,32,2,128]{3,2,1,0:T(2,128)S(1)}, u32[]{:S(2)}, u32[]{:S(2)}) %collective-permute-start.3) | collective-permute-done | bytes 98336 | tf_op jit(solution)/shard_map/ppermute | solution.py:423
  17.3 0.2 fold.1
  17.5 0.1 collective-permute-start.5
  17.6 0.2 span_1_outer.1.refs_1_.refs_0_
  17.8 0.2 span_0_outer.1.refs_0_
  18.0 2.6 %span_2.1.refs_2_.refs_1_ = f32[3,8,128,128]{3,2,1,0:T(8,128)S(1)} custom-call(f32[3,36,144,128]{3,2,1,0:T(8,128)S(1)} %get-tuple-element.18.vel_ref.vel_in, f32[15,8,128]{2,1,0:T(8,128)S(1)} %copy-done, f32[8,128]{1,0:T(8,128)S(1)} %get-tuple-element.20.refs_0_.mine_ref), custom_call_target="tpu_custom_call" | custom-call | flops 3145728 | bytes 3145728 | tf_op jit(solution)/shard_map/span_2/pallas_call | solution.py:495
  20.5 0.7 %collective-permute-done.5.far_ref = f32[8,128]{1,0:T(8,128)S(1)} collective-permute-done((f32[8,128]{1,0:T(8,128)S(1)}, f32[8,128]{1,0:T(8,128)S(1)}, u32[]{:S(2)}, u32[]{:S(2)}) %collective-permute-start.5) | collective-permute-done | bytes 4128 | tf_op jit(solution)/shard_map/ppermute | solution.py:423
  21.2 1.1 %collective-permute-start.6 = (f32[8,128]{1,0:T(8,128)S(1)}, f32[8,128]{1,0:T(8,128)S(1)}, u32[]{:S(2)}, u32[]{:S(2)}) collective-permute-start(f32[8,128]{1,0:T(8,128)S(1)} %merged.2._.mine_ref), channel_id=1, source_target_pairs={{16,0},{20,4},{24,8},{28,12},{0,16},{4,20},{8,24},{12,28},{17,1},{... | collective-permute-start | bytes 12296 | tf_op jit(solution)/shard_map/ppermute | solution.py:423
  22.3 0.0 collective-permute-done.4.inner_ref
  22.3 3.1 %span_3.1._.refs_2_.refs_3_ = f32[3,8,128,128]{3,2,1,0:T(8,128)S(1)} custom-call(f32[3,36,144,128]{3,2,1,0:T(8,128)S(1)} %get-tuple-element.18.vel_ref.vel_in, f32[128,128]{1,0:T(8,128)S(1)} %collective-permute-done.4.inner_ref, f32[15,8,128]{2,1,0:T(8,128)S(1)} %copy-done, f32[8,128]{1,0:T(8,128)S(1)} %merged.2._.mine_ref), custom_call_target="tpu_custom_call" | custom-call | flops 3145728 | bytes 3145728 | tf_op jit(solution)/shard_map/span_3/pallas_call | solution.py:506
  25.4 0.3 collective-permute-done.6.far_ref
  25.7 2.0 %collective-permute-start.7 = (f32[8,128]{1,0:T(8,128)S(1)}, f32[8,128]{1,0:T(8,128)S(1)}, u32[]{:S(2)}, u32[]{:S(2)}) collective-permute-start(f32[8,128]{1,0:T(8,128)S(1)} %merged.3.top), channel_id=1, source_target_pairs={{4,0},{0,4},{12,8},{8,12},{20,16},{16,20},{28,24},{24,28},{5,1},{1... | collective-permute-start | bytes 12296 | tf_op jit(solution)/shard_map/ppermute | solution.py:423
  27.7 0.0 collective-permute-done.1.odd_ref
  27.7 0.0 collective-permute-done.even_ref
  27.7 0.1 theta_in.1
  27.8 0.1 collective-permute-start.9
  27.9 1.6 %collective-permute-start.8 = (f32[8,128]{1,0:T(8,128)S(1)}, f32[8,128]{1,0:T(8,128)S(1)}, u32[]{:S(2)}, u32[]{:S(2)}) collective-permute-start(f32[8,128]{1,0:T(8,128)S(1)} %get-tuple-element.22._), channel_id=1, source_target_pairs={{1,0},{0,1},{3,2},{2,3},{5,4},{4,5},{7,6},{6,7},{9,8},{8,9},{11,10... | collective-permute-start | bytes 12296 | tf_op jit(solution)/shard_map/ppermute | solution.py:423
  29.5 1.6 %span_4.1.refs_4_ = f32[3,4,128,128]{3,2,1,0:T(8,128)S(1)} custom-call(f32[3,36,144,128]{3,2,1,0:T(8,128)S(1)} %get-tuple-element.21.vel_ref.vel_in, f32[128,128]{1,0:T(8,128)S(1)} %collective-permute-done.4.inner_ref, f32[15,8,128]{2,1,0:T(8,128)S(1)} %copy-done, f32[8,128]{1,0:T(8,128)S(1)} %get-tuple-element.22._), custom_call_target="tpu_custom_call" | custom-call | flops 3145728 | bytes 3145728 | tf_op jit(solution)/shard_map/span_4/pallas_call | solution.py:506
  31.1 0.0 collective-permute-done.7.far
  31.1 0.0 collective-permute-done.9.odd
  31.1 0.0 collective-permute-done.8.even
  31.1 5.3 %finish.1 = (f32[3,32,128,128]{3,2,1,0:T(8,128)}, f32[1]{0:T(128)}, f32[3,36,144,128]{3,2,1,0:T(8,128)S(1)}) custom-call(f32[3,36,144,128]{3,2,1,0:T(8,128)S(1)} %get-tuple-element.21.vel_ref.vel_in, f32[128,128]{1,0:T(8,128)S(1)} %collective-permute-done.4.inner_ref, f32[15,8,128]{2,1,0:T(8,128)S(1)} %copy-done, ...), custom_call_target="tpu_custom_call", output_to_operand_aliasing={{2}: (0, {})} | custom-call | tf_op jit(solution)/shard_map/finish/pallas_call | solution.py:572
  (3 shorter events, 0.0 us)
Async XLA Ops:
  0.6 10.8 %copy-start = (f32[15,8,128]{2,1,0:T(8,128)S(1)}, f32[15,8,128]{2,1,0:T(8,128)}, u32[]{:S(2)}) copy-start(f32[15,8,128]{2,1,0:T(8,128)} %constant.28.clone.coef_ref) | copy-start | bytes 184324
  1.8 25.9 %collective-permute-start.1 = (f32[3,2,128,128]{3,2,1,0:T(8,128)S(1)}, f32[3,2,128,128]{3,2,1,0:T(8,128)S(1)}, u32[]{:S(2)}, u32[]{:S(2)}) collective-permute-start(f32[3,2,128,128]{3,2,1,0:T(8,128)S(1)} %get-tuple-element.26), channel_id=1, source_target_pairs={{28,0},{8,4},{4,8},{16,12},{12,16},{24,20},{20,24},{0,28},{29,1},{... | collective-permute-start | bytes 1179656 | tf_op jit(solution)/shard_map/ppermute | solution.py:423
  7.9 19.8 %collective-permute-start = (f32[3,2,128,128]{3,2,1,0:T(8,128)S(1)}, f32[3,2,128,128]{3,2,1,0:T(8,128)S(1)}, u32[]{:S(2)}, u32[]{:S(2)}) collective-permute-start(f32[3,2,128,128]{3,2,1,0:T(8,128)S(1)} %get-tuple-element.27), channel_id=1, source_target_pairs={{4,0},{0,4},{12,8},{8,12},{20,16},{16,20},{28,24},{24,28},{5,1},{1... | collective-permute-start | bytes 1179656 | tf_op jit(solution)/shard_map/ppermute | solution.py:423
  11.4 1.4 %collective-permute-start.2 = (f32[3,32,2,128]{3,2,1,0:T(2,128)S(1)}, f32[3,32,2,128]{3,2,1,0:T(2,128)S(1)}, u32[]{:S(2)}, u32[]{:S(2)}) collective-permute-start(f32[3,32,2,128]{3,2,1,0:T(2,128)S(1)} %get-tuple-element.14), channel_id=1, source_target_pairs={{1,0},{0,1},{3,2},{2,3},{5,4},{4,5},{7,6},{6,7},{9,8},{8,9},{11,10... | collective-permute-start | bytes 294920 | tf_op jit(solution)/shard_map/ppermute | solution.py:423
  12.8 4.5 %collective-permute-start.3 = (f32[3,32,2,128]{3,2,1,0:T(2,128)S(1)}, f32[3,32,2,128]{3,2,1,0:T(2,128)S(1)}, u32[]{:S(2)}, u32[]{:S(2)}) collective-permute-start(f32[3,32,2,128]{3,2,1,0:T(2,128)S(1)} %carried.1.refs_0_), channel_id=1, source_target_pairs={{3,0},{2,1},{1,2},{0,3},{7,4},{6,5},{5,6},{4,7},{11,8},{10,9},{9,1... | collective-permute-start | bytes 294920 | tf_op jit(solution)/shard_map/ppermute | solution.py:423
  14.3 8.0 %collective-permute-start.4 = (f32[128,128]{1,0:T(8,128)S(1)}, f32[128,128]{1,0:T(8,128)S(1)}, u32[]{:S(2)}, u32[]{:S(2)}) collective-permute-start(f32[128,128]{1,0:T(8,128)S(1)} %get-tuple-element.19), channel_id=1, source_target_pairs={{16,0},{20,4},{24,8},{28,12},{0,16},{4,20},{8,24},{12,28},{17,1},{... | collective-permute-start | bytes 196616 | tf_op jit(solution)/shard_map/ppermute | solution.py:423
  17.5 3.7 %collective-permute-start.5 = (f32[8,128]{1,0:T(8,128)S(1)}, f32[8,128]{1,0:T(8,128)S(1)}, u32[]{:S(2)}, u32[]{:S(2)}) collective-permute-start(f32[8,128]{1,0:T(8,128)S(1)} %get-tuple-element.20.refs_0_.mine_ref), channel_id=1, source_target_pairs={{8,0},{12,4},{0,8},{4,12},{24,16},{28,20},{16,24},{20,28},{9,1},{1... | collective-permute-start | bytes 12296 | tf_op jit(solution)/shard_map/ppermute | solution.py:423
  21.2 4.5 %collective-permute-start.6 = (f32[8,128]{1,0:T(8,128)S(1)}, f32[8,128]{1,0:T(8,128)S(1)}, u32[]{:S(2)}, u32[]{:S(2)}) collective-permute-start(f32[8,128]{1,0:T(8,128)S(1)} %merged.2._.mine_ref), channel_id=1, source_target_pairs={{16,0},{20,4},{24,8},{28,12},{0,16},{4,20},{8,24},{12,28},{17,1},{... | collective-permute-start | bytes 12296 | tf_op jit(solution)/shard_map/ppermute | solution.py:423
  25.7 5.4 %collective-permute-start.7 = (f32[8,128]{1,0:T(8,128)S(1)}, f32[8,128]{1,0:T(8,128)S(1)}, u32[]{:S(2)}, u32[]{:S(2)}) collective-permute-start(f32[8,128]{1,0:T(8,128)S(1)} %merged.3.top), channel_id=1, source_target_pairs={{4,0},{0,4},{12,8},{8,12},{20,16},{16,20},{28,24},{24,28},{5,1},{1... | collective-permute-start | bytes 12296 | tf_op jit(solution)/shard_map/ppermute | solution.py:423
  27.8 3.3 %collective-permute-start.9 = (f32[8,128]{1,0:T(8,128)S(1)}, f32[8,128]{1,0:T(8,128)S(1)}, u32[]{:S(2)}, u32[]{:S(2)}) collective-permute-start(f32[8,128]{1,0:T(8,128)S(1)} %get-tuple-element.23), channel_id=1, source_target_pairs={{3,0},{2,1},{1,2},{0,3},{7,4},{6,5},{5,6},{4,7},{11,8},{10,9},{9,1... | collective-permute-start | bytes 12296 | tf_op jit(solution)/shard_map/ppermute | solution.py:423
  27.9 3.2 %collective-permute-start.8 = (f32[8,128]{1,0:T(8,128)S(1)}, f32[8,128]{1,0:T(8,128)S(1)}, u32[]{:S(2)}, u32[]{:S(2)}) collective-permute-start(f32[8,128]{1,0:T(8,128)S(1)} %get-tuple-element.22._), channel_id=1, source_target_pairs={{1,0},{0,1},{3,2},{2,3},{5,4},{4,5},{7,6},{6,7},{9,8},{8,9},{11,10... | collective-permute-start | bytes 12296 | tf_op jit(solution)/shard_map/ppermute | solution.py:423

commit v20 on v19

--- a/solution.py
+++ b/solution.py
@@ -273,7 +273,7 @@
     refs[-1][...] = jnp.maximum(mine_ref[...], far_ref[...])
 
 
-def theta_in(even_ref, odd_ref, vel_in, _, even_tile, odd_tile, vel_ref):
+def theta_in(odd_ref, even_ref, vel_in, _, even_tile, odd_tile, vel_ref):
     del vel_in
     planes, axial = vel_ref.shape[1] - 2 * HALO, vel_ref.shape[2] - 2 * PAD
     cells = pl.ds(PAD, axial)
@@ -566,7 +566,7 @@
         in_specs=[vmem] * 4,
         out_specs=(vmem,) * 3,
         input_output_aliases={2: 2},
-    )(theta_even, theta_odd, vel, parts[-1])
+    )(theta_odd, theta_even, vel, parts[-1])
     corner_even, corner_odd = across_even(tile_even, "ax"), across_odd(tile_odd, "ax")
     parts.append(with_ghosts(4, tile_even))
     increment, time_step, _ = call(

time: 36.5 us -> 35.8 us (0.981)
  starting transfers between devices: 13.7 us -> 11.8 us
  waiting for transfers between devices: 1.8 us -> 2.9 us
    ppermute x10, starting transfers between devices: 13.7 us -> 11.8 us  [routed(): return lax.ppermute(block, axis, [(source(i), i) for i in range(count)])]
    ppermute x10, waiting for transfers between devices: 1.8 us -> 2.9 us  [routed(): return lax.ppermute(block, axis, [(source(i), i) for i in range(count)])]
  transfers between devices with their start and end apart: 10 -> 10, of which waited for: 4 -> 4; matrix products, arithmetic and copies ran while one was open for 0% -> 0% of each run, Pallas kernels for 37% -> 38%
where the time goes in v20:
time: 35.8 us; the launch traced here: 35.6 us
  Pallas kernels  18.9 us (53%)
  starting transfers between devices  11.8 us (33%)
  waiting for transfers between devices  2.9 us (8%)
  local copies, waits for them, and re-layouts  1.18 us (3%)
  between operations  0.78 us (2%)
    ppermute x10, starting transfers between devices, routed(): return lax.ppermute(block, axis, [(source(i), i) for i in range(count)])  11.8 us
    pallas_call x1, Pallas kernels, per_device(): call(functools.partial(finish, spans), 'finish', 0, scratch=8, out_shape=...  5.28 us
    pallas_call x5, Pallas kernels, without_ghosts(): call(functools.partial(ahead, *spans[n], rounds), name, velocity.size * 2...  5.19 us
    pallas_call x2, Pallas kernels, with_ghosts(): call(functools.partial(ahead_with_ghosts, *spans[n]), f'span_{n}', veloci...  4.65 us
    pallas_call x1, Pallas kernels, per_device(): call(functools.partial(first_pass, theta_step), 'first_pass', 0, out_shap...  3.47 us
    ppermute x10, waiting for transfers between devices, routed(): return lax.ppermute(block, axis, [(source(i), i) for i in range(count)])  2.9 us
    dynamic_slice x1, local copies, waits for them, and re-layouts, per_device(): lax.dynamic_slice_in_dim(velocity, even_end, HALO, 1)  1.18 us
  transfers between devices with their start and end apart: 10, of which 4 were waited for; matrix products, arithmetic and copies ran while one was open for 0% of the time, Pallas kernels for 38%

profile of v20, /device:TPU:0, one launch (start us, length us, event | category | flops | bytes accessed | tf_op | source)
XLA Modules:
  0.0 35.6 jit_solution(14885889802509430643)
XLA Ops:
  0.6 0.0 copy-start
  0.7 1.2 %constant_dynamic-slice_fusion = (f32[3,2,128,128]{3,2,1,0:T(8,128)S(1)}, f32[3,2,128,128]{3,2,1,0:T(8,128)S(1)}) fusion(f32[3,32,128,128]{3,2,1,0:T(8,128)} %v_ref.1, s32[]{:T(128)S(6)} %select_n.18, s32[]{:T(128)S(6)} %select_n.17), kind=kLoop, calls=%fused_computation | loop fusion | bytes 1572872 | tf_op jit(solution)/shard_map/dynamic_slice | solution.py:472
  1.8 3.0 %collective-permute-start.1 = (f32[3,2,128,128]{3,2,1,0:T(8,128)S(1)}, f32[3,2,128,128]{3,2,1,0:T(8,128)S(1)}, u32[]{:S(2)}, u32[]{:S(2)}) collective-permute-start(f32[3,2,128,128]{3,2,1,0:T(8,128)S(1)} %get-tuple-element.26), channel_id=1, source_target_pairs={{4,0},{0,4},{12,8},{8,12},{20,16},{16,20},{28,24},{24,28},{5,1},{1... | collective-permute-start | bytes 1179656 | tf_op jit(solution)/shard_map/ppermute | solution.py:423
  4.9 3.5 %collective-permute-start = (f32[3,2,128,128]{3,2,1,0:T(8,128)S(1)}, f32[3,2,128,128]{3,2,1,0:T(8,128)S(1)}, u32[]{:S(2)}, u32[]{:S(2)}) collective-permute-start(f32[3,2,128,128]{3,2,1,0:T(8,128)S(1)} %get-tuple-element.27), channel_id=1, source_target_pairs={{28,0},{8,4},{4,8},{16,12},{12,16},{24,20},{20,24},{0,28},{29,1},{... | collective-permute-start | bytes 1179656 | tf_op jit(solution)/shard_map/ppermute | solution.py:423
  8.4 3.5 %first_pass.1 = (f32[3,36,144,128]{3,2,1,0:T(8,128)S(1)}, f32[3,32,2,128]{3,2,1,0:T(2,128)S(1)}, f32[3,32,2,128]{3,2,1,0:T(2,128)S(1)}, f32[128,128]{1,0:T(8,128)S(1)}, f32[8,128]{1,0:T(8,128)S(1)}) custom-call(f32[3,32,128,128]{3,2,1,0:T(8,128)} %v_ref.1), custom_call_target="tpu_custom_call" | custom-call | tf_op jit(solution)/shard_map/first_pass/pallas_call | solution.py:478
  11.9 0.1 collective-permute-start.2
  12.0 0.0 copy-done
  12.0 1.2 %span_0_middle.1._.refs_0_ = f32[3,4,128,128]{3,2,1,0:T(8,128)S(1)} custom-call(f32[3,36,144,128]{3,2,1,0:T(8,128)S(1)} %get-tuple-element.17.vel_ref.vel_in, f32[15,8,128]{2,1,0:T(8,128)S(1)} %copy-done, f32[8,128]{1,0:T(8,128)S(1)} %get-tuple-element.15.refs_0_.pay_ref), custom_call_target="tpu_custom_call" | custom-call | flops 3145728 | bytes 3145728 | tf_op jit(solution)/shard_map/span_0_middle/pallas_call | solution.py:495
  13.1 0.1 collective-permute-done.2.even_ref
  13.3 1.5 %collective-permute-start.3 = (f32[3,32,2,128]{3,2,1,0:T(2,128)S(1)}, f32[3,32,2,128]{3,2,1,0:T(2,128)S(1)}, u32[]{:S(2)}, u32[]{:S(2)}) collective-permute-start(f32[3,32,2,128]{3,2,1,0:T(2,128)S(1)} %carried.1.refs_0_), channel_id=1, source_target_pairs={{3,0},{2,1},{1,2},{0,3},{7,4},{6,5},{5,6},{4,7},{11,8},{10,9},{9,1... | collective-permute-start | bytes 294920 | tf_op jit(solution)/shard_map/ppermute | solution.py:423
  14.8 0.0 collective-permute-start.4
  14.8 1.1 %span_1_middle.1._.refs_0_ = f32[3,4,128,128]{3,2,1,0:T(8,128)S(1)} custom-call(f32[3,36,144,128]{3,2,1,0:T(8,128)S(1)} %get-tuple-element.17.vel_ref.vel_in, f32[15,8,128]{2,1,0:T(8,128)S(1)} %copy-done, f32[3,32,2,128]{3,2,1,0:T(2,128)S(1)} %carried.1.refs_0_), custom_call_target="tpu_custom_call" | custom-call | flops 3145728 | bytes 3145728 | tf_op jit(solution)/shard_map/span_1_middle/pallas_call | solution.py:495
  16.0 1.8 %collective-permute-done.3.odd_ref = f32[3,32,2,128]{3,2,1,0:T(2,128)S(1)} collective-permute-done((f32[3,32,2,128]{3,2,1,0:T(2,128)S(1)}, f32[3,32,2,128]{3,2,1,0:T(2,128)S(1)}, u32[]{:S(2)}, u32[]{:S(2)}) %collective-permute-start.3) | collective-permute-done | bytes 98336 | tf_op jit(solution)/shard_map/ppermute | solution.py:423
  17.8 0.2 fold.1
  18.0 0.1 collective-permute-start.5
  18.1 0.2 span_1_outer.1.refs_1_.refs_0_
  18.3 0.2 span_0_outer.1.refs_0_
  18.4 2.6 %span_2.1.refs_2_.refs_1_ = f32[3,8,128,128]{3,2,1,0:T(8,128)S(1)} custom-call(f32[3,36,144,128]{3,2,1,0:T(8,128)S(1)} %get-tuple-element.18.vel_ref.vel_in, f32[15,8,128]{2,1,0:T(8,128)S(1)} %copy-done, f32[8,128]{1,0:T(8,128)S(1)} %get-tuple-element.20.refs_0_.mine_ref), custom_call_target="tpu_custom_call" | custom-call | flops 3145728 | bytes 3145728 | tf_op jit(solution)/shard_map/span_2/pallas_call | solution.py:495
  21.0 0.7 %collective-permute-done.5.far_ref = f32[8,128]{1,0:T(8,128)S(1)} collective-permute-done((f32[8,128]{1,0:T(8,128)S(1)}, f32[8,128]{1,0:T(8,128)S(1)}, u32[]{:S(2)}, u32[]{:S(2)}) %collective-permute-start.5) | collective-permute-done | bytes 4128 | tf_op jit(solution)/shard_map/ppermute | solution.py:423
  21.7 1.1 %collective-permute-start.6 = (f32[8,128]{1,0:T(8,128)S(1)}, f32[8,128]{1,0:T(8,128)S(1)}, u32[]{:S(2)}, u32[]{:S(2)}) collective-permute-start(f32[8,128]{1,0:T(8,128)S(1)} %merged.2._.mine_ref), channel_id=1, source_target_pairs={{16,0},{20,4},{24,8},{28,12},{0,16},{4,20},{8,24},{12,28},{17,1},{... | collective-permute-start | bytes 12296 | tf_op jit(solution)/shard_map/ppermute | solution.py:423
  22.8 0.0 collective-permute-done.4.inner_ref
  22.8 3.1 %span_3.1._.refs_2_.refs_3_ = f32[3,8,128,128]{3,2,1,0:T(8,128)S(1)} custom-call(f32[3,36,144,128]{3,2,1,0:T(8,128)S(1)} %get-tuple-element.18.vel_ref.vel_in, f32[128,128]{1,0:T(8,128)S(1)} %collective-permute-done.4.inner_ref, f32[15,8,128]{2,1,0:T(8,128)S(1)} %copy-done, f32[8,128]{1,0:T(8,128)S(1)} %merged.2._.mine_ref), custom_call_target="tpu_custom_call" | custom-call | flops 3145728 | bytes 3145728 | tf_op jit(solution)/shard_map/span_3/pallas_call | solution.py:506
  25.9 0.3 collective-permute-done.6.far_ref
  26.2 0.8 %collective-permute-start.7 = (f32[8,128]{1,0:T(8,128)S(1)}, f32[8,128]{1,0:T(8,128)S(1)}, u32[]{:S(2)}, u32[]{:S(2)}) collective-permute-start(f32[8,128]{1,0:T(8,128)S(1)} %merged.3.top), channel_id=1, source_target_pairs={{4,0},{0,4},{12,8},{8,12},{20,16},{16,20},{28,24},{24,28},{5,1},{1... | collective-permute-start | bytes 12296 | tf_op jit(solution)/shard_map/ppermute | solution.py:423
  27.0 0.0 collective-permute-done.1.even_ref
  27.0 0.0 collective-permute-done.odd_ref
  27.0 0.1 theta_in.1
  27.1 0.7 %collective-permute-start.9 = (f32[8,128]{1,0:T(8,128)S(1)}, f32[8,128]{1,0:T(8,128)S(1)}, u32[]{:S(2)}, u32[]{:S(2)}) collective-permute-start(f32[8,128]{1,0:T(8,128)S(1)} %get-tuple-element.23), channel_id=1, source_target_pairs={{3,0},{2,1},{1,2},{0,3},{7,4},{6,5},{5,6},{4,7},{11,8},{10,9},{9,1... | collective-permute-start | bytes 12296 | tf_op jit(solution)/shard_map/ppermute | solution.py:423
  27.7 1.0 %collective-permute-start.8 = (f32[8,128]{1,0:T(8,128)S(1)}, f32[8,128]{1,0:T(8,128)S(1)}, u32[]{:S(2)}, u32[]{:S(2)}) collective-permute-start(f32[8,128]{1,0:T(8,128)S(1)} %get-tuple-element.22._), channel_id=1, source_target_pairs={{1,0},{0,1},{3,2},{2,3},{5,4},{4,5},{7,6},{6,7},{9,8},{8,9},{11,10... | collective-permute-start | bytes 12296 | tf_op jit(solution)/shard_map/ppermute | solution.py:423
  28.7 1.6 %span_4.1.refs_4_ = f32[3,4,128,128]{3,2,1,0:T(8,128)S(1)} custom-call(f32[3,36,144,128]{3,2,1,0:T(8,128)S(1)} %get-tuple-element.21.vel_ref.vel_in, f32[128,128]{1,0:T(8,128)S(1)} %collective-permute-done.4.inner_ref, f32[15,8,128]{2,1,0:T(8,128)S(1)} %copy-done, f32[8,128]{1,0:T(8,128)S(1)} %get-tuple-element.22._), custom_call_target="tpu_custom_call" | custom-call | flops 3145728 | bytes 3145728 | tf_op jit(solution)/shard_map/span_4/pallas_call | solution.py:506
  30.3 0.0 collective-permute-done.7.far
  30.3 0.0 collective-permute-done.9.odd
  30.3 0.0 collective-permute-done.8.even
  30.3 5.3 %finish.1 = (f32[3,32,128,128]{3,2,1,0:T(8,128)}, f32[1]{0:T(128)}, f32[3,36,144,128]{3,2,1,0:T(8,128)S(1)}) custom-call(f32[3,36,144,128]{3,2,1,0:T(8,128)S(1)} %get-tuple-element.21.vel_ref.vel_in, f32[128,128]{1,0:T(8,128)S(1)} %collective-permute-done.4.inner_ref, f32[15,8,128]{2,1,0:T(8,128)S(1)} %copy-done, ...), custom_call_target="tpu_custom_call", output_to_operand_aliasing={{2}: (0, {})} | custom-call | tf_op jit(solution)/shard_map/finish/pallas_call | solution.py:572
  (3 shorter events, 0.0 us)
Async XLA Ops:
  0.6 11.3 %copy-start = (f32[15,8,128]{2,1,0:T(8,128)S(1)}, f32[15,8,128]{2,1,0:T(8,128)}, u32[]{:S(2)}) copy-start(f32[15,8,128]{2,1,0:T(8,128)} %constant.28.clone.coef_ref) | copy-start | bytes 184324
  1.8 25.1 %collective-permute-start.1 = (f32[3,2,128,128]{3,2,1,0:T(8,128)S(1)}, f32[3,2,128,128]{3,2,1,0:T(8,128)S(1)}, u32[]{:S(2)}, u32[]{:S(2)}) collective-permute-start(f32[3,2,128,128]{3,2,1,0:T(8,128)S(1)} %get-tuple-element.26), channel_id=1, source_target_pairs={{4,0},{0,4},{12,8},{8,12},{20,16},{16,20},{28,24},{24,28},{5,1},{1... | collective-permute-start | bytes 1179656 | tf_op jit(solution)/shard_map/ppermute | solution.py:423
  4.9 22.1 %collective-permute-start = (f32[3,2,128,128]{3,2,1,0:T(8,128)S(1)}, f32[3,2,128,128]{3,2,1,0:T(8,128)S(1)}, u32[]{:S(2)}, u32[]{:S(2)}) collective-permute-start(f32[3,2,128,128]{3,2,1,0:T(8,128)S(1)} %get-tuple-element.27), channel_id=1, source_target_pairs={{28,0},{8,4},{4,8},{16,12},{12,16},{24,20},{20,24},{0,28},{29,1},{... | collective-permute-start | bytes 1179656 | tf_op jit(solution)/shard_map/ppermute | solution.py:423
  11.9 1.4 %collective-permute-start.2 = (f32[3,32,2,128]{3,2,1,0:T(2,128)S(1)}, f32[3,32,2,128]{3,2,1,0:T(2,128)S(1)}, u32[]{:S(2)}, u32[]{:S(2)}) collective-permute-start(f32[3,32,2,128]{3,2,1,0:T(2,128)S(1)} %get-tuple-element.14), channel_id=1, source_target_pairs={{1,0},{0,1},{3,2},{2,3},{5,4},{4,5},{7,6},{6,7},{9,8},{8,9},{11,10... | collective-permute-start | bytes 294920 | tf_op jit(solution)/shard_map/ppermute | solution.py:423
  13.3 4.5 %collective-permute-start.3 = (f32[3,32,2,128]{3,2,1,0:T(2,128)S(1)}, f32[3,32,2,128]{3,2,1,0:T(2,128)S(1)}, u32[]{:S(2)}, u32[]{:S(2)}) collective-permute-start(f32[3,32,2,128]{3,2,1,0:T(2,128)S(1)} %carried.1.refs_0_), channel_id=1, source_target_pairs={{3,0},{2,1},{1,2},{0,3},{7,4},{6,5},{5,6},{4,7},{11,8},{10,9},{9,1... | collective-permute-start | bytes 294920 | tf_op jit(solution)/shard_map/ppermute | solution.py:423
  14.8 8.0 %collective-permute-start.4 = (f32[128,128]{1,0:T(8,128)S(1)}, f32[128,128]{1,0:T(8,128)S(1)}, u32[]{:S(2)}, u32[]{:S(2)}) collective-permute-start(f32[128,128]{1,0:T(8,128)S(1)} %get-tuple-element.19), channel_id=1, source_target_pairs={{16,0},{20,4},{24,8},{28,12},{0,16},{4,20},{8,24},{12,28},{17,1},{... | collective-permute-start | bytes 196616 | tf_op jit(solution)/shard_map/ppermute | solution.py:423
  18.0 3.7 %collective-permute-start.5 = (f32[8,128]{1,0:T(8,128)S(1)}, f32[8,128]{1,0:T(8,128)S(1)}, u32[]{:S(2)}, u32[]{:S(2)}) collective-permute-start(f32[8,128]{1,0:T(8,128)S(1)} %get-tuple-element.20.refs_0_.mine_ref), channel_id=1, source_target_pairs={{8,0},{12,4},{0,8},{4,12},{24,16},{28,20},{16,24},{20,28},{9,1},{1... | collective-permute-start | bytes 12296 | tf_op jit(solution)/shard_map/ppermute | solution.py:423
  21.7 4.5 %collective-permute-start.6 = (f32[8,128]{1,0:T(8,128)S(1)}, f32[8,128]{1,0:T(8,128)S(1)}, u32[]{:S(2)}, u32[]{:S(2)}) collective-permute-start(f32[8,128]{1,0:T(8,128)S(1)} %merged.2._.mine_ref), channel_id=1, source_target_pairs={{16,0},{20,4},{24,8},{28,12},{0,16},{4,20},{8,24},{12,28},{17,1},{... | collective-permute-start | bytes 12296 | tf_op jit(solution)/shard_map/ppermute | solution.py:423
  26.2 4.1 %collective-permute-start.7 = (f32[8,128]{1,0:T(8,128)S(1)}, f32[8,128]{1,0:T(8,128)S(1)}, u32[]{:S(2)}, u32[]{:S(2)}) collective-permute-start(f32[8,128]{1,0:T(8,128)S(1)} %merged.3.top), channel_id=1, source_target_pairs={{4,0},{0,4},{12,8},{8,12},{20,16},{16,20},{28,24},{24,28},{5,1},{1... | collective-permute-start | bytes 12296 | tf_op jit(solution)/shard_map/ppermute | solution.py:423
  27.1 3.3 %collective-permute-start.9 = (f32[8,128]{1,0:T(8,128)S(1)}, f32[8,128]{1,0:T(8,128)S(1)}, u32[]{:S(2)}, u32[]{:S(2)}) collective-permute-start(f32[8,128]{1,0:T(8,128)S(1)} %get-tuple-element.23), channel_id=1, source_target_pairs={{3,0},{2,1},{1,2},{0,3},{7,4},{6,5},{5,6},{4,7},{11,8},{10,9},{9,1... | collective-permute-start | bytes 12296 | tf_op jit(solution)/shard_map/ppermute | solution.py:423
  27.7 2.6 %collective-permute-start.8 = (f32[8,128]{1,0:T(8,128)S(1)}, f32[8,128]{1,0:T(8,128)S(1)}, u32[]{:S(2)}, u32[]{:S(2)}) collective-permute-start(f32[8,128]{1,0:T(8,128)S(1)} %get-tuple-element.22._), channel_id=1, source_target_pairs={{1,0},{0,1},{3,2},{2,3},{5,4},{4,5},{7,6},{6,7},{9,8},{8,9},{11,10... | collective-permute-start | bytes 12296 | tf_op jit(solution)/shard_map/ppermute | solution.py:423

commit v21 on v20

--- a/solution.py
+++ b/solution.py
@@ -17,7 +17,7 @@
 PAD = 8
 HALO = 2
 BLOCK = 4
-GROUP = 4
+GROUP = 2
 UNROLL = 4
 
 (

time: 35.8 us -> 36.3 us (1.014)
  Pallas kernels: 18.9 us -> 19.4 us
    pallas_call x1, Pallas kernels: 3.47 us -> 3.97 us  [per_device(): call(functools.partial(first_pass, theta_step), 'first_pass', 0, out_shap...]
  transfers between devices with their start and end apart: 10 -> 10, of which waited for: 4 -> 4; matrix products, arithmetic and copies ran while one was open for 0% -> 0% of each run, Pallas kernels for 38% -> 39%
where the time goes in v21:
time: 36.3 us; the launch traced here: 36.1 us
  Pallas kernels  19.4 us (53%)
  starting transfers between devices  11.8 us (33%)
  waiting for transfers between devices  2.9 us (8%)
  local copies, waits for them, and re-layouts  1.18 us (3%)
  between operations  0.78 us (2%)
    ppermute x10, starting transfers between devices, routed(): return lax.ppermute(block, axis, [(source(i), i) for i in range(count)])  11.8 us
    pallas_call x1, Pallas kernels, per_device(): call(functools.partial(finish, spans), 'finish', 0, scratch=8, out_shape=...  5.28 us
    pallas_call x5, Pallas kernels, without_ghosts(): call(functools.partial(ahead, *spans[n], rounds), name, velocity.size * 2...  5.19 us
    pallas_call x2, Pallas kernels, with_ghosts(): call(functools.partial(ahead_with_ghosts, *spans[n]), f'span_{n}', veloci...  4.65 us
    pallas_call x1, Pallas kernels, per_device(): call(functools.partial(first_pass, theta_step), 'first_pass', 0, out_shap...  3.97 us
    ppermute x10, waiting for transfers between devices, routed(): return lax.ppermute(block, axis, [(source(i), i) for i in range(count)])  2.9 us
    dynamic_slice x1, local copies, waits for them, and re-layouts, per_device(): lax.dynamic_slice_in_dim(velocity, even_end, HALO, 1)  1.18 us
  transfers between devices with their start and end apart: 10, of which 4 were waited for; matrix products, arithmetic and copies ran while one was open for 0% of the time, Pallas kernels for 39%

profile of v21, /device:TPU:0, one launch (start us, length us, event | category | flops | bytes accessed | tf_op | source)
XLA Modules:
  0.0 36.1 jit_solution(7968573673844004814)
XLA Ops:
  0.6 0.0 copy-start
  0.7 1.2 %constant_dynamic-slice_fusion = (f32[3,2,128,128]{3,2,1,0:T(8,128)S(1)}, f32[3,2,128,128]{3,2,1,0:T(8,128)S(1)}) fusion(f32[3,32,128,128]{3,2,1,0:T(8,128)} %v_ref.1, s32[]{:T(128)S(6)} %select_n.18, s32[]{:T(128)S(6)} %select_n.17), kind=kLoop, calls=%fused_computation | loop fusion | bytes 1572872 | tf_op jit(solution)/shard_map/dynamic_slice | solution.py:472
  1.8 3.0 %collective-permute-start.1 = (f32[3,2,128,128]{3,2,1,0:T(8,128)S(1)}, f32[3,2,128,128]{3,2,1,0:T(8,128)S(1)}, u32[]{:S(2)}, u32[]{:S(2)}) collective-permute-start(f32[3,2,128,128]{3,2,1,0:T(8,128)S(1)} %get-tuple-element.26), channel_id=1, source_target_pairs={{4,0},{0,4},{12,8},{8,12},{20,16},{16,20},{28,24},{24,28},{5,1},{1... | collective-permute-start | bytes 1179656 | tf_op jit(solution)/shard_map/ppermute | solution.py:423
  4.9 3.5 %collective-permute-start = (f32[3,2,128,128]{3,2,1,0:T(8,128)S(1)}, f32[3,2,128,128]{3,2,1,0:T(8,128)S(1)}, u32[]{:S(2)}, u32[]{:S(2)}) collective-permute-start(f32[3,2,128,128]{3,2,1,0:T(8,128)S(1)} %get-tuple-element.27), channel_id=1, source_target_pairs={{28,0},{8,4},{4,8},{16,12},{12,16},{24,20},{20,24},{0,28},{29,1},{... | collective-permute-start | bytes 1179656 | tf_op jit(solution)/shard_map/ppermute | solution.py:423
  8.4 4.0 %first_pass.1 = (f32[3,36,144,128]{3,2,1,0:T(8,128)S(1)}, f32[3,32,2,128]{3,2,1,0:T(2,128)S(1)}, f32[3,32,2,128]{3,2,1,0:T(2,128)S(1)}, f32[128,128]{1,0:T(8,128)S(1)}, f32[8,128]{1,0:T(8,128)S(1)}) custom-call(f32[3,32,128,128]{3,2,1,0:T(8,128)} %v_ref.1), custom_call_target="tpu_custom_call" | custom-call | tf_op jit(solution)/shard_map/first_pass/pallas_call | solution.py:478
  12.4 0.1 collective-permute-start.2
  12.5 0.0 copy-done
  12.5 1.2 %span_0_middle.1._.refs_0_ = f32[3,4,128,128]{3,2,1,0:T(8,128)S(1)} custom-call(f32[3,36,144,128]{3,2,1,0:T(8,128)S(1)} %get-tuple-element.17.vel_ref.vel_in, f32[15,8,128]{2,1,0:T(8,128)S(1)} %copy-done, f32[8,128]{1,0:T(8,128)S(1)} %get-tuple-element.15.refs_0_.pay_ref), custom_call_target="tpu_custom_call" | custom-call | flops 3145728 | bytes 3145728 | tf_op jit(solution)/shard_map/span_0_middle/pallas_call | solution.py:495
  13.6 0.1 collective-permute-done.2.even_ref
  13.8 1.5 %collective-permute-start.3 = (f32[3,32,2,128]{3,2,1,0:T(2,128)S(1)}, f32[3,32,2,128]{3,2,1,0:T(2,128)S(1)}, u32[]{:S(2)}, u32[]{:S(2)}) collective-permute-start(f32[3,32,2,128]{3,2,1,0:T(2,128)S(1)} %carried.1.refs_0_), channel_id=1, source_target_pairs={{3,0},{2,1},{1,2},{0,3},{7,4},{6,5},{5,6},{4,7},{11,8},{10,9},{9,1... | collective-permute-start | bytes 294920 | tf_op jit(solution)/shard_map/ppermute | solution.py:423
  15.3 0.0 collective-permute-start.4
  15.3 1.1 %span_1_middle.1._.refs_0_ = f32[3,4,128,128]{3,2,1,0:T(8,128)S(1)} custom-call(f32[3,36,144,128]{3,2,1,0:T(8,128)S(1)} %get-tuple-element.17.vel_ref.vel_in, f32[15,8,128]{2,1,0:T(8,128)S(1)} %copy-done, f32[3,32,2,128]{3,2,1,0:T(2,128)S(1)} %carried.1.refs_0_), custom_call_target="tpu_custom_call" | custom-call | flops 3145728 | bytes 3145728 | tf_op jit(solution)/shard_map/span_1_middle/pallas_call | solution.py:495
  16.5 1.8 %collective-permute-done.3.odd_ref = f32[3,32,2,128]{3,2,1,0:T(2,128)S(1)} collective-permute-done((f32[3,32,2,128]{3,2,1,0:T(2,128)S(1)}, f32[3,32,2,128]{3,2,1,0:T(2,128)S(1)}, u32[]{:S(2)}, u32[]{:S(2)}) %collective-permute-start.3) | collective-permute-done | bytes 98336 | tf_op jit(solution)/shard_map/ppermute | solution.py:423
  18.3 0.2 fold.1
  18.5 0.1 collective-permute-start.5
  18.6 0.2 span_1_outer.1.refs_1_.refs_0_
  18.8 0.2 span_0_outer.1.refs_0_
  18.9 2.6 %span_2.1.refs_2_.refs_1_ = f32[3,8,128,128]{3,2,1,0:T(8,128)S(1)} custom-call(f32[3,36,144,128]{3,2,1,0:T(8,128)S(1)} %get-tuple-element.18.vel_ref.vel_in, f32[15,8,128]{2,1,0:T(8,128)S(1)} %copy-done, f32[8,128]{1,0:T(8,128)S(1)} %get-tuple-element.20.refs_0_.mine_ref), custom_call_target="tpu_custom_call" | custom-call | flops 3145728 | bytes 3145728 | tf_op jit(solution)/shard_map/span_2/pallas_call | solution.py:495
  21.5 0.7 %collective-permute-done.5.far_ref = f32[8,128]{1,0:T(8,128)S(1)} collective-permute-done((f32[8,128]{1,0:T(8,128)S(1)}, f32[8,128]{1,0:T(8,128)S(1)}, u32[]{:S(2)}, u32[]{:S(2)}) %collective-permute-start.5) | collective-permute-done | bytes 4128 | tf_op jit(solution)/shard_map/ppermute | solution.py:423
  22.2 1.1 %collective-permute-start.6 = (f32[8,128]{1,0:T(8,128)S(1)}, f32[8,128]{1,0:T(8,128)S(1)}, u32[]{:S(2)}, u32[]{:S(2)}) collective-permute-start(f32[8,128]{1,0:T(8,128)S(1)} %merged.2._.mine_ref), channel_id=1, source_target_pairs={{16,0},{20,4},{24,8},{28,12},{0,16},{4,20},{8,24},{12,28},{17,1},{... | collective-permute-start | bytes 12296 | tf_op jit(solution)/shard_map/ppermute | solution.py:423
  23.3 0.0 collective-permute-done.4.inner_ref
  23.3 3.1 %span_3.1._.refs_2_.refs_3_ = f32[3,8,128,128]{3,2,1,0:T(8,128)S(1)} custom-call(f32[3,36,144,128]{3,2,1,0:T(8,128)S(1)} %get-tuple-element.18.vel_ref.vel_in, f32[128,128]{1,0:T(8,128)S(1)} %collective-permute-done.4.inner_ref, f32[15,8,128]{2,1,0:T(8,128)S(1)} %copy-done, f32[8,128]{1,0:T(8,128)S(1)} %merged.2._.mine_ref), custom_call_target="tpu_custom_call" | custom-call | flops 3145728 | bytes 3145728 | tf_op jit(solution)/shard_map/span_3/pallas_call | solution.py:506
  26.4 0.3 collective-permute-done.6.far_ref
  26.7 0.8 %collective-permute-start.7 = (f32[8,128]{1,0:T(8,128)S(1)}, f32[8,128]{1,0:T(8,128)S(1)}, u32[]{:S(2)}, u32[]{:S(2)}) collective-permute-start(f32[8,128]{1,0:T(8,128)S(1)} %merged.3.top), channel_id=1, source_target_pairs={{4,0},{0,4},{12,8},{8,12},{20,16},{16,20},{28,24},{24,28},{5,1},{1... | collective-permute-start | bytes 12296 | tf_op jit(solution)/shard_map/ppermute | solution.py:423
  27.5 0.0 collective-permute-done.1.even_ref
  27.5 0.0 collective-permute-done.odd_ref
  27.5 0.1 theta_in.1
  27.6 0.7 %collective-permute-start.9 = (f32[8,128]{1,0:T(8,128)S(1)}, f32[8,128]{1,0:T(8,128)S(1)}, u32[]{:S(2)}, u32[]{:S(2)}) collective-permute-start(f32[8,128]{1,0:T(8,128)S(1)} %get-tuple-element.23), channel_id=1, source_target_pairs={{3,0},{2,1},{1,2},{0,3},{7,4},{6,5},{5,6},{4,7},{11,8},{10,9},{9,1... | collective-permute-start | bytes 12296 | tf_op jit(solution)/shard_map/ppermute | solution.py:423
  28.3 1.0 %collective-permute-start.8 = (f32[8,128]{1,0:T(8,128)S(1)}, f32[8,128]{1,0:T(8,128)S(1)}, u32[]{:S(2)}, u32[]{:S(2)}) collective-permute-start(f32[8,128]{1,0:T(8,128)S(1)} %get-tuple-element.22._), channel_id=1, source_target_pairs={{1,0},{0,1},{3,2},{2,3},{5,4},{4,5},{7,6},{6,7},{9,8},{8,9},{11,10... | collective-permute-start | bytes 12296 | tf_op jit(solution)/shard_map/ppermute | solution.py:423
  29.2 1.6 %span_4.1.refs_4_ = f32[3,4,128,128]{3,2,1,0:T(8,128)S(1)} custom-call(f32[3,36,144,128]{3,2,1,0:T(8,128)S(1)} %get-tuple-element.21.vel_ref.vel_in, f32[128,128]{1,0:T(8,128)S(1)} %collective-permute-done.4.inner_ref, f32[15,8,128]{2,1,0:T(8,128)S(1)} %copy-done, f32[8,128]{1,0:T(8,128)S(1)} %get-tuple-element.22._), custom_call_target="tpu_custom_call" | custom-call | flops 3145728 | bytes 3145728 | tf_op jit(solution)/shard_map/span_4/pallas_call | solution.py:506
  30.8 0.0 collective-permute-done.7.far
  30.8 0.0 collective-permute-done.9.odd
  30.8 0.0 collective-permute-done.8.even
  30.8 5.3 %finish.1 = (f32[3,32,128,128]{3,2,1,0:T(8,128)}, f32[1]{0:T(128)}, f32[3,36,144,128]{3,2,1,0:T(8,128)S(1)}) custom-call(f32[3,36,144,128]{3,2,1,0:T(8,128)S(1)} %get-tuple-element.21.vel_ref.vel_in, f32[128,128]{1,0:T(8,128)S(1)} %collective-permute-done.4.inner_ref, f32[15,8,128]{2,1,0:T(8,128)S(1)} %copy-done, ...), custom_call_target="tpu_custom_call", output_to_operand_aliasing={{2}: (0, {})} | custom-call | tf_op jit(solution)/shard_map/finish/pallas_call | solution.py:572
  (3 shorter events, 0.0 us)
Async XLA Ops:
  0.6 11.9 %copy-start = (f32[15,8,128]{2,1,0:T(8,128)S(1)}, f32[15,8,128]{2,1,0:T(8,128)}, u32[]{:S(2)}) copy-start(f32[15,8,128]{2,1,0:T(8,128)} %constant.28.clone.coef_ref) | copy-start | bytes 184324
  1.8 25.6 %collective-permute-start.1 = (f32[3,2,128,128]{3,2,1,0:T(8,128)S(1)}, f32[3,2,128,128]{3,2,1,0:T(8,128)S(1)}, u32[]{:S(2)}, u32[]{:S(2)}) collective-permute-start(f32[3,2,128,128]{3,2,1,0:T(8,128)S(1)} %get-tuple-element.26), channel_id=1, source_target_pairs={{4,0},{0,4},{12,8},{8,12},{20,16},{16,20},{28,24},{24,28},{5,1},{1... | collective-permute-start | bytes 1179656 | tf_op jit(solution)/shard_map/ppermute | solution.py:423
  4.9 22.6 %collective-permute-start = (f32[3,2,128,128]{3,2,1,0:T(8,128)S(1)}, f32[3,2,128,128]{3,2,1,0:T(8,128)S(1)}, u32[]{:S(2)}, u32[]{:S(2)}) collective-permute-start(f32[3,2,128,128]{3,2,1,0:T(8,128)S(1)} %get-tuple-element.27), channel_id=1, source_target_pairs={{28,0},{8,4},{4,8},{16,12},{12,16},{24,20},{20,24},{0,28},{29,1},{... | collective-permute-start | bytes 1179656 | tf_op jit(solution)/shard_map/ppermute | solution.py:423
  12.4 1.4 %collective-permute-start.2 = (f32[3,32,2,128]{3,2,1,0:T(2,128)S(1)}, f32[3,32,2,128]{3,2,1,0:T(2,128)S(1)}, u32[]{:S(2)}, u32[]{:S(2)}) collective-permute-start(f32[3,32,2,128]{3,2,1,0:T(2,128)S(1)} %get-tuple-element.14), channel_id=1, source_target_pairs={{1,0},{0,1},{3,2},{2,3},{5,4},{4,5},{7,6},{6,7},{9,8},{8,9},{11,10... | collective-permute-start | bytes 294920 | tf_op jit(solution)/shard_map/ppermute | solution.py:423
  13.8 4.5 %collective-permute-start.3 = (f32[3,32,2,128]{3,2,1,0:T(2,128)S(1)}, f32[3,32,2,128]{3,2,1,0:T(2,128)S(1)}, u32[]{:S(2)}, u32[]{:S(2)}) collective-permute-start(f32[3,32,2,128]{3,2,1,0:T(2,128)S(1)} %carried.1.refs_0_), channel_id=1, source_target_pairs={{3,0},{2,1},{1,2},{0,3},{7,4},{6,5},{5,6},{4,7},{11,8},{10,9},{9,1... | collective-permute-start | bytes 294920 | tf_op jit(solution)/shard_map/ppermute | solution.py:423
  15.3 8.0 %collective-permute-start.4 = (f32[128,128]{1,0:T(8,128)S(1)}, f32[128,128]{1,0:T(8,128)S(1)}, u32[]{:S(2)}, u32[]{:S(2)}) collective-permute-start(f32[128,128]{1,0:T(8,128)S(1)} %get-tuple-element.19), channel_id=1, source_target_pairs={{16,0},{20,4},{24,8},{28,12},{0,16},{4,20},{8,24},{12,28},{17,1},{... | collective-permute-start | bytes 196616 | tf_op jit(solution)/shard_map/ppermute | solution.py:423
  18.5 3.7 %collective-permute-start.5 = (f32[8,128]{1,0:T(8,128)S(1)}, f32[8,128]{1,0:T(8,128)S(1)}, u32[]{:S(2)}, u32[]{:S(2)}) collective-permute-start(f32[8,128]{1,0:T(8,128)S(1)} %get-tuple-element.20.refs_0_.mine_ref), channel_id=1, source_target_pairs={{8,0},{12,4},{0,8},{4,12},{24,16},{28,20},{16,24},{20,28},{9,1},{1... | collective-permute-start | bytes 12296 | tf_op jit(solution)/shard_map/ppermute | solution.py:423
  22.2 4.5 %collective-permute-start.6 = (f32[8,128]{1,0:T(8,128)S(1)}, f32[8,128]{1,0:T(8,128)S(1)}, u32[]{:S(2)}, u32[]{:S(2)}) collective-permute-start(f32[8,128]{1,0:T(8,128)S(1)} %merged.2._.mine_ref), channel_id=1, source_target_pairs={{16,0},{20,4},{24,8},{28,12},{0,16},{4,20},{8,24},{12,28},{17,1},{... | collective-permute-start | bytes 12296 | tf_op jit(solution)/shard_map/ppermute | solution.py:423
  26.7 4.1 %collective-permute-start.7 = (f32[8,128]{1,0:T(8,128)S(1)}, f32[8,128]{1,0:T(8,128)S(1)}, u32[]{:S(2)}, u32[]{:S(2)}) collective-permute-start(f32[8,128]{1,0:T(8,128)S(1)} %merged.3.top), channel_id=1, source_target_pairs={{4,0},{0,4},{12,8},{8,12},{20,16},{16,20},{28,24},{24,28},{5,1},{1... | collective-permute-start | bytes 12296 | tf_op jit(solution)/shard_map/ppermute | solution.py:423
  27.6 3.3 %collective-permute-start.9 = (f32[8,128]{1,0:T(8,128)S(1)}, f32[8,128]{1,0:T(8,128)S(1)}, u32[]{:S(2)}, u32[]{:S(2)}) collective-permute-start(f32[8,128]{1,0:T(8,128)S(1)} %get-tuple-element.23), channel_id=1, source_target_pairs={{3,0},{2,1},{1,2},{0,3},{7,4},{6,5},{5,6},{4,7},{11,8},{10,9},{9,1... | collective-permute-start | bytes 12296 | tf_op jit(solution)/shard_map/ppermute | solution.py:423
  28.3 2.6 %collective-permute-start.8 = (f32[8,128]{1,0:T(8,128)S(1)}, f32[8,128]{1,0:T(8,128)S(1)}, u32[]{:S(2)}, u32[]{:S(2)}) collective-permute-start(f32[8,128]{1,0:T(8,128)S(1)} %get-tuple-element.22._), channel_id=1, source_target_pairs={{1,0},{0,1},{3,2},{2,3},{5,4},{4,5},{7,6},{6,7},{9,8},{8,9},{11,10... | collective-permute-start | bytes 12296 | tf_op jit(solution)/shard_map/ppermute | solution.py:423
